TPU v7x, 256 devices: a whole 4x4x8 slice. The times are simulated.
256 devices in a mesh: dp: 64 (over x_hi, y, z), mp: 4 (over x_lo, core).
Axes of the slice: x: 4 (x_hi: 2, x_lo: 2; x = x_hi * 2 + x_lo), y: 4, z: 8, core: 2. Of those that a mesh axis runs over, the one named last changes fastest.
Arguments:
- head_out: bfloat16 [3, 8192, 4096], P(None, 'dp', 'mp'), may hold values from -6 to 6
- residual: bfloat16 [3, 8192, 4096], P(None, 'dp', 'mp'), may hold values from -6 to 6
- out_weight: bfloat16 [4096, 4096], P('dp', 'mp'), may hold values from -0.09375 to 0.09375
- strategy_table: bfloat16 [64, 4096], P(None, 'mp'), may hold values from -3 to 3
- meta_graph: int32 [64, 64], replicated, may hold values from 0 to 3, as said below
- strategy_ids: int32 [3, 8192], P(None, 'dp'), may hold values from 0 to 63
- cotangent: bfloat16 [3, 8192, 4096], P(None, 'dp', 'mp'), may hold values from -16 to 16
Outputs:
- layer_out: bfloat16 [3, 8192, 4096], P(None, 'dp', 'mp')
- head_grad: bfloat16 [3, 8192, 4096], P(None, 'dp', 'mp')
- weight_grad: float32 [4096, 4096], P('dp', 'mp')
- table_grad: float32 [64, 4096], P(None, 'mp')
Inputs may be any that keep to these rules, and one draw needn't show every extreme that they name: `meta_graph`: entries are zero on and above the diagonal; the last strategy meets the first with weight 3.
All inputs are finite; a program needn't handle non-finite values.
Results may differ from a plain program's by a relative error of at most 0.009.
Values may be sent and summed in bfloat16 or wider, within the bound.
No kernel may reach another device: no remote copies, remote signals or barrier semaphores. Data moves between devices by JAX's collectives and lax.ppermute only.
A program may use at most 128 MiB of HBM per device.

v0:
```python
import math

import jax
import jax.numpy as jnp
from jax import lax
from jax.sharding import PartitionSpec as P


def mixture(meta_graph):
    counts = meta_graph.astype(jnp.float32)
    totals = jnp.maximum(jnp.sum(counts, axis=1, keepdims=True), 1.0)
    return jnp.eye(meta_graph.shape[0], dtype=jnp.float32) + counts / totals


def on_device(head_out, residual, out_weight, strategy_table, meta_graph, strategy_ids, cotangent):
    highest = lax.Precision.HIGHEST
    batches, local_rows, head_cols = head_out.shape
    strategies = meta_graph.shape[0]
    mixing = mixture(meta_graph)
    table = jnp.dot(mixing, strategy_table.astype(jnp.float32), precision=highest)
    grad_scale = 1.0 / math.sqrt(batches * local_rows * lax.axis_size("dp"))
    model_width = out_weight.shape[0] * lax.axis_size("dp")
    full_weight = lax.all_gather(out_weight, "dp", axis=0, tiled=True)
    weight_acc = jnp.zeros((model_width, head_cols), jnp.float32)
    table_acc = jnp.zeros(table.shape, jnp.float32)
    outputs = []
    head_grads = []
    for batch in range(batches):
        current = head_out[batch]
        partial_sum = lax.dot_general(
            current, full_weight, (((1,), (1,)), ((), ())), preferred_element_type=jnp.float32
        )
        projected = lax.psum_scatter(
            partial_sum.astype(jnp.bfloat16), "mp", scatter_dimension=1, tiled=True
        ).astype(jnp.float32)
        one_hot = (
            strategy_ids[batch][:, None] == lax.broadcasted_iota(jnp.int32, (1, strategies), 1)
        ).astype(jnp.float32)
        gating = 1.0 + jnp.dot(one_hot, table, precision=highest)
        outputs.append(
            (residual[batch].astype(jnp.float32) + projected * gating).astype(jnp.bfloat16)
        )
        grad_local = (cotangent[batch].astype(jnp.float32) * gating).astype(jnp.bfloat16)
        full_grad = lax.all_gather(grad_local, "mp", axis=1, tiled=True)
        head_grad = jnp.dot(full_grad, full_weight, preferred_element_type=jnp.float32)
        head_grads.append(head_grad.astype(jnp.bfloat16))
        cond_grad = cotangent[batch].astype(jnp.float32) * projected
        table_acc = table_acc + lax.dot_general(
            one_hot,
            cond_grad,
            (((0,), (0,)), ((), ())),
            precision=highest,
            preferred_element_type=jnp.float32,
        )
        if batch + 1 < batches:
            weight_acc = weight_acc + lax.dot_general(
                full_grad, current, (((0,), (0,)), ((), ())), preferred_element_type=jnp.float32
            )
    weight_acc = weight_acc + lax.dot_general(
        full_grad, current, (((0,), (0,)), ((), ())), preferred_element_type=jnp.float32
    )
    weight_sum = lax.psum_scatter(weight_acc, "dp", scatter_dimension=0, tiled=True)
    table_sum = lax.psum(table_acc, "dp")
    table_grad = jnp.dot(mixing.T, table_sum, precision=highest) * grad_scale
    return (jnp.stack(outputs), jnp.stack(head_grads), weight_sum * grad_scale, table_grad)


def solution(mesh):
    placed = (
        P(None, "dp", "mp"),
        P(None, "dp", "mp"),
        P("dp", "mp"),
        P(None, "mp"),
        P(),
        P(None, "dp"),
        P(None, "dp", "mp"),
    )
    return jax.shard_map(
        on_device,
        mesh=mesh,
        in_specs=placed,
        out_specs=(P(None, "dp", "mp"), P(None, "dp", "mp"), P("dp", "mp"), P(None, "mp")),
        check_vma=False,
    )
```

profile of v0, /device:TPU:6, one launch (start us, length us, event | category | flops | bytes accessed | tf_op | source)
XLA Modules:
  0.0 1375.8 jit_solution(10051374428289011234)
XLA Ops:
  8.0 155.8 %all-gather.5.cloned.1.call-done = bf16[4096,1024]{1,0:T(8,128)(2,1)} async-done(((bf16[64,1024]{1,0:T(8,128)(2,1)}), bf16[4096,1024]{1,0:T(8,128)(2,1)}) %all-gather.5.cloned.1.call-update) | async-done | bytes 8388624 | tf_op jit(solution)/shard_map/all_gather | solution.py:23
  163.8 7.4 convolution_convert_fusion
  171.3 7.2 convolution_convert_fusion.1
  178.6 7.5 convolution_convert_fusion.2
  187.5 4.4 reduce-scatter.9.cloned.1.call-done
  191.9 26.7 %reduce-scatter.7.cloned.1.call-done = bf16[128,1024]{1,0:T(8,128)(2,1)} async-done(((bf16[128,4096]{1,0:T(8,128)(2,1)}), bf16[128,1024]{1,0:T(8,128)(2,1)}) %reduce-scatter.7.cloned.1.call-update) | async-done | bytes 262160 | tf_op jit(solution)/shard_map/reduce_scatter | solution.py:33
  218.6 26.2 %reduce-scatter.5.cloned.1.call-done = bf16[128,1024]{1,0:T(8,128)(2,1)} async-done(((bf16[128,4096]{1,0:T(8,128)(2,1)}), bf16[128,1024]{1,0:T(8,128)(2,1)}) %reduce-scatter.5.cloned.1.call-update) | async-done | bytes 262160 | tf_op jit(solution)/shard_map/reduce_scatter | solution.py:33
  244.8 2.9 fusion.15
  249.1 1.4 fusion.10
  250.5 1.4 convolution_add_fusion.4
  251.9 2.1 convolution_add_fusion.3
  254.3 18.1 %all-gather.9.cloned.1.call-done = bf16[128,4096]{1,0:T(8,128)(2,1)} async-done(((bf16[128,1024]{1,0:T(8,128)(2,1)}), bf16[128,4096]{1,0:T(8,128)(2,1)}) %all-gather.9.cloned.1.call-update) | async-done | bytes 1048592 | tf_op jit(solution)/shard_map/all_gather | solution.py:44
  272.3 9.3 fusion.21
  281.7 17.3 %all-gather.7.cloned.1.call-done = bf16[128,4096]{1,0:T(8,128)(2,1)} async-done(((bf16[128,1024]{1,0:T(8,128)(2,1)}), bf16[128,4096]{1,0:T(8,128)(2,1)}) %all-gather.7.cloned.1.call-update) | async-done | bytes 1048592 | tf_op jit(solution)/shard_map/all_gather | solution.py:44
  299.0 9.3 fusion.24
  308.3 17.4 %all-gather.11.cloned.1.call-done = bf16[128,4096]{1,0:T(8,128)(2,1)} async-done(((bf16[128,1024]{1,0:T(8,128)(2,1)}), bf16[128,4096]{1,0:T(8,128)(2,1)}) %all-gather.11.cloned.1.call-update) | async-done | bytes 1048592 | tf_op jit(solution)/shard_map/all_gather | solution.py:44
  325.7 18.5 %add_add_fusion = f32[4096,1024]{1,0:T(8,128)} fusion(f32[4096,1024]{1,0:T(8,128)} %fusion.24, f32[4096,1024]{1,0:T(8,128)} %fusion.21, bf16[128,4096]{1,0:T(8,128)(2,1)} %all-gather.11.cloned.1.call-done, bf16[3,128,1024]{2,1,0:T(8,128)(2,1)S(1)} %copy-done.5), kind=kOutput, calls=%fused_computation | convolution fusion | flops 1082130432 | bytes 51642368 | tf_op jit(solution)/shard_map/dot_general | solution.py:59
  346.1 622.6 %all-reduce.2.cloned.1.call-done = f32[64,1024]{1,0:T(8,128)} async-done(((f32[64,1024]{1,0:T(8,128)}), f32[64,1024]{1,0:T(8,128)}) %all-reduce.2.cloned.1.call-update) | async-done | bytes 262160 | tf_op jit(solution)/shard_map/psum | solution.py:63
  968.7 2.3 convolution_multiply_fusion
  971.0 4.8 fusion
  975.8 1.3 fusion.2
  977.2 1.3 fusion.1
  979.5 388.1 %reduce-scatter.11.cloned.1.call-done = f32[64,1024]{1,0:T(8,128)} async-done(((f32[4096,1024]{1,0:T(8,128)}), f32[64,1024]{1,0:T(8,128)}) %reduce-scatter.11.cloned.1.call-update) | async-done | bytes 262160 | tf_op jit(solution)/shard_map/reduce_scatter | solution.py:62
  1367.6 1.7 broadcast_multiply_fusion
  (53 shorter events, 6.7 us)
Async XLA Ops:
  7.2 179.2 %copy-start = (bf16[64,1024]{1,0:T(8,128)(2,1)S(1)}, bf16[64,1024]{1,0:T(8,128)(2,1)}, u32[]{:S(2)}) copy-start(bf16[64,1024]{1,0:T(8,128)(2,1)} %param.10) | copy-start | bytes 393220
  7.2 164.1 %copy-start.5 = (bf16[3,128,1024]{2,1,0:T(8,128)(2,1)S(1)}, bf16[3,128,1024]{2,1,0:T(8,128)(2,1)}, u32[]{:S(2)}) copy-start(bf16[3,128,1024]{2,1,0:T(8,128)(2,1)} %param.7) | copy-start | bytes 2359300
  7.2 156.6 %all-gather.5.cloned.1.call-start = ((), (), s32[]{:S(2)}) async-start(), calls=%async_computation.4 | async-start | bytes 8519680 | tf_op jit(solution)/shard_map/all_gather | solution.py:23
  7.9 184.0 %reduce-scatter.9.cloned.1.call-start = ((), (), s32[]{:S(2)}) async-start(), calls=%async_computation.7 | async-start | bytes 1310720 | tf_op jit(solution)/shard_map/reduce_scatter | solution.py:33
  171.2 15.0 %copy-start.8 = (s32[64,64]{1,0:T(8,128)S(1)}, s32[64,64]{1,0:T(8,128)}, u32[]{:S(2)}) copy-start(s32[64,64]{1,0:T(8,128)} %param.11) | copy-start | bytes 49156
  171.2 15.1 %copy-start.10 = (s32[3,128]{1,0:T(4,128)S(1)}, s32[3,128]{1,0:T(4,128)}, u32[]{:S(2)}) copy-start(s32[3,128]{1,0:T(4,128)} %param.12) | copy-start | bytes 4612
  171.2 47.3 %reduce-scatter.7.cloned.1.call-start = ((), (), s32[]{:S(2)}) async-start(), calls=%async_computation.6 | async-start | bytes 1310720 | tf_op jit(solution)/shard_map/reduce_scatter | solution.py:33
  178.5 66.3 %copy-start.6 = (bf16[3,128,1024]{2,1,0:T(8,128)(2,1)S(1)}, bf16[3,128,1024]{2,1,0:T(8,128)(2,1)}, u32[]{:S(2)}) copy-start(bf16[3,128,1024]{2,1,0:T(8,128)(2,1)} %param.13) | copy-start | bytes 2359300
  178.6 66.3 %reduce-scatter.5.cloned.1.call-start = ((), (), s32[]{:S(2)}) async-start(), calls=%async_computation.5 | async-start | bytes 1310720 | tf_op jit(solution)/shard_map/reduce_scatter | solution.py:33
  186.1 86.2 %all-gather.9.cloned.1.call-start = ((), (), s32[]{:S(2)}) async-start(), calls=%async_computation.9 | async-start | bytes 1310720 | tf_op jit(solution)/shard_map/all_gather | solution.py:44
  247.8 51.2 %all-gather.7.cloned.1.call-start = ((), (), s32[]{:S(2)}) async-start(), calls=%async_computation.8 | async-start | bytes 1310720 | tf_op jit(solution)/shard_map/all_gather | solution.py:44
  248.3 77.4 %all-gather.11.cloned.1.call-start = ((), (), s32[]{:S(2)}) async-start(), calls=%async_computation.10 | async-start | bytes 1310720 | tf_op jit(solution)/shard_map/all_gather | solution.py:44
  249.1 719.6 %all-reduce.2.cloned.1.call-start = ((), (), s32[]{:S(2)}) async-start(), calls=%async_computation.12 | async-start | bytes 524288 | tf_op jit(solution)/shard_map/psum | solution.py:63
  254.1 1113.5 %reduce-scatter.11.cloned.1.call-start = ((), (), s32[]{:S(2)}) async-start(), calls=%async_computation.11 | async-start | bytes 17039360 | tf_op jit(solution)/shard_map/reduce_scatter | solution.py:62
  344.2 0.9 copy-start.7
  344.2 624.5 %copy-start.9 = (s32[64,64]{1,0:T(8,128)S(1)}, s32[64,64]{1,0:T(8,128)}, u32[]{:S(2)}) copy-start(s32[64,64]{1,0:T(8,128)} %param.11) | copy-start | bytes 49156
  344.2 626.8 %copy-start.3 = (bf16[128,4096]{1,0:T(8,128)(2,1)S(1)}, bf16[128,4096]{1,0:T(8,128)(2,1)}, u32[]{:S(2)}) copy-start(bf16[128,4096]{1,0:T(8,128)(2,1)} %all-gather.7.cloned.1.call-done) | copy-start | bytes 3145732
  346.1 629.7 %copy-start.4 = (bf16[128,4096]{1,0:T(8,128)(2,1)S(1)}, bf16[128,4096]{1,0:T(8,128)(2,1)}, u32[]{:S(2)}) copy-start(bf16[128,4096]{1,0:T(8,128)(2,1)} %all-gather.11.cloned.1.call-done) | copy-start | bytes 3145732
  968.7 7.1 slice-start
  971.0 4.8 slice-start.1
  975.8 1.4 copy-start.2
  975.8 393.4 %copy-start.1 = (bf16[64,1024]{1,0:T(8,128)(2,1)S(1)}, bf16[64,1024]{1,0:T(8,128)(2,1)}, u32[]{:S(2)}) copy-start(bf16[64,1024]{1,0:T(8,128)(2,1)} %param.10) | copy-start | bytes 393220
Sparse Core Ops, SparseCore 0:
  11.8 151.9 all-gather.4
  171.3 20.5 reduce-scatter.8
  194.6 23.9 reduce-scatter.6
  221.0 23.7 reduce-scatter.4
  247.9 24.4 all-gather.8
  274.7 24.1 all-gather.6
  301.5 24.2 all-gather.10
  328.5 640.0 all-reduce.1
  971.2 396.3 reduce-scatter.10
where the time goes:
time: 1380 us
  waiting for transfers between devices  1280 us (93%)
  matrix products  77.9 us (6%)
  between operations  14.1 us (1%)
    psum x1, waiting for transfers between devices, on_device(): table_sum = lax.psum(table_acc, 'dp')  623 us
    reduce_scatter x1, waiting for transfers between devices, on_device(): lax.psum_scatter(weight_acc, 'dp', scatter_dimension=0, tiled=True)  388 us
    all_gather x1, waiting for transfers between devices, on_device(): full_weight = lax.all_gather(out_weight, 'dp', axis=0, tiled=True)  156 us
    reduce_scatter x3, waiting for transfers between devices, on_device(): lax.psum_scatter(partial_sum.astype(jnp.bfloat16), 'mp', scatter_dimensio...  57.3 us
    all_gather x3, waiting for transfers between devices, on_device(): full_grad = lax.all_gather(grad_local, 'mp', axis=1, tiled=True)  52.8 us
    dot_general x3, matrix products, on_device(): lax.dot_general(full_grad, current, (((0,), (0,)), ((), ())), preferred_e...  37.1 us
  transfers between devices with their start and end apart: 9, of which 9 were waited for; matrix products, arithmetic and copies ran while one was open for 5% of the time, Pallas kernels for 0%

commit v1 on v0

v1 whole, which is shorter than its diff:
```python
import math

import jax
import jax.numpy as jnp
from jax import lax
from jax.sharding import Mesh, PartitionSpec as P

XH, NY, NZ, XL, NC = 2, 4, 8, 2, 2
BF = jnp.bfloat16
F32 = jnp.float32
HIGHEST = lax.Precision.HIGHEST


def swap(a, axis):
    return lax.ppermute(a, axis, [(0, 1), (1, 0)])


def exchange(a, axis):
    return lax.all_to_all(a, axis, 0, 0, tiled=True)


def spread(a, axis, n):
    return exchange(jnp.broadcast_to(a[None], (n,) + a.shape), axis)


def pick(a, at, dim):
    return lax.dynamic_index_in_dim(a, at, dim, keepdims=False)


def in_order(index, own, other, dim):
    first = jnp.where(index == 0, own, other)
    second = jnp.where(index == 0, other, own)
    return jnp.stack([first, second], axis=dim)


def mixture(meta_graph):
    counts = meta_graph.astype(F32)
    totals = jnp.maximum(jnp.sum(counts, axis=1, keepdims=True), 1.0)
    return jnp.eye(meta_graph.shape[0], dtype=F32) + counts / totals


def members(ids, strategies):
    return (lax.broadcasted_iota(jnp.int32, (strategies, 1), 0) == ids[None, :]).astype(F32)


def rows_of(one_hot, table):
    return lax.dot_general(one_hot, table, (((0,), (0,)), ((), ())), precision=HIGHEST, preferred_element_type=F32)


def on_device(head_out, residual, out_weight, strategy_table, meta_graph, strategy_ids, cotangent):
    batches, local_rows, cols = head_out.shape
    rows, half, wide = batches * local_rows, batches * local_rows // 2, cols // 2
    strategies = meta_graph.shape[0]
    wr = out_weight.shape[0]
    pad = 16
    xh, y, xl, c = (lax.axis_index(name) for name in ("xh", "y", "xl", "c"))
    grad_scale = 1.0 / math.sqrt(rows * XH * NY * NZ)

    ho = head_out.reshape(rows, cols)
    cot = cotangent.reshape(rows, cols)
    ids = strategy_ids.reshape(rows)

    cot_parts = cot.reshape(NC, half, cols)
    other = swap(pick(cot_parts, 1 - c, 0), "c")
    mine = in_order(c, pick(cot_parts, c, 0), other, 0)
    by_y = mine.reshape(NC, half, 2, wide).transpose(0, 2, 1, 3).reshape(NY, half, wide)
    tag = pick(ids.reshape(NC, half), c, 0).astype(BF)
    tag = jnp.broadcast_to(jnp.pad(tag, (0, wide - half))[None, None], (NY, pad, wide))
    got = exchange(jnp.concatenate([by_y, tag], axis=1), "y")
    cot_y = got[:, :half].reshape(NY * half, wide)
    ids_y = got[:, half, :half].astype(jnp.int32).reshape(NY * half)

    ho_y = spread(ho, "y", NY).reshape(NY * rows, cols)

    unit = in_order(xh, out_weight, swap(out_weight, "xh"), 0)
    weight = lax.all_gather(unit, "z", axis=1, tiled=True).reshape(cols, cols)

    mixing = mixture(meta_graph)
    table = jnp.dot(mixing, strategy_table.astype(F32), precision=HIGHEST)
    there = swap(strategy_table, "c")
    owner = jnp.where(y // 2 == c, strategy_table, there).reshape(strategies, 2, wide)
    table_y = jnp.dot(mixing, pick(owner, y % 2, 1).astype(F32), precision=HIGHEST)
    hot_y = members(ids_y, strategies)
    gating_y = 1.0 + rows_of(hot_y, table_y)
    grad_y = (cot_y.astype(F32) * gating_y).astype(BF)

    both = jnp.concatenate([jnp.where(xl == 0, grad_y, far) if i == 0 else jnp.where(xl == 0, far, grad_y)
                            for i, far in enumerate([swap(grad_y, "xl")] * 2)], axis=1)
    grads = in_order(c, both.reshape(NY, half, cols), swap(both, "c").reshape(NY, half, cols), 1)
    grads = grads.reshape(NY * rows, cols)

    partial_sum = lax.dot_general(ho_y, weight, (((1,), (1,)), ((), ())), preferred_element_type=F32)
    parts = partial_sum.astype(BF).reshape(NY, NC, half, cols)
    chip = pick(parts, c, 1).astype(F32) + swap(pick(parts, 1 - c, 1), "c").astype(F32)
    chip = chip.reshape(NY * half, XL, wide)
    away = swap(pick(chip, 1 - xl, 1).astype(BF), "xl")
    projected = pick(chip, xl, 1) + away.astype(F32)

    table_part = jnp.dot(hot_y, cot_y.astype(F32) * projected, precision=HIGHEST)
    table_part = table_part.reshape(NC, strategies // NC, wide)
    table_sum = pick(table_part, c, 0) + swap(pick(table_part, 1 - c, 0), "c")
    table_sum = table_sum + swap(table_sum, "xh")
    table_sum = jnp.sum(spread(table_sum, "z", NZ), axis=0)
    table_all = spread(table_sum, "y", NY).reshape(NC, 2, strategies // NC, wide)
    rest = swap(pick(table_all, 1 - c, 0), "c")
    table_sum = in_order(c, pick(table_all, c, 0), rest, 1)
    table_sum = table_sum.reshape(2, strategies, wide).transpose(1, 0, 2).reshape(strategies, cols)
    table_grad = jnp.dot(mixing.T, table_sum, precision=HIGHEST) * grad_scale

    home = exchange(projected.astype(BF).reshape(NY, half, wide), "y")
    home = home.reshape(NC, 2, half, wide)
    back = swap(pick(home, 1 - c, 0), "c")
    proj = in_order(c, pick(home, c, 0), back, 1).reshape(2, rows, wide)
    gating = 1.0 + rows_of(members(ids, strategies), table)
    proj = jnp.concatenate([proj[0], proj[1]], axis=1).astype(F32)
    layer_out = (residual.reshape(rows, cols).astype(F32) + proj * gating).astype(BF)

    head_grad = jnp.dot(grads, weight, preferred_element_type=F32).astype(BF)
    head_grad = exchange(head_grad.reshape(NY, rows, cols), "y").astype(F32)
    head_grad = jnp.sum(head_grad, axis=0).astype(BF)

    wg = lax.dot_general(grads, ho_y, (((0,), (0,)), ((), ())), preferred_element_type=F32).astype(BF)
    wg = lax.psum_scatter(wg.reshape(XH, NZ * wr, cols), "z", scatter_dimension=1, tiled=True)
    weight_sum = pick(wg, xh, 0).astype(F32) + swap(pick(wg, 1 - xh, 0), "xh").astype(F32)

    shape = head_out.shape
    return layer_out.reshape(shape), head_grad.reshape(shape), weight_sum * grad_scale, table_grad


def solution(mesh):
    fine = Mesh(mesh.devices.reshape(XH, NY, NZ, XL, NC), ("xh", "y", "z", "xl", "c"))
    dp, mp = ("xh", "y", "z"), ("xl", "c")
    tokens = P(None, dp, mp)
    return jax.shard_map(
        on_device,
        mesh=fine,
        in_specs=(tokens, tokens, P(dp, mp), P(None, mp), P(), P(None, dp), tokens),
        out_specs=(tokens, tokens, P(dp, mp), P(None, mp)),
        check_vma=False,
    )
```

time: 1380 us -> 223 us (0.16)
  the two profiles are of different devices: /device:TPU:6 before, /device:TPU:1 now
where the time goes in v1:
time: 223 us; the launch traced here: 222 us
  waiting for transfers between devices  60.9 us (27%)
  starting transfers between devices  57 us (26%)
  local copies, waits for them, and re-layouts  35.4 us (16%)
  matrix products  29.1 us (13%)
  other arithmetic  25.3 us (11%)
  between operations  14.4 us (6%)
    ppermute x12, waiting for transfers between devices, swap(): return lax.ppermute(a, axis, [(0, 1), (1, 0)])  33.8 us
    all_to_all x6, starting transfers between devices, exchange(): return lax.all_to_all(a, axis, 0, 0, tiled=True)  29.4 us
    ppermute x12, starting transfers between devices, swap(): return lax.ppermute(a, axis, [(0, 1), (1, 0)])  27.6 us
    all_to_all x6, waiting for transfers between devices, exchange(): return lax.all_to_all(a, axis, 0, 0, tiled=True)  27.1 us
    dot_general x1, matrix products, on_device(): lax.dot_general(grads, ho_y, (((0,), (0,)), ((), ())), preferred_element_...  7.67 us
    dot_general x1, matrix products, on_device(): lax.dot_general(ho_y, weight, (((1,), (1,)), ((), ())), preferred_element...  7.64 us
    dot_general x1, matrix products, on_device(): head_grad = jnp.dot(grads, weight, preferred_element_type=F32).astype(BF)  6.44 us
    squeeze x6, local copies, waits for them, and re-layouts, pick(): return lax.dynamic_index_in_dim(a, at, dim, keepdims=False)  5.81 us
  transfers between devices with their start and end apart: 20, of which 11 were waited for; matrix products, arithmetic and copies ran while one was open for 32% of the time, Pallas kernels for 0%

profile of v1, /device:TPU:1, one launch (start us, length us, event | category | flops | bytes accessed | tf_op | source)
XLA Modules:
  0.0 222.2 jit_solution(416264249081806633)
XLA Ops:
  7.2 3.7 %collective-permute-start = (bf16[64,1024]{1,0:T(8,128)(2,1)}, bf16[64,1024]{1,0:T(8,128)(2,1)S(1)}, u32[]{:S(2)}, u32[]{:S(2)}) collective-permute-start(bf16[64,1024]{1,0:T(8,128)(2,1)} %param.9), channel_id=1, source_target_pairs={{0,128},{128,0},{1,129},{129,1},{2,130},{130,2},{3,131},{131,3},{4... | collective-permute-start | bytes 393224 | tf_op jit(solution)/shard_map/ppermute | solution.py:15
  16.8 4.3 %all-to-all-start.2 = ((bf16[4,208,512]{2,1,0:T(8,128)(2,1)}), bf16[4,208,512]{2,1,0:T(8,128)(2,1)S(1)}, u32[]{:S(2)}, u32[]{:S(2)}) async-start(bf16[4,208,512]{2,1,0:T(8,128)(2,1)} %pad_maximum_fusion.2), calls=%async_computation.2 | async-start | bytes 1703936 | tf_op jit(solution)/shard_map/all_to_all | solution.py:19
  22.4 9.6 %all-to-all-done.2 = bf16[4,208,512]{2,1,0:T(8,128)(2,1)S(1)} async-done(((bf16[4,208,512]{2,1,0:T(8,128)(2,1)}), bf16[4,208,512]{2,1,0:T(8,128)(2,1)S(1)}, u32[]{:S(2)}, u32[]{:S(2)}) %all-to-all-start.2) | async-done | bytes 852000 | tf_op jit(solution)/shard_map/all_to_all | solution.py:19
  37.5 4.6 %all-to-all-start = ((bf16[4,384,1024]{2,1,0:T(8,128)(2,1)}), bf16[4,384,1024]{2,1,0:T(8,128)(2,1)}, u32[]{:S(2)}, u32[]{:S(2)}) async-start(bf16[4,384,1024]{2,1,0:T(8,128)(2,1)} %broadcast_in_dim.11), calls=%async_computation | async-start | bytes 6291456 | tf_op jit(solution)/shard_map/all_to_all | solution.py:19
  42.1 8.9 %collective-permute-done.6 = bf16[768,512]{0,1:T(8,128)(2,1)} collective-permute-done((bf16[768,512]{0,1:T(8,128)(2,1)}, bf16[768,512]{0,1:T(8,128)(2,1)}, u32[]{:S(2)}, u32[]{:S(2)}) %collective-permute-start.6) | collective-permute-done | bytes 786464 | tf_op jit(solution)/shard_map/ppermute | solution.py:15
  53.8 4.0 %collective-permute-start.7 = (bf16[768,1024]{0,1:T(8,128)(2,1)}, bf16[768,1024]{0,1:T(8,128)(2,1)}, u32[]{:S(2)}, u32[]{:S(2)}) collective-permute-start(bf16[768,1024]{0,1:T(8,128)(2,1)} %pad_maximum_fusion.1), channel_id=1, source_target_pairs={{0,1},{1,0},{2,3},{3,2},{4,5},{5,4},{6,7},{7,6},{8,9},{9,8},{10,11... | collective-permute-start | bytes 4718600 | tf_op jit(solution)/shard_map/ppermute | solution.py:15
  57.8 3.4 %collective-permute-done.7 = bf16[768,1024]{0,1:T(8,128)(2,1)} collective-permute-done((bf16[768,1024]{0,1:T(8,128)(2,1)}, bf16[768,1024]{0,1:T(8,128)(2,1)}, u32[]{:S(2)}, u32[]{:S(2)}) %collective-permute-start.7) | collective-permute-done | bytes 1572896 | tf_op jit(solution)/shard_map/ppermute | solution.py:15
  61.2 3.8 %broadcast_select_fusion.1 = (bf16[768,1024]{0,1:T(8,128)(2,1)}, bf16[768,1024]{0,1:T(8,128)(2,1)}) fusion(bf16[768,1024]{0,1:T(8,128)(2,1)} %collective-permute-done.7, pred[]{:T(512)S(6)} %eq.26, bf16[768,512]{0,1:T(8,128)(2,1)S(1)} %get-tuple-element.7, bf16[768,512]{0,1:T(8,128)(2,1)S(1)} %get-tuple-element.6), kind=kLoop, calls=%fused_computation.16 | loop fusion | flops 4718592 | bytes 6291457 | tf_op jit(solution)/shard_map/jit(_where)/select_n | solution.py:31
  76.5 7.6 %fusion = bf16[1536,1024]{0,1:T(8,128)(2,1)} fusion(bf16[1024,1024]{1,0:T(8,128)(2,1)} %bitcast.139, bf16[1536,1024]{1,0:T(8,128)(2,1)} %bitcast.5), kind=kOutput, calls=%fused_computation.2 | convolution fusion | flops 3222798336 | bytes 8388608 | tf_op jit(solution)/shard_map/dot_general | solution.py:92
  84.1 4.6 %copy.31 = bf16[1536,1024]{1,0:T(8,128)(2,1)} copy(bf16[1536,1024]{0,1:T(8,128)(2,1)} %fusion) | data formatting | bytes 6291456 | tf_op jit(solution)/shard_map/convert_element_type | solution.py:93
  91.6 4.2 %collective-permute-start.1 = (bf16[4,192,1024]{2,1,0:T(8,128)(2,1)}, bf16[4,192,1024]{2,1,0:T(8,128)(2,1)S(1)}, u32[]{:S(2)}, u32[]{:S(2)}) collective-permute-start(bf16[4,192,1024]{2,1,0:T(8,128)(2,1)} %dynamic-slice_bitcast_fusion), channel_id=1, source_target_pairs={{0,1},{1,0},{2,3},{3,2},{4,5},{5,4},{6,7},{7,6},{8,9},{9,8},{10,11... | collective-permute-start | bytes 4718600 | tf_op jit(solution)/shard_map/ppermute | solution.py:15
  95.8 6.4 %convolution_convert_fusion = bf16[1536,1024]{1,0:T(8,128)(2,1)} fusion(bf16[1536,1024]{1,0:T(8,128)(2,1)S(1)} %bitcast.122, bf16[1024,1024]{1,0:T(8,128)(2,1)} %bitcast.140), kind=kOutput, calls=%fused_computation | convolution fusion | flops 3222798336 | bytes 8388608 | tf_op jit(solution)/shard_map/dot_general | solution.py:118
  102.3 4.7 %all-to-all-start.3 = ((bf16[4,384,1024]{2,1,0:T(8,128)(2,1)}), bf16[4,384,1024]{2,1,0:T(8,128)(2,1)}, u32[]{:S(2)}, u32[]{:S(2)}) async-start(bf16[4,384,1024]{2,1,0:T(8,128)(2,1)} %bitcast.120), calls=%async_computation.3 | async-start | bytes 6291456 | tf_op jit(solution)/shard_map/all_to_all | solution.py:19
  107.0 7.7 %convolution_convert_fusion.2 = bf16[1024,1024]{1,0:T(8,128)(2,1)} fusion(bf16[1536,1024]{1,0:T(8,128)(2,1)} %bitcast.121, bf16[1536,1024]{1,0:T(8,128)(2,1)} %bitcast.5), kind=kOutput, calls=%fused_computation.5 | convolution fusion | flops 3222274048 | bytes 8388608 | tf_op jit(solution)/shard_map/dot_general | solution.py:122
  114.7 3.7 %convert_add_fusion = f32[4,192,1024]{2,1,0:T(8,128)} fusion(bf16[4,192,1024]{2,1,0:T(8,128)(2,1)S(1)} %collective-permute-done.1, bf16[4,2,192,1024]{3,2,1,0:T(8,128)(2,1)} %bitcast.117, s32[]{:T(128)S(6)} %select_n.152), kind=kLoop, calls=%fused_computation.4 | loop fusion | flops 2359296 | bytes 6291460 | tf_op jit(solution)/shard_map/add | solution.py:94
  118.4 5.6 %reshape.136 = f32[768,2,512]{2,1,0:T(2,128)} reshape(f32[4,192,1024]{2,1,0:T(8,128)} %convert_add_fusion) | data formatting | bytes 6291456 | tf_op jit(solution)/shard_map/reshape | solution.py:95
  132.3 15.5 %collective-permute-done.2 = bf16[768,512]{1,0:T(8,128)(2,1)} collective-permute-done((bf16[768,512]{1,0:T(8,128)(2,1)}, bf16[768,512]{1,0:T(8,128)(2,1)}, u32[]{:S(2)}, u32[]{:S(2)}) %collective-permute-start.2) | collective-permute-done | bytes 786464 | tf_op jit(solution)/shard_map/ppermute | solution.py:15
  150.1 4.2 %all-to-all-start.1 = ((bf16[4,192,512]{2,1,0:T(8,128)(2,1)}), bf16[4,192,512]{2,1,0:T(8,128)(2,1)}, u32[]{:S(2)}, u32[]{:S(2)}) async-start(bf16[4,192,512]{2,1,0:T(8,128)(2,1)} %bitcast.123), calls=%async_computation.1 | async-start | bytes 1572864 | tf_op jit(solution)/shard_map/all_to_all | solution.py:19
  166.5 8.2 %all-to-all-start.4 = ((f32[8,32,512]{2,1,0:T(8,128)}), f32[8,32,512]{2,1,0:T(8,128)S(1)}, u32[]{:S(2)}, u32[]{:S(2)}) async-start(f32[8,32,512]{2,1,0:T(8,128)} %broadcast_in_dim.13), calls=%async_computation.5 | async-start | bytes 1048576 | tf_op jit(solution)/shard_map/all_to_all | solution.py:19
  178.4 3.6 %reduce_sum.31 = bf16[384,1024]{1,0:T(8,128)(2,1)} reduce(bf16[4,384,1024]{2,1,0:T(8,128)(2,1)} %all-to-all-done.3, bf16[]{:T(256)} %constant.102.clone.1), dimensions={0}, to_apply=%region_1.2 | reduce | flops 1179648 | bytes 3932162 | tf_op jit(solution)/shard_map/reduce_sum | solution.py:120
  182.1 7.9 %all-to-all-done.4 = f32[8,32,512]{2,1,0:T(8,128)S(1)} async-done(((f32[8,32,512]{2,1,0:T(8,128)}), f32[8,32,512]{2,1,0:T(8,128)S(1)}, u32[]{:S(2)}, u32[]{:S(2)}) %all-to-all-start.4) | async-done | bytes 524320 | tf_op jit(solution)/shard_map/all_to_all | solution.py:19
  190.8 3.4 %all-to-all-start.5 = ((f32[4,32,512]{2,1,0:T(8,128)}), f32[4,32,512]{2,1,0:T(8,128)S(1)}, u32[]{:S(2)}, u32[]{:S(2)}) async-start(f32[4,32,512]{2,1,0:T(8,128)} %broadcast_in_dim.14), calls=%async_computation.6 | async-start | bytes 524288 | tf_op jit(solution)/shard_map/all_to_all | solution.py:19
  195.4 4.3 %all-to-all-done.5 = f32[4,32,512]{2,1,0:T(8,128)S(1)} async-done(((f32[4,32,512]{2,1,0:T(8,128)}), f32[4,32,512]{2,1,0:T(8,128)S(1)}, u32[]{:S(2)}, u32[]{:S(2)}) %all-to-all-start.5) | async-done | bytes 262176 | tf_op jit(solution)/shard_map/all_to_all | solution.py:19
  199.7 4.4 %collective-permute-start.11 = (f32[2,32,512]{2,1,0:T(8,128)S(1)}, f32[2,32,512]{2,1,0:T(8,128)S(1)}, u32[]{:S(2)}, u32[]{:S(2)}) collective-permute-start(f32[2,32,512]{2,1,0:T(8,128)S(1)} %dynamic-slice_bitcast_fusion.3), channel_id=1, source_target_pairs={{0,1},{1,0},{2,3},{3,2},{4,5},{5,4},{6,7},{7,6},{8,9},{9,8},{10,11... | collective-permute-start | bytes 393224 | tf_op jit(solution)/shard_map/ppermute | solution.py:15
  (96 shorter events, 69.5 us)
Async XLA Ops:
  7.2 8.4 %copy-start.2 = (bf16[3,128,1024]{2,1,0:T(8,128)(2,1)S(1)}, bf16[3,128,1024]{2,1,0:T(8,128)(2,1)}, u32[]{:S(2)}) copy-start(bf16[3,128,1024]{2,1,0:T(8,128)(2,1)} %param.13) | copy-start | bytes 2359300
  7.2 7.5 %collective-permute-start = (bf16[64,1024]{1,0:T(8,128)(2,1)}, bf16[64,1024]{1,0:T(8,128)(2,1)S(1)}, u32[]{:S(2)}, u32[]{:S(2)}) collective-permute-start(bf16[64,1024]{1,0:T(8,128)(2,1)} %param.9), channel_id=1, source_target_pairs={{0,128},{128,0},{1,129},{129,1},{2,130},{130,2},{3,131},{131,3},{4... | collective-permute-start | bytes 393224 | tf_op jit(solution)/shard_map/ppermute | solution.py:15
  10.8 11.0 %collective-permute-start.5 = (bf16[64,1024]{1,0:T(8,128)(2,1)}, bf16[64,1024]{1,0:T(8,128)(2,1)S(1)}, u32[]{:S(2)}, u32[]{:S(2)}) collective-permute-start(bf16[64,1024]{1,0:T(8,128)(2,1)} %param.10), channel_id=1, source_target_pairs={{0,1},{1,0},{2,3},{3,2},{4,5},{5,4},{6,7},{7,6},{8,9},{9,8},{10,11... | collective-permute-start | bytes 393224 | tf_op jit(solution)/shard_map/ppermute | solution.py:15
  12.8 2.8 %collective-permute-start.4 = (bf16[192,1024]{1,0:T(8,128)(2,1)S(1)}, bf16[192,1024]{1,0:T(8,128)(2,1)S(1)}, u32[]{:S(2)}, u32[]{:S(2)}) collective-permute-start(bf16[192,1024]{1,0:T(8,128)(2,1)S(1)} %dynamic-slice_bitcast_fusion.1), channel_id=1, source_target_pairs={{0,1},{1,0},{2,3},{3,2},{4,5},{5,4},{6,7},{7,6},{8,9},{9,8},{10,11... | collective-permute-start | bytes 1179656 | tf_op jit(solution)/shard_map/ppermute | solution.py:15
  16.8 15.2 %all-to-all-start.2 = ((bf16[4,208,512]{2,1,0:T(8,128)(2,1)}), bf16[4,208,512]{2,1,0:T(8,128)(2,1)S(1)}, u32[]{:S(2)}, u32[]{:S(2)}) async-start(bf16[4,208,512]{2,1,0:T(8,128)(2,1)} %pad_maximum_fusion.2), calls=%async_computation.2 | async-start | bytes 1703936 | tf_op jit(solution)/shard_map/all_to_all | solution.py:19
  21.1 55.3 %all-gather.2.cloned.1.call-start = ((), (), s32[]{:S(2)}) async-start(), calls=%async_computation.7 | async-start | bytes 2359296 | tf_op jit(solution)/shard_map/all_gather | solution.py:76
  34.7 16.3 %collective-permute-start.6 = (bf16[768,512]{0,1:T(8,128)(2,1)}, bf16[768,512]{0,1:T(8,128)(2,1)}, u32[]{:S(2)}, u32[]{:S(2)}) collective-permute-start(bf16[768,512]{0,1:T(8,128)(2,1)} %multiply_convert_fusion), channel_id=1, source_target_pairs={{0,2},{2,0},{1,3},{3,1},{4,6},{6,4},{5,7},{7,5},{8,10},{10,8},{9,1... | collective-permute-start | bytes 2359304 | tf_op jit(solution)/shard_map/ppermute | solution.py:15
  37.5 39.0 %all-to-all-start = ((bf16[4,384,1024]{2,1,0:T(8,128)(2,1)}), bf16[4,384,1024]{2,1,0:T(8,128)(2,1)}, u32[]{:S(2)}, u32[]{:S(2)}) async-start(bf16[4,384,1024]{2,1,0:T(8,128)(2,1)} %broadcast_in_dim.11), calls=%async_computation | async-start | bytes 6291456 | tf_op jit(solution)/shard_map/all_to_all | solution.py:19
  53.8 7.4 %collective-permute-start.7 = (bf16[768,1024]{0,1:T(8,128)(2,1)}, bf16[768,1024]{0,1:T(8,128)(2,1)}, u32[]{:S(2)}, u32[]{:S(2)}) collective-permute-start(bf16[768,1024]{0,1:T(8,128)(2,1)} %pad_maximum_fusion.1), channel_id=1, source_target_pairs={{0,1},{1,0},{2,3},{3,2},{4,5},{5,4},{6,7},{7,6},{8,9},{9,8},{10,11... | collective-permute-start | bytes 4718600 | tf_op jit(solution)/shard_map/ppermute | solution.py:15
  88.7 7.1 %copy-start.1 = (bf16[4,2,192,1024]{3,2,1,0:T(8,128)(2,1)S(1)}, bf16[4,2,192,1024]{3,2,1,0:T(8,128)(2,1)}, u32[]{:S(2)}) copy-start(bf16[4,2,192,1024]{3,2,1,0:T(8,128)(2,1)} %copy.36) | copy-start | bytes 9437188
  91.6 23.1 %collective-permute-start.1 = (bf16[4,192,1024]{2,1,0:T(8,128)(2,1)}, bf16[4,192,1024]{2,1,0:T(8,128)(2,1)S(1)}, u32[]{:S(2)}, u32[]{:S(2)}) collective-permute-start(bf16[4,192,1024]{2,1,0:T(8,128)(2,1)} %dynamic-slice_bitcast_fusion), channel_id=1, source_target_pairs={{0,1},{1,0},{2,3},{3,2},{4,5},{5,4},{6,7},{7,6},{8,9},{9,8},{10,11... | collective-permute-start | bytes 4718600 | tf_op jit(solution)/shard_map/ppermute | solution.py:15
  102.3 47.9 %all-to-all-start.3 = ((bf16[4,384,1024]{2,1,0:T(8,128)(2,1)}), bf16[4,384,1024]{2,1,0:T(8,128)(2,1)}, u32[]{:S(2)}, u32[]{:S(2)}) async-start(bf16[4,384,1024]{2,1,0:T(8,128)(2,1)} %bitcast.120), calls=%async_computation.3 | async-start | bytes 6291456 | tf_op jit(solution)/shard_map/all_to_all | solution.py:19
  106.9 99.2 %reduce-scatter.2.cloned.1.call-start = ((), (), s32[]{:S(2)}) async-start(), calls=%async_computation.8 | async-start | bytes 2359296 | tf_op jit(solution)/shard_map/reduce_scatter | solution.py:123
  128.3 19.5 %collective-permute-start.2 = (bf16[768,512]{1,0:T(8,128)(2,1)}, bf16[768,512]{1,0:T(8,128)(2,1)}, u32[]{:S(2)}, u32[]{:S(2)}) collective-permute-start(bf16[768,512]{1,0:T(8,128)(2,1)} %bitcast.115), channel_id=1, source_target_pairs={{0,2},{2,0},{1,3},{3,1},{4,6},{6,4},{5,7},{7,5},{8,10},{10,8},{9,1... | collective-permute-start | bytes 2359304 | tf_op jit(solution)/shard_map/ppermute | solution.py:15
  150.1 15.5 %all-to-all-start.1 = ((bf16[4,192,512]{2,1,0:T(8,128)(2,1)}), bf16[4,192,512]{2,1,0:T(8,128)(2,1)}, u32[]{:S(2)}, u32[]{:S(2)}) async-start(bf16[4,192,512]{2,1,0:T(8,128)(2,1)} %bitcast.123), calls=%async_computation.1 | async-start | bytes 1572864 | tf_op jit(solution)/shard_map/all_to_all | solution.py:19
  156.4 2.0 collective-permute-start.9
  158.4 4.9 %collective-permute-start.10 = (f32[32,512]{1,0:T(8,128)S(1)}, f32[32,512]{1,0:T(8,128)S(1)}, u32[]{:S(2)}, u32[]{:S(2)}) collective-permute-start(f32[32,512]{1,0:T(8,128)S(1)} %bitcast_add_fusion.2), channel_id=1, source_target_pairs={{0,128},{128,0},{1,129},{129,1},{2,130},{130,2},{3,131},{131,3},{4... | collective-permute-start | bytes 196616 | tf_op jit(solution)/shard_map/ppermute | solution.py:15
  166.5 23.5 %all-to-all-start.4 = ((f32[8,32,512]{2,1,0:T(8,128)}), f32[8,32,512]{2,1,0:T(8,128)S(1)}, u32[]{:S(2)}, u32[]{:S(2)}) async-start(f32[8,32,512]{2,1,0:T(8,128)} %broadcast_in_dim.13), calls=%async_computation.5 | async-start | bytes 1048576 | tf_op jit(solution)/shard_map/all_to_all | solution.py:19
  175.8 18.5 %collective-permute-start.3 = (bf16[2,192,512]{2,1,0:T(8,128)(2,1)S(1)}, bf16[2,192,512]{2,1,0:T(8,128)(2,1)S(1)}, u32[]{:S(2)}, u32[]{:S(2)}) collective-permute-start(bf16[2,192,512]{2,1,0:T(8,128)(2,1)S(1)} %dynamic-slice_bitcast_fusion.2), channel_id=1, source_target_pairs={{0,1},{1,0},{2,3},{3,2},{4,5},{5,4},{6,7},{7,6},{8,9},{9,8},{10,11... | collective-permute-start | bytes 1179656 | tf_op jit(solution)/shard_map/ppermute | solution.py:15
  190.8 8.9 %all-to-all-start.5 = ((f32[4,32,512]{2,1,0:T(8,128)}), f32[4,32,512]{2,1,0:T(8,128)S(1)}, u32[]{:S(2)}, u32[]{:S(2)}) async-start(f32[4,32,512]{2,1,0:T(8,128)} %broadcast_in_dim.14), calls=%async_computation.6 | async-start | bytes 524288 | tf_op jit(solution)/shard_map/all_to_all | solution.py:19
  194.2 9.9 %copy-start.6 = (s32[3,128]{1,0:T(4,128)S(1)}, s32[3,128]{1,0:T(4,128)}, u32[]{:S(2)}) copy-start(s32[3,128]{1,0:T(4,128)} %param.12) | copy-start | bytes 4612
  194.2 9.9 %copy-start.7 = (bf16[3,128,1024]{2,1,0:T(8,128)(2,1)S(1)}, bf16[3,128,1024]{2,1,0:T(8,128)(2,1)}, u32[]{:S(2)}) copy-start(bf16[3,128,1024]{2,1,0:T(8,128)(2,1)} %param.8) | copy-start | bytes 2359300
  199.7 6.3 %collective-permute-start.11 = (f32[2,32,512]{2,1,0:T(8,128)S(1)}, f32[2,32,512]{2,1,0:T(8,128)S(1)}, u32[]{:S(2)}, u32[]{:S(2)}) collective-permute-start(f32[2,32,512]{2,1,0:T(8,128)S(1)} %dynamic-slice_bitcast_fusion.3), channel_id=1, source_target_pairs={{0,1},{1,0},{2,3},{3,2},{4,5},{5,4},{6,7},{7,6},{8,9},{9,8},{10,11... | collective-permute-start | bytes 393224 | tf_op jit(solution)/shard_map/ppermute | solution.py:15
  207.0 6.7 %collective-permute-start.8 = (bf16[64,1024]{1,0:T(8,128)(2,1)S(1)}, bf16[64,1024]{1,0:T(8,128)(2,1)S(1)}, u32[]{:S(2)}, u32[]{:S(2)}) collective-permute-start(bf16[64,1024]{1,0:T(8,128)(2,1)S(1)} %dynamic-slice_bitcast_fusion.4), channel_id=1, source_target_pairs={{0,128},{128,0},{1,129},{129,1},{2,130},{130,2},{3,131},{131,3},{4... | collective-permute-start | bytes 393224 | tf_op jit(solution)/shard_map/ppermute | solution.py:15
  (4 other events, 15.6 us)
Sparse Core Ops, SparseCore 0:
  24.3 41.3 all-gather.1
  114.8 40.6 reduce-scatter.1

commit v2 on v1

--- a/solution.py
+++ b/solution.py
@@ -3,6 +3,8 @@
 import jax
 import jax.numpy as jnp
 from jax import lax
+from jax.experimental import pallas as pl
+from jax.experimental.pallas import tpu as pltpu
 from jax.sharding import Mesh, PartitionSpec as P
 
 XH, NY, NZ, XL, NC = 2, 4, 8, 2, 2
@@ -21,6 +23,80 @@
 
 def spread(a, axis, n):
     return exchange(jnp.broadcast_to(a[None], (n,) + a.shape), axis)
+
+
+def turn(a, k):
+    return lax.ppermute(a, "y", [(i, (i + k) % NY) for i in range(NY)])
+
+
+def gather_y(a, y):
+    half = a.shape[1] // 2
+    up, down = turn(a, 1), turn(a, -1)
+    out = jnp.zeros((NY,) + a.shape, a.dtype)
+    for piece, k in ((a, 0), (up, 1), (down, 3)):
+        out = lax.dynamic_update_slice(out, piece[None], ((y - k) % NY, 0, 0))
+    out = lax.dynamic_update_slice(out, turn(up[:, :half], 1)[None], ((y + 2) % NY, 0, 0))
+    return lax.dynamic_update_slice(out, turn(down[:, half:], -1)[None], ((y + 2) % NY, 0, half))
+
+
+def scatter_y(a, y):
+    half = a.shape[2] // 2
+    block = lambda k: pick(a, (y + k) % NY, 0)
+    far = block(2)
+    up, down = turn(far[:, :half], 1), turn(far[:, half:], -1)
+    next_up, next_down = block(1), block(3)
+    add = lambda p, q: (p.astype(F32) + q.astype(F32)).astype(BF)
+    next_up = jnp.concatenate([add(next_up[:, :half], up), next_up[:, half:]], axis=1)
+    next_down = jnp.concatenate([next_down[:, :half], add(next_down[:, half:], down)], axis=1)
+    return block(0).astype(F32) + turn(next_up, 1).astype(F32) + turn(next_down, -1).astype(F32)
+
+
+VMEM = pl.BlockSpec(memory_space=pltpu.VMEM)
+SMEM = pl.BlockSpec(memory_space=pltpu.SMEM)
+STEP = 256
+
+
+def call(body, at, operands, out_shape):
+    size = lambda a: math.prod(a.shape) * a.dtype.itemsize
+    moved = sum(size(a) for a in operands) + size(out_shape)
+    return pl.pallas_call(
+        body,
+        out_shape=out_shape,
+        in_specs=[SMEM] + [VMEM] * len(operands),
+        out_specs=VMEM,
+        compiler_params=pltpu.CompilerParams(vmem_limit_bytes=32 * 2**20),
+        cost_estimate=pl.CostEstimate(flops=3 * 2**30, bytes_accessed=moved, transcendentals=0),
+    )(at, *operands)
+
+
+def project_body(at, ho, w, out):
+    rows = ho[:, at[0]].reshape(-1, ho.shape[-1])
+    for x in range(XL):
+        for n in range(0, w.shape[1], STEP):
+            out[x, :, n : n + STEP] = lax.dot_general(
+                rows, w[x, n : n + STEP, :], (((1,), (1,)), ((), ())), preferred_element_type=F32
+            ).astype(BF)
+
+
+def weight_body(at, near, far, near_c, far_c, ho, out):
+    xl, c = at[0], at[1]
+    mine = ho[:, c].reshape(-1, ho.shape[-1])
+    theirs = ho[:, 1 - c].reshape(-1, ho.shape[-1])
+    over = (((0,), (0,)), ((), ()))
+    for x, p, q in ((xl, near, near_c), (1 - xl, far, far_c)):
+        for n in range(0, out.shape[-1], STEP):
+            total = lax.dot_general(p[...], mine[:, n : n + STEP], over, preferred_element_type=F32)
+            total += lax.dot_general(q[...], theirs[:, n : n + STEP], over, preferred_element_type=F32)
+            out[x, :, n : n + STEP] = total.astype(BF)
+
+
+def head_body(at, near, far, near_c, far_c, w, out):
+    xl, c = at[0], at[1]
+    for half, p, q in ((c, near, far), (1 - c, near_c, far_c)):
+        for n in range(0, out.shape[-1], STEP):
+            total = jnp.dot(p[...], w[xl, :, n : n + STEP], preferred_element_type=F32)
+            total += jnp.dot(q[...], w[1 - xl, :, n : n + STEP], preferred_element_type=F32)
+            out[:, half, :, n : n + STEP] = total.astype(BF).reshape(NY, -1, STEP)
 
 
 def pick(a, at, dim):
@@ -70,10 +146,10 @@
     cot_y = got[:, :half].reshape(NY * half, wide)
     ids_y = got[:, half, :half].astype(jnp.int32).reshape(NY * half)
 
-    ho_y = spread(ho, "y", NY).reshape(NY * rows, cols)
+    ho_y = gather_y(ho, y).reshape(NY, NC, half, cols)
 
     unit = in_order(xh, out_weight, swap(out_weight, "xh"), 0)
-    weight = lax.all_gather(unit, "z", axis=1, tiled=True).reshape(cols, cols)
+    weight = lax.all_gather(unit, "z", axis=1, tiled=True)
 
     mixing = mixture(meta_graph)
     table = jnp.dot(mixing, strategy_table.astype(F32), precision=HIGHEST)
@@ -84,23 +160,27 @@
     gating_y = 1.0 + rows_of(hot_y, table_y)
     grad_y = (cot_y.astype(F32) * gating_y).astype(BF)
 
-    both = jnp.concatenate([jnp.where(xl == 0, grad_y, far) if i == 0 else jnp.where(xl == 0, far, grad_y)
-                            for i, far in enumerate([swap(grad_y, "xl")] * 2)], axis=1)
-    grads = in_order(c, both.reshape(NY, half, cols), swap(both, "c").reshape(NY, half, cols), 1)
-    grads = grads.reshape(NY * rows, cols)
-
-    partial_sum = lax.dot_general(ho_y, weight, (((1,), (1,)), ((), ())), preferred_element_type=F32)
-    parts = partial_sum.astype(BF).reshape(NY, NC, half, cols)
-    chip = pick(parts, c, 1).astype(F32) + swap(pick(parts, 1 - c, 1), "c").astype(F32)
-    chip = chip.reshape(NY * half, XL, wide)
-    away = swap(pick(chip, 1 - xl, 1).astype(BF), "xl")
-    projected = pick(chip, xl, 1) + away.astype(F32)
+    far = swap(grad_y, "xl")
+    pieces = (grad_y, far, swap(grad_y, "c"), swap(far, "c"))
+    at = jnp.stack([xl, c]).astype(jnp.int32)
+
+    wg = call(weight_body, at, pieces + (ho_y,), jax.ShapeDtypeStruct((XH, NZ * wr, cols), BF))
+    wg = lax.psum_scatter(wg, "z", scatter_dimension=1, tiled=True)
+    weight_sum = pick(wg, xh, 0).astype(F32) + swap(pick(wg, 1 - xh, 0), "xh").astype(F32)
+
+    project = lambda core: call(
+        project_body, core.reshape(1).astype(jnp.int32), (ho_y, weight), jax.ShapeDtypeStruct((XL, NY * half, wide), BF)
+    )
+    theirs = swap(project(1 - c), "c")
+    keep = project(c)
+    chip = lambda x: pick(keep, x, 0).astype(F32) + pick(theirs, x, 0).astype(F32)
+    projected = chip(xl) + swap(chip(1 - xl).astype(BF), "xl").astype(F32)
 
     table_part = jnp.dot(hot_y, cot_y.astype(F32) * projected, precision=HIGHEST)
     table_part = table_part.reshape(NC, strategies // NC, wide)
     table_sum = pick(table_part, c, 0) + swap(pick(table_part, 1 - c, 0), "c")
     table_sum = table_sum + swap(table_sum, "xh")
-    table_sum = jnp.sum(spread(table_sum, "z", NZ), axis=0)
+    table_sum = jnp.sum(spread(table_sum.astype(BF), "z", NZ).astype(F32), axis=0)
     table_all = spread(table_sum, "y", NY).reshape(NC, 2, strategies // NC, wide)
     rest = swap(pick(table_all, 1 - c, 0), "c")
     table_sum = in_order(c, pick(table_all, c, 0), rest, 1)
@@ -115,13 +195,8 @@
     proj = jnp.concatenate([proj[0], proj[1]], axis=1).astype(F32)
     layer_out = (residual.reshape(rows, cols).astype(F32) + proj * gating).astype(BF)
 
-    head_grad = jnp.dot(grads, weight, preferred_element_type=F32).astype(BF)
-    head_grad = exchange(head_grad.reshape(NY, rows, cols), "y").astype(F32)
-    head_grad = jnp.sum(head_grad, axis=0).astype(BF)
-
-    wg = lax.dot_general(grads, ho_y, (((0,), (0,)), ((), ())), preferred_element_type=F32).astype(BF)
-    wg = lax.psum_scatter(wg.reshape(XH, NZ * wr, cols), "z", scatter_dimension=1, tiled=True)
-    weight_sum = pick(wg, xh, 0).astype(F32) + swap(pick(wg, 1 - xh, 0), "xh").astype(F32)
+    head_grad = call(head_body, at, pieces + (weight,), jax.ShapeDtypeStruct((NY, NC, half, cols), BF))
+    head_grad = scatter_y(head_grad.reshape(NY, rows, cols), y).astype(BF)
 
     shape = head_out.shape
     return layer_out.reshape(shape), head_grad.reshape(shape), weight_sum * grad_scale, table_grad

time: 223 us -> 187 us (0.84)
  matrix products: 29.1 us -> 7.61 us
  Pallas kernels: 0 us -> 15.6 us
  waiting for transfers between devices: 60.9 us -> 49.2 us
  local copies, waits for them, and re-layouts: 35.4 us -> 24.6 us
  other arithmetic: 25.3 us -> 16.4 us
    dot_general x3 -> x0, matrix products: 21.7 us -> none  [the longest x1 7.67 us: on_device(): lax.dot_general(grads, ho_y, (((0,), (0,)), ((), ())), preferred_element_...]
    ppermute x0 -> x8, waiting for transfers between devices: none -> 16 us  [turn(): return lax.ppermute(a, 'y', [(i, (i + k) % NY) for i in range(NY)])]
    ppermute x12 -> x13, waiting for transfers between devices: 33.8 us -> 17.8 us  [swap(): return lax.ppermute(a, axis, [(0, 1), (1, 0)])]
    pallas_call x0 -> x4, Pallas kernels: none -> 15.6 us  [call(): pl.pallas_call(body, out_shape=out_shape, in_specs=[SMEM] + [VMEM] * len(...]
    all_to_all x6 -> x4, waiting for transfers between devices: 27.1 us -> 15.3 us  [exchange(): return lax.all_to_all(a, axis, 0, 0, tiled=True)]
    all_to_all x6 -> x4, starting transfers between devices: 29.4 us -> 19.3 us  [exchange(): return lax.all_to_all(a, axis, 0, 0, tiled=True)]
    ppermute x0 -> x8, starting transfers between devices: none -> 9.09 us  [turn(): return lax.ppermute(a, 'y', [(i, (i + k) % NY) for i in range(NY)])]
    convert_element_type x3 -> x0, local copies, waits for them, and re-layouts: 8.42 us -> none  [the longest x1 4.64 us: on_device(): parts = partial_sum.astype(BF).reshape(NY, NC, half, cols)]
  transfers between devices with their start and end apart: 20 -> 27, of which waited for: 11 -> 10; matrix products, arithmetic and copies ran while one was open for 32% -> 20% of each run, Pallas kernels for 0% -> 8%
where the time goes in v2:
time: 187 us; the launch traced here: 186 us
  starting transfers between devices  57.8 us (31%)
  waiting for transfers between devices  49.2 us (26%)
  local copies, waits for them, and re-layouts  24.6 us (13%)
  other arithmetic  16.4 us (9%)
  Pallas kernels  15.6 us (8%)
  between operations  14.6 us (8%)
  matrix products  7.61 us (4%)
    ppermute x13, starting transfers between devices, swap(): return lax.ppermute(a, axis, [(0, 1), (1, 0)])  29.3 us
    all_to_all x4, starting transfers between devices, exchange(): return lax.all_to_all(a, axis, 0, 0, tiled=True)  19.3 us
    ppermute x13, waiting for transfers between devices, swap(): return lax.ppermute(a, axis, [(0, 1), (1, 0)])  17.8 us
    ppermute x8, waiting for transfers between devices, turn(): return lax.ppermute(a, 'y', [(i, (i + k) % NY) for i in range(NY)])  16 us
    pallas_call x4, Pallas kernels, call(): pl.pallas_call(body, out_shape=out_shape, in_specs=[SMEM] + [VMEM] * len(...  15.6 us
    all_to_all x4, waiting for transfers between devices, exchange(): return lax.all_to_all(a, axis, 0, 0, tiled=True)  15.3 us
    ppermute x8, starting transfers between devices, turn(): return lax.ppermute(a, 'y', [(i, (i + k) % NY) for i in range(NY)])  9.09 us
    unnamed x32, local copies, waits for them, and re-layouts  7.68 us
  transfers between devices with their start and end apart: 27, of which 10 were waited for; matrix products, arithmetic and copies ran while one was open for 20% of the time, Pallas kernels for 8%

profile of v2, /device:TPU:1, one launch (start us, length us, event | category | flops | bytes accessed | tf_op | source)
XLA Modules:
  0.0 185.7 jit_solution(15534641061939743954)
XLA Ops:
  7.3 3.7 %collective-permute-start.4 = (bf16[64,1024]{1,0:T(8,128)(2,1)}, bf16[64,1024]{1,0:T(8,128)(2,1)S(1)}, u32[]{:S(2)}, u32[]{:S(2)}) collective-permute-start(bf16[64,1024]{1,0:T(8,128)(2,1)} %param.9), channel_id=1, source_target_pairs={{0,128},{128,0},{1,129},{129,1},{2,130},{130,2},{3,131},{131,3},{4... | collective-permute-start | bytes 393224 | tf_op jit(solution)/shard_map/ppermute | solution.py:17
  10.9 2.6 %collective-permute-done.4 = bf16[64,1024]{1,0:T(8,128)(2,1)S(1)} collective-permute-done((bf16[64,1024]{1,0:T(8,128)(2,1)}, bf16[64,1024]{1,0:T(8,128)(2,1)S(1)}, u32[]{:S(2)}, u32[]{:S(2)}) %collective-permute-start.4) | collective-permute-done | bytes 131104 | tf_op jit(solution)/shard_map/ppermute | solution.py:17
  15.2 3.9 %collective-permute-start.8 = (bf16[192,1024]{1,0:T(8,128)(2,1)S(1)}, bf16[192,1024]{1,0:T(8,128)(2,1)S(1)}, u32[]{:S(2)}, u32[]{:S(2)}) collective-permute-start(bf16[192,1024]{1,0:T(8,128)(2,1)S(1)} %dynamic-slice_bitcast_fusion.3), channel_id=1, source_target_pairs={{0,1},{1,0},{2,3},{3,2},{4,5},{5,4},{6,7},{7,6},{8,9},{9,8},{10,11... | collective-permute-start | bytes 1179656 | tf_op jit(solution)/shard_map/ppermute | solution.py:17
  19.1 2.7 %collective-permute-start.1 = (bf16[384,1024]{1,0:T(8,128)(2,1)}, bf16[384,1024]{1,0:T(8,128)(2,1)}, u32[]{:S(2)}, u32[]{:S(2)}) collective-permute-start(bf16[384,1024]{1,0:T(8,128)(2,1)} %bitcast.3), channel_id=1, source_target_pairs={{0,96},{32,0},{64,32},{96,64},{1,97},{33,1},{65,33},{97,65},{2,98}... | collective-permute-start | bytes 2359304 | tf_op jit(solution)/shard_map/ppermute | solution.py:29
  23.9 4.2 %all-to-all-start.1 = ((bf16[4,208,512]{2,1,0:T(8,128)(2,1)}), bf16[4,208,512]{2,1,0:T(8,128)(2,1)}, u32[]{:S(2)}, u32[]{:S(2)}) async-start(bf16[4,208,512]{2,1,0:T(8,128)(2,1)} %pad_maximum_fusion), calls=%async_computation.1 | async-start | bytes 1703936 | tf_op jit(solution)/shard_map/all_to_all | solution.py:21
  31.3 8.5 %collective-permute-done = bf16[384,1024]{1,0:T(8,128)(2,1)} collective-permute-done((bf16[384,1024]{1,0:T(8,128)(2,1)}, bf16[384,1024]{1,0:T(8,128)(2,1)}, u32[]{:S(2)}, u32[]{:S(2)}) %collective-permute-start) | collective-permute-done | bytes 786464 | tf_op jit(solution)/shard_map/ppermute | solution.py:29
  43.3 2.7 %collective-permute-start.3 = (bf16[384,512]{1,0:T(8,128)(2,1)}, bf16[384,512]{1,0:T(8,128)(2,1)}, u32[]{:S(2)}, u32[]{:S(2)}) collective-permute-start(bf16[384,512]{1,0:T(8,128)(2,1)} %slice.59), channel_id=1, source_target_pairs={{0,96},{32,0},{64,32},{96,64},{1,97},{33,1},{65,33},{97,65},{2,98}... | collective-permute-start | bytes 1179656 | tf_op jit(solution)/shard_map/ppermute | solution.py:29
  46.0 2.7 %all-to-all-done.1 = bf16[4,208,512]{2,1,0:T(8,128)(2,1)} async-done(((bf16[4,208,512]{2,1,0:T(8,128)(2,1)}), bf16[4,208,512]{2,1,0:T(8,128)(2,1)}, u32[]{:S(2)}, u32[]{:S(2)}) %all-to-all-start.1) | async-done | bytes 852000 | tf_op jit(solution)/shard_map/all_to_all | solution.py:21
  59.9 10.6 %collective-permute-done.10.far = bf16[768,512]{1,0:T(8,128)(2,1)} collective-permute-done((bf16[768,512]{1,0:T(8,128)(2,1)}, bf16[768,512]{1,0:T(8,128)(2,1)}, u32[]{:S(2)}, u32[]{:S(2)}) %collective-permute-start.10) | collective-permute-done | bytes 786464 | tf_op jit(solution)/shard_map/ppermute | solution.py:17
  74.3 3.0 %shard_map.103 = bf16[2,768,512]{2,1,0:T(8,128)(2,1)} custom-call(s32[1]{0:T(128)} %bitcast.11.at, bf16[4,2,192,1024]{3,2,1,0:T(8,128)(2,1)S(1)} %bitcast.118, bf16[2,512,1024]{2,1,0:T(8,128)(2,1)S(1)} %copy-done.4), custom_call_target="tpu_custom_call" | custom-call | flops 3221225472 | bytes 6815744 | tf_op jit(solution)/shard_map/pallas_call | solution.py:62
  77.4 5.3 %shard_map.105 = bf16[2,512,1024]{2,1,0:T(8,128)(2,1)S(1)} custom-call(s32[2]{0:T(128)S(1)} %pad_add_fusion.at, bf16[768,512]{1,0:T(8,128)(2,1)} %fusion.near, bf16[768,512]{1,0:T(8,128)(2,1)} %collective-permute-done.10.far, bf16[768,512]{1,0:T(8,128)(2,1)} %collective-permute-done.11.near_c, bf16[768,512]{1,0:T(8,128)(2,1)} %collective-permute-done.12.far_c, ...), custom_call_target="tpu_custom_call" | custom-call | flops 3221225472 | bytes 8388608 | tf_op jit(solution)/shard_map/pallas_call | solution.py:62
  85.7 5.4 %shard_map.104 = bf16[4,2,192,1024]{3,2,1,0:T(8,128)(2,1)S(1)} custom-call(s32[2]{0:T(128)S(1)} %pad_add_fusion.at, bf16[768,512]{1,0:T(8,128)(2,1)} %fusion.near, bf16[768,512]{1,0:T(8,128)(2,1)} %collective-permute-done.10.far, bf16[768,512]{1,0:T(8,128)(2,1)} %collective-permute-done.11.near_c, bf16[768,512]{1,0:T(8,128)(2,1)} %collective-permute-done.12.far_c, ...), custom_call_target="tpu_custom_call" | custom-call | flops 3221225472 | bytes 8388608 | tf_op jit(solution)/shard_map/pallas_call | solution.py:62
  104.6 7.5 %collective-permute-done.13 = bf16[384,512]{1,0:T(8,128)(2,1)} collective-permute-done((bf16[384,512]{1,0:T(8,128)(2,1)}, bf16[384,512]{1,0:T(8,128)(2,1)}, u32[]{:S(2)}, u32[]{:S(2)}) %collective-permute-start.13) | collective-permute-done | bytes 393248 | tf_op jit(solution)/shard_map/ppermute | solution.py:29
  114.3 3.1 %collective-permute-done.6 = bf16[768,512]{1,0:T(8,128)(2,1)S(1)} collective-permute-done((bf16[768,512]{1,0:T(8,128)(2,1)}, bf16[768,512]{1,0:T(8,128)(2,1)S(1)}, u32[]{:S(2)}, u32[]{:S(2)}) %collective-permute-start.6) | collective-permute-done | bytes 786464 | tf_op jit(solution)/shard_map/ppermute | solution.py:17
  121.9 3.1 %collective-permute-start.19 = (f32[32,512]{1,0:T(8,128)S(1)}, f32[32,512]{1,0:T(8,128)S(1)}, u32[]{:S(2)}, u32[]{:S(2)}) collective-permute-start(f32[32,512]{1,0:T(8,128)S(1)} %bitcast_add_fusion.2), channel_id=1, source_target_pairs={{0,128},{128,0},{1,129},{129,1},{2,130},{130,2},{3,131},{131,3},{4... | collective-permute-start | bytes 196616 | tf_op jit(solution)/shard_map/ppermute | solution.py:17
  127.6 8.2 %all-to-all-start.2 = ((bf16[8,32,512]{2,1,0:T(8,128)(2,1)}), bf16[8,32,512]{2,1,0:T(8,128)(2,1)S(1)}, u32[]{:S(2)}, u32[]{:S(2)}) async-start(bf16[8,32,512]{2,1,0:T(8,128)(2,1)} %broadcast_in_dim.40), calls=%async_computation.3 | async-start | bytes 524288 | tf_op jit(solution)/shard_map/all_to_all | solution.py:21
  135.7 2.3 %fusion.5 = bf16[768,512]{1,0:T(8,128)(2,1)} fusion(bf16[768,512]{1,0:T(8,128)(2,1)S(1)} %collective-permute-done.6, bf16[2,768,512]{2,1,0:T(8,128)(2,1)} %collective-permute-done.5, s32[]{:T(128)S(6)} %select_n.167, bf16[2,768,512]{2,1,0:T(8,128)(2,1)S(1)} %shard_map.102), kind=kLoop, calls=%fused_computation.12 | loop fusion | flops 2359296 | bytes 3145732 | tf_op jit(solution)/shard_map/convert_element_type | solution.py:190
  138.1 7.2 %all-to-all-done.2 = bf16[8,32,512]{2,1,0:T(8,128)(2,1)S(1)} async-done(((bf16[8,32,512]{2,1,0:T(8,128)(2,1)}), bf16[8,32,512]{2,1,0:T(8,128)(2,1)S(1)}, u32[]{:S(2)}, u32[]{:S(2)}) %all-to-all-start.2) | async-done | bytes 262176 | tf_op jit(solution)/shard_map/all_to_all | solution.py:21
  145.3 3.5 %all-to-all-start = ((bf16[4,192,512]{2,1,0:T(8,128)(2,1)}), bf16[4,192,512]{2,1,0:T(8,128)(2,1)S(1)}, u32[]{:S(2)}, u32[]{:S(2)}) async-start(bf16[4,192,512]{2,1,0:T(8,128)(2,1)} %bitcast.14), calls=%async_computation | async-start | bytes 1572864 | tf_op jit(solution)/shard_map/all_to_all | solution.py:21
  149.1 2.9 %fusion.3 = bf16[384,1024]{1,0:T(8,128)(2,1)} fusion(bf16[384,1024]{1,0:T(8,128)(2,1)} %collective-permute-done.16, bf16[384,1024]{1,0:T(8,128)(2,1)} %collective-permute-done.14, bf16[4,384,1024]{2,1,0:T(8,128)(2,1)} %bitcast.122, s32[]{:T(128)S(6)} %select_n.157), kind=kLoop, calls=%fused_computation.6 | loop fusion | flops 2359296 | bytes 3145732 | tf_op jit(solution)/shard_map/convert_element_type | solution.py:199
  152.1 5.4 %all-to-all-done = bf16[4,192,512]{2,1,0:T(8,128)(2,1)S(1)} async-done(((bf16[4,192,512]{2,1,0:T(8,128)(2,1)}), bf16[4,192,512]{2,1,0:T(8,128)(2,1)S(1)}, u32[]{:S(2)}, u32[]{:S(2)}) %all-to-all-start) | async-done | bytes 786464 | tf_op jit(solution)/shard_map/all_to_all | solution.py:21
  158.2 3.4 %all-to-all-start.3 = ((f32[4,32,512]{2,1,0:T(8,128)}), f32[4,32,512]{2,1,0:T(8,128)S(1)}, u32[]{:S(2)}, u32[]{:S(2)}) async-start(f32[4,32,512]{2,1,0:T(8,128)} %broadcast_in_dim.41), calls=%async_computation.4 | async-start | bytes 524288 | tf_op jit(solution)/shard_map/all_to_all | solution.py:21
  162.6 4.3 %collective-permute-start.17 = (bf16[64,1024]{1,0:T(8,128)(2,1)S(1)}, bf16[64,1024]{1,0:T(8,128)(2,1)S(1)}, u32[]{:S(2)}, u32[]{:S(2)}) collective-permute-start(bf16[64,1024]{1,0:T(8,128)(2,1)S(1)} %dynamic-slice_bitcast_fusion.6), channel_id=1, source_target_pairs={{0,128},{128,0},{1,129},{129,1},{2,130},{130,2},{3,131},{131,3},{4... | collective-permute-start | bytes 393224 | tf_op jit(solution)/shard_map/ppermute | solution.py:17
  166.9 4.3 %collective-permute-start.7 = (bf16[2,192,512]{2,1,0:T(8,128)(2,1)S(1)}, bf16[2,192,512]{2,1,0:T(8,128)(2,1)S(1)}, u32[]{:S(2)}, u32[]{:S(2)}) collective-permute-start(bf16[2,192,512]{2,1,0:T(8,128)(2,1)S(1)} %dynamic-slice_bitcast_fusion.4), channel_id=1, source_target_pairs={{0,1},{1,0},{2,3},{3,2},{4,5},{5,4},{6,7},{7,6},{8,9},{9,8},{10,11... | collective-permute-start | bytes 1179656 | tf_op jit(solution)/shard_map/ppermute | solution.py:17
  (128 shorter events, 60.6 us)
Async XLA Ops:
  7.2 65.5 %all-gather.2.cloned.1.call-start = ((), (), s32[]{:S(2)}) async-start(), calls=%async_computation.5 | async-start | bytes 2359296 | tf_op jit(solution)/shard_map/all_gather | solution.py:152
  7.3 6.2 %collective-permute-start.4 = (bf16[64,1024]{1,0:T(8,128)(2,1)}, bf16[64,1024]{1,0:T(8,128)(2,1)S(1)}, u32[]{:S(2)}, u32[]{:S(2)}) collective-permute-start(bf16[64,1024]{1,0:T(8,128)(2,1)} %param.9), channel_id=1, source_target_pairs={{0,128},{128,0},{1,129},{129,1},{2,130},{130,2},{3,131},{131,3},{4... | collective-permute-start | bytes 393224 | tf_op jit(solution)/shard_map/ppermute | solution.py:17
  15.2 7.5 %collective-permute-start.8 = (bf16[192,1024]{1,0:T(8,128)(2,1)S(1)}, bf16[192,1024]{1,0:T(8,128)(2,1)S(1)}, u32[]{:S(2)}, u32[]{:S(2)}) collective-permute-start(bf16[192,1024]{1,0:T(8,128)(2,1)S(1)} %dynamic-slice_bitcast_fusion.3), channel_id=1, source_target_pairs={{0,1},{1,0},{2,3},{3,2},{4,5},{5,4},{6,7},{7,6},{8,9},{9,8},{10,11... | collective-permute-start | bytes 1179656 | tf_op jit(solution)/shard_map/ppermute | solution.py:17
  19.1 20.6 %collective-permute-start = (bf16[384,1024]{1,0:T(8,128)(2,1)}, bf16[384,1024]{1,0:T(8,128)(2,1)}, u32[]{:S(2)}, u32[]{:S(2)}) collective-permute-start(bf16[384,1024]{1,0:T(8,128)(2,1)} %bitcast.3), channel_id=1, source_target_pairs={{0,32},{32,64},{64,96},{96,0},{1,33},{33,65},{65,97},{97,1},{2,34}... | collective-permute-start | bytes 2359304 | tf_op jit(solution)/shard_map/ppermute | solution.py:29
  19.1 22.4 %collective-permute-start.1 = (bf16[384,1024]{1,0:T(8,128)(2,1)}, bf16[384,1024]{1,0:T(8,128)(2,1)}, u32[]{:S(2)}, u32[]{:S(2)}) collective-permute-start(bf16[384,1024]{1,0:T(8,128)(2,1)} %bitcast.3), channel_id=1, source_target_pairs={{0,96},{32,0},{64,32},{96,64},{1,97},{33,1},{65,33},{97,65},{2,98}... | collective-permute-start | bytes 2359304 | tf_op jit(solution)/shard_map/ppermute | solution.py:29
  21.8 8.0 %collective-permute-start.9 = (bf16[64,1024]{1,0:T(8,128)(2,1)S(1)}, bf16[64,1024]{1,0:T(8,128)(2,1)}, u32[]{:S(2)}, u32[]{:S(2)}) collective-permute-start(bf16[64,1024]{1,0:T(8,128)(2,1)S(1)} %copy-done.12), channel_id=1, source_target_pairs={{0,1},{1,0},{2,3},{3,2},{4,5},{5,4},{6,7},{7,6},{8,9},{9,8},{10,11... | collective-permute-start | bytes 393224 | tf_op jit(solution)/shard_map/ppermute | solution.py:17
  23.9 24.8 %all-to-all-start.1 = ((bf16[4,208,512]{2,1,0:T(8,128)(2,1)}), bf16[4,208,512]{2,1,0:T(8,128)(2,1)}, u32[]{:S(2)}, u32[]{:S(2)}) async-start(bf16[4,208,512]{2,1,0:T(8,128)(2,1)} %pad_maximum_fusion), calls=%async_computation.1 | async-start | bytes 1703936 | tf_op jit(solution)/shard_map/all_to_all | solution.py:21
  28.1 133.5 %reduce-scatter.2.cloned.1.call-start = ((), (), s32[]{:S(2)}) async-start(), calls=%async_computation.6 | async-start | bytes 2359296 | tf_op jit(solution)/shard_map/reduce_scatter | solution.py:168
  41.5 16.3 %collective-permute-start.2 = (bf16[384,512]{1,0:T(8,128)(2,1)}, bf16[384,512]{1,0:T(8,128)(2,1)}, u32[]{:S(2)}, u32[]{:S(2)}) collective-permute-start(bf16[384,512]{1,0:T(8,128)(2,1)} %slice.58), channel_id=1, source_target_pairs={{0,32},{32,64},{64,96},{96,0},{1,33},{33,65},{65,97},{97,1},{2,34}... | collective-permute-start | bytes 1179656 | tf_op jit(solution)/shard_map/ppermute | solution.py:29
  43.3 15.5 %collective-permute-start.3 = (bf16[384,512]{1,0:T(8,128)(2,1)}, bf16[384,512]{1,0:T(8,128)(2,1)}, u32[]{:S(2)}, u32[]{:S(2)}) collective-permute-start(bf16[384,512]{1,0:T(8,128)(2,1)} %slice.59), channel_id=1, source_target_pairs={{0,96},{32,0},{64,32},{96,64},{1,97},{33,1},{65,33},{97,65},{2,98}... | collective-permute-start | bytes 1179656 | tf_op jit(solution)/shard_map/ppermute | solution.py:29
  52.4 18.0 %collective-permute-start.10 = (bf16[768,512]{1,0:T(8,128)(2,1)}, bf16[768,512]{1,0:T(8,128)(2,1)}, u32[]{:S(2)}, u32[]{:S(2)}) collective-permute-start(bf16[768,512]{1,0:T(8,128)(2,1)} %fusion.near), channel_id=1, source_target_pairs={{0,2},{2,0},{1,3},{3,1},{4,6},{6,4},{5,7},{7,5},{8,10},{10,8},{9,1... | collective-permute-start | bytes 2359304 | tf_op jit(solution)/shard_map/ppermute | solution.py:17
  56.0 21.3 %collective-permute-start.11 = (bf16[768,512]{1,0:T(8,128)(2,1)}, bf16[768,512]{1,0:T(8,128)(2,1)}, u32[]{:S(2)}, u32[]{:S(2)}) collective-permute-start(bf16[768,512]{1,0:T(8,128)(2,1)} %fusion.near), channel_id=1, source_target_pairs={{0,1},{1,0},{2,3},{3,2},{4,5},{5,4},{6,7},{7,6},{8,9},{9,8},{10,11... | collective-permute-start | bytes 2359304 | tf_op jit(solution)/shard_map/ppermute | solution.py:17
  70.5 6.9 %collective-permute-start.12 = (bf16[768,512]{1,0:T(8,128)(2,1)}, bf16[768,512]{1,0:T(8,128)(2,1)}, u32[]{:S(2)}, u32[]{:S(2)}) collective-permute-start(bf16[768,512]{1,0:T(8,128)(2,1)} %collective-permute-done.10.far), channel_id=1, source_target_pairs={{0,1},{1,0},{2,3},{3,2},{4,5},{5,4},{6,7},{7,6},{8,9},{9,8},{10,11... | collective-permute-start | bytes 2359304 | tf_op jit(solution)/shard_map/ppermute | solution.py:17
  77.3 19.0 %collective-permute-start.5 = (bf16[2,768,512]{2,1,0:T(8,128)(2,1)}, bf16[2,768,512]{2,1,0:T(8,128)(2,1)}, u32[]{:S(2)}, u32[]{:S(2)}) collective-permute-start(bf16[2,768,512]{2,1,0:T(8,128)(2,1)} %shard_map.103), channel_id=1, source_target_pairs={{0,1},{1,0},{2,3},{3,2},{4,5},{5,4},{6,7},{7,6},{8,9},{9,8},{10,11... | collective-permute-start | bytes 4718600 | tf_op jit(solution)/shard_map/ppermute | solution.py:17
  98.5 18.9 %collective-permute-start.6 = (bf16[768,512]{1,0:T(8,128)(2,1)}, bf16[768,512]{1,0:T(8,128)(2,1)S(1)}, u32[]{:S(2)}, u32[]{:S(2)}) collective-permute-start(bf16[768,512]{1,0:T(8,128)(2,1)} %fusion.6), channel_id=1, source_target_pairs={{0,2},{2,0},{1,3},{3,1},{4,6},{6,4},{5,7},{7,5},{8,10},{10,8},{9,1... | collective-permute-start | bytes 2359304 | tf_op jit(solution)/shard_map/ppermute | solution.py:17
  100.7 11.4 %collective-permute-start.13 = (bf16[384,512]{1,0:T(8,128)(2,1)}, bf16[384,512]{1,0:T(8,128)(2,1)}, u32[]{:S(2)}, u32[]{:S(2)}) collective-permute-start(bf16[384,512]{1,0:T(8,128)(2,1)} %get-tuple-element.11), channel_id=1, source_target_pairs={{0,32},{32,64},{64,96},{96,0},{1,33},{33,65},{65,97},{97,1},{2,34}... | collective-permute-start | bytes 1179656 | tf_op jit(solution)/shard_map/ppermute | solution.py:29
  102.3 18.7 %collective-permute-start.15 = (bf16[384,512]{1,0:T(8,128)(2,1)}, bf16[384,512]{1,0:T(8,128)(2,1)S(1)}, u32[]{:S(2)}, u32[]{:S(2)}) collective-permute-start(bf16[384,512]{1,0:T(8,128)(2,1)} %get-tuple-element.12), channel_id=1, source_target_pairs={{0,96},{32,0},{64,32},{96,64},{1,97},{33,1},{65,33},{97,65},{2,98}... | collective-permute-start | bytes 1179656 | tf_op jit(solution)/shard_map/ppermute | solution.py:29
  114.2 34.9 %collective-permute-start.14 = (bf16[384,1024]{1,0:T(8,128)(2,1)}, bf16[384,1024]{1,0:T(8,128)(2,1)}, u32[]{:S(2)}, u32[]{:S(2)}) collective-permute-start(bf16[384,1024]{1,0:T(8,128)(2,1)} %pad_maximum_fusion.2), channel_id=1, source_target_pairs={{0,32},{32,64},{64,96},{96,0},{1,33},{33,65},{65,97},{97,1},{2,34}... | collective-permute-start | bytes 2359304 | tf_op jit(solution)/shard_map/ppermute | solution.py:29
  125.1 24.0 %collective-permute-start.16 = (bf16[384,1024]{1,0:T(8,128)(2,1)S(1)}, bf16[384,1024]{1,0:T(8,128)(2,1)}, u32[]{:S(2)}, u32[]{:S(2)}) collective-permute-start(bf16[384,1024]{1,0:T(8,128)(2,1)S(1)} %pad_maximum_fusion.3), channel_id=1, source_target_pairs={{0,96},{32,0},{64,32},{96,64},{1,97},{33,1},{65,33},{97,65},{2,98}... | collective-permute-start | bytes 2359304 | tf_op jit(solution)/shard_map/ppermute | solution.py:29
  127.6 17.7 %all-to-all-start.2 = ((bf16[8,32,512]{2,1,0:T(8,128)(2,1)}), bf16[8,32,512]{2,1,0:T(8,128)(2,1)S(1)}, u32[]{:S(2)}, u32[]{:S(2)}) async-start(bf16[8,32,512]{2,1,0:T(8,128)(2,1)} %broadcast_in_dim.40), calls=%async_computation.3 | async-start | bytes 524288 | tf_op jit(solution)/shard_map/all_to_all | solution.py:21
  145.3 12.2 %all-to-all-start = ((bf16[4,192,512]{2,1,0:T(8,128)(2,1)}), bf16[4,192,512]{2,1,0:T(8,128)(2,1)S(1)}, u32[]{:S(2)}, u32[]{:S(2)}) async-start(bf16[4,192,512]{2,1,0:T(8,128)(2,1)} %bitcast.14), calls=%async_computation | async-start | bytes 1572864 | tf_op jit(solution)/shard_map/all_to_all | solution.py:21
  158.2 13.1 %all-to-all-start.3 = ((f32[4,32,512]{2,1,0:T(8,128)}), f32[4,32,512]{2,1,0:T(8,128)S(1)}, u32[]{:S(2)}, u32[]{:S(2)}) async-start(f32[4,32,512]{2,1,0:T(8,128)} %broadcast_in_dim.41), calls=%async_computation.4 | async-start | bytes 524288 | tf_op jit(solution)/shard_map/all_to_all | solution.py:21
  162.6 10.3 %collective-permute-start.17 = (bf16[64,1024]{1,0:T(8,128)(2,1)S(1)}, bf16[64,1024]{1,0:T(8,128)(2,1)S(1)}, u32[]{:S(2)}, u32[]{:S(2)}) collective-permute-start(bf16[64,1024]{1,0:T(8,128)(2,1)S(1)} %dynamic-slice_bitcast_fusion.6), channel_id=1, source_target_pairs={{0,128},{128,0},{1,129},{129,1},{2,130},{130,2},{3,131},{131,3},{4... | collective-permute-start | bytes 393224 | tf_op jit(solution)/shard_map/ppermute | solution.py:17
  166.9 8.9 %collective-permute-start.7 = (bf16[2,192,512]{2,1,0:T(8,128)(2,1)S(1)}, bf16[2,192,512]{2,1,0:T(8,128)(2,1)S(1)}, u32[]{:S(2)}, u32[]{:S(2)}) collective-permute-start(bf16[2,192,512]{2,1,0:T(8,128)(2,1)S(1)} %dynamic-slice_bitcast_fusion.4), channel_id=1, source_target_pairs={{0,1},{1,0},{2,3},{3,2},{4,5},{5,4},{6,7},{7,6},{8,9},{9,8},{10,11... | collective-permute-start | bytes 1179656 | tf_op jit(solution)/shard_map/ppermute | solution.py:17
  (19 other events, 143.2 us)
Sparse Core Ops, SparseCore 0:
  15.3 42.1 all-gather.1
  84.2 38.7 reduce-scatter.1

commit v3 on v2

--- a/solution.py
+++ b/solution.py
@@ -29,9 +29,11 @@
     return lax.ppermute(a, "y", [(i, (i + k) % NY) for i in range(NY)])
 
 
-def gather_y(a, y):
+def gather_y(a, y, after):
+    at_none = y.reshape(1).astype(jnp.int32)
     half = a.shape[1] // 2
-    up, down = turn(a, 1), turn(a, -1)
+    sent = call(copy_body, at_none, (a,), jax.ShapeDtypeStruct(a.shape, a.dtype), after)
+    up, down = turn(sent, 1), turn(sent, -1)
     out = jnp.zeros((NY,) + a.shape, a.dtype)
     for piece, k in ((a, 0), (up, 1), (down, 3)):
         out = lax.dynamic_update_slice(out, piece[None], ((y - k) % NY, 0, 0))
@@ -56,17 +58,30 @@
 STEP = 256
 
 
-def call(body, at, operands, out_shape):
+def call(body, at, operands, out_shape, after=()):
     size = lambda a: math.prod(a.shape) * a.dtype.itemsize
     moved = sum(size(a) for a in operands) + size(out_shape)
     return pl.pallas_call(
-        body,
+        lambda *refs: body(*refs[: len(operands) + 1], refs[-1]),
         out_shape=out_shape,
-        in_specs=[SMEM] + [VMEM] * len(operands),
+        in_specs=[SMEM] + [VMEM] * len(operands) + [pl.BlockSpec(memory_space=pl.ANY)] * len(after),
         out_specs=VMEM,
         compiler_params=pltpu.CompilerParams(vmem_limit_bytes=32 * 2**20),
         cost_estimate=pl.CostEstimate(flops=3 * 2**30, bytes_accessed=moved, transcendentals=0),
-    )(at, *operands)
+    )(at, *operands, *after)
+
+
+def copy_body(at, a, out):
+    out[...] = a[...]
+
+
+def add_body(at, a, b, out):
+    out[...] = a[...].astype(F32) + b[...].astype(F32)
+
+
+def pair_body(at, own, other, out):
+    out[at[0]] = own[...]
+    out[1 - at[0]] = other[...]
 
 
 def project_body(at, ho, w, out):
@@ -146,9 +161,15 @@
     cot_y = got[:, :half].reshape(NY * half, wide)
     ids_y = got[:, half, :half].astype(jnp.int32).reshape(NY * half)
 
-    ho_y = gather_y(ho, y).reshape(NY, NC, half, cols)
-
-    unit = in_order(xh, out_weight, swap(out_weight, "xh"), 0)
+    ho_y = gather_y(ho, y, (got,)).reshape(NY, NC, half, cols)
+
+    unit = call(
+        pair_body,
+        xh.reshape(1).astype(jnp.int32),
+        (out_weight, swap(out_weight, "xh")),
+        jax.ShapeDtypeStruct((XH,) + out_weight.shape, BF),
+        (other,),
+    )
     weight = lax.all_gather(unit, "z", axis=1, tiled=True)
 
     mixing = mixture(meta_graph)
@@ -164,38 +185,44 @@
     pieces = (grad_y, far, swap(grad_y, "c"), swap(far, "c"))
     at = jnp.stack([xl, c]).astype(jnp.int32)
 
-    wg = call(weight_body, at, pieces + (ho_y,), jax.ShapeDtypeStruct((XH, NZ * wr, cols), BF))
-    wg = lax.psum_scatter(wg, "z", scatter_dimension=1, tiled=True)
-    weight_sum = pick(wg, xh, 0).astype(F32) + swap(pick(wg, 1 - xh, 0), "xh").astype(F32)
-
-    project = lambda core: call(
-        project_body, core.reshape(1).astype(jnp.int32), (ho_y, weight), jax.ShapeDtypeStruct((XL, NY * half, wide), BF)
+    project = lambda core, after: call(
+        project_body, core.reshape(1).astype(jnp.int32), (ho_y, weight), jax.ShapeDtypeStruct((XL, NY * half, wide), BF), after
     )
-    theirs = swap(project(1 - c), "c")
-    keep = project(c)
+    theirs = swap(project(1 - c, ()), "c")
+    keep = project(c, ())
     chip = lambda x: pick(keep, x, 0).astype(F32) + pick(theirs, x, 0).astype(F32)
     projected = chip(xl) + swap(chip(1 - xl).astype(BF), "xl").astype(F32)
 
+    wg = call(weight_body, at, pieces + (ho_y,), jax.ShapeDtypeStruct((XH, NZ * wr, cols), BF))
+    wg_part = lax.psum_scatter(wg, "z", scatter_dimension=1, tiled=True)
+    weight_sum = pick(wg_part, xh, 0).astype(F32) + swap(pick(wg_part, 1 - xh, 0), "xh").astype(F32)
+
+    home = exchange(projected.astype(BF).reshape(NY, half, wide), "y")
     table_part = jnp.dot(hot_y, cot_y.astype(F32) * projected, precision=HIGHEST)
     table_part = table_part.reshape(NC, strategies // NC, wide)
     table_sum = pick(table_part, c, 0) + swap(pick(table_part, 1 - c, 0), "c")
     table_sum = table_sum + swap(table_sum, "xh")
-    table_sum = jnp.sum(spread(table_sum.astype(BF), "z", NZ).astype(F32), axis=0)
+    for bit in (1, 2, 4):
+        sent = table_sum.astype(BF)
+        far_sum = lax.ppermute(sent, "z", [(i, i ^ bit) for i in range(NZ)])
+        if bit < 4:
+            table_sum = sent.astype(F32) + far_sum.astype(F32)
+        else:
+            table_sum = call(add_body, at, (sent, far_sum), jax.ShapeDtypeStruct(sent.shape, F32), (home,))
     table_all = spread(table_sum, "y", NY).reshape(NC, 2, strategies // NC, wide)
     rest = swap(pick(table_all, 1 - c, 0), "c")
     table_sum = in_order(c, pick(table_all, c, 0), rest, 1)
     table_sum = table_sum.reshape(2, strategies, wide).transpose(1, 0, 2).reshape(strategies, cols)
     table_grad = jnp.dot(mixing.T, table_sum, precision=HIGHEST) * grad_scale
 
-    home = exchange(projected.astype(BF).reshape(NY, half, wide), "y")
-    home = home.reshape(NC, 2, half, wide)
-    back = swap(pick(home, 1 - c, 0), "c")
-    proj = in_order(c, pick(home, c, 0), back, 1).reshape(2, rows, wide)
+    parts = home.reshape(NC, 2, half, wide)
+    back = swap(pick(parts, 1 - c, 0), "c")
+    proj = in_order(c, pick(parts, c, 0), back, 1).reshape(2, rows, wide)
     gating = 1.0 + rows_of(members(ids, strategies), table)
     proj = jnp.concatenate([proj[0], proj[1]], axis=1).astype(F32)
     layer_out = (residual.reshape(rows, cols).astype(F32) + proj * gating).astype(BF)
 
-    head_grad = call(head_body, at, pieces + (weight,), jax.ShapeDtypeStruct((NY, NC, half, cols), BF))
+    head_grad = call(head_body, at, pieces + (weight,), jax.ShapeDtypeStruct((NY, NC, half, cols), BF), (keep,))
     head_grad = scatter_y(head_grad.reshape(NY, rows, cols), y).astype(BF)
 
     shape = head_out.shape

time: 187 us -> 180 us (0.963)
  waiting for transfers between devices: 49.2 us -> 45.4 us
  other arithmetic: 16.4 us -> 13 us
  Pallas kernels: 15.6 us -> 17.6 us
    ppermute x0 -> x3, starting transfers between devices: none -> 9.9 us  [on_device(): far_sum = lax.ppermute(sent, 'z', [(i, i ^ bit) for i in range(NZ)])]
    ppermute x13, waiting for transfers between devices: 17.8 us -> 8.19 us  [swap(): return lax.ppermute(a, axis, [(0, 1), (1, 0)])]
    all_to_all x4 -> x3, starting transfers between devices: 19.3 us -> 11.8 us  [exchange(): return lax.all_to_all(a, axis, 0, 0, tiled=True)]
    ppermute x13, starting transfers between devices: 29.3 us -> 22 us  [swap(): return lax.ppermute(a, axis, [(0, 1), (1, 0)])]
    unnamed x32 -> x36, local copies, waits for them, and re-layouts: 7.68 us -> 11.9 us
    ppermute x8, starting transfers between devices: 9.09 us -> 12.5 us  [turn(): return lax.ppermute(a, 'y', [(i, (i + k) % NY) for i in range(NY)])]
    all_to_all x4 -> x3, waiting for transfers between devices: 15.3 us -> 18 us  [exchange(): return lax.all_to_all(a, axis, 0, 0, tiled=True)]
    pallas_call x4 -> x7, Pallas kernels: 15.6 us -> 17.6 us  [call(): pl.pallas_call(lambda *refs: body(*refs[:len(operands) + 1], refs[-1]), o...]
  transfers between devices with their start and end apart: 27 -> 29, of which waited for: 10 -> 11; matrix products, arithmetic and copies ran while one was open for 20% -> 17% of each run, Pallas kernels for 8% -> 10%
where the time goes in v3:
time: 180 us; the launch traced here: 179 us
  starting transfers between devices  56.3 us (31%)
  waiting for transfers between devices  45.4 us (25%)
  local copies, waits for them, and re-layouts  24.1 us (13%)
  Pallas kernels  17.6 us (10%)
  between operations  14.5 us (8%)
  other arithmetic  13 us (7%)
  matrix products  7.61 us (4%)
    ppermute x13, starting transfers between devices, swap(): return lax.ppermute(a, axis, [(0, 1), (1, 0)])  22 us
    all_to_all x3, waiting for transfers between devices, exchange(): return lax.all_to_all(a, axis, 0, 0, tiled=True)  18 us
    ppermute x8, waiting for transfers between devices, turn(): return lax.ppermute(a, 'y', [(i, (i + k) % NY) for i in range(NY)])  17.8 us
    pallas_call x7, Pallas kernels, call(): pl.pallas_call(lambda *refs: body(*refs[:len(operands) + 1], refs[-1]), o...  17.6 us
    ppermute x8, starting transfers between devices, turn(): return lax.ppermute(a, 'y', [(i, (i + k) % NY) for i in range(NY)])  12.5 us
    unnamed x36, local copies, waits for them, and re-layouts  11.9 us
    all_to_all x3, starting transfers between devices, exchange(): return lax.all_to_all(a, axis, 0, 0, tiled=True)  11.8 us
    ppermute x3, starting transfers between devices, on_device(): far_sum = lax.ppermute(sent, 'z', [(i, i ^ bit) for i in range(NZ)])  9.9 us
  transfers between devices with their start and end apart: 29, of which 11 were waited for; matrix products, arithmetic and copies ran while one was open for 17% of the time, Pallas kernels for 10%

profile of v3, /device:TPU:1, one launch (start us, length us, event | category | flops | bytes accessed | tf_op | source)
XLA Modules:
  0.0 178.6 jit_solution(6684015229483665601)
XLA Ops:
  8.2 3.3 %collective-permute-start = (bf16[192,1024]{1,0:T(8,128)(2,1)S(1)}, bf16[192,1024]{1,0:T(8,128)(2,1)S(1)}, u32[]{:S(2)}, u32[]{:S(2)}) collective-permute-start(bf16[192,1024]{1,0:T(8,128)(2,1)S(1)} %dynamic-slice_bitcast_fusion.4), channel_id=1, source_target_pairs={{0,1},{1,0},{2,3},{3,2},{4,5},{5,4},{6,7},{7,6},{8,9},{9,8},{10,11... | collective-permute-start | bytes 1179656 | tf_op jit(solution)/shard_map/ppermute | solution.py:17
  14.6 3.7 %collective-permute-done.5.refs_2_ = bf16[64,1024]{1,0:T(8,128)(2,1)S(1)} collective-permute-done((bf16[64,1024]{1,0:T(8,128)(2,1)}, bf16[64,1024]{1,0:T(8,128)(2,1)S(1)}, u32[]{:S(2)}, u32[]{:S(2)}) %collective-permute-start.5) | collective-permute-done | bytes 131104 | tf_op jit(solution)/shard_map/ppermute | solution.py:17
  21.7 3.6 %all-to-all-start = ((bf16[4,208,512]{2,1,0:T(8,128)(2,1)}), bf16[4,208,512]{2,1,0:T(8,128)(2,1)S(1)}, u32[]{:S(2)}, u32[]{:S(2)}) async-start(bf16[4,208,512]{2,1,0:T(8,128)(2,1)} %pad_maximum_fusion), calls=%async_computation | async-start | bytes 1703936 | tf_op jit(solution)/shard_map/all_to_all | solution.py:21
  26.0 11.5 %all-to-all-done.refs_2_ = bf16[4,208,512]{2,1,0:T(8,128)(2,1)S(1)} async-done(((bf16[4,208,512]{2,1,0:T(8,128)(2,1)}), bf16[4,208,512]{2,1,0:T(8,128)(2,1)S(1)}, u32[]{:S(2)}, u32[]{:S(2)}) %all-to-all-start) | async-done | bytes 852000 | tf_op jit(solution)/shard_map/all_to_all | solution.py:21
  45.1 2.9 %collective-permute-start.11 = (bf16[768,512]{1,0:T(8,128)(2,1)}, bf16[768,512]{1,0:T(8,128)(2,1)}, u32[]{:S(2)}, u32[]{:S(2)}) collective-permute-start(bf16[768,512]{1,0:T(8,128)(2,1)} %fusion.refs_1_), channel_id=1, source_target_pairs={{0,1},{1,0},{2,3},{3,2},{4,5},{5,4},{6,7},{7,6},{8,9},{9,8},{10,11... | collective-permute-start | bytes 2359304 | tf_op jit(solution)/shard_map/ppermute | solution.py:17
  47.9 9.2 %collective-permute-done.1 = bf16[384,1024]{1,0:T(8,128)(2,1)} collective-permute-done((bf16[384,1024]{1,0:T(8,128)(2,1)}, bf16[384,1024]{1,0:T(8,128)(2,1)}, u32[]{:S(2)}, u32[]{:S(2)}) %collective-permute-start.1) | collective-permute-done | bytes 786464 | tf_op jit(solution)/shard_map/ppermute | solution.py:29
  59.3 2.7 %collective-permute-start.4 = (bf16[384,512]{1,0:T(8,128)(2,1)S(1)}, bf16[384,512]{1,0:T(8,128)(2,1)S(1)}, u32[]{:S(2)}, u32[]{:S(2)}) collective-permute-start(bf16[384,512]{1,0:T(8,128)(2,1)S(1)} %slice.61), channel_id=1, source_target_pairs={{0,96},{32,0},{64,32},{96,64},{1,97},{33,1},{65,33},{97,65},{2,98}... | collective-permute-start | bytes 1179656 | tf_op jit(solution)/shard_map/ppermute | solution.py:29
  62.1 3.3 %collective-permute-start.12 = (bf16[768,512]{1,0:T(8,128)(2,1)}, bf16[768,512]{1,0:T(8,128)(2,1)}, u32[]{:S(2)}, u32[]{:S(2)}) collective-permute-start(bf16[768,512]{1,0:T(8,128)(2,1)} %collective-permute-done.10.refs_2_), channel_id=1, source_target_pairs={{0,1},{1,0},{2,3},{3,2},{4,5},{5,4},{6,7},{7,6},{8,9},{9,8},{10,11... | collective-permute-start | bytes 2359304 | tf_op jit(solution)/shard_map/ppermute | solution.py:17
  67.9 2.7 %copy-done.6 = bf16[2,512,1024]{2,1,0:T(8,128)(2,1)S(1)} copy-done((bf16[2,512,1024]{2,1,0:T(8,128)(2,1)S(1)}, bf16[2,512,1024]{2,1,0:T(8,128)(2,1)}, u32[]{:S(2)}) %copy-start.6) | copy-done | bytes 2097176
  70.6 3.0 %shard_map.105 = bf16[2,768,512]{2,1,0:T(8,128)(2,1)} custom-call(s32[1]{0:T(128)} %bitcast.17.refs_0_, bf16[4,2,192,1024]{3,2,1,0:T(8,128)(2,1)S(1)} %bitcast.116, bf16[2,512,1024]{2,1,0:T(8,128)(2,1)S(1)} %copy-done.6), custom_call_target="tpu_custom_call" | custom-call | flops 3221225472 | bytes 6815744 | tf_op jit(solution)/shard_map/pallas_call | solution.py:64
  73.6 3.6 %collective-permute-start.6 = (bf16[2,768,512]{2,1,0:T(8,128)(2,1)}, bf16[2,768,512]{2,1,0:T(8,128)(2,1)}, u32[]{:S(2)}, u32[]{:S(2)}) collective-permute-start(bf16[2,768,512]{2,1,0:T(8,128)(2,1)} %shard_map.105), channel_id=1, source_target_pairs={{0,1},{1,0},{2,3},{3,2},{4,5},{5,4},{6,7},{7,6},{8,9},{9,8},{10,11... | collective-permute-start | bytes 4718600 | tf_op jit(solution)/shard_map/ppermute | solution.py:17
  77.3 5.4 %shard_map.107 = bf16[2,512,1024]{2,1,0:T(8,128)(2,1)S(1)} custom-call(s32[2]{0:T(128)S(1)} %pad_add_fusion.refs_0_, bf16[768,512]{1,0:T(8,128)(2,1)} %fusion.refs_1_, bf16[768,512]{1,0:T(8,128)(2,1)} %collective-permute-done.10.refs_2_, bf16[768,512]{1,0:T(8,128)(2,1)} %collective-permute-done.11.refs_3_, bf16[768,512]{1,0:T(8,128)(2,1)} %collective-permute-done.12.refs_4_, ...), custom_call_target="tpu_custom_call" | custom-call | flops 3221225472 | bytes 8388608 | tf_op jit(solution)/shard_map/pallas_call | solution.py:64
  89.3 5.3 %shard_map.106 = bf16[4,2,192,1024]{3,2,1,0:T(8,128)(2,1)S(1)} custom-call(s32[2]{0:T(128)S(1)} %pad_add_fusion.refs_0_, bf16[768,512]{1,0:T(8,128)(2,1)} %fusion.refs_1_, bf16[768,512]{1,0:T(8,128)(2,1)} %collective-permute-done.10.refs_2_, bf16[768,512]{1,0:T(8,128)(2,1)} %collective-permute-done.11.refs_3_, ...), custom_call_target="tpu_custom_call" | custom-call | flops 3221225472 | bytes 8388608 | tf_op jit(solution)/shard_map/pallas_call | solution.py:64
  100.9 3.5 %collective-permute-start.15 = (bf16[384,512]{1,0:T(8,128)(2,1)}, bf16[384,512]{1,0:T(8,128)(2,1)S(1)}, u32[]{:S(2)}, u32[]{:S(2)}) collective-permute-start(bf16[384,512]{1,0:T(8,128)(2,1)} %get-tuple-element.12), channel_id=1, source_target_pairs={{0,96},{32,0},{64,32},{96,64},{1,97},{33,1},{65,33},{97,65},{2,98}... | collective-permute-start | bytes 1179656 | tf_op jit(solution)/shard_map/ppermute | solution.py:29
  104.4 8.6 %collective-permute-done.13 = bf16[384,512]{1,0:T(8,128)(2,1)} collective-permute-done((bf16[384,512]{1,0:T(8,128)(2,1)}, bf16[384,512]{1,0:T(8,128)(2,1)}, u32[]{:S(2)}, u32[]{:S(2)}) %collective-permute-start.13) | collective-permute-done | bytes 393248 | tf_op jit(solution)/shard_map/ppermute | solution.py:29
  115.1 3.3 %collective-permute-done.7 = bf16[768,512]{1,0:T(8,128)(2,1)S(1)} collective-permute-done((bf16[768,512]{1,0:T(8,128)(2,1)}, bf16[768,512]{1,0:T(8,128)(2,1)S(1)}, u32[]{:S(2)}, u32[]{:S(2)}) %collective-permute-start.7) | collective-permute-done | bytes 786464 | tf_op jit(solution)/shard_map/ppermute | solution.py:17
  123.7 3.5 %collective-permute-start.16 = (bf16[384,1024]{1,0:T(8,128)(2,1)S(1)}, bf16[384,1024]{1,0:T(8,128)(2,1)}, u32[]{:S(2)}, u32[]{:S(2)}) collective-permute-start(bf16[384,1024]{1,0:T(8,128)(2,1)S(1)} %pad_maximum_fusion.3), channel_id=1, source_target_pairs={{0,96},{32,0},{64,32},{96,64},{1,97},{33,1},{65,33},{97,65},{2,98}... | collective-permute-start | bytes 2359304 | tf_op jit(solution)/shard_map/ppermute | solution.py:29
  131.4 3.5 %all-to-all-start.1 = ((bf16[4,192,512]{2,1,0:T(8,128)(2,1)}), bf16[4,192,512]{2,1,0:T(8,128)(2,1)S(1)}, u32[]{:S(2)}, u32[]{:S(2)}) async-start(bf16[4,192,512]{2,1,0:T(8,128)(2,1)} %bitcast.20), calls=%async_computation.1 | async-start | bytes 1572864 | tf_op jit(solution)/shard_map/all_to_all | solution.py:21
  134.9 3.0 %collective-permute-start.21 = (bf16[32,512]{1,0:T(8,128)(2,1)S(1)}, bf16[32,512]{1,0:T(8,128)(2,1)S(1)}, u32[]{:S(2)}, u32[]{:S(2)}) collective-permute-start(bf16[32,512]{1,0:T(8,128)(2,1)S(1)} %add_convert_fusion.4), channel_id=1, source_target_pairs={{0,8},{4,12},{8,0},{12,4},{16,24},{20,28},{24,16},{28,20},{1,9},{5... | collective-permute-start | bytes 98312 | tf_op jit(solution)/shard_map/ppermute | solution.py:207
  139.6 5.1 %collective-permute-start.22 = (bf16[32,512]{1,0:T(8,128)(2,1)S(1)}, bf16[32,512]{1,0:T(8,128)(2,1)S(1)}, u32[]{:S(2)}, u32[]{:S(2)}) collective-permute-start(bf16[32,512]{1,0:T(8,128)(2,1)S(1)} %add_convert_fusion.3.refs_1_), channel_id=1, source_target_pairs={{0,16},{4,20},{8,24},{12,28},{16,0},{20,4},{24,8},{28,12},{1,17},{... | collective-permute-start | bytes 98312 | tf_op jit(solution)/shard_map/ppermute | solution.py:207
  147.9 4.0 %all-to-all-done.1.refs_3_ = bf16[4,192,512]{2,1,0:T(8,128)(2,1)S(1)} async-done(((bf16[4,192,512]{2,1,0:T(8,128)(2,1)}), bf16[4,192,512]{2,1,0:T(8,128)(2,1)S(1)}, u32[]{:S(2)}, u32[]{:S(2)}) %all-to-all-start.1) | async-done | bytes 786464 | tf_op jit(solution)/shard_map/all_to_all | solution.py:21
  153.1 4.7 %all-to-all-start.2 = ((f32[4,32,512]{2,1,0:T(8,128)}), f32[4,32,512]{2,1,0:T(8,128)S(1)}, u32[]{:S(2)}, u32[]{:S(2)}) async-start(f32[4,32,512]{2,1,0:T(8,128)} %broadcast_in_dim.34), calls=%async_computation.3 | async-start | bytes 524288 | tf_op jit(solution)/shard_map/all_to_all | solution.py:21
  157.9 3.0 %fusion.3 = bf16[384,1024]{1,0:T(8,128)(2,1)} fusion(bf16[384,1024]{1,0:T(8,128)(2,1)} %collective-permute-done.16, bf16[384,1024]{1,0:T(8,128)(2,1)} %collective-permute-done.14, bf16[4,384,1024]{2,1,0:T(8,128)(2,1)} %bitcast.122, s32[]{:T(128)S(6)} %select_n.147), kind=kLoop, calls=%fused_computation.6 | loop fusion | flops 2359296 | bytes 3145732 | tf_op jit(solution)/shard_map/convert_element_type | solution.py:226
  163.4 3.0 %collective-permute-start.23 = (f32[2,32,512]{2,1,0:T(8,128)S(1)}, f32[2,32,512]{2,1,0:T(8,128)S(1)}, u32[]{:S(2)}, u32[]{:S(2)}) collective-permute-start(f32[2,32,512]{2,1,0:T(8,128)S(1)} %dynamic-slice_bitcast_fusion.5), channel_id=1, source_target_pairs={{0,1},{1,0},{2,3},{3,2},{4,5},{5,4},{6,7},{7,6},{8,9},{9,8},{10,11... | collective-permute-start | bytes 393224 | tf_op jit(solution)/shard_map/ppermute | solution.py:17
  (137 shorter events, 58.7 us)
Async XLA Ops:
  7.2 60.7 %all-gather.2.cloned.1.call-start = ((), (), s32[]{:S(2)}) async-start(), calls=%async_computation.4 | async-start | bytes 2359296 | tf_op jit(solution)/shard_map/all_gather | solution.py:173
  8.2 10.1 %collective-permute-start = (bf16[192,1024]{1,0:T(8,128)(2,1)S(1)}, bf16[192,1024]{1,0:T(8,128)(2,1)S(1)}, u32[]{:S(2)}, u32[]{:S(2)}) collective-permute-start(bf16[192,1024]{1,0:T(8,128)(2,1)S(1)} %dynamic-slice_bitcast_fusion.4), channel_id=1, source_target_pairs={{0,1},{1,0},{2,3},{3,2},{4,5},{5,4},{6,7},{7,6},{8,9},{9,8},{10,11... | collective-permute-start | bytes 1179656 | tf_op jit(solution)/shard_map/ppermute | solution.py:17
  11.6 6.8 %collective-permute-start.5 = (bf16[64,1024]{1,0:T(8,128)(2,1)}, bf16[64,1024]{1,0:T(8,128)(2,1)S(1)}, u32[]{:S(2)}, u32[]{:S(2)}) collective-permute-start(bf16[64,1024]{1,0:T(8,128)(2,1)} %refs_1_.1), channel_id=1, source_target_pairs={{0,128},{128,0},{1,129},{129,1},{2,130},{130,2},{3,131},{131,3},{4... | collective-permute-start | bytes 393224 | tf_op jit(solution)/shard_map/ppermute | solution.py:17
  12.6 12.8 %collective-permute-start.9 = (bf16[64,1024]{1,0:T(8,128)(2,1)}, bf16[64,1024]{1,0:T(8,128)(2,1)S(1)}, u32[]{:S(2)}, u32[]{:S(2)}) collective-permute-start(bf16[64,1024]{1,0:T(8,128)(2,1)} %param.10), channel_id=1, source_target_pairs={{0,1},{1,0},{2,3},{3,2},{4,5},{5,4},{6,7},{7,6},{8,9},{9,8},{10,11... | collective-permute-start | bytes 393224 | tf_op jit(solution)/shard_map/ppermute | solution.py:17
  21.7 15.8 %all-to-all-start = ((bf16[4,208,512]{2,1,0:T(8,128)(2,1)}), bf16[4,208,512]{2,1,0:T(8,128)(2,1)S(1)}, u32[]{:S(2)}, u32[]{:S(2)}) async-start(bf16[4,208,512]{2,1,0:T(8,128)(2,1)} %pad_maximum_fusion), calls=%async_computation | async-start | bytes 1703936 | tf_op jit(solution)/shard_map/all_to_all | solution.py:21
  25.3 119.4 %reduce-scatter.2.cloned.1.call-start = ((), (), s32[]{:S(2)}) async-start(), calls=%async_computation.5 | async-start | bytes 2359296 | tf_op jit(solution)/shard_map/reduce_scatter | solution.py:197
  38.4 18.8 %collective-permute-start.1 = (bf16[384,1024]{1,0:T(8,128)(2,1)}, bf16[384,1024]{1,0:T(8,128)(2,1)}, u32[]{:S(2)}, u32[]{:S(2)}) collective-permute-start(bf16[384,1024]{1,0:T(8,128)(2,1)} %shard_map.102), channel_id=1, source_target_pairs={{0,32},{32,64},{64,96},{96,0},{1,33},{33,65},{65,97},{97,1},{2,34}... | collective-permute-start | bytes 2359304 | tf_op jit(solution)/shard_map/ppermute | solution.py:29
  38.7 19.6 %collective-permute-start.2 = (bf16[384,1024]{1,0:T(8,128)(2,1)}, bf16[384,1024]{1,0:T(8,128)(2,1)}, u32[]{:S(2)}, u32[]{:S(2)}) collective-permute-start(bf16[384,1024]{1,0:T(8,128)(2,1)} %shard_map.102), channel_id=1, source_target_pairs={{0,96},{32,0},{64,32},{96,64},{1,97},{33,1},{65,33},{97,65},{2,98}... | collective-permute-start | bytes 2359304 | tf_op jit(solution)/shard_map/ppermute | solution.py:29
  43.9 18.2 %collective-permute-start.10 = (bf16[768,512]{1,0:T(8,128)(2,1)}, bf16[768,512]{1,0:T(8,128)(2,1)}, u32[]{:S(2)}, u32[]{:S(2)}) collective-permute-start(bf16[768,512]{1,0:T(8,128)(2,1)} %fusion.refs_1_), channel_id=1, source_target_pairs={{0,2},{2,0},{1,3},{3,1},{4,6},{6,4},{5,7},{7,5},{8,10},{10,8},{9,1... | collective-permute-start | bytes 2359304 | tf_op jit(solution)/shard_map/ppermute | solution.py:17
  45.1 32.2 %collective-permute-start.11 = (bf16[768,512]{1,0:T(8,128)(2,1)}, bf16[768,512]{1,0:T(8,128)(2,1)}, u32[]{:S(2)}, u32[]{:S(2)}) collective-permute-start(bf16[768,512]{1,0:T(8,128)(2,1)} %fusion.refs_1_), channel_id=1, source_target_pairs={{0,1},{1,0},{2,3},{3,2},{4,5},{5,4},{6,7},{7,6},{8,9},{9,8},{10,11... | collective-permute-start | bytes 2359304 | tf_op jit(solution)/shard_map/ppermute | solution.py:17
  58.2 9.5 %collective-permute-start.3 = (bf16[384,512]{1,0:T(8,128)(2,1)S(1)}, bf16[384,512]{1,0:T(8,128)(2,1)S(1)}, u32[]{:S(2)}, u32[]{:S(2)}) collective-permute-start(bf16[384,512]{1,0:T(8,128)(2,1)S(1)} %slice.60), channel_id=1, source_target_pairs={{0,32},{32,64},{64,96},{96,0},{1,33},{33,65},{65,97},{97,1},{2,34}... | collective-permute-start | bytes 1179656 | tf_op jit(solution)/shard_map/ppermute | solution.py:29
  59.3 8.4 %collective-permute-start.4 = (bf16[384,512]{1,0:T(8,128)(2,1)S(1)}, bf16[384,512]{1,0:T(8,128)(2,1)S(1)}, u32[]{:S(2)}, u32[]{:S(2)}) collective-permute-start(bf16[384,512]{1,0:T(8,128)(2,1)S(1)} %slice.61), channel_id=1, source_target_pairs={{0,96},{32,0},{64,32},{96,64},{1,97},{33,1},{65,33},{97,65},{2,98}... | collective-permute-start | bytes 1179656 | tf_op jit(solution)/shard_map/ppermute | solution.py:29
  62.1 15.2 %collective-permute-start.12 = (bf16[768,512]{1,0:T(8,128)(2,1)}, bf16[768,512]{1,0:T(8,128)(2,1)}, u32[]{:S(2)}, u32[]{:S(2)}) collective-permute-start(bf16[768,512]{1,0:T(8,128)(2,1)} %collective-permute-done.10.refs_2_), channel_id=1, source_target_pairs={{0,1},{1,0},{2,3},{3,2},{4,5},{5,4},{6,7},{7,6},{8,9},{9,8},{10,11... | collective-permute-start | bytes 2359304 | tf_op jit(solution)/shard_map/ppermute | solution.py:17
  73.6 23.0 %collective-permute-start.6 = (bf16[2,768,512]{2,1,0:T(8,128)(2,1)}, bf16[2,768,512]{2,1,0:T(8,128)(2,1)}, u32[]{:S(2)}, u32[]{:S(2)}) collective-permute-start(bf16[2,768,512]{2,1,0:T(8,128)(2,1)} %shard_map.105), channel_id=1, source_target_pairs={{0,1},{1,0},{2,3},{3,2},{4,5},{5,4},{6,7},{7,6},{8,9},{9,8},{10,11... | collective-permute-start | bytes 4718600 | tf_op jit(solution)/shard_map/ppermute | solution.py:17
  98.8 19.5 %collective-permute-start.7 = (bf16[768,512]{1,0:T(8,128)(2,1)}, bf16[768,512]{1,0:T(8,128)(2,1)S(1)}, u32[]{:S(2)}, u32[]{:S(2)}) collective-permute-start(bf16[768,512]{1,0:T(8,128)(2,1)} %fusion.6), channel_id=1, source_target_pairs={{0,2},{2,0},{1,3},{3,1},{4,6},{6,4},{5,7},{7,5},{8,10},{10,8},{9,1... | collective-permute-start | bytes 2359304 | tf_op jit(solution)/shard_map/ppermute | solution.py:17
  99.8 13.2 %collective-permute-start.13 = (bf16[384,512]{1,0:T(8,128)(2,1)}, bf16[384,512]{1,0:T(8,128)(2,1)}, u32[]{:S(2)}, u32[]{:S(2)}) collective-permute-start(bf16[384,512]{1,0:T(8,128)(2,1)} %get-tuple-element.11), channel_id=1, source_target_pairs={{0,32},{32,64},{64,96},{96,0},{1,33},{33,65},{65,97},{97,1},{2,34}... | collective-permute-start | bytes 1179656 | tf_op jit(solution)/shard_map/ppermute | solution.py:29
  100.9 20.4 %collective-permute-start.15 = (bf16[384,512]{1,0:T(8,128)(2,1)}, bf16[384,512]{1,0:T(8,128)(2,1)S(1)}, u32[]{:S(2)}, u32[]{:S(2)}) collective-permute-start(bf16[384,512]{1,0:T(8,128)(2,1)} %get-tuple-element.12), channel_id=1, source_target_pairs={{0,96},{32,0},{64,32},{96,64},{1,97},{33,1},{65,33},{97,65},{2,98}... | collective-permute-start | bytes 1179656 | tf_op jit(solution)/shard_map/ppermute | solution.py:29
  115.1 42.8 %collective-permute-start.14 = (bf16[384,1024]{1,0:T(8,128)(2,1)}, bf16[384,1024]{1,0:T(8,128)(2,1)}, u32[]{:S(2)}, u32[]{:S(2)}) collective-permute-start(bf16[384,1024]{1,0:T(8,128)(2,1)} %pad_maximum_fusion.2), channel_id=1, source_target_pairs={{0,32},{32,64},{64,96},{96,0},{1,33},{33,65},{65,97},{97,1},{2,34}... | collective-permute-start | bytes 2359304 | tf_op jit(solution)/shard_map/ppermute | solution.py:29
  123.7 34.2 %collective-permute-start.16 = (bf16[384,1024]{1,0:T(8,128)(2,1)S(1)}, bf16[384,1024]{1,0:T(8,128)(2,1)}, u32[]{:S(2)}, u32[]{:S(2)}) collective-permute-start(bf16[384,1024]{1,0:T(8,128)(2,1)S(1)} %pad_maximum_fusion.3), channel_id=1, source_target_pairs={{0,96},{32,0},{64,32},{96,64},{1,97},{33,1},{65,33},{97,65},{2,98}... | collective-permute-start | bytes 2359304 | tf_op jit(solution)/shard_map/ppermute | solution.py:29
  127.2 7.6 %collective-permute-start.20 = (bf16[32,512]{1,0:T(8,128)(2,1)S(1)}, bf16[32,512]{1,0:T(8,128)(2,1)S(1)}, u32[]{:S(2)}, u32[]{:S(2)}) collective-permute-start(bf16[32,512]{1,0:T(8,128)(2,1)S(1)} %add_convert_fusion.5), channel_id=1, source_target_pairs={{0,4},{4,0},{8,12},{12,8},{16,20},{20,16},{24,28},{28,24},{1,5},{5... | collective-permute-start | bytes 98312 | tf_op jit(solution)/shard_map/ppermute | solution.py:207
  131.4 20.5 %all-to-all-start.1 = ((bf16[4,192,512]{2,1,0:T(8,128)(2,1)}), bf16[4,192,512]{2,1,0:T(8,128)(2,1)S(1)}, u32[]{:S(2)}, u32[]{:S(2)}) async-start(bf16[4,192,512]{2,1,0:T(8,128)(2,1)} %bitcast.20), calls=%async_computation.1 | async-start | bytes 1572864 | tf_op jit(solution)/shard_map/all_to_all | solution.py:21
  139.6 8.3 %collective-permute-start.22 = (bf16[32,512]{1,0:T(8,128)(2,1)S(1)}, bf16[32,512]{1,0:T(8,128)(2,1)S(1)}, u32[]{:S(2)}, u32[]{:S(2)}) collective-permute-start(bf16[32,512]{1,0:T(8,128)(2,1)S(1)} %add_convert_fusion.3.refs_1_), channel_id=1, source_target_pairs={{0,16},{4,20},{8,24},{12,28},{16,0},{20,4},{24,8},{28,12},{1,17},{... | collective-permute-start | bytes 98312 | tf_op jit(solution)/shard_map/ppermute | solution.py:207
  145.6 20.8 %collective-permute-start.17 = (bf16[64,1024]{1,0:T(8,128)(2,1)S(1)}, bf16[64,1024]{1,0:T(8,128)(2,1)S(1)}, u32[]{:S(2)}, u32[]{:S(2)}) collective-permute-start(bf16[64,1024]{1,0:T(8,128)(2,1)S(1)} %dynamic-slice_bitcast_fusion.6), channel_id=1, source_target_pairs={{0,128},{128,0},{1,129},{129,1},{2,130},{130,2},{3,131},{131,3},{4... | collective-permute-start | bytes 393224 | tf_op jit(solution)/shard_map/ppermute | solution.py:17
  153.1 10.2 %all-to-all-start.2 = ((f32[4,32,512]{2,1,0:T(8,128)}), f32[4,32,512]{2,1,0:T(8,128)S(1)}, u32[]{:S(2)}, u32[]{:S(2)}) async-start(f32[4,32,512]{2,1,0:T(8,128)} %broadcast_in_dim.34), calls=%async_computation.3 | async-start | bytes 524288 | tf_op jit(solution)/shard_map/all_to_all | solution.py:21
  (23 other events, 102.2 us)
Sparse Core Ops, SparseCore 0:
  20.1 38.8 all-gather.1
  84.1 39.3 reduce-scatter.1

commit v4 on v3

--- a/solution.py
+++ b/solution.py
@@ -29,11 +29,10 @@
     return lax.ppermute(a, "y", [(i, (i + k) % NY) for i in range(NY)])
 
 
-def gather_y(a, y, after):
-    at_none = y.reshape(1).astype(jnp.int32)
-    half = a.shape[1] // 2
-    sent = call(copy_body, at_none, (a,), jax.ShapeDtypeStruct(a.shape, a.dtype), after)
-    up, down = turn(sent, 1), turn(sent, -1)
+def gather_y(a, y, first):
+    half, head = a.shape[1] // 2, first[0].shape[0]
+    up = jnp.concatenate([first[0], turn(a[head:], 1)], axis=0)
+    down = jnp.concatenate([first[1], turn(a[head:], -1)], axis=0)
     out = jnp.zeros((NY,) + a.shape, a.dtype)
     for piece, k in ((a, 0), (up, 1), (down, 3)):
         out = lax.dynamic_update_slice(out, piece[None], ((y - k) % NY, 0, 0))
@@ -41,16 +40,16 @@
     return lax.dynamic_update_slice(out, turn(down[:, half:], -1)[None], ((y + 2) % NY, 0, half))
 
 
-def scatter_y(a, y):
+def far_blocks(a, y):
     half = a.shape[2] // 2
-    block = lambda k: pick(a, (y + k) % NY, 0)
-    far = block(2)
-    up, down = turn(far[:, :half], 1), turn(far[:, half:], -1)
-    next_up, next_down = block(1), block(3)
-    add = lambda p, q: (p.astype(F32) + q.astype(F32)).astype(BF)
-    next_up = jnp.concatenate([add(next_up[:, :half], up), next_up[:, half:]], axis=1)
-    next_down = jnp.concatenate([next_down[:, :half], add(next_down[:, half:], down)], axis=1)
-    return block(0).astype(F32) + turn(next_up, 1).astype(F32) + turn(next_down, -1).astype(F32)
+    far = pick(a, (y + 2) % NY, 0)
+    return turn(far[:, :half], 1), turn(far[:, half:], -1)
+
+
+def scatter_y(a, far, y):
+    block = jax.ShapeDtypeStruct(a.shape[1:], BF)
+    up, down = call(pass_body, y.reshape(1).astype(jnp.int32), (a,) + far, (block, block))
+    return pick(a, y, 0).astype(F32) + turn(up, 1).astype(F32) + turn(down, -1).astype(F32)
 
 
 VMEM = pl.BlockSpec(memory_space=pltpu.VMEM)
@@ -59,20 +58,28 @@
 
 
 def call(body, at, operands, out_shape, after=()):
-    size = lambda a: math.prod(a.shape) * a.dtype.itemsize
-    moved = sum(size(a) for a in operands) + size(out_shape)
+    count = len(operands) + 1
     return pl.pallas_call(
-        lambda *refs: body(*refs[: len(operands) + 1], refs[-1]),
+        lambda *refs: body(*refs[:count], *refs[count + len(after) :]),
         out_shape=out_shape,
         in_specs=[SMEM] + [VMEM] * len(operands) + [pl.BlockSpec(memory_space=pl.ANY)] * len(after),
-        out_specs=VMEM,
-        compiler_params=pltpu.CompilerParams(vmem_limit_bytes=32 * 2**20),
-        cost_estimate=pl.CostEstimate(flops=3 * 2**30, bytes_accessed=moved, transcendentals=0),
+        out_specs=jax.tree.map(lambda _: VMEM, out_shape),
+        compiler_params=pltpu.CompilerParams(vmem_limit_bytes=16 * 2**20),
+        cost_estimate=pl.CostEstimate(flops=2**20, bytes_accessed=2**10, transcendentals=0),
     )(at, *operands, *after)
 
 
-def copy_body(at, a, out):
-    out[...] = a[...]
+def pass_body(at, a, from_below, from_above, up, down):
+    half = from_below.shape[1]
+    above, below = lax.rem(at[0] + 1, NY), lax.rem(at[0] + NY - 1, NY)
+    up[:, :half] = (a[above, :, :half].astype(F32) + from_below[...].astype(F32)).astype(BF)
+    up[:, half:] = a[above, :, half:]
+    down[:, :half] = a[below, :, :half]
+    down[:, half:] = (a[below, :, half:].astype(F32) + from_above[...].astype(F32)).astype(BF)
+
+
+def take_body(at, a, out):
+    out[...] = a[at[0]]
 
 
 def add_body(at, a, b, out):
@@ -82,6 +89,19 @@
 def pair_body(at, own, other, out):
     out[at[0]] = own[...]
     out[1 - at[0]] = other[...]
+
+
+def merge_body(at, keep, theirs, away, cot, hot, home, table):
+    x = at[0]
+    projected = keep[x].astype(F32) + theirs[x].astype(F32) + away[...].astype(F32)
+    home[...] = projected.astype(BF)
+    rest = cot[...].astype(F32) * projected
+    total = jnp.zeros(table.shape, F32)
+    for _ in range(3):
+        part = rest.astype(BF)
+        total += jnp.dot(hot[...], part, preferred_element_type=F32)
+        rest = rest - part.astype(F32)
+    table[...] = total
 
 
 def project_body(at, ho, w, out):
@@ -151,6 +171,8 @@
     cot = cotangent.reshape(rows, cols)
     ids = strategy_ids.reshape(rows)
 
+    first = turn(ho[: rows // 4], 1), turn(ho[: rows // 4], -1)
+
     cot_parts = cot.reshape(NC, half, cols)
     other = swap(pick(cot_parts, 1 - c, 0), "c")
     mine = in_order(c, pick(cot_parts, c, 0), other, 0)
@@ -161,14 +183,14 @@
     cot_y = got[:, :half].reshape(NY * half, wide)
     ids_y = got[:, half, :half].astype(jnp.int32).reshape(NY * half)
 
-    ho_y = gather_y(ho, y, (got,)).reshape(NY, NC, half, cols)
+    ho_y = gather_y(ho, y, first).reshape(NY, NC, half, cols)
 
     unit = call(
         pair_body,
         xh.reshape(1).astype(jnp.int32),
         (out_weight, swap(out_weight, "xh")),
         jax.ShapeDtypeStruct((XH,) + out_weight.shape, BF),
-        (other,),
+        (other,) + first,
     )
     weight = lax.all_gather(unit, "z", axis=1, tiled=True)
 
@@ -188,17 +210,27 @@
     project = lambda core, after: call(
         project_body, core.reshape(1).astype(jnp.int32), (ho_y, weight), jax.ShapeDtypeStruct((XL, NY * half, wide), BF), after
     )
-    theirs = swap(project(1 - c, ()), "c")
+    theirs = swap(project(1 - c, (far,)), "c")
     keep = project(c, ())
     chip = lambda x: pick(keep, x, 0).astype(F32) + pick(theirs, x, 0).astype(F32)
-    projected = chip(xl) + swap(chip(1 - xl).astype(BF), "xl").astype(F32)
-
-    wg = call(weight_body, at, pieces + (ho_y,), jax.ShapeDtypeStruct((XH, NZ * wr, cols), BF))
+    away = chip(1 - xl).astype(BF)
+    wg = call(weight_body, at, pieces + (ho_y,), jax.ShapeDtypeStruct((XH, NZ * wr, cols), BF), (away,))
+    head_grad = call(head_body, at, pieces + (weight,), jax.ShapeDtypeStruct((NY, NC, half, cols), BF), (wg,))
+    head_grad = head_grad.reshape(NY, rows, cols)
+    head_far = far_blocks(head_grad, y)
+    home, table_part = call(
+        merge_body,
+        at,
+        (keep, theirs, swap(away, "xl"), cot_y, hot_y.astype(BF)),
+        (jax.ShapeDtypeStruct(away.shape, BF), jax.ShapeDtypeStruct((strategies, wide), F32)),
+        head_far,
+    )
+
     wg_part = lax.psum_scatter(wg, "z", scatter_dimension=1, tiled=True)
-    weight_sum = pick(wg_part, xh, 0).astype(F32) + swap(pick(wg_part, 1 - xh, 0), "xh").astype(F32)
-
-    home = exchange(projected.astype(BF).reshape(NY, half, wide), "y")
-    table_part = jnp.dot(hot_y, cot_y.astype(F32) * projected, precision=HIGHEST)
+    wg_other = swap(pick(wg_part, 1 - xh, 0), "xh")
+    weight_sum = pick(wg_part, xh, 0).astype(F32) + wg_other.astype(F32)
+
+    home = exchange(home.reshape(NY, half, wide), "y")
     table_part = table_part.reshape(NC, strategies // NC, wide)
     table_sum = pick(table_part, c, 0) + swap(pick(table_part, 1 - c, 0), "c")
     table_sum = table_sum + swap(table_sum, "xh")
@@ -210,7 +242,8 @@
         else:
             table_sum = call(add_body, at, (sent, far_sum), jax.ShapeDtypeStruct(sent.shape, F32), (home,))
     table_all = spread(table_sum, "y", NY).reshape(NC, 2, strategies // NC, wide)
-    rest = swap(pick(table_all, 1 - c, 0), "c")
+    rest = jax.ShapeDtypeStruct(table_all.shape[1:], F32)
+    rest = swap(call(take_body, (1 - c).reshape(1).astype(jnp.int32), (table_all,), rest, (wg_other,)), "c")
     table_sum = in_order(c, pick(table_all, c, 0), rest, 1)
     table_sum = table_sum.reshape(2, strategies, wide).transpose(1, 0, 2).reshape(strategies, cols)
     table_grad = jnp.dot(mixing.T, table_sum, precision=HIGHEST) * grad_scale
@@ -222,8 +255,7 @@
     proj = jnp.concatenate([proj[0], proj[1]], axis=1).astype(F32)
     layer_out = (residual.reshape(rows, cols).astype(F32) + proj * gating).astype(BF)
 
-    head_grad = call(head_body, at, pieces + (weight,), jax.ShapeDtypeStruct((NY, NC, half, cols), BF), (keep,))
-    head_grad = scatter_y(head_grad.reshape(NY, rows, cols), y).astype(BF)
+    head_grad = scatter_y(head_grad, head_far, y).astype(BF)
 
     shape = head_out.shape
     return layer_out.reshape(shape), head_grad.reshape(shape), weight_sum * grad_scale, table_grad

time: 180 us -> 193 us (1.072)
  waiting for transfers between devices: 45.4 us -> 55.2 us
  local copies, waits for them, and re-layouts: 24.1 us -> 28.3 us
  starting transfers between devices: 56.3 us -> 53.4 us
  Pallas kernels: 17.6 us -> 20.4 us
    ppermute x13, waiting for transfers between devices: 8.19 us -> 20.1 us  [swap(): return lax.ppermute(a, axis, [(0, 1), (1, 0)])]
    ppermute x13, starting transfers between devices: 22 us -> 16.1 us  [swap(): return lax.ppermute(a, axis, [(0, 1), (1, 0)])]
    ppermute x8 -> x10, waiting for transfers between devices: 17.8 us -> 13.2 us  [turn(): return lax.ppermute(a, 'y', [(i, (i + k) % NY) for i in range(NY)])]
    convert_element_type x5 -> x3, other arithmetic: 8.79 us -> 5.48 us  [the longest x1 2.79 us: on_device(): away = chip(1 - xl).astype(BF)]
    all_to_all x3, waiting for transfers between devices: 18 us -> 21.1 us  [exchange(): return lax.all_to_all(a, axis, 0, 0, tiled=True)]
    pallas_call x7 -> x9, Pallas kernels: 17.6 us -> 20.4 us  [call(): pl.pallas_call(lambda *refs: body(*refs[:count], *refs[count + len(after)...]
    dynamic_update_slice x3, local copies, waits for them, and re-layouts: 2.43 us -> 0.18 us  [gather_y(): out = lax.dynamic_update_slice(out, piece[None], ((y - k) % NY, 0, 0))]
    dot_general x1 -> x0, matrix products: 2.22 us -> none  [on_device(): jnp.dot(hot_y, cot_y.astype(F32) * projected, precision=HIGHEST)]
  transfers between devices with their start and end apart: 29 -> 31, of which waited for: 11 -> 11; matrix products, arithmetic and copies ran while one was open for 17% -> 19% of each run, Pallas kernels for 10% -> 6%
where the time goes in v4:
time: 193 us; the launch traced here: 192 us
  waiting for transfers between devices  55.2 us (29%)
  starting transfers between devices  53.4 us (28%)
  local copies, waits for them, and re-layouts  28.3 us (15%)
  Pallas kernels  20.4 us (11%)
  between operations  14.7 us (8%)
  other arithmetic  12.3 us (6%)
  matrix products  7.91 us (4%)
    all_to_all x3, waiting for transfers between devices, exchange(): return lax.all_to_all(a, axis, 0, 0, tiled=True)  21.1 us
    pallas_call x9, Pallas kernels, call(): pl.pallas_call(lambda *refs: body(*refs[:count], *refs[count + len(after)...  20.4 us
    ppermute x13, waiting for transfers between devices, swap(): return lax.ppermute(a, axis, [(0, 1), (1, 0)])  20.1 us
    ppermute x13, starting transfers between devices, swap(): return lax.ppermute(a, axis, [(0, 1), (1, 0)])  16.1 us
    ppermute x10, starting transfers between devices, turn(): return lax.ppermute(a, 'y', [(i, (i + k) % NY) for i in range(NY)])  13.6 us
    ppermute x10, waiting for transfers between devices, turn(): return lax.ppermute(a, 'y', [(i, (i + k) % NY) for i in range(NY)])  13.2 us
    all_to_all x3, starting transfers between devices, exchange(): return lax.all_to_all(a, axis, 0, 0, tiled=True)  12 us
    ppermute x3, starting transfers between devices, on_device(): far_sum = lax.ppermute(sent, 'z', [(i, i ^ bit) for i in range(NZ)])  11.6 us
  transfers between devices with their start and end apart: 31, of which 11 were waited for; matrix products, arithmetic and copies ran while one was open for 19% of the time, Pallas kernels for 6%

profile of v4, /device:TPU:1, one launch (start us, length us, event | category | flops | bytes accessed | tf_op | source)
XLA Modules:
  0.0 192.0 jit_solution(12059192381743432768)
XLA Ops:
  8.3 3.3 %collective-permute-start.7 = (bf16[192,1024]{1,0:T(8,128)(2,1)S(1)}, bf16[192,1024]{1,0:T(8,128)(2,1)S(1)}, u32[]{:S(2)}, u32[]{:S(2)}) collective-permute-start(bf16[192,1024]{1,0:T(8,128)(2,1)S(1)} %dynamic-slice_bitcast_fusion.2), channel_id=1, source_target_pairs={{0,1},{1,0},{2,3},{3,2},{4,5},{5,4},{6,7},{7,6},{8,9},{9,8},{10,11... | collective-permute-start | bytes 1179656 | tf_op jit(solution)/shard_map/ppermute | solution.py:17
  12.7 2.7 %collective-permute-start.2 = (bf16[96,1024]{1,0:T(8,128)(2,1)S(1)}, bf16[96,1024]{1,0:T(8,128)(2,1)S(1)}, u32[]{:S(2)}, u32[]{:S(2)}) collective-permute-start(bf16[96,1024]{1,0:T(8,128)(2,1)S(1)} %slice.52), channel_id=1, source_target_pairs={{0,96},{32,0},{64,32},{96,64},{1,97},{33,1},{65,33},{97,65},{2,98}... | collective-permute-start | bytes 589832 | tf_op jit(solution)/shard_map/ppermute | solution.py:29
  16.5 5.0 %collective-permute-done.6.refs_2_ = bf16[64,1024]{1,0:T(8,128)(2,1)S(1)} collective-permute-done((bf16[64,1024]{1,0:T(8,128)(2,1)}, bf16[64,1024]{1,0:T(8,128)(2,1)S(1)}, u32[]{:S(2)}, u32[]{:S(2)}) %collective-permute-start.6) | collective-permute-done | bytes 131104 | tf_op jit(solution)/shard_map/ppermute | solution.py:17
  24.2 2.7 %collective-permute-start.3 = (bf16[288,1024]{1,0:T(8,128)(2,1)}, bf16[288,1024]{1,0:T(8,128)(2,1)}, u32[]{:S(2)}, u32[]{:S(2)}) collective-permute-start(bf16[288,1024]{1,0:T(8,128)(2,1)} %slice.53), channel_id=1, source_target_pairs={{0,96},{32,0},{64,32},{96,64},{1,97},{33,1},{65,33},{97,65},{2,98}... | collective-permute-start | bytes 1769480 | tf_op jit(solution)/shard_map/ppermute | solution.py:29
  37.5 4.4 %all-to-all-start = ((bf16[4,208,512]{2,1,0:T(8,128)(2,1)}), bf16[4,208,512]{2,1,0:T(8,128)(2,1)}, u32[]{:S(2)}, u32[]{:S(2)}) async-start(bf16[4,208,512]{2,1,0:T(8,128)(2,1)} %pad_maximum_fusion), calls=%async_computation | async-start | bytes 1703936 | tf_op jit(solution)/shard_map/all_to_all | solution.py:21
  51.3 3.6 %all-to-all-done = bf16[4,208,512]{2,1,0:T(8,128)(2,1)} async-done(((bf16[4,208,512]{2,1,0:T(8,128)(2,1)}), bf16[4,208,512]{2,1,0:T(8,128)(2,1)}, u32[]{:S(2)}, u32[]{:S(2)}) %all-to-all-start) | async-done | bytes 852000 | tf_op jit(solution)/shard_map/all_to_all | solution.py:21
  59.0 4.1 %collective-permute-done.4 = bf16[384,512]{1,0:T(8,128)(2,1)} collective-permute-done((bf16[384,512]{1,0:T(8,128)(2,1)}, bf16[384,512]{1,0:T(8,128)(2,1)}, u32[]{:S(2)}, u32[]{:S(2)}) %collective-permute-start.4) | collective-permute-done | bytes 393248 | tf_op jit(solution)/shard_map/ppermute | solution.py:29
  65.2 11.4 %collective-permute-done.9.refs_3_.refs_2_ = bf16[768,512]{1,0:T(8,128)(2,1)} collective-permute-done((bf16[768,512]{1,0:T(8,128)(2,1)}, bf16[768,512]{1,0:T(8,128)(2,1)}, u32[]{:S(2)}, u32[]{:S(2)}) %collective-permute-start.9) | collective-permute-done | bytes 786464 | tf_op jit(solution)/shard_map/ppermute | solution.py:17
  78.2 3.0 %shard_map.104 = bf16[2,768,512]{2,1,0:T(8,128)(2,1)} custom-call(s32[1]{0:T(128)} %bitcast.13.refs_0_, bf16[4,2,192,1024]{3,2,1,0:T(8,128)(2,1)S(1)} %bitcast.100, bf16[2,512,1024]{2,1,0:T(8,128)(2,1)S(1)} %copy-done, bf16[768,512]{1,0:T(8,128)(2,1)} %collective-permute-done.9.refs_3_.refs_2_), custom_call_target="tpu_custom_call" | custom-call | flops 1048576 | bytes 1024 | tf_op jit(solution)/shard_map/pallas_call | solution.py:62
  81.2 2.5 %collective-permute-start.10 = (bf16[2,768,512]{2,1,0:T(8,128)(2,1)}, bf16[2,768,512]{2,1,0:T(8,128)(2,1)}, u32[]{:S(2)}, u32[]{:S(2)}) collective-permute-start(bf16[2,768,512]{2,1,0:T(8,128)(2,1)} %shard_map.104), channel_id=1, source_target_pairs={{0,1},{1,0},{2,3},{3,2},{4,5},{5,4},{6,7},{7,6},{8,9},{9,8},{10,11... | collective-permute-start | bytes 4718600 | tf_op jit(solution)/shard_map/ppermute | solution.py:17
  87.7 2.8 %fusion.3.refs_6_ = bf16[768,512]{1,0:T(8,128)(2,1)} fusion(bf16[2,768,512]{2,1,0:T(8,128)(2,1)} %collective-permute-done.10.refs_2_, s32[]{:T(128)S(6)} %select_n.145, bf16[2,768,512]{2,1,0:T(8,128)(2,1)S(1)} %shard_map.103.refs_1_), kind=kLoop, calls=%fused_computation.9 | loop fusion | flops 1572864 | bytes 2359300 | tf_op jit(solution)/shard_map/convert_element_type | solution.py:216
  90.5 5.3 %shard_map.105.refs_6_ = bf16[2,512,1024]{2,1,0:T(8,128)(2,1)S(1)} custom-call(s32[2]{0:T(128)S(1)} %pad_add_fusion.refs_0_, bf16[768,512]{1,0:T(8,128)(2,1)} %multiply_convert_fusion.refs_1_, bf16[768,512]{1,0:T(8,128)(2,1)} %collective-permute-done.9.refs_3_.refs_2_, bf16[768,512]{1,0:T(8,128)(2,1)} %collective-permute-done.12.refs_3_, ...), custom_call_target="tpu_custom_call" | custom-call | flops 1048576 | bytes 1024 | tf_op jit(solution)/shard_map/pallas_call | solution.py:62
  100.5 5.3 %shard_map.106 = bf16[4,2,192,1024]{3,2,1,0:T(8,128)(2,1)S(1)} custom-call(s32[2]{0:T(128)S(1)} %pad_add_fusion.refs_0_, bf16[768,512]{1,0:T(8,128)(2,1)} %multiply_convert_fusion.refs_1_, bf16[768,512]{1,0:T(8,128)(2,1)} %collective-permute-done.9.refs_3_.refs_2_, bf16[768,512]{1,0:T(8,128)(2,1)} %collective-permute-done.12.refs_3_, ...), custom_call_target="tpu_custom_call" | custom-call | flops 1048576 | bytes 1024 | tf_op jit(solution)/shard_map/pallas_call | solution.py:62
  106.3 2.4 %collective-permute-start.15 = (bf16[384,512]{1,0:T(8,128)(2,1)S(1)}, bf16[384,512]{1,0:T(8,128)(2,1)S(1)}, u32[]{:S(2)}, u32[]{:S(2)}) collective-permute-start(bf16[384,512]{1,0:T(8,128)(2,1)S(1)} %get-tuple-element.18), channel_id=1, source_target_pairs={{0,96},{32,0},{64,32},{96,64},{1,97},{33,1},{65,33},{97,65},{2,98}... | collective-permute-start | bytes 1179656 | tf_op jit(solution)/shard_map/ppermute | solution.py:29
  108.7 9.1 %collective-permute-done.14.refs_6_.refs_2_ = bf16[384,512]{1,0:T(8,128)(2,1)S(1)} collective-permute-done((bf16[384,512]{1,0:T(8,128)(2,1)S(1)}, bf16[384,512]{1,0:T(8,128)(2,1)S(1)}, u32[]{:S(2)}, u32[]{:S(2)}) %collective-permute-start.14) | collective-permute-done | bytes 393248 | tf_op jit(solution)/shard_map/ppermute | solution.py:29
  117.8 2.4 %shard_map.107 = (bf16[768,512]{1,0:T(8,128)(2,1)S(1)}, f32[64,512]{1,0:T(8,128)S(1)}) custom-call(s32[2]{0:T(128)S(1)} %pad_add_fusion.refs_0_, bf16[2,768,512]{2,1,0:T(8,128)(2,1)S(1)} %copy-done.6, bf16[2,768,512]{2,1,0:T(8,128)(2,1)} %collective-permute-done.10.refs_2_, bf16[768,512]{1,0:T(8,128)(2,1)S(1)} %collective-permute-done.11.refs_3_, ...), custom_call_target="tpu_custom_call" | custom-call | flops 1048576 | bytes 1024 | tf_op jit(solution)/shard_map/pallas_call | solution.py:62
  125.7 2.7 %collective-permute-start.18 = (bf16[384,1024]{1,0:T(8,128)(2,1)}, bf16[384,1024]{1,0:T(8,128)(2,1)}, u32[]{:S(2)}, u32[]{:S(2)}) collective-permute-start(bf16[384,1024]{1,0:T(8,128)(2,1)} %get-tuple-element.10), channel_id=1, source_target_pairs={{0,96},{32,0},{64,32},{96,64},{1,97},{33,1},{65,33},{97,65},{2,98}... | collective-permute-start | bytes 2359304 | tf_op jit(solution)/shard_map/ppermute | solution.py:29
  128.4 4.2 %all-to-all-start.1 = ((bf16[4,192,512]{2,1,0:T(8,128)(2,1)}), bf16[4,192,512]{2,1,0:T(8,128)(2,1)}, u32[]{:S(2)}, u32[]{:S(2)}) async-start(bf16[4,192,512]{2,1,0:T(8,128)(2,1)} %bitcast.110), calls=%async_computation.1 | async-start | bytes 1572864 | tf_op jit(solution)/shard_map/all_to_all | solution.py:21
  136.3 2.8 %collective-permute-start.23 = (bf16[32,512]{1,0:T(8,128)(2,1)S(1)}, bf16[32,512]{1,0:T(8,128)(2,1)S(1)}, u32[]{:S(2)}, u32[]{:S(2)}) collective-permute-start(bf16[32,512]{1,0:T(8,128)(2,1)S(1)} %add_convert_fusion.2), channel_id=1, source_target_pairs={{0,8},{4,12},{8,0},{12,4},{16,24},{20,28},{24,16},{28,20},{1,9},{5... | collective-permute-start | bytes 98312 | tf_op jit(solution)/shard_map/ppermute | solution.py:239
  139.2 16.1 %all-to-all-done.1.refs_3_ = bf16[4,192,512]{2,1,0:T(8,128)(2,1)} async-done(((bf16[4,192,512]{2,1,0:T(8,128)(2,1)}), bf16[4,192,512]{2,1,0:T(8,128)(2,1)}, u32[]{:S(2)}, u32[]{:S(2)}) %all-to-all-start.1) | async-done | bytes 786464 | tf_op jit(solution)/shard_map/all_to_all | solution.py:21
  158.5 7.1 %collective-permute-start.24 = (bf16[32,512]{1,0:T(8,128)(2,1)S(1)}, bf16[32,512]{1,0:T(8,128)(2,1)S(1)}, u32[]{:S(2)}, u32[]{:S(2)}) collective-permute-start(bf16[32,512]{1,0:T(8,128)(2,1)S(1)} %add_convert_fusion.1.refs_1_), channel_id=1, source_target_pairs={{0,16},{4,20},{8,24},{12,28},{16,0},{20,4},{24,8},{28,12},{1,17},{... | collective-permute-start | bytes 98312 | tf_op jit(solution)/shard_map/ppermute | solution.py:239
  165.6 2.7 %fusion.1 = bf16[384,1024]{1,0:T(8,128)(2,1)} fusion(bf16[384,1024]{1,0:T(8,128)(2,1)} %collective-permute-done.18, bf16[384,1024]{1,0:T(8,128)(2,1)} %collective-permute-done.17, bf16[4,384,1024]{2,1,0:T(8,128)(2,1)S(1)} %bitcast.105, s32[]{:T(128)S(6)} %select_n.148), kind=kLoop, calls=%fused_computation.2 | loop fusion | flops 2359296 | bytes 3145732 | tf_op jit(solution)/shard_map/convert_element_type | solution.py:258
  169.6 3.4 %all-to-all-start.2 = ((f32[4,32,512]{2,1,0:T(8,128)}), f32[4,32,512]{2,1,0:T(8,128)S(1)}, u32[]{:S(2)}, u32[]{:S(2)}) async-start(f32[4,32,512]{2,1,0:T(8,128)} %broadcast_in_dim.34), calls=%async_computation.3 | async-start | bytes 524288 | tf_op jit(solution)/shard_map/all_to_all | solution.py:21
  179.2 2.5 %collective-permute-done.19.refs_2_ = bf16[64,1024]{1,0:T(8,128)(2,1)S(1)} collective-permute-done((bf16[64,1024]{1,0:T(8,128)(2,1)S(1)}, bf16[64,1024]{1,0:T(8,128)(2,1)S(1)}, u32[]{:S(2)}, u32[]{:S(2)}) %collective-permute-start.19) | collective-permute-done | bytes 131104 | tf_op jit(solution)/shard_map/ppermute | solution.py:17
  (160 shorter events, 65.9 us)
Async XLA Ops:
  7.2 69.4 %all-gather.2.cloned.1.call-start = ((), (), s32[]{:S(2)}) async-start(), calls=%async_computation.4 | async-start | bytes 2359296 | tf_op jit(solution)/shard_map/all_gather | solution.py:195
  8.3 13.3 %collective-permute-start.7 = (bf16[192,1024]{1,0:T(8,128)(2,1)S(1)}, bf16[192,1024]{1,0:T(8,128)(2,1)S(1)}, u32[]{:S(2)}, u32[]{:S(2)}) collective-permute-start(bf16[192,1024]{1,0:T(8,128)(2,1)S(1)} %dynamic-slice_bitcast_fusion.2), channel_id=1, source_target_pairs={{0,1},{1,0},{2,3},{3,2},{4,5},{5,4},{6,7},{7,6},{8,9},{9,8},{10,11... | collective-permute-start | bytes 1179656 | tf_op jit(solution)/shard_map/ppermute | solution.py:17
  12.6 8.9 %collective-permute-start = (bf16[96,1024]{1,0:T(8,128)(2,1)S(1)}, bf16[96,1024]{1,0:T(8,128)(2,1)S(1)}, u32[]{:S(2)}, u32[]{:S(2)}) collective-permute-start(bf16[96,1024]{1,0:T(8,128)(2,1)S(1)} %slice.52), channel_id=1, source_target_pairs={{0,32},{32,64},{64,96},{96,0},{1,33},{33,65},{65,97},{97,1},{2,34}... | collective-permute-start | bytes 589832 | tf_op jit(solution)/shard_map/ppermute | solution.py:29
  12.7 8.9 %collective-permute-start.2 = (bf16[96,1024]{1,0:T(8,128)(2,1)S(1)}, bf16[96,1024]{1,0:T(8,128)(2,1)S(1)}, u32[]{:S(2)}, u32[]{:S(2)}) collective-permute-start(bf16[96,1024]{1,0:T(8,128)(2,1)S(1)} %slice.52), channel_id=1, source_target_pairs={{0,96},{32,0},{64,32},{96,64},{1,97},{33,1},{65,33},{97,65},{2,98}... | collective-permute-start | bytes 589832 | tf_op jit(solution)/shard_map/ppermute | solution.py:29
  24.2 19.6 %collective-permute-start.1 = (bf16[288,1024]{1,0:T(8,128)(2,1)}, bf16[288,1024]{1,0:T(8,128)(2,1)}, u32[]{:S(2)}, u32[]{:S(2)}) collective-permute-start(bf16[288,1024]{1,0:T(8,128)(2,1)} %slice.53), channel_id=1, source_target_pairs={{0,32},{32,64},{64,96},{96,0},{1,33},{33,65},{65,97},{97,1},{2,34}... | collective-permute-start | bytes 1769480 | tf_op jit(solution)/shard_map/ppermute | solution.py:29
  24.2 23.0 %collective-permute-start.3 = (bf16[288,1024]{1,0:T(8,128)(2,1)}, bf16[288,1024]{1,0:T(8,128)(2,1)}, u32[]{:S(2)}, u32[]{:S(2)}) collective-permute-start(bf16[288,1024]{1,0:T(8,128)(2,1)} %slice.53), channel_id=1, source_target_pairs={{0,96},{32,0},{64,32},{96,64},{1,97},{33,1},{65,33},{97,65},{2,98}... | collective-permute-start | bytes 1769480 | tf_op jit(solution)/shard_map/ppermute | solution.py:29
  37.5 17.4 %all-to-all-start = ((bf16[4,208,512]{2,1,0:T(8,128)(2,1)}), bf16[4,208,512]{2,1,0:T(8,128)(2,1)}, u32[]{:S(2)}, u32[]{:S(2)}) async-start(bf16[4,208,512]{2,1,0:T(8,128)(2,1)} %pad_maximum_fusion), calls=%async_computation | async-start | bytes 1703936 | tf_op jit(solution)/shard_map/all_to_all | solution.py:21
  41.9 132.5 %reduce-scatter.2.cloned.1.call-start = ((), (), s32[]{:S(2)}) async-start(), calls=%async_computation.5 | async-start | bytes 2359296 | tf_op jit(solution)/shard_map/reduce_scatter | solution.py:229
  45.8 17.3 %collective-permute-start.4 = (bf16[384,512]{1,0:T(8,128)(2,1)}, bf16[384,512]{1,0:T(8,128)(2,1)}, u32[]{:S(2)}, u32[]{:S(2)}) collective-permute-start(bf16[384,512]{1,0:T(8,128)(2,1)} %slice.54), channel_id=1, source_target_pairs={{0,32},{32,64},{64,96},{96,0},{1,33},{33,65},{65,97},{97,1},{2,34}... | collective-permute-start | bytes 1179656 | tf_op jit(solution)/shard_map/ppermute | solution.py:29
  50.0 14.2 %collective-permute-start.5 = (bf16[384,512]{1,0:T(8,128)(2,1)}, bf16[384,512]{1,0:T(8,128)(2,1)}, u32[]{:S(2)}, u32[]{:S(2)}) collective-permute-start(bf16[384,512]{1,0:T(8,128)(2,1)} %slice.55), channel_id=1, source_target_pairs={{0,96},{32,0},{64,32},{96,64},{1,97},{33,1},{65,33},{97,65},{2,98}... | collective-permute-start | bytes 1179656 | tf_op jit(solution)/shard_map/ppermute | solution.py:29
  58.8 17.8 %collective-permute-start.9 = (bf16[768,512]{1,0:T(8,128)(2,1)}, bf16[768,512]{1,0:T(8,128)(2,1)}, u32[]{:S(2)}, u32[]{:S(2)}) collective-permute-start(bf16[768,512]{1,0:T(8,128)(2,1)} %multiply_convert_fusion.refs_1_), channel_id=1, source_target_pairs={{0,2},{2,0},{1,3},{3,1},{4,6},{6,4},{5,7},{7,5},{8,10},{10,8},{9,1... | collective-permute-start | bytes 2359304 | tf_op jit(solution)/shard_map/ppermute | solution.py:17
  83.7 6.8 %collective-permute-start.12 = (bf16[768,512]{1,0:T(8,128)(2,1)}, bf16[768,512]{1,0:T(8,128)(2,1)}, u32[]{:S(2)}, u32[]{:S(2)}) collective-permute-start(bf16[768,512]{1,0:T(8,128)(2,1)} %multiply_convert_fusion.refs_1_), channel_id=1, source_target_pairs={{0,1},{1,0},{2,3},{3,2},{4,5},{5,4},{6,7},{7,6},{8,9},{9,8},{10,11... | collective-permute-start | bytes 2359304 | tf_op jit(solution)/shard_map/ppermute | solution.py:17
  83.7 6.8 %collective-permute-start.13 = (bf16[768,512]{1,0:T(8,128)(2,1)}, bf16[768,512]{1,0:T(8,128)(2,1)}, u32[]{:S(2)}, u32[]{:S(2)}) collective-permute-start(bf16[768,512]{1,0:T(8,128)(2,1)} %collective-permute-done.9.refs_3_.refs_2_), channel_id=1, source_target_pairs={{0,1},{1,0},{2,3},{3,2},{4,5},{5,4},{6,7},{7,6},{8,9},{9,8},{10,11... | collective-permute-start | bytes 2359304 | tf_op jit(solution)/shard_map/ppermute | solution.py:17
  97.2 20.5 %collective-permute-start.11 = (bf16[768,512]{1,0:T(8,128)(2,1)}, bf16[768,512]{1,0:T(8,128)(2,1)S(1)}, u32[]{:S(2)}, u32[]{:S(2)}) collective-permute-start(bf16[768,512]{1,0:T(8,128)(2,1)} %fusion.3.refs_6_), channel_id=1, source_target_pairs={{0,2},{2,0},{1,3},{3,1},{4,6},{6,4},{5,7},{7,5},{8,10},{10,8},{9,1... | collective-permute-start | bytes 2359304 | tf_op jit(solution)/shard_map/ppermute | solution.py:17
  106.0 11.8 %collective-permute-start.14 = (bf16[384,512]{1,0:T(8,128)(2,1)S(1)}, bf16[384,512]{1,0:T(8,128)(2,1)S(1)}, u32[]{:S(2)}, u32[]{:S(2)}) collective-permute-start(bf16[384,512]{1,0:T(8,128)(2,1)S(1)} %get-tuple-element.19), channel_id=1, source_target_pairs={{0,32},{32,64},{64,96},{96,0},{1,33},{33,65},{65,97},{97,1},{2,34}... | collective-permute-start | bytes 1179656 | tf_op jit(solution)/shard_map/ppermute | solution.py:29
  106.3 11.5 %collective-permute-start.15 = (bf16[384,512]{1,0:T(8,128)(2,1)S(1)}, bf16[384,512]{1,0:T(8,128)(2,1)S(1)}, u32[]{:S(2)}, u32[]{:S(2)}) collective-permute-start(bf16[384,512]{1,0:T(8,128)(2,1)S(1)} %get-tuple-element.18), channel_id=1, source_target_pairs={{0,96},{32,0},{64,32},{96,64},{1,97},{33,1},{65,33},{97,65},{2,98}... | collective-permute-start | bytes 1179656 | tf_op jit(solution)/shard_map/ppermute | solution.py:29
  122.2 10.4 %collective-permute-start.21 = (f32[32,512]{1,0:T(8,128)S(1)}, f32[32,512]{1,0:T(8,128)S(1)}, u32[]{:S(2)}, u32[]{:S(2)}) collective-permute-start(f32[32,512]{1,0:T(8,128)S(1)} %bitcast_add_fusion), channel_id=1, source_target_pairs={{0,128},{128,0},{1,129},{129,1},{2,130},{130,2},{3,131},{131,3},{4... | collective-permute-start | bytes 196616 | tf_op jit(solution)/shard_map/ppermute | solution.py:17
  125.7 40.0 %collective-permute-start.17 = (bf16[384,1024]{1,0:T(8,128)(2,1)}, bf16[384,1024]{1,0:T(8,128)(2,1)}, u32[]{:S(2)}, u32[]{:S(2)}) collective-permute-start(bf16[384,1024]{1,0:T(8,128)(2,1)} %get-tuple-element.9), channel_id=1, source_target_pairs={{0,32},{32,64},{64,96},{96,0},{1,33},{33,65},{65,97},{97,1},{2,34}... | collective-permute-start | bytes 2359304 | tf_op jit(solution)/shard_map/ppermute | solution.py:29
  125.7 40.0 %collective-permute-start.18 = (bf16[384,1024]{1,0:T(8,128)(2,1)}, bf16[384,1024]{1,0:T(8,128)(2,1)}, u32[]{:S(2)}, u32[]{:S(2)}) collective-permute-start(bf16[384,1024]{1,0:T(8,128)(2,1)} %get-tuple-element.10), channel_id=1, source_target_pairs={{0,96},{32,0},{64,32},{96,64},{1,97},{33,1},{65,33},{97,65},{2,98}... | collective-permute-start | bytes 2359304 | tf_op jit(solution)/shard_map/ppermute | solution.py:29
  128.4 26.8 %all-to-all-start.1 = ((bf16[4,192,512]{2,1,0:T(8,128)(2,1)}), bf16[4,192,512]{2,1,0:T(8,128)(2,1)}, u32[]{:S(2)}, u32[]{:S(2)}) async-start(bf16[4,192,512]{2,1,0:T(8,128)(2,1)} %bitcast.110), calls=%async_computation.1 | async-start | bytes 1572864 | tf_op jit(solution)/shard_map/all_to_all | solution.py:21
  136.3 22.2 %collective-permute-start.23 = (bf16[32,512]{1,0:T(8,128)(2,1)S(1)}, bf16[32,512]{1,0:T(8,128)(2,1)S(1)}, u32[]{:S(2)}, u32[]{:S(2)}) collective-permute-start(bf16[32,512]{1,0:T(8,128)(2,1)S(1)} %add_convert_fusion.2), channel_id=1, source_target_pairs={{0,8},{4,12},{8,0},{12,4},{16,24},{20,28},{24,16},{28,20},{1,9},{5... | collective-permute-start | bytes 98312 | tf_op jit(solution)/shard_map/ppermute | solution.py:239
  157.0 16.0 %collective-permute-start.16 = (bf16[2,192,512]{2,1,0:T(8,128)(2,1)}, bf16[2,192,512]{2,1,0:T(8,128)(2,1)}, u32[]{:S(2)}, u32[]{:S(2)}) collective-permute-start(bf16[2,192,512]{2,1,0:T(8,128)(2,1)} %dynamic-slice_bitcast_fusion.1), channel_id=1, source_target_pairs={{0,1},{1,0},{2,3},{3,2},{4,5},{5,4},{6,7},{7,6},{8,9},{9,8},{10,11... | collective-permute-start | bytes 1179656 | tf_op jit(solution)/shard_map/ppermute | solution.py:17
  158.5 9.8 %collective-permute-start.24 = (bf16[32,512]{1,0:T(8,128)(2,1)S(1)}, bf16[32,512]{1,0:T(8,128)(2,1)S(1)}, u32[]{:S(2)}, u32[]{:S(2)}) collective-permute-start(bf16[32,512]{1,0:T(8,128)(2,1)S(1)} %add_convert_fusion.1.refs_1_), channel_id=1, source_target_pairs={{0,16},{4,20},{8,24},{12,28},{16,0},{20,4},{24,8},{28,12},{1,17},{... | collective-permute-start | bytes 98312 | tf_op jit(solution)/shard_map/ppermute | solution.py:239
  169.6 9.6 %all-to-all-start.2 = ((f32[4,32,512]{2,1,0:T(8,128)}), f32[4,32,512]{2,1,0:T(8,128)S(1)}, u32[]{:S(2)}, u32[]{:S(2)}) async-start(f32[4,32,512]{2,1,0:T(8,128)} %broadcast_in_dim.34), calls=%async_computation.3 | async-start | bytes 524288 | tf_op jit(solution)/shard_map/all_to_all | solution.py:21
  (34 other events, 194.8 us)
Sparse Core Ops, SparseCore 0:
  23.5 38.2 all-gather.1
  97.4 36.6 reduce-scatter.1

commit v5 on v4

--- a/solution.py
+++ b/solution.py
@@ -29,10 +29,9 @@
     return lax.ppermute(a, "y", [(i, (i + k) % NY) for i in range(NY)])
 
 
-def gather_y(a, y, first):
-    half, head = a.shape[1] // 2, first[0].shape[0]
-    up = jnp.concatenate([first[0], turn(a[head:], 1)], axis=0)
-    down = jnp.concatenate([first[1], turn(a[head:], -1)], axis=0)
+def gather_y(a, y):
+    half = a.shape[1] // 2
+    up, down = turn(a, 1), turn(a, -1)
     out = jnp.zeros((NY,) + a.shape, a.dtype)
     for piece, k in ((a, 0), (up, 1), (down, 3)):
         out = lax.dynamic_update_slice(out, piece[None], ((y - k) % NY, 0, 0))
@@ -46,9 +45,9 @@
     return turn(far[:, :half], 1), turn(far[:, half:], -1)
 
 
-def scatter_y(a, far, y):
+def scatter_y(a, far, y, after):
     block = jax.ShapeDtypeStruct(a.shape[1:], BF)
-    up, down = call(pass_body, y.reshape(1).astype(jnp.int32), (a,) + far, (block, block))
+    up, down = call(pass_body, y.reshape(1).astype(jnp.int32), (a,) + far, (block, block), after)
     return pick(a, y, 0).astype(F32) + turn(up, 1).astype(F32) + turn(down, -1).astype(F32)
 
 
@@ -91,16 +90,46 @@
     out[1 - at[0]] = other[...]
 
 
-def merge_body(at, keep, theirs, away, cot, hot, home, table):
-    x = at[0]
-    projected = keep[x].astype(F32) + theirs[x].astype(F32) + away[...].astype(F32)
-    home[...] = projected.astype(BF)
-    rest = cot[...].astype(F32) * projected
+def split3(a):
+    parts = []
+    for _ in range(3):
+        parts.append(a.astype(BF))
+        a = a - parts[-1].astype(F32)
+    return parts
+
+
+def hot_of(got, k, rows, strategies):
+    ids = got[k, rows : rows + 16, :].astype(F32)[:1, :rows]
+    return (lax.broadcasted_iota(jnp.int32, (strategies, rows), 0).astype(F32) == ids).astype(BF)
+
+
+def table_body(at, mixing, own, there, out):
+    where = pl.ds(pl.multiple_of(at[1] * out.shape[1], 128), out.shape[1])
+    table = jnp.where(at[0] == 1, own[:, where].astype(F32), there[:, where].astype(F32))
+    out[...] = jnp.dot(mixing[...], table, precision=HIGHEST, preferred_element_type=F32)
+
+
+def gate_body(at, got, table, out):
+    rows = out.shape[0] // NY
+    parts = split3(table[...])
+    for k in range(NY):
+        hot = hot_of(got, k, rows, table.shape[0])
+        gating = jnp.ones((rows, out.shape[1]), F32)
+        for part in reversed(parts):
+            gating += lax.dot_general(hot, part, (((0,), (0,)), ((), ())), preferred_element_type=F32)
+        out[k * rows : (k + 1) * rows, :] = (got[k, :rows, :].astype(F32) * gating).astype(BF)
+
+
+def merge_body(at, keep, theirs, away, got, home, table):
+    x, rows = at[0], home.shape[0] // NY
     total = jnp.zeros(table.shape, F32)
-    for _ in range(3):
-        part = rest.astype(BF)
-        total += jnp.dot(hot[...], part, preferred_element_type=F32)
-        rest = rest - part.astype(F32)
+    for k in range(NY):
+        span = slice(k * rows, (k + 1) * rows)
+        projected = keep[x, span, :].astype(F32) + theirs[x, span, :].astype(F32) + away[span, :].astype(F32)
+        home[span, :] = projected.astype(BF)
+        hot = hot_of(got, k, rows, table.shape[0])
+        for part in split3(got[k, :rows, :].astype(F32) * projected):
+            total += jnp.dot(hot, part, preferred_element_type=F32)
     table[...] = total
 
 
@@ -171,8 +200,6 @@
     cot = cotangent.reshape(rows, cols)
     ids = strategy_ids.reshape(rows)
 
-    first = turn(ho[: rows // 4], 1), turn(ho[: rows // 4], -1)
-
     cot_parts = cot.reshape(NC, half, cols)
     other = swap(pick(cot_parts, 1 - c, 0), "c")
     mine = in_order(c, pick(cot_parts, c, 0), other, 0)
@@ -180,28 +207,24 @@
     tag = pick(ids.reshape(NC, half), c, 0).astype(BF)
     tag = jnp.broadcast_to(jnp.pad(tag, (0, wide - half))[None, None], (NY, pad, wide))
     got = exchange(jnp.concatenate([by_y, tag], axis=1), "y")
-    cot_y = got[:, :half].reshape(NY * half, wide)
-    ids_y = got[:, half, :half].astype(jnp.int32).reshape(NY * half)
-
-    ho_y = gather_y(ho, y, first).reshape(NY, NC, half, cols)
+
+    ho_y = gather_y(ho, y).reshape(NY, NC, half, cols)
 
     unit = call(
         pair_body,
         xh.reshape(1).astype(jnp.int32),
         (out_weight, swap(out_weight, "xh")),
         jax.ShapeDtypeStruct((XH,) + out_weight.shape, BF),
-        (other,) + first,
+        (other,),
     )
     weight = lax.all_gather(unit, "z", axis=1, tiled=True)
 
     mixing = mixture(meta_graph)
     table = jnp.dot(mixing, strategy_table.astype(F32), precision=HIGHEST)
     there = swap(strategy_table, "c")
-    owner = jnp.where(y // 2 == c, strategy_table, there).reshape(strategies, 2, wide)
-    table_y = jnp.dot(mixing, pick(owner, y % 2, 1).astype(F32), precision=HIGHEST)
-    hot_y = members(ids_y, strategies)
-    gating_y = 1.0 + rows_of(hot_y, table_y)
-    grad_y = (cot_y.astype(F32) * gating_y).astype(BF)
+    source = jnp.stack([(y // 2 == c).astype(jnp.int32), (y % 2).astype(jnp.int32)])
+    table_y = call(table_body, source, (mixing, strategy_table, there), jax.ShapeDtypeStruct((strategies, wide), F32))
+    grad_y = call(gate_body, source, (got, table_y), jax.ShapeDtypeStruct((NY * half, wide), BF))
 
     far = swap(grad_y, "xl")
     pieces = (grad_y, far, swap(grad_y, "c"), swap(far, "c"))
@@ -221,7 +244,7 @@
     home, table_part = call(
         merge_body,
         at,
-        (keep, theirs, swap(away, "xl"), cot_y, hot_y.astype(BF)),
+        (keep, theirs, swap(away, "xl"), got),
         (jax.ShapeDtypeStruct(away.shape, BF), jax.ShapeDtypeStruct((strategies, wide), F32)),
         head_far,
     )
@@ -255,7 +278,7 @@
     proj = jnp.concatenate([proj[0], proj[1]], axis=1).astype(F32)
     layer_out = (residual.reshape(rows, cols).astype(F32) + proj * gating).astype(BF)
 
-    head_grad = scatter_y(head_grad, head_far, y).astype(BF)
+    head_grad = scatter_y(head_grad, head_far, y, (home,)).astype(BF)
 
     shape = head_out.shape
     return layer_out.reshape(shape), head_grad.reshape(shape), weight_sum * grad_scale, table_grad

time: 193 us -> 184 us (0.953)
  waiting for transfers between devices: 55.2 us -> 43.4 us
  Pallas kernels: 20.4 us -> 24.6 us
  matrix products: 7.91 us -> 3.96 us
  starting transfers between devices: 53.4 us -> 56.9 us
    all_to_all x3, waiting for transfers between devices: 21.1 us -> 3.3 us  [exchange(): return lax.all_to_all(a, axis, 0, 0, tiled=True)]
    ppermute x10 -> x8, waiting for transfers between devices: 13.2 us -> 22.2 us  [turn(): return lax.ppermute(a, 'y', [(i, (i + k) % NY) for i in range(NY)])]
    ppermute x13, starting transfers between devices: 16.1 us -> 24.2 us  [swap(): return lax.ppermute(a, axis, [(0, 1), (1, 0)])]
    pallas_call x9 -> x11, Pallas kernels: 20.4 us -> 24.6 us  [call(): pl.pallas_call(lambda *refs: body(*refs[:count], *refs[count + len(after)...]
    ppermute x13, waiting for transfers between devices: 20.1 us -> 16.1 us  [swap(): return lax.ppermute(a, axis, [(0, 1), (1, 0)])]
    slice x3 -> x0, local copies, waits for them, and re-layouts: 3.07 us -> none  [the longest x1 1.26 us: on_device(): cot_y = got[:, :half].reshape(NY * half, wide)]
    ppermute x10 -> x8, starting transfers between devices: 13.6 us -> 10.9 us  [turn(): return lax.ppermute(a, 'y', [(i, (i + k) % NY) for i in range(NY)])]
    dynamic_update_slice x3, local copies, waits for them, and re-layouts: 0.18 us -> 2.43 us  [gather_y(): out = lax.dynamic_update_slice(out, piece[None], ((y - k) % NY, 0, 0))]
  transfers between devices with their start and end apart: 31 -> 29, of which waited for: 11 -> 10; matrix products, arithmetic and copies ran while one was open for 19% -> 16% of each run, Pallas kernels for 6% -> 8%
where the time goes in v5:
time: 184 us; the launch traced here: 183 us
  starting transfers between devices  56.9 us (31%)
  waiting for transfers between devices  43.4 us (24%)
  local copies, waits for them, and re-layouts  26.4 us (14%)
  Pallas kernels  24.6 us (13%)
  between operations  14.5 us (8%)
  other arithmetic  13 us (7%)
  matrix products  3.96 us (2%)
    pallas_call x11, Pallas kernels, call(): pl.pallas_call(lambda *refs: body(*refs[:count], *refs[count + len(after)...  24.6 us
    ppermute x13, starting transfers between devices, swap(): return lax.ppermute(a, axis, [(0, 1), (1, 0)])  24.2 us
    ppermute x8, waiting for transfers between devices, turn(): return lax.ppermute(a, 'y', [(i, (i + k) % NY) for i in range(NY)])  22.2 us
    ppermute x13, waiting for transfers between devices, swap(): return lax.ppermute(a, axis, [(0, 1), (1, 0)])  16.1 us
    unnamed x46, local copies, waits for them, and re-layouts  12 us
    all_to_all x3, starting transfers between devices, exchange(): return lax.all_to_all(a, axis, 0, 0, tiled=True)  11.9 us
    ppermute x8, starting transfers between devices, turn(): return lax.ppermute(a, 'y', [(i, (i + k) % NY) for i in range(NY)])  10.9 us
    ppermute x3, starting transfers between devices, on_device(): far_sum = lax.ppermute(sent, 'z', [(i, i ^ bit) for i in range(NZ)])  9.99 us
  transfers between devices with their start and end apart: 29, of which 10 were waited for; matrix products, arithmetic and copies ran while one was open for 16% of the time, Pallas kernels for 8%

profile of v5, /device:TPU:1, one launch (start us, length us, event | category | flops | bytes accessed | tf_op | source)
XLA Modules:
  0.0 182.7 jit_solution(11925690671612927127)
XLA Ops:
  8.3 3.3 %collective-permute-start.5 = (bf16[192,1024]{1,0:T(8,128)(2,1)S(1)}, bf16[192,1024]{1,0:T(8,128)(2,1)S(1)}, u32[]{:S(2)}, u32[]{:S(2)}) collective-permute-start(bf16[192,1024]{1,0:T(8,128)(2,1)S(1)} %dynamic-slice_bitcast_fusion.2), channel_id=1, source_target_pairs={{0,1},{1,0},{2,3},{3,2},{4,5},{5,4},{6,7},{7,6},{8,9},{9,8},{10,11... | collective-permute-start | bytes 1179656 | tf_op jit(solution)/shard_map/ppermute | solution.py:17
  12.6 5.7 %collective-permute-done.4.refs_2_ = bf16[64,1024]{1,0:T(8,128)(2,1)S(1)} collective-permute-done((bf16[64,1024]{1,0:T(8,128)(2,1)}, bf16[64,1024]{1,0:T(8,128)(2,1)S(1)}, u32[]{:S(2)}, u32[]{:S(2)}) %collective-permute-start.4) | collective-permute-done | bytes 131104 | tf_op jit(solution)/shard_map/ppermute | solution.py:17
  20.1 2.7 %collective-permute-start.1 = (bf16[384,1024]{1,0:T(8,128)(2,1)}, bf16[384,1024]{1,0:T(8,128)(2,1)}, u32[]{:S(2)}, u32[]{:S(2)}) collective-permute-start(bf16[384,1024]{1,0:T(8,128)(2,1)} %bitcast.114), channel_id=1, source_target_pairs={{0,96},{32,0},{64,32},{96,64},{1,97},{33,1},{65,33},{97,65},{2,98}... | collective-permute-start | bytes 2359304 | tf_op jit(solution)/shard_map/ppermute | solution.py:29
  25.7 4.2 %all-to-all-start = ((bf16[4,208,512]{2,1,0:T(8,128)(2,1)}), bf16[4,208,512]{2,1,0:T(8,128)(2,1)}, u32[]{:S(2)}, u32[]{:S(2)}) async-start(bf16[4,208,512]{2,1,0:T(8,128)(2,1)} %pad_maximum_fusion), calls=%async_computation | async-start | bytes 1703936 | tf_op jit(solution)/shard_map/all_to_all | solution.py:21
  32.3 7.6 %collective-permute-done = bf16[384,1024]{1,0:T(8,128)(2,1)} collective-permute-done((bf16[384,1024]{1,0:T(8,128)(2,1)}, bf16[384,1024]{1,0:T(8,128)(2,1)}, u32[]{:S(2)}, u32[]{:S(2)}) %collective-permute-start) | collective-permute-done | bytes 786464 | tf_op jit(solution)/shard_map/ppermute | solution.py:29
  43.4 2.7 %collective-permute-start.3 = (bf16[384,512]{1,0:T(8,128)(2,1)}, bf16[384,512]{1,0:T(8,128)(2,1)}, u32[]{:S(2)}, u32[]{:S(2)}) collective-permute-start(bf16[384,512]{1,0:T(8,128)(2,1)} %slice.35), channel_id=1, source_target_pairs={{0,96},{32,0},{64,32},{96,64},{1,97},{33,1},{65,33},{97,65},{2,98}... | collective-permute-start | bytes 1179656 | tf_op jit(solution)/shard_map/ppermute | solution.py:29
  48.5 2.9 %shard_map.105.refs_1_ = bf16[768,512]{1,0:T(8,128)(2,1)} custom-call(s32[2]{0:T(128)S(1)} %pad_add_fusion.1.refs_0_, bf16[4,208,512]{2,1,0:T(8,128)(2,1)} %all-to-all-done.refs_1_.refs_4_, f32[64,512]{1,0:T(8,128)S(1)} %shard_map.104.refs_2_), custom_call_target="tpu_custom_call" | custom-call | flops 1048576 | bytes 1024 | tf_op jit(solution)/shard_map/pallas_call | solution.py:61
  55.0 3.0 %collective-permute-done.2 = bf16[384,512]{1,0:T(8,128)(2,1)} collective-permute-done((bf16[384,512]{1,0:T(8,128)(2,1)}, bf16[384,512]{1,0:T(8,128)(2,1)}, u32[]{:S(2)}, u32[]{:S(2)}) %collective-permute-start.2) | collective-permute-done | bytes 393248 | tf_op jit(solution)/shard_map/ppermute | solution.py:29
  60.0 7.5 %collective-permute-done.7.refs_3_.refs_2_ = bf16[768,512]{1,0:T(8,128)(2,1)} collective-permute-done((bf16[768,512]{1,0:T(8,128)(2,1)}, bf16[768,512]{1,0:T(8,128)(2,1)}, u32[]{:S(2)}, u32[]{:S(2)}) %collective-permute-start.7) | collective-permute-done | bytes 786464 | tf_op jit(solution)/shard_map/ppermute | solution.py:17
  69.2 3.0 %shard_map.106 = bf16[2,768,512]{2,1,0:T(8,128)(2,1)} custom-call(s32[1]{0:T(128)} %bitcast.13.refs_0_, bf16[4,2,192,1024]{3,2,1,0:T(8,128)(2,1)S(1)} %bitcast.99, bf16[2,512,1024]{2,1,0:T(8,128)(2,1)S(1)} %copy-done, bf16[768,512]{1,0:T(8,128)(2,1)} %collective-permute-done.7.refs_3_.refs_2_), custom_call_target="tpu_custom_call" | custom-call | flops 1048576 | bytes 1024 | tf_op jit(solution)/shard_map/pallas_call | solution.py:61
  72.2 4.1 %collective-permute-start.8 = (bf16[2,768,512]{2,1,0:T(8,128)(2,1)}, bf16[2,768,512]{2,1,0:T(8,128)(2,1)}, u32[]{:S(2)}, u32[]{:S(2)}) collective-permute-start(bf16[2,768,512]{2,1,0:T(8,128)(2,1)} %shard_map.106), channel_id=1, source_target_pairs={{0,1},{1,0},{2,3},{3,2},{4,5},{5,4},{6,7},{7,6},{8,9},{9,8},{10,11... | collective-permute-start | bytes 4718600 | tf_op jit(solution)/shard_map/ppermute | solution.py:17
  80.3 2.8 %fusion.3.refs_6_ = bf16[768,512]{1,0:T(8,128)(2,1)} fusion(bf16[2,768,512]{2,1,0:T(8,128)(2,1)} %collective-permute-done.8.refs_2_, s32[]{:T(128)S(6)} %select_n.130, bf16[2,768,512]{2,1,0:T(8,128)(2,1)S(1)} %shard_map.103.refs_1_), kind=kLoop, calls=%fused_computation.8 | loop fusion | flops 1572864 | bytes 2359300 | tf_op jit(solution)/shard_map/convert_element_type | solution.py:239
  83.1 5.3 %shard_map.107.refs_6_ = bf16[2,512,1024]{2,1,0:T(8,128)(2,1)S(1)} custom-call(s32[2]{0:T(128)S(1)} %pad_add_fusion.refs_0_, bf16[768,512]{1,0:T(8,128)(2,1)} %shard_map.105.refs_1_, bf16[768,512]{1,0:T(8,128)(2,1)} %collective-permute-done.7.refs_3_.refs_2_, bf16[768,512]{1,0:T(8,128)(2,1)} %collective-permute-done.10.refs_3_, ...), custom_call_target="tpu_custom_call" | custom-call | flops 1048576 | bytes 1024 | tf_op jit(solution)/shard_map/pallas_call | solution.py:61
  94.2 5.3 %shard_map.108 = bf16[4,2,192,1024]{3,2,1,0:T(8,128)(2,1)S(1)} custom-call(s32[2]{0:T(128)S(1)} %pad_add_fusion.refs_0_, bf16[768,512]{1,0:T(8,128)(2,1)} %shard_map.105.refs_1_, bf16[768,512]{1,0:T(8,128)(2,1)} %collective-permute-done.7.refs_3_.refs_2_, bf16[768,512]{1,0:T(8,128)(2,1)} %collective-permute-done.10.refs_3_, ...), custom_call_target="tpu_custom_call" | custom-call | flops 1048576 | bytes 1024 | tf_op jit(solution)/shard_map/pallas_call | solution.py:61
  102.4 9.1 %collective-permute-done.12.refs_5_.refs_2_ = bf16[384,512]{1,0:T(8,128)(2,1)S(1)} collective-permute-done((bf16[384,512]{1,0:T(8,128)(2,1)S(1)}, bf16[384,512]{1,0:T(8,128)(2,1)S(1)}, u32[]{:S(2)}, u32[]{:S(2)}) %collective-permute-start.12) | collective-permute-done | bytes 393248 | tf_op jit(solution)/shard_map/ppermute | solution.py:29
  111.5 2.7 %shard_map.109 = (bf16[768,512]{1,0:T(8,128)(2,1)S(1)}, f32[64,512]{1,0:T(8,128)S(1)}) custom-call(s32[2]{0:T(128)S(1)} %pad_add_fusion.refs_0_, bf16[2,768,512]{2,1,0:T(8,128)(2,1)S(1)} %copy-done.6, bf16[2,768,512]{2,1,0:T(8,128)(2,1)} %collective-permute-done.8.refs_2_, bf16[768,512]{1,0:T(8,128)(2,1)S(1)} %collective-permute-done.9.refs_3_, ...), custom_call_target="tpu_custom_call" | custom-call | flops 1048576 | bytes 1024 | tf_op jit(solution)/shard_map/pallas_call | solution.py:61
  117.4 4.2 %all-to-all-start.1 = ((bf16[4,192,512]{2,1,0:T(8,128)(2,1)}), bf16[4,192,512]{2,1,0:T(8,128)(2,1)}, u32[]{:S(2)}, u32[]{:S(2)}) async-start(bf16[4,192,512]{2,1,0:T(8,128)(2,1)} %bitcast.107), calls=%async_computation.1 | async-start | bytes 1572864 | tf_op jit(solution)/shard_map/all_to_all | solution.py:21
  125.0 2.8 %collective-permute-done.19 = f32[32,512]{1,0:T(8,128)S(1)} collective-permute-done((f32[32,512]{1,0:T(8,128)S(1)}, f32[32,512]{1,0:T(8,128)S(1)}, u32[]{:S(2)}, u32[]{:S(2)}) %collective-permute-start.19) | collective-permute-done | bytes 65568 | tf_op jit(solution)/shard_map/ppermute | solution.py:17
  131.9 3.0 %collective-permute-start.21 = (bf16[32,512]{1,0:T(8,128)(2,1)}, bf16[32,512]{1,0:T(8,128)(2,1)}, u32[]{:S(2)}, u32[]{:S(2)}) collective-permute-start(bf16[32,512]{1,0:T(8,128)(2,1)} %add_convert_fusion.2), channel_id=1, source_target_pairs={{0,8},{4,12},{8,0},{12,4},{16,24},{20,28},{24,16},{28,20},{1,9},{5... | collective-permute-start | bytes 98312 | tf_op jit(solution)/shard_map/ppermute | solution.py:262
  139.7 5.3 %collective-permute-start.22 = (bf16[32,512]{1,0:T(8,128)(2,1)}, bf16[32,512]{1,0:T(8,128)(2,1)}, u32[]{:S(2)}, u32[]{:S(2)}) collective-permute-start(bf16[32,512]{1,0:T(8,128)(2,1)} %add_convert_fusion.1.refs_1_), channel_id=1, source_target_pairs={{0,16},{4,20},{8,24},{12,28},{16,0},{20,4},{24,8},{28,12},{1,17},{... | collective-permute-start | bytes 98312 | tf_op jit(solution)/shard_map/ppermute | solution.py:262
  152.4 3.4 %all-to-all-start.2 = ((f32[4,32,512]{2,1,0:T(8,128)}), f32[4,32,512]{2,1,0:T(8,128)S(1)}, u32[]{:S(2)}, u32[]{:S(2)}) async-start(f32[4,32,512]{2,1,0:T(8,128)} %broadcast_in_dim.34), calls=%async_computation.3 | async-start | bytes 524288 | tf_op jit(solution)/shard_map/all_to_all | solution.py:21
  163.2 2.6 %collective-permute-done.15 = bf16[384,1024]{1,0:T(8,128)(2,1)} collective-permute-done((bf16[384,1024]{1,0:T(8,128)(2,1)}, bf16[384,1024]{1,0:T(8,128)(2,1)}, u32[]{:S(2)}, u32[]{:S(2)}) %collective-permute-start.15) | collective-permute-done | bytes 786464 | tf_op jit(solution)/shard_map/ppermute | solution.py:29
  165.8 2.7 %fusion.1 = bf16[384,1024]{1,0:T(8,128)(2,1)} fusion(bf16[384,1024]{1,0:T(8,128)(2,1)} %collective-permute-done.16, bf16[384,1024]{1,0:T(8,128)(2,1)} %collective-permute-done.15, bf16[4,384,1024]{2,1,0:T(8,128)(2,1)S(1)} %bitcast.104, s32[]{:T(128)S(6)} %select_n.133), kind=kLoop, calls=%fused_computation.2 | loop fusion | flops 2359296 | bytes 3145732 | tf_op jit(solution)/shard_map/convert_element_type | solution.py:281
  169.4 3.6 %collective-permute-start.23 = (f32[2,32,512]{2,1,0:T(8,128)S(1)}, f32[2,32,512]{2,1,0:T(8,128)S(1)}, u32[]{:S(2)}, u32[]{:S(2)}) collective-permute-start(f32[2,32,512]{2,1,0:T(8,128)S(1)} %shard_map.112), channel_id=1, source_target_pairs={{0,1},{1,0},{2,3},{3,2},{4,5},{5,4},{6,7},{7,6},{8,9},{9,8},{10,11... | collective-permute-start | bytes 393224 | tf_op jit(solution)/shard_map/ppermute | solution.py:17
  (137 shorter events, 68.9 us)
Async XLA Ops:
  7.2 60.4 %all-gather.2.cloned.1.call-start = ((), (), s32[]{:S(2)}) async-start(), calls=%async_computation.4 | async-start | bytes 2359296 | tf_op jit(solution)/shard_map/all_gather | solution.py:220
  8.3 10.1 %collective-permute-start.5 = (bf16[192,1024]{1,0:T(8,128)(2,1)S(1)}, bf16[192,1024]{1,0:T(8,128)(2,1)S(1)}, u32[]{:S(2)}, u32[]{:S(2)}) collective-permute-start(bf16[192,1024]{1,0:T(8,128)(2,1)S(1)} %dynamic-slice_bitcast_fusion.2), channel_id=1, source_target_pairs={{0,1},{1,0},{2,3},{3,2},{4,5},{5,4},{6,7},{7,6},{8,9},{9,8},{10,11... | collective-permute-start | bytes 1179656 | tf_op jit(solution)/shard_map/ppermute | solution.py:17
  11.6 6.8 %collective-permute-start.4 = (bf16[64,1024]{1,0:T(8,128)(2,1)}, bf16[64,1024]{1,0:T(8,128)(2,1)S(1)}, u32[]{:S(2)}, u32[]{:S(2)}) collective-permute-start(bf16[64,1024]{1,0:T(8,128)(2,1)} %refs_1_.1), channel_id=1, source_target_pairs={{0,128},{128,0},{1,129},{129,1},{2,130},{130,2},{3,131},{131,3},{4... | collective-permute-start | bytes 393224 | tf_op jit(solution)/shard_map/ppermute | solution.py:17
  20.0 19.8 %collective-permute-start = (bf16[384,1024]{1,0:T(8,128)(2,1)}, bf16[384,1024]{1,0:T(8,128)(2,1)}, u32[]{:S(2)}, u32[]{:S(2)}) collective-permute-start(bf16[384,1024]{1,0:T(8,128)(2,1)} %bitcast.113), channel_id=1, source_target_pairs={{0,32},{32,64},{64,96},{96,0},{1,33},{33,65},{65,97},{97,1},{2,34}... | collective-permute-start | bytes 2359304 | tf_op jit(solution)/shard_map/ppermute | solution.py:29
  20.1 21.5 %collective-permute-start.1 = (bf16[384,1024]{1,0:T(8,128)(2,1)}, bf16[384,1024]{1,0:T(8,128)(2,1)}, u32[]{:S(2)}, u32[]{:S(2)}) collective-permute-start(bf16[384,1024]{1,0:T(8,128)(2,1)} %bitcast.114), channel_id=1, source_target_pairs={{0,96},{32,0},{64,32},{96,64},{1,97},{33,1},{65,33},{97,65},{2,98}... | collective-permute-start | bytes 2359304 | tf_op jit(solution)/shard_map/ppermute | solution.py:29
  22.8 8.6 %collective-permute-start.6 = (bf16[64,1024]{1,0:T(8,128)(2,1)S(1)}, bf16[64,1024]{1,0:T(8,128)(2,1)S(1)}, u32[]{:S(2)}, u32[]{:S(2)}) collective-permute-start(bf16[64,1024]{1,0:T(8,128)(2,1)S(1)} %copy-done.10), channel_id=1, source_target_pairs={{0,1},{1,0},{2,3},{3,2},{4,5},{5,4},{6,7},{7,6},{8,9},{9,8},{10,11... | collective-permute-start | bytes 393224 | tf_op jit(solution)/shard_map/ppermute | solution.py:17
  25.7 22.8 %all-to-all-start = ((bf16[4,208,512]{2,1,0:T(8,128)(2,1)}), bf16[4,208,512]{2,1,0:T(8,128)(2,1)}, u32[]{:S(2)}, u32[]{:S(2)}) async-start(bf16[4,208,512]{2,1,0:T(8,128)(2,1)} %pad_maximum_fusion), calls=%async_computation | async-start | bytes 1703936 | tf_op jit(solution)/shard_map/all_to_all | solution.py:21
  30.0 129.2 %reduce-scatter.2.cloned.1.call-start = ((), (), s32[]{:S(2)}) async-start(), calls=%async_computation.5 | async-start | bytes 2359296 | tf_op jit(solution)/shard_map/reduce_scatter | solution.py:252
  41.6 16.3 %collective-permute-start.2 = (bf16[384,512]{1,0:T(8,128)(2,1)}, bf16[384,512]{1,0:T(8,128)(2,1)}, u32[]{:S(2)}, u32[]{:S(2)}) collective-permute-start(bf16[384,512]{1,0:T(8,128)(2,1)} %slice.34), channel_id=1, source_target_pairs={{0,32},{32,64},{64,96},{96,0},{1,33},{33,65},{65,97},{97,1},{2,34}... | collective-permute-start | bytes 1179656 | tf_op jit(solution)/shard_map/ppermute | solution.py:29
  43.4 15.6 %collective-permute-start.3 = (bf16[384,512]{1,0:T(8,128)(2,1)}, bf16[384,512]{1,0:T(8,128)(2,1)}, u32[]{:S(2)}, u32[]{:S(2)}) collective-permute-start(bf16[384,512]{1,0:T(8,128)(2,1)} %slice.35), channel_id=1, source_target_pairs={{0,96},{32,0},{64,32},{96,64},{1,97},{33,1},{65,33},{97,65},{2,98}... | collective-permute-start | bytes 1179656 | tf_op jit(solution)/shard_map/ppermute | solution.py:29
  51.4 16.2 %collective-permute-start.7 = (bf16[768,512]{1,0:T(8,128)(2,1)}, bf16[768,512]{1,0:T(8,128)(2,1)}, u32[]{:S(2)}, u32[]{:S(2)}) collective-permute-start(bf16[768,512]{1,0:T(8,128)(2,1)} %shard_map.105.refs_1_), channel_id=1, source_target_pairs={{0,2},{2,0},{1,3},{3,1},{4,6},{6,4},{5,7},{7,5},{8,10},{10,8},{9,1... | collective-permute-start | bytes 2359304 | tf_op jit(solution)/shard_map/ppermute | solution.py:17
  72.2 8.1 %collective-permute-start.8 = (bf16[2,768,512]{2,1,0:T(8,128)(2,1)}, bf16[2,768,512]{2,1,0:T(8,128)(2,1)}, u32[]{:S(2)}, u32[]{:S(2)}) collective-permute-start(bf16[2,768,512]{2,1,0:T(8,128)(2,1)} %shard_map.106), channel_id=1, source_target_pairs={{0,1},{1,0},{2,3},{3,2},{4,5},{5,4},{6,7},{7,6},{8,9},{9,8},{10,11... | collective-permute-start | bytes 4718600 | tf_op jit(solution)/shard_map/ppermute | solution.py:17
  76.2 6.8 %collective-permute-start.10 = (bf16[768,512]{1,0:T(8,128)(2,1)}, bf16[768,512]{1,0:T(8,128)(2,1)}, u32[]{:S(2)}, u32[]{:S(2)}) collective-permute-start(bf16[768,512]{1,0:T(8,128)(2,1)} %shard_map.105.refs_1_), channel_id=1, source_target_pairs={{0,1},{1,0},{2,3},{3,2},{4,5},{5,4},{6,7},{7,6},{8,9},{9,8},{10,11... | collective-permute-start | bytes 2359304 | tf_op jit(solution)/shard_map/ppermute | solution.py:17
  76.2 6.8 %collective-permute-start.11 = (bf16[768,512]{1,0:T(8,128)(2,1)}, bf16[768,512]{1,0:T(8,128)(2,1)}, u32[]{:S(2)}, u32[]{:S(2)}) collective-permute-start(bf16[768,512]{1,0:T(8,128)(2,1)} %collective-permute-done.7.refs_3_.refs_2_), channel_id=1, source_target_pairs={{0,1},{1,0},{2,3},{3,2},{4,5},{5,4},{6,7},{7,6},{8,9},{9,8},{10,11... | collective-permute-start | bytes 2359304 | tf_op jit(solution)/shard_map/ppermute | solution.py:17
  89.8 21.7 %collective-permute-start.9 = (bf16[768,512]{1,0:T(8,128)(2,1)}, bf16[768,512]{1,0:T(8,128)(2,1)S(1)}, u32[]{:S(2)}, u32[]{:S(2)}) collective-permute-start(bf16[768,512]{1,0:T(8,128)(2,1)} %fusion.3.refs_6_), channel_id=1, source_target_pairs={{0,2},{2,0},{1,3},{3,1},{4,6},{6,4},{5,7},{7,5},{8,10},{10,8},{9,1... | collective-permute-start | bytes 2359304 | tf_op jit(solution)/shard_map/ppermute | solution.py:17
  99.7 11.8 %collective-permute-start.12 = (bf16[384,512]{1,0:T(8,128)(2,1)S(1)}, bf16[384,512]{1,0:T(8,128)(2,1)S(1)}, u32[]{:S(2)}, u32[]{:S(2)}) collective-permute-start(bf16[384,512]{1,0:T(8,128)(2,1)S(1)} %get-tuple-element.19), channel_id=1, source_target_pairs={{0,32},{32,64},{64,96},{96,0},{1,33},{33,65},{65,97},{97,1},{2,34}... | collective-permute-start | bytes 1179656 | tf_op jit(solution)/shard_map/ppermute | solution.py:29
  100.3 11.2 %collective-permute-start.13 = (bf16[384,512]{1,0:T(8,128)(2,1)S(1)}, bf16[384,512]{1,0:T(8,128)(2,1)S(1)}, u32[]{:S(2)}, u32[]{:S(2)}) collective-permute-start(bf16[384,512]{1,0:T(8,128)(2,1)S(1)} %get-tuple-element.18), channel_id=1, source_target_pairs={{0,96},{32,0},{64,32},{96,64},{1,97},{33,1},{65,33},{97,65},{2,98}... | collective-permute-start | bytes 1179656 | tf_op jit(solution)/shard_map/ppermute | solution.py:29
  117.4 17.5 %all-to-all-start.1 = ((bf16[4,192,512]{2,1,0:T(8,128)(2,1)}), bf16[4,192,512]{2,1,0:T(8,128)(2,1)}, u32[]{:S(2)}, u32[]{:S(2)}) async-start(bf16[4,192,512]{2,1,0:T(8,128)(2,1)} %bitcast.107), calls=%async_computation.1 | async-start | bytes 1572864 | tf_op jit(solution)/shard_map/all_to_all | solution.py:21
  136.6 19.2 %collective-permute-start.14 = (bf16[2,192,512]{2,1,0:T(8,128)(2,1)}, bf16[2,192,512]{2,1,0:T(8,128)(2,1)}, u32[]{:S(2)}, u32[]{:S(2)}) collective-permute-start(bf16[2,192,512]{2,1,0:T(8,128)(2,1)} %dynamic-slice_bitcast_fusion.1), channel_id=1, source_target_pairs={{0,1},{1,0},{2,3},{3,2},{4,5},{5,4},{6,7},{7,6},{8,9},{9,8},{10,11... | collective-permute-start | bytes 1179656 | tf_op jit(solution)/shard_map/ppermute | solution.py:17
  139.7 11.2 %collective-permute-start.22 = (bf16[32,512]{1,0:T(8,128)(2,1)}, bf16[32,512]{1,0:T(8,128)(2,1)}, u32[]{:S(2)}, u32[]{:S(2)}) collective-permute-start(bf16[32,512]{1,0:T(8,128)(2,1)} %add_convert_fusion.1.refs_1_), channel_id=1, source_target_pairs={{0,16},{4,20},{8,24},{12,28},{16,0},{20,4},{24,8},{28,12},{1,17},{... | collective-permute-start | bytes 98312 | tf_op jit(solution)/shard_map/ppermute | solution.py:262
  147.2 18.6 %collective-permute-start.15 = (bf16[384,1024]{1,0:T(8,128)(2,1)}, bf16[384,1024]{1,0:T(8,128)(2,1)}, u32[]{:S(2)}, u32[]{:S(2)}) collective-permute-start(bf16[384,1024]{1,0:T(8,128)(2,1)} %get-tuple-element.9), channel_id=1, source_target_pairs={{0,32},{32,64},{64,96},{96,0},{1,33},{33,65},{65,97},{97,1},{2,34}... | collective-permute-start | bytes 2359304 | tf_op jit(solution)/shard_map/ppermute | solution.py:29
  148.5 17.3 %collective-permute-start.16 = (bf16[384,1024]{1,0:T(8,128)(2,1)}, bf16[384,1024]{1,0:T(8,128)(2,1)}, u32[]{:S(2)}, u32[]{:S(2)}) collective-permute-start(bf16[384,1024]{1,0:T(8,128)(2,1)} %get-tuple-element.10), channel_id=1, source_target_pairs={{0,96},{32,0},{64,32},{96,64},{1,97},{33,1},{65,33},{97,65},{2,98}... | collective-permute-start | bytes 2359304 | tf_op jit(solution)/shard_map/ppermute | solution.py:29
  152.4 16.9 %all-to-all-start.2 = ((f32[4,32,512]{2,1,0:T(8,128)}), f32[4,32,512]{2,1,0:T(8,128)S(1)}, u32[]{:S(2)}, u32[]{:S(2)}) async-start(f32[4,32,512]{2,1,0:T(8,128)} %broadcast_in_dim.34), calls=%async_computation.3 | async-start | bytes 524288 | tf_op jit(solution)/shard_map/all_to_all | solution.py:21
  160.7 8.6 %collective-permute-start.17 = (bf16[64,1024]{1,0:T(8,128)(2,1)}, bf16[64,1024]{1,0:T(8,128)(2,1)S(1)}, u32[]{:S(2)}, u32[]{:S(2)}) collective-permute-start(bf16[64,1024]{1,0:T(8,128)(2,1)} %dynamic-slice_bitcast_fusion.3), channel_id=1, source_target_pairs={{0,128},{128,0},{1,129},{129,1},{2,130},{130,2},{3,131},{131,3},{4... | collective-permute-start | bytes 393224 | tf_op jit(solution)/shard_map/ppermute | solution.py:17
  (28 other events, 127.9 us)
Sparse Core Ops, SparseCore 0:
  20.2 38.8 all-gather.1
  89.9 38.3 reduce-scatter.1

commit v6 on v5

--- a/solution.py
+++ b/solution.py
@@ -120,17 +120,27 @@
         out[k * rows : (k + 1) * rows, :] = (got[k, :rows, :].astype(F32) * gating).astype(BF)
 
 
-def merge_body(at, keep, theirs, away, got, home, table):
-    x, rows = at[0], home.shape[0] // NY
-    total = jnp.zeros(table.shape, F32)
-    for k in range(NY):
-        span = slice(k * rows, (k + 1) * rows)
-        projected = keep[x, span, :].astype(F32) + theirs[x, span, :].astype(F32) + away[span, :].astype(F32)
-        home[span, :] = projected.astype(BF)
-        hot = hot_of(got, k, rows, table.shape[0])
-        for part in split3(got[k, :rows, :].astype(F32) * projected):
-            total += jnp.dot(hot, part, preferred_element_type=F32)
-    table[...] = total
+def home_body(at, stay, away, home):
+    home[...] = (stay[...] + away[...].astype(F32)).astype(BF)
+
+
+def keep_body(at, ho, w, theirs, near, far, away, stay, table):
+    rows, half = ho[:, at[1]].reshape(-1, ho.shape[-1]), ho.shape[2]
+    hot = [hot_of(near, k, half, table.shape[1]) for k in range(NY)]
+    for which, x, cot in ((0, at[0], near), (1, 1 - at[0], far)):
+        for n in range(0, w.shape[1], STEP):
+            span = slice(n, n + STEP)
+            chip = lax.dot_general(rows, w[x, span, :], (((1,), (1,)), ((), ())), preferred_element_type=F32)
+            chip = chip.astype(BF).astype(F32) + theirs[x, :, span].astype(F32)
+            if which:
+                away[:, span] = chip.astype(BF)
+            else:
+                stay[:, span] = chip
+            total = jnp.zeros((table.shape[1], STEP), F32)
+            for k in range(NY):
+                for part in split3(cot[k, :half, span].astype(F32) * chip[k * half : (k + 1) * half]):
+                    total += jnp.dot(hot[k], part, preferred_element_type=F32)
+            table[which, :, span] = total
 
 
 def project_body(at, ho, w, out):
@@ -224,46 +234,52 @@
     there = swap(strategy_table, "c")
     source = jnp.stack([(y // 2 == c).astype(jnp.int32), (y % 2).astype(jnp.int32)])
     table_y = call(table_body, source, (mixing, strategy_table, there), jax.ShapeDtypeStruct((strategies, wide), F32))
-    grad_y = call(gate_body, source, (got, table_y), jax.ShapeDtypeStruct((NY * half, wide), BF))
-
-    far = swap(grad_y, "xl")
-    pieces = (grad_y, far, swap(grad_y, "c"), swap(far, "c"))
+    gate = lambda block, table: call(gate_body, source, (block, table), jax.ShapeDtypeStruct((NY * half, wide), BF))
+    got_far = swap(got, "xl")
+
+    near, far = gate(got, table_y), gate(got_far, swap(table_y, "xl"))
+    pieces = (near, far, swap(near, "c"), swap(far, "c"))
     at = jnp.stack([xl, c]).astype(jnp.int32)
 
-    project = lambda core, after: call(
-        project_body, core.reshape(1).astype(jnp.int32), (ho_y, weight), jax.ShapeDtypeStruct((XL, NY * half, wide), BF), after
+    give = call(
+        project_body,
+        (1 - c).reshape(1).astype(jnp.int32),
+        (ho_y, weight),
+        jax.ShapeDtypeStruct((XL, NY * half, wide), BF),
+        (far,),
     )
-    theirs = swap(project(1 - c, (far,)), "c")
-    keep = project(c, ())
-    chip = lambda x: pick(keep, x, 0).astype(F32) + pick(theirs, x, 0).astype(F32)
-    away = chip(1 - xl).astype(BF)
-    wg = call(weight_body, at, pieces + (ho_y,), jax.ShapeDtypeStruct((XH, NZ * wr, cols), BF), (away,))
-    head_grad = call(head_body, at, pieces + (weight,), jax.ShapeDtypeStruct((NY, NC, half, cols), BF), (wg,))
+    theirs = swap(give, "c")
+    wg = call(weight_body, at, pieces + (ho_y,), jax.ShapeDtypeStruct((XH, NZ * wr, cols), BF), (give,))
+    away, stay, table_part = call(
+        keep_body,
+        at,
+        (ho_y, weight, theirs, got, got_far),
+        (
+            jax.ShapeDtypeStruct((NY * half, wide), BF),
+            jax.ShapeDtypeStruct((NY * half, wide), F32),
+            jax.ShapeDtypeStruct((XL, strategies, wide), F32),
+        ),
+        (wg,),
+    )
+    head_grad = call(head_body, at, pieces + (weight,), jax.ShapeDtypeStruct((NY, NC, half, cols), BF), (away,))
     head_grad = head_grad.reshape(NY, rows, cols)
     head_far = far_blocks(head_grad, y)
-    home, table_part = call(
-        merge_body,
-        at,
-        (keep, theirs, swap(away, "xl"), got),
-        (jax.ShapeDtypeStruct(away.shape, BF), jax.ShapeDtypeStruct((strategies, wide), F32)),
-        head_far,
-    )
-
     wg_part = lax.psum_scatter(wg, "z", scatter_dimension=1, tiled=True)
     wg_other = swap(pick(wg_part, 1 - xh, 0), "xh")
     weight_sum = pick(wg_part, xh, 0).astype(F32) + wg_other.astype(F32)
 
+    table_part = table_part.reshape(XL, NC, strategies // NC, wide)
+    table_sum = pick(table_part, c, 1) + swap(pick(table_part, 1 - c, 1), "c")
+    table_sum = table_sum[0] + swap(table_sum[1], "xl")
+    table_sum = table_sum + swap(table_sum, "xh")
+    beside = lambda a, bit: lax.ppermute(a, "z", [(i, i ^ bit) for i in range(NZ)])
+    sent = table_sum.astype(BF)
+    sent = (sent.astype(F32) + beside(sent, 1).astype(F32)).astype(BF)
+    home = jax.ShapeDtypeStruct(away.shape, BF)
+    home = call(home_body, at, (stay, swap(away, "xl")), home, head_far + (sent,))
     home = exchange(home.reshape(NY, half, wide), "y")
-    table_part = table_part.reshape(NC, strategies // NC, wide)
-    table_sum = pick(table_part, c, 0) + swap(pick(table_part, 1 - c, 0), "c")
-    table_sum = table_sum + swap(table_sum, "xh")
-    for bit in (1, 2, 4):
-        sent = table_sum.astype(BF)
-        far_sum = lax.ppermute(sent, "z", [(i, i ^ bit) for i in range(NZ)])
-        if bit < 4:
-            table_sum = sent.astype(F32) + far_sum.astype(F32)
-        else:
-            table_sum = call(add_body, at, (sent, far_sum), jax.ShapeDtypeStruct(sent.shape, F32), (home,))
+    sent = (sent.astype(F32) + beside(sent, 2).astype(F32)).astype(BF)
+    table_sum = call(add_body, at, (sent, beside(sent, 4)), jax.ShapeDtypeStruct(sent.shape, F32), (home,))
     table_all = spread(table_sum, "y", NY).reshape(NC, 2, strategies // NC, wide)
     rest = jax.ShapeDtypeStruct(table_all.shape[1:], F32)
     rest = swap(call(take_body, (1 - c).reshape(1).astype(jnp.int32), (table_all,), rest, (wg_other,)), "c")

time: 184 us -> 203 us (1.10)
  waiting for transfers between devices: 43.4 us -> 62.1 us
  Pallas kernels: 24.6 us -> 29.1 us
  other arithmetic: 13 us -> 9.7 us
    ppermute x13 -> x15, waiting for transfers between devices: 16.1 us -> 28 us  [swap(): return lax.ppermute(a, axis, [(0, 1), (1, 0)])]
    all_to_all x3, waiting for transfers between devices: 3.3 us -> 9.08 us  [exchange(): return lax.all_to_all(a, axis, 0, 0, tiled=True)]
    pallas_call x11 -> x12, Pallas kernels: 24.6 us -> 29.1 us  [call(): pl.pallas_call(lambda *refs: body(*refs[:count], *refs[count + len(after)...]
    ppermute x13 -> x15, starting transfers between devices: 24.2 us -> 22.8 us  [swap(): return lax.ppermute(a, axis, [(0, 1), (1, 0)])]
    unnamed x46 -> x42, local copies, waits for them, and re-layouts: 12 us -> 11.7 us
  transfers between devices with their start and end apart: 29 -> 31, of which waited for: 10 -> 12; matrix products, arithmetic and copies ran while one was open for 16% -> 12% of each run, Pallas kernels for 8% -> 13%
where the time goes in v6:
time: 203 us; the launch traced here: 202 us
  waiting for transfers between devices  62.1 us (31%)
  starting transfers between devices  57.3 us (28%)
  Pallas kernels  29.1 us (14%)
  local copies, waits for them, and re-layouts  25.5 us (13%)
  between operations  14.5 us (7%)
  other arithmetic  9.7 us (5%)
  matrix products  3.95 us (2%)
    pallas_call x12, Pallas kernels, call(): pl.pallas_call(lambda *refs: body(*refs[:count], *refs[count + len(after)...  29.1 us
    ppermute x15, waiting for transfers between devices, swap(): return lax.ppermute(a, axis, [(0, 1), (1, 0)])  28 us
    ppermute x8, waiting for transfers between devices, turn(): return lax.ppermute(a, 'y', [(i, (i + k) % NY) for i in range(NY)])  23 us
    ppermute x15, starting transfers between devices, swap(): return lax.ppermute(a, axis, [(0, 1), (1, 0)])  22.8 us
    all_to_all x3, starting transfers between devices, exchange(): return lax.all_to_all(a, axis, 0, 0, tiled=True)  11.9 us
    ppermute x3, starting transfers between devices, on_device(): lax.ppermute(a, 'z', [(i, i ^ bit) for i in range(NZ)])  11.7 us
    unnamed x42, local copies, waits for them, and re-layouts  11.7 us
    ppermute x8, starting transfers between devices, turn(): return lax.ppermute(a, 'y', [(i, (i + k) % NY) for i in range(NY)])  10.9 us
  transfers between devices with their start and end apart: 31, of which 12 were waited for; matrix products, arithmetic and copies ran while one was open for 12% of the time, Pallas kernels for 13%

profile of v6, /device:TPU:1, one launch (start us, length us, event | category | flops | bytes accessed | tf_op | source)
XLA Modules:
  0.0 202.2 jit_solution(1666957031771411816)
XLA Ops:
  8.3 3.3 %collective-permute-start.5 = (bf16[192,1024]{1,0:T(8,128)(2,1)S(1)}, bf16[192,1024]{1,0:T(8,128)(2,1)S(1)}, u32[]{:S(2)}, u32[]{:S(2)}) collective-permute-start(bf16[192,1024]{1,0:T(8,128)(2,1)S(1)} %dynamic-slice_bitcast_fusion.2), channel_id=1, source_target_pairs={{0,1},{1,0},{2,3},{3,2},{4,5},{5,4},{6,7},{7,6},{8,9},{9,8},{10,11... | collective-permute-start | bytes 1179656 | tf_op jit(solution)/shard_map/ppermute | solution.py:17
  12.6 5.7 %collective-permute-done.4.refs_2_ = bf16[64,1024]{1,0:T(8,128)(2,1)S(1)} collective-permute-done((bf16[64,1024]{1,0:T(8,128)(2,1)}, bf16[64,1024]{1,0:T(8,128)(2,1)S(1)}, u32[]{:S(2)}, u32[]{:S(2)}) %collective-permute-start.4) | collective-permute-done | bytes 131104 | tf_op jit(solution)/shard_map/ppermute | solution.py:17
  26.7 4.2 %all-to-all-start = ((bf16[4,208,512]{2,1,0:T(8,128)(2,1)}), bf16[4,208,512]{2,1,0:T(8,128)(2,1)}, u32[]{:S(2)}, u32[]{:S(2)}) async-start(bf16[4,208,512]{2,1,0:T(8,128)(2,1)} %pad_maximum_fusion), calls=%async_computation | async-start | bytes 1703936 | tf_op jit(solution)/shard_map/all_to_all | solution.py:21
  33.2 6.7 %collective-permute-done = bf16[384,1024]{1,0:T(8,128)(2,1)} collective-permute-done((bf16[384,1024]{1,0:T(8,128)(2,1)}, bf16[384,1024]{1,0:T(8,128)(2,1)}, u32[]{:S(2)}, u32[]{:S(2)}) %collective-permute-start) | collective-permute-done | bytes 786464 | tf_op jit(solution)/shard_map/ppermute | solution.py:29
  43.4 2.7 %collective-permute-start.3 = (bf16[384,512]{1,0:T(8,128)(2,1)}, bf16[384,512]{1,0:T(8,128)(2,1)}, u32[]{:S(2)}, u32[]{:S(2)}) collective-permute-start(bf16[384,512]{1,0:T(8,128)(2,1)} %slice.43), channel_id=1, source_target_pairs={{0,96},{32,0},{64,32},{96,64},{1,97},{33,1},{65,33},{97,65},{2,98}... | collective-permute-start | bytes 1179656 | tf_op jit(solution)/shard_map/ppermute | solution.py:29
  52.1 5.8 %collective-permute-done.2 = bf16[384,512]{1,0:T(8,128)(2,1)} collective-permute-done((bf16[384,512]{1,0:T(8,128)(2,1)}, bf16[384,512]{1,0:T(8,128)(2,1)}, u32[]{:S(2)}, u32[]{:S(2)}) %collective-permute-start.2) | collective-permute-done | bytes 393248 | tf_op jit(solution)/shard_map/ppermute | solution.py:29
  60.0 6.0 %collective-permute-done.6.refs_1_.refs_5_ = bf16[4,208,512]{2,1,0:T(8,128)(2,1)S(1)} collective-permute-done((bf16[4,208,512]{2,1,0:T(8,128)(2,1)}, bf16[4,208,512]{2,1,0:T(8,128)(2,1)S(1)}, u32[]{:S(2)}, u32[]{:S(2)}) %collective-permute-start.6) | collective-permute-done | bytes 852000 | tf_op jit(solution)/shard_map/ppermute | solution.py:17
  70.8 3.0 %shard_map.105.refs_6_ = bf16[2,768,512]{2,1,0:T(8,128)(2,1)} custom-call(s32[1]{0:T(128)} %bitcast.13.refs_0_, bf16[4,2,192,1024]{3,2,1,0:T(8,128)(2,1)S(1)} %bitcast.107, bf16[2,512,1024]{2,1,0:T(8,128)(2,1)S(1)} %copy-done.2, bf16[768,512]{1,0:T(8,128)(2,1)} %shard_map.104.refs_3_.refs_2_), custom_call_target="tpu_custom_call" | custom-call | flops 1048576 | bytes 1024 | tf_op jit(solution)/shard_map/pallas_call | solution.py:61
  73.7 4.1 %collective-permute-start.9 = (bf16[2,768,512]{2,1,0:T(8,128)(2,1)}, bf16[2,768,512]{2,1,0:T(8,128)(2,1)}, u32[]{:S(2)}, u32[]{:S(2)}) collective-permute-start(bf16[2,768,512]{2,1,0:T(8,128)(2,1)} %shard_map.105.refs_6_), channel_id=1, source_target_pairs={{0,1},{1,0},{2,3},{3,2},{4,5},{5,4},{6,7},{7,6},{8,9},{9,8},{10,11... | collective-permute-start | bytes 4718600 | tf_op jit(solution)/shard_map/ppermute | solution.py:17
  77.8 2.8 %shard_map.106.refs_1_ = bf16[768,512]{1,0:T(8,128)(2,1)} custom-call(s32[2]{0:T(128)S(1)} %pad_add_fusion.1.refs_0_, bf16[4,208,512]{2,1,0:T(8,128)(2,1)} %all-to-all-done.refs_1_.refs_4_, f32[64,512]{1,0:T(8,128)S(1)} %shard_map.103.refs_2_), custom_call_target="tpu_custom_call" | custom-call | flops 1048576 | bytes 1024 | tf_op jit(solution)/shard_map/pallas_call | solution.py:61
  84.4 5.3 %shard_map.107.refs_6_ = bf16[2,512,1024]{2,1,0:T(8,128)(2,1)S(1)} custom-call(s32[2]{0:T(128)S(1)} %pad_add_fusion.refs_0_, bf16[768,512]{1,0:T(8,128)(2,1)} %shard_map.106.refs_1_, bf16[768,512]{1,0:T(8,128)(2,1)} %shard_map.104.refs_3_.refs_2_, bf16[768,512]{1,0:T(8,128)(2,1)} %collective-permute-done.10.refs_3_, ...), custom_call_target="tpu_custom_call" | custom-call | flops 1048576 | bytes 1024 | tf_op jit(solution)/shard_map/pallas_call | solution.py:61
  95.4 6.1 %shard_map.108 = (bf16[768,512]{1,0:T(8,128)(2,1)S(1)}, f32[768,512]{1,0:T(8,128)S(1)}, f32[2,64,512]{2,1,0:T(8,128)S(1)}) custom-call(s32[2]{0:T(128)S(1)} %pad_add_fusion.refs_0_, bf16[4,2,192,1024]{3,2,1,0:T(8,128)(2,1)S(1)} %bitcast.109, bf16[2,512,1024]{2,1,0:T(8,128)(2,1)S(1)} %copy-done.3, bf16[2,768,512]{2,1,0:T(8,128)(2,1)} %collective-permute-done.9.refs_3_, ...), custom_call_target="tpu_custom_call" | custom-call | flops 1048576 | bytes 1024 | tf_op jit(solution)/shard_map/pallas_call | solution.py:61
  103.0 5.3 %shard_map.109 = bf16[4,2,192,1024]{3,2,1,0:T(8,128)(2,1)S(1)} custom-call(s32[2]{0:T(128)S(1)} %pad_add_fusion.refs_0_, bf16[768,512]{1,0:T(8,128)(2,1)} %shard_map.106.refs_1_, bf16[768,512]{1,0:T(8,128)(2,1)} %shard_map.104.refs_3_.refs_2_, bf16[768,512]{1,0:T(8,128)(2,1)} %collective-permute-done.10.refs_3_, ...), custom_call_target="tpu_custom_call" | custom-call | flops 1048576 | bytes 1024 | tf_op jit(solution)/shard_map/pallas_call | solution.py:61
  108.9 13.1 %collective-permute-done.16 = f32[32,512]{1,0:T(8,128)S(1)} collective-permute-done((f32[32,512]{1,0:T(8,128)S(1)}, f32[32,512]{1,0:T(8,128)S(1)}, u32[]{:S(2)}, u32[]{:S(2)}) %collective-permute-start.16) | collective-permute-done | bytes 65568 | tf_op jit(solution)/shard_map/ppermute | solution.py:17
  122.1 2.9 %collective-permute-start.17 = (f32[32,512]{1,0:T(8,128)S(1)}, f32[32,512]{1,0:T(8,128)S(1)}, u32[]{:S(2)}, u32[]{:S(2)}) collective-permute-start(f32[32,512]{1,0:T(8,128)S(1)} %fusion.13), channel_id=1, source_target_pairs={{0,128},{128,0},{1,129},{129,1},{2,130},{130,2},{3,131},{131,3},{4... | collective-permute-start | bytes 196616 | tf_op jit(solution)/shard_map/ppermute | solution.py:17
  131.6 3.9 %collective-permute-done.13.refs_3_.refs_2_ = bf16[384,512]{1,0:T(8,128)(2,1)S(1)} collective-permute-done((bf16[384,512]{1,0:T(8,128)(2,1)S(1)}, bf16[384,512]{1,0:T(8,128)(2,1)S(1)}, u32[]{:S(2)}, u32[]{:S(2)}) %collective-permute-start.13) | collective-permute-done | bytes 393248 | tf_op jit(solution)/shard_map/ppermute | solution.py:29
  137.1 4.2 %all-to-all-start.1 = ((bf16[4,192,512]{2,1,0:T(8,128)(2,1)}), bf16[4,192,512]{2,1,0:T(8,128)(2,1)}, u32[]{:S(2)}, u32[]{:S(2)}) async-start(bf16[4,192,512]{2,1,0:T(8,128)(2,1)} %bitcast.113), calls=%async_computation.1 | async-start | bytes 1572864 | tf_op jit(solution)/shard_map/all_to_all | solution.py:21
  141.4 3.1 %collective-permute-start.23 = (bf16[32,512]{1,0:T(8,128)(2,1)}, bf16[32,512]{1,0:T(8,128)(2,1)}, u32[]{:S(2)}, u32[]{:S(2)}) collective-permute-start(bf16[32,512]{1,0:T(8,128)(2,1)} %copy-done.14), channel_id=1, source_target_pairs={{0,8},{4,12},{8,0},{12,4},{16,24},{20,28},{24,16},{28,20},{1,9},{5... | collective-permute-start | bytes 98312 | tf_op jit(solution)/shard_map/ppermute | solution.py:275
  144.4 6.6 %all-to-all-done.1.refs_4_.refs_3_ = bf16[4,192,512]{2,1,0:T(8,128)(2,1)} async-done(((bf16[4,192,512]{2,1,0:T(8,128)(2,1)}), bf16[4,192,512]{2,1,0:T(8,128)(2,1)}, u32[]{:S(2)}, u32[]{:S(2)}) %all-to-all-start.1) | async-done | bytes 786464 | tf_op jit(solution)/shard_map/all_to_all | solution.py:21
  152.8 3.6 %collective-permute-start.19 = (bf16[2,192,512]{2,1,0:T(8,128)(2,1)}, bf16[2,192,512]{2,1,0:T(8,128)(2,1)}, u32[]{:S(2)}, u32[]{:S(2)}) collective-permute-start(bf16[2,192,512]{2,1,0:T(8,128)(2,1)} %dynamic-slice_bitcast_fusion.1), channel_id=1, source_target_pairs={{0,1},{1,0},{2,3},{3,2},{4,5},{5,4},{6,7},{7,6},{8,9},{9,8},{10,11... | collective-permute-start | bytes 1179656 | tf_op jit(solution)/shard_map/ppermute | solution.py:17
  157.8 6.7 %collective-permute-start.24 = (bf16[32,512]{1,0:T(8,128)(2,1)}, bf16[32,512]{1,0:T(8,128)(2,1)}, u32[]{:S(2)}, u32[]{:S(2)}) collective-permute-start(bf16[32,512]{1,0:T(8,128)(2,1)} %add_convert_fusion.refs_1_), channel_id=1, source_target_pairs={{0,16},{4,20},{8,24},{12,28},{16,0},{20,4},{24,8},{28,12},{1,17},{... | collective-permute-start | bytes 98312 | tf_op jit(solution)/shard_map/ppermute | solution.py:275
  172.0 3.4 %all-to-all-start.2 = ((f32[4,32,512]{2,1,0:T(8,128)}), f32[4,32,512]{2,1,0:T(8,128)S(1)}, u32[]{:S(2)}, u32[]{:S(2)}) async-start(f32[4,32,512]{2,1,0:T(8,128)} %broadcast_in_dim.34), calls=%async_computation.3 | async-start | bytes 524288 | tf_op jit(solution)/shard_map/all_to_all | solution.py:21
  180.5 6.7 %collective-permute-done.20 = bf16[384,1024]{1,0:T(8,128)(2,1)} collective-permute-done((bf16[384,1024]{1,0:T(8,128)(2,1)}, bf16[384,1024]{1,0:T(8,128)(2,1)}, u32[]{:S(2)}, u32[]{:S(2)}) %collective-permute-start.20) | collective-permute-done | bytes 786464 | tf_op jit(solution)/shard_map/ppermute | solution.py:29
  187.2 2.7 %fusion.1 = bf16[384,1024]{1,0:T(8,128)(2,1)} fusion(bf16[384,1024]{1,0:T(8,128)(2,1)} %collective-permute-done.21, bf16[384,1024]{1,0:T(8,128)(2,1)} %collective-permute-done.20, bf16[4,384,1024]{2,1,0:T(8,128)(2,1)S(1)} %bitcast.112, s32[]{:T(128)S(6)} %select_n.127), kind=kLoop, calls=%fused_computation.2 | loop fusion | flops 2359296 | bytes 3145732 | tf_op jit(solution)/shard_map/convert_element_type | solution.py:297
  (139 shorter events, 69.8 us)
Async XLA Ops:
  7.2 62.0 %all-gather.2.cloned.1.call-start = ((), (), s32[]{:S(2)}) async-start(), calls=%async_computation.4 | async-start | bytes 2359296 | tf_op jit(solution)/shard_map/all_gather | solution.py:230
  8.3 10.1 %collective-permute-start.5 = (bf16[192,1024]{1,0:T(8,128)(2,1)S(1)}, bf16[192,1024]{1,0:T(8,128)(2,1)S(1)}, u32[]{:S(2)}, u32[]{:S(2)}) collective-permute-start(bf16[192,1024]{1,0:T(8,128)(2,1)S(1)} %dynamic-slice_bitcast_fusion.2), channel_id=1, source_target_pairs={{0,1},{1,0},{2,3},{3,2},{4,5},{5,4},{6,7},{7,6},{8,9},{9,8},{10,11... | collective-permute-start | bytes 1179656 | tf_op jit(solution)/shard_map/ppermute | solution.py:17
  20.0 19.8 %collective-permute-start = (bf16[384,1024]{1,0:T(8,128)(2,1)}, bf16[384,1024]{1,0:T(8,128)(2,1)}, u32[]{:S(2)}, u32[]{:S(2)}) collective-permute-start(bf16[384,1024]{1,0:T(8,128)(2,1)} %bitcast.121), channel_id=1, source_target_pairs={{0,32},{32,64},{64,96},{96,0},{1,33},{33,65},{65,97},{97,1},{2,34}... | collective-permute-start | bytes 2359304 | tf_op jit(solution)/shard_map/ppermute | solution.py:29
  20.1 21.5 %collective-permute-start.1 = (bf16[384,1024]{1,0:T(8,128)(2,1)}, bf16[384,1024]{1,0:T(8,128)(2,1)}, u32[]{:S(2)}, u32[]{:S(2)}) collective-permute-start(bf16[384,1024]{1,0:T(8,128)(2,1)} %bitcast.122), channel_id=1, source_target_pairs={{0,96},{32,0},{64,32},{96,64},{1,97},{33,1},{65,33},{97,65},{2,98}... | collective-permute-start | bytes 2359304 | tf_op jit(solution)/shard_map/ppermute | solution.py:29
  22.8 9.4 %collective-permute-start.7 = (bf16[64,1024]{1,0:T(8,128)(2,1)S(1)}, bf16[64,1024]{1,0:T(8,128)(2,1)S(1)}, u32[]{:S(2)}, u32[]{:S(2)}) collective-permute-start(bf16[64,1024]{1,0:T(8,128)(2,1)S(1)} %copy-done.9), channel_id=1, source_target_pairs={{0,1},{1,0},{2,3},{3,2},{4,5},{5,4},{6,7},{7,6},{8,9},{9,8},{10,11... | collective-permute-start | bytes 393224 | tf_op jit(solution)/shard_map/ppermute | solution.py:17
  26.7 21.8 %all-to-all-start = ((bf16[4,208,512]{2,1,0:T(8,128)(2,1)}), bf16[4,208,512]{2,1,0:T(8,128)(2,1)}, u32[]{:S(2)}, u32[]{:S(2)}) async-start(bf16[4,208,512]{2,1,0:T(8,128)(2,1)} %pad_maximum_fusion), calls=%async_computation | async-start | bytes 1703936 | tf_op jit(solution)/shard_map/all_to_all | solution.py:21
  31.0 147.8 %reduce-scatter.2.cloned.1.call-start = ((), (), s32[]{:S(2)}) async-start(), calls=%async_computation.5 | async-start | bytes 2359296 | tf_op jit(solution)/shard_map/reduce_scatter | solution.py:267
  33.1 27.0 %collective-permute-start.8 = (f32[64,512]{1,0:T(8,128)S(1)}, f32[64,512]{1,0:T(8,128)S(1)}, u32[]{:S(2)}, u32[]{:S(2)}) collective-permute-start(f32[64,512]{1,0:T(8,128)S(1)} %shard_map.103.refs_2_), channel_id=1, source_target_pairs={{0,2},{2,0},{1,3},{3,1},{4,6},{6,4},{5,7},{7,5},{8,10},{10,8},{9,1... | collective-permute-start | bytes 393224 | tf_op jit(solution)/shard_map/ppermute | solution.py:17
  41.6 16.3 %collective-permute-start.2 = (bf16[384,512]{1,0:T(8,128)(2,1)}, bf16[384,512]{1,0:T(8,128)(2,1)}, u32[]{:S(2)}, u32[]{:S(2)}) collective-permute-start(bf16[384,512]{1,0:T(8,128)(2,1)} %slice.42), channel_id=1, source_target_pairs={{0,32},{32,64},{64,96},{96,0},{1,33},{33,65},{65,97},{97,1},{2,34}... | collective-permute-start | bytes 1179656 | tf_op jit(solution)/shard_map/ppermute | solution.py:29
  43.4 15.6 %collective-permute-start.3 = (bf16[384,512]{1,0:T(8,128)(2,1)}, bf16[384,512]{1,0:T(8,128)(2,1)}, u32[]{:S(2)}, u32[]{:S(2)}) collective-permute-start(bf16[384,512]{1,0:T(8,128)(2,1)} %slice.43), channel_id=1, source_target_pairs={{0,96},{32,0},{64,32},{96,64},{1,97},{33,1},{65,33},{97,65},{2,98}... | collective-permute-start | bytes 1179656 | tf_op jit(solution)/shard_map/ppermute | solution.py:29
  48.5 17.5 %collective-permute-start.6 = (bf16[4,208,512]{2,1,0:T(8,128)(2,1)}, bf16[4,208,512]{2,1,0:T(8,128)(2,1)S(1)}, u32[]{:S(2)}, u32[]{:S(2)}) collective-permute-start(bf16[4,208,512]{2,1,0:T(8,128)(2,1)} %all-to-all-done.refs_1_.refs_4_), channel_id=1, source_target_pairs={{0,2},{2,0},{1,3},{3,1},{4,6},{6,4},{5,7},{7,5},{8,10},{10,8},{9,1... | collective-permute-start | bytes 2555912 | tf_op jit(solution)/shard_map/ppermute | solution.py:17
  73.7 17.4 %collective-permute-start.9 = (bf16[2,768,512]{2,1,0:T(8,128)(2,1)}, bf16[2,768,512]{2,1,0:T(8,128)(2,1)}, u32[]{:S(2)}, u32[]{:S(2)}) collective-permute-start(bf16[2,768,512]{2,1,0:T(8,128)(2,1)} %shard_map.105.refs_6_), channel_id=1, source_target_pairs={{0,1},{1,0},{2,3},{3,2},{4,5},{5,4},{6,7},{7,6},{8,9},{9,8},{10,11... | collective-permute-start | bytes 4718600 | tf_op jit(solution)/shard_map/ppermute | solution.py:17
  101.8 33.7 %collective-permute-start.12 = (bf16[768,512]{1,0:T(8,128)(2,1)S(1)}, bf16[768,512]{1,0:T(8,128)(2,1)S(1)}, u32[]{:S(2)}, u32[]{:S(2)}) collective-permute-start(bf16[768,512]{1,0:T(8,128)(2,1)S(1)} %get-tuple-element.10.refs_6_), channel_id=1, source_target_pairs={{0,2},{2,0},{1,3},{3,1},{4,6},{6,4},{5,7},{7,5},{8,10},{10,8},{9,1... | collective-permute-start | bytes 2359304 | tf_op jit(solution)/shard_map/ppermute | solution.py:17
  108.4 13.7 %collective-permute-start.16 = (f32[32,512]{1,0:T(8,128)S(1)}, f32[32,512]{1,0:T(8,128)S(1)}, u32[]{:S(2)}, u32[]{:S(2)}) collective-permute-start(f32[32,512]{1,0:T(8,128)S(1)} %slice_bitcast_fusion), channel_id=1, source_target_pairs={{0,2},{2,0},{1,3},{3,1},{4,6},{6,4},{5,7},{7,5},{8,10},{10,8},{9,1... | collective-permute-start | bytes 196616 | tf_op jit(solution)/shard_map/ppermute | solution.py:17
  125.0 10.5 %collective-permute-start.13 = (bf16[384,512]{1,0:T(8,128)(2,1)S(1)}, bf16[384,512]{1,0:T(8,128)(2,1)S(1)}, u32[]{:S(2)}, u32[]{:S(2)}) collective-permute-start(bf16[384,512]{1,0:T(8,128)(2,1)S(1)} %get-tuple-element.21), channel_id=1, source_target_pairs={{0,32},{32,64},{64,96},{96,0},{1,33},{33,65},{65,97},{97,1},{2,34}... | collective-permute-start | bytes 1179656 | tf_op jit(solution)/shard_map/ppermute | solution.py:29
  125.6 9.9 %collective-permute-start.14 = (bf16[384,512]{1,0:T(8,128)(2,1)S(1)}, bf16[384,512]{1,0:T(8,128)(2,1)S(1)}, u32[]{:S(2)}, u32[]{:S(2)}) collective-permute-start(bf16[384,512]{1,0:T(8,128)(2,1)S(1)} %get-tuple-element.20), channel_id=1, source_target_pairs={{0,96},{32,0},{64,32},{96,64},{1,97},{33,1},{65,33},{97,65},{2,98}... | collective-permute-start | bytes 1179656 | tf_op jit(solution)/shard_map/ppermute | solution.py:29
  137.1 13.9 %all-to-all-start.1 = ((bf16[4,192,512]{2,1,0:T(8,128)(2,1)}), bf16[4,192,512]{2,1,0:T(8,128)(2,1)}, u32[]{:S(2)}, u32[]{:S(2)}) async-start(bf16[4,192,512]{2,1,0:T(8,128)(2,1)} %bitcast.113), calls=%async_computation.1 | async-start | bytes 1572864 | tf_op jit(solution)/shard_map/all_to_all | solution.py:21
  141.4 15.1 %collective-permute-start.23 = (bf16[32,512]{1,0:T(8,128)(2,1)}, bf16[32,512]{1,0:T(8,128)(2,1)}, u32[]{:S(2)}, u32[]{:S(2)}) collective-permute-start(bf16[32,512]{1,0:T(8,128)(2,1)} %copy-done.14), channel_id=1, source_target_pairs={{0,8},{4,12},{8,0},{12,4},{16,24},{20,28},{24,16},{28,20},{1,9},{5... | collective-permute-start | bytes 98312 | tf_op jit(solution)/shard_map/ppermute | solution.py:275
  152.8 22.6 %collective-permute-start.19 = (bf16[2,192,512]{2,1,0:T(8,128)(2,1)}, bf16[2,192,512]{2,1,0:T(8,128)(2,1)}, u32[]{:S(2)}, u32[]{:S(2)}) collective-permute-start(bf16[2,192,512]{2,1,0:T(8,128)(2,1)} %dynamic-slice_bitcast_fusion.1), channel_id=1, source_target_pairs={{0,1},{1,0},{2,3},{3,2},{4,5},{5,4},{6,7},{7,6},{8,9},{9,8},{10,11... | collective-permute-start | bytes 1179656 | tf_op jit(solution)/shard_map/ppermute | solution.py:17
  157.8 12.6 %collective-permute-start.24 = (bf16[32,512]{1,0:T(8,128)(2,1)}, bf16[32,512]{1,0:T(8,128)(2,1)}, u32[]{:S(2)}, u32[]{:S(2)}) collective-permute-start(bf16[32,512]{1,0:T(8,128)(2,1)} %add_convert_fusion.refs_1_), channel_id=1, source_target_pairs={{0,16},{4,20},{8,24},{12,28},{16,0},{20,4},{24,8},{28,12},{1,17},{... | collective-permute-start | bytes 98312 | tf_op jit(solution)/shard_map/ppermute | solution.py:275
  166.8 20.4 %collective-permute-start.20 = (bf16[384,1024]{1,0:T(8,128)(2,1)}, bf16[384,1024]{1,0:T(8,128)(2,1)}, u32[]{:S(2)}, u32[]{:S(2)}) collective-permute-start(bf16[384,1024]{1,0:T(8,128)(2,1)} %get-tuple-element.12), channel_id=1, source_target_pairs={{0,32},{32,64},{64,96},{96,0},{1,33},{33,65},{65,97},{97,1},{2,34}... | collective-permute-start | bytes 2359304 | tf_op jit(solution)/shard_map/ppermute | solution.py:29
  167.1 20.1 %collective-permute-start.21 = (bf16[384,1024]{1,0:T(8,128)(2,1)}, bf16[384,1024]{1,0:T(8,128)(2,1)}, u32[]{:S(2)}, u32[]{:S(2)}) collective-permute-start(bf16[384,1024]{1,0:T(8,128)(2,1)} %get-tuple-element.13), channel_id=1, source_target_pairs={{0,96},{32,0},{64,32},{96,64},{1,97},{33,1},{65,33},{97,65},{2,98}... | collective-permute-start | bytes 2359304 | tf_op jit(solution)/shard_map/ppermute | solution.py:29
  172.0 17.9 %all-to-all-start.2 = ((f32[4,32,512]{2,1,0:T(8,128)}), f32[4,32,512]{2,1,0:T(8,128)S(1)}, u32[]{:S(2)}, u32[]{:S(2)}) async-start(f32[4,32,512]{2,1,0:T(8,128)} %broadcast_in_dim.34), calls=%async_computation.3 | async-start | bytes 524288 | tf_op jit(solution)/shard_map/all_to_all | solution.py:21
  180.3 9.6 %collective-permute-start.22 = (bf16[64,1024]{1,0:T(8,128)(2,1)}, bf16[64,1024]{1,0:T(8,128)(2,1)S(1)}, u32[]{:S(2)}, u32[]{:S(2)}) collective-permute-start(bf16[64,1024]{1,0:T(8,128)(2,1)} %dynamic-slice_bitcast_fusion.3), channel_id=1, source_target_pairs={{0,128},{128,0},{1,129},{129,1},{2,130},{130,2},{3,131},{131,3},{4... | collective-permute-start | bytes 393224 | tf_op jit(solution)/shard_map/ppermute | solution.py:17
  (28 other events, 117.1 us)
Sparse Core Ops, SparseCore 0:
  20.2 38.8 all-gather.1
  91.2 38.4 reduce-scatter.1

commit v7 on v6

--- a/solution.py
+++ b/solution.py
@@ -45,10 +45,10 @@
     return turn(far[:, :half], 1), turn(far[:, half:], -1)
 
 
-def scatter_y(a, far, y, after):
+def near_blocks(a, far, y, after):
     block = jax.ShapeDtypeStruct(a.shape[1:], BF)
     up, down = call(pass_body, y.reshape(1).astype(jnp.int32), (a,) + far, (block, block), after)
-    return pick(a, y, 0).astype(F32) + turn(up, 1).astype(F32) + turn(down, -1).astype(F32)
+    return turn(up, 1), turn(down, -1)
 
 
 VMEM = pl.BlockSpec(memory_space=pltpu.VMEM)
@@ -246,10 +246,13 @@
         (1 - c).reshape(1).astype(jnp.int32),
         (ho_y, weight),
         jax.ShapeDtypeStruct((XL, NY * half, wide), BF),
-        (far,),
+        (far, near),
     )
     theirs = swap(give, "c")
     wg = call(weight_body, at, pieces + (ho_y,), jax.ShapeDtypeStruct((XH, NZ * wr, cols), BF), (give,))
+    head_grad = call(head_body, at, pieces + (weight,), jax.ShapeDtypeStruct((NY, NC, half, cols), BF), (wg,))
+    head_grad = head_grad.reshape(NY, rows, cols)
+    head_far = far_blocks(head_grad, y)
     away, stay, table_part = call(
         keep_body,
         at,
@@ -259,27 +262,27 @@
             jax.ShapeDtypeStruct((NY * half, wide), F32),
             jax.ShapeDtypeStruct((XL, strategies, wide), F32),
         ),
-        (wg,),
-    )
-    head_grad = call(head_body, at, pieces + (weight,), jax.ShapeDtypeStruct((NY, NC, half, cols), BF), (away,))
-    head_grad = head_grad.reshape(NY, rows, cols)
-    head_far = far_blocks(head_grad, y)
+        (head_grad,),
+    )
+
     wg_part = lax.psum_scatter(wg, "z", scatter_dimension=1, tiled=True)
     wg_other = swap(pick(wg_part, 1 - xh, 0), "xh")
     weight_sum = pick(wg_part, xh, 0).astype(F32) + wg_other.astype(F32)
 
     table_part = table_part.reshape(XL, NC, strategies // NC, wide)
-    table_sum = pick(table_part, c, 1) + swap(pick(table_part, 1 - c, 1), "c")
+    sent = (pick(table_part, c, 1) + swap(pick(table_part, 1 - c, 1), "c")).astype(BF)
+    head_near = near_blocks(head_grad, head_far, y, (sent,))
+    for bit in (1, 2, 4):
+        if bit == 4:
+            home = jax.ShapeDtypeStruct(away.shape, BF)
+            home = call(home_body, at, (stay, swap(away, "xl")), home, head_near + (sent,))
+            home = exchange(home.reshape(NY, half, wide), "y")
+        table_sum = sent.astype(F32) + lax.ppermute(sent, "z", [(i, i ^ bit) for i in range(NZ)]).astype(F32)
+        sent = table_sum.astype(BF)
     table_sum = table_sum[0] + swap(table_sum[1], "xl")
-    table_sum = table_sum + swap(table_sum, "xh")
-    beside = lambda a, bit: lax.ppermute(a, "z", [(i, i ^ bit) for i in range(NZ)])
-    sent = table_sum.astype(BF)
-    sent = (sent.astype(F32) + beside(sent, 1).astype(F32)).astype(BF)
-    home = jax.ShapeDtypeStruct(away.shape, BF)
-    home = call(home_body, at, (stay, swap(away, "xl")), home, head_far + (sent,))
-    home = exchange(home.reshape(NY, half, wide), "y")
-    sent = (sent.astype(F32) + beside(sent, 2).astype(F32)).astype(BF)
-    table_sum = call(add_body, at, (sent, beside(sent, 4)), jax.ShapeDtypeStruct(sent.shape, F32), (home,))
+    table_sum = call(
+        add_body, at, (table_sum, swap(table_sum, "xh")), jax.ShapeDtypeStruct(table_sum.shape, F32), (home,)
+    )
     table_all = spread(table_sum, "y", NY).reshape(NC, 2, strategies // NC, wide)
     rest = jax.ShapeDtypeStruct(table_all.shape[1:], F32)
     rest = swap(call(take_body, (1 - c).reshape(1).astype(jnp.int32), (table_all,), rest, (wg_other,)), "c")
@@ -294,10 +297,10 @@
     proj = jnp.concatenate([proj[0], proj[1]], axis=1).astype(F32)
     layer_out = (residual.reshape(rows, cols).astype(F32) + proj * gating).astype(BF)
 
-    head_grad = scatter_y(head_grad, head_far, y, (home,)).astype(BF)
+    head_grad = pick(head_grad, y, 0).astype(F32) + head_near[0].astype(F32) + head_near[1].astype(F32)
 
     shape = head_out.shape
-    return layer_out.reshape(shape), head_grad.reshape(shape), weight_sum * grad_scale, table_grad
+    return layer_out.reshape(shape), head_grad.astype(BF).reshape(shape), weight_sum * grad_scale, table_grad
 
 
 def solution(mesh):

time: 203 us -> 170 us (0.84)
  waiting for transfers between devices: 62.1 us -> 48.3 us
  local copies, waits for them, and re-layouts: 25.5 us -> 16.9 us
  starting transfers between devices: 57.3 us -> 51 us
  other arithmetic: 9.7 us -> 4.84 us
    ppermute x15, waiting for transfers between devices: 28 us -> 8.27 us  [swap(): return lax.ppermute(a, axis, [(0, 1), (1, 0)])]
    ppermute x8, waiting for transfers between devices: 23 us -> 14.2 us  [turn(): return lax.ppermute(a, 'y', [(i, (i + k) % NY) for i in range(NY)])]
    ppermute x3, waiting for transfers between devices: 1.93 us -> 9.72 us  [on_device(): lax.ppermute(sent, 'z', [(i, i ^ bit) for i in range(NZ)]).astype(F32)]
    all_to_all x3, waiting for transfers between devices: 9.08 us -> 16 us  [exchange(): return lax.all_to_all(a, axis, 0, 0, tiled=True)]
    ppermute x3, starting transfers between devices: 11.7 us -> 6.66 us  [on_device(): lax.ppermute(sent, 'z', [(i, i ^ bit) for i in range(NZ)]).astype(F32)]
    unnamed x42 -> x26, local copies, waits for them, and re-layouts: 11.7 us -> 7.05 us
    another operation x6, other arithmetic: 2.48 us -> 0.29 us  [in_order(): return jnp.stack([first, second], axis=dim)]
    convert_element_type x3 -> x2, other arithmetic: 4.08 us -> 2.36 us  [the longest x1 2.34 us: on_device(): head_grad.astype(BF).reshape(shape)]
  transfers between devices with their start and end apart: 31 -> 31, of which waited for: 12 -> 12; matrix products, arithmetic and copies ran while one was open for 12% -> 10% of each run, Pallas kernels for 13% -> 17%
where the time goes in v7:
time: 170 us; the launch traced here: 169 us
  starting transfers between devices  51 us (30%)
  waiting for transfers between devices  48.3 us (28%)
  Pallas kernels  28.8 us (17%)
  local copies, waits for them, and re-layouts  16.9 us (10%)
  between operations  14.5 us (9%)
  other arithmetic  4.84 us (3%)
  matrix products  4.39 us (3%)
    pallas_call x12, Pallas kernels, call(): pl.pallas_call(lambda *refs: body(*refs[:count], *refs[count + len(after)...  28.8 us
    ppermute x15, starting transfers between devices, swap(): return lax.ppermute(a, axis, [(0, 1), (1, 0)])  22 us
    all_to_all x3, waiting for transfers between devices, exchange(): return lax.all_to_all(a, axis, 0, 0, tiled=True)  16 us
    ppermute x8, waiting for transfers between devices, turn(): return lax.ppermute(a, 'y', [(i, (i + k) % NY) for i in range(NY)])  14.2 us
    all_to_all x3, starting transfers between devices, exchange(): return lax.all_to_all(a, axis, 0, 0, tiled=True)  11.2 us
    ppermute x8, starting transfers between devices, turn(): return lax.ppermute(a, 'y', [(i, (i + k) % NY) for i in range(NY)])  11.1 us
    ppermute x3, waiting for transfers between devices, on_device(): lax.ppermute(sent, 'z', [(i, i ^ bit) for i in range(NZ)]).astype(F32)  9.72 us
    ppermute x15, waiting for transfers between devices, swap(): return lax.ppermute(a, axis, [(0, 1), (1, 0)])  8.27 us
  transfers between devices with their start and end apart: 31, of which 12 were waited for; matrix products, arithmetic and copies ran while one was open for 10% of the time, Pallas kernels for 17%

profile of v7, /device:TPU:1, one launch (start us, length us, event | category | flops | bytes accessed | tf_op | source)
XLA Modules:
  0.0 168.8 jit_solution(14408162273184650878)
XLA Ops:
  8.3 3.3 %collective-permute-start.5 = (bf16[192,1024]{1,0:T(8,128)(2,1)S(1)}, bf16[192,1024]{1,0:T(8,128)(2,1)S(1)}, u32[]{:S(2)}, u32[]{:S(2)}) collective-permute-start(bf16[192,1024]{1,0:T(8,128)(2,1)S(1)} %dynamic-slice_bitcast_fusion.2), channel_id=1, source_target_pairs={{0,1},{1,0},{2,3},{3,2},{4,5},{5,4},{6,7},{7,6},{8,9},{9,8},{10,11... | collective-permute-start | bytes 1179656 | tf_op jit(solution)/shard_map/ppermute | solution.py:17
  12.7 5.7 %collective-permute-done.4.refs_2_ = bf16[64,1024]{1,0:T(8,128)(2,1)S(1)} collective-permute-done((bf16[64,1024]{1,0:T(8,128)(2,1)}, bf16[64,1024]{1,0:T(8,128)(2,1)S(1)}, u32[]{:S(2)}, u32[]{:S(2)}) %collective-permute-start.4) | collective-permute-done | bytes 131104 | tf_op jit(solution)/shard_map/ppermute | solution.py:17
  21.4 4.2 %all-to-all-start = ((bf16[4,208,512]{2,1,0:T(8,128)(2,1)}), bf16[4,208,512]{2,1,0:T(8,128)(2,1)}, u32[]{:S(2)}, u32[]{:S(2)}) async-start(bf16[4,208,512]{2,1,0:T(8,128)(2,1)} %pad_maximum_fusion), calls=%async_computation | async-start | bytes 1703936 | tf_op jit(solution)/shard_map/all_to_all | solution.py:21
  30.1 7.8 %all-to-all-done.refs_1_.refs_4_ = bf16[4,208,512]{2,1,0:T(8,128)(2,1)} async-done(((bf16[4,208,512]{2,1,0:T(8,128)(2,1)}), bf16[4,208,512]{2,1,0:T(8,128)(2,1)}, u32[]{:S(2)}, u32[]{:S(2)}) %all-to-all-start) | async-done | bytes 852000 | tf_op jit(solution)/shard_map/all_to_all | solution.py:21
  42.0 12.5 %collective-permute-done = bf16[384,1024]{1,0:T(8,128)(2,1)} collective-permute-done((bf16[384,1024]{1,0:T(8,128)(2,1)}, bf16[384,1024]{1,0:T(8,128)(2,1)}, u32[]{:S(2)}, u32[]{:S(2)}) %collective-permute-start) | collective-permute-done | bytes 786464 | tf_op jit(solution)/shard_map/ppermute | solution.py:29
  56.6 2.7 %collective-permute-start.3 = (bf16[384,512]{1,0:T(8,128)(2,1)S(1)}, bf16[384,512]{1,0:T(8,128)(2,1)S(1)}, u32[]{:S(2)}, u32[]{:S(2)}) collective-permute-start(bf16[384,512]{1,0:T(8,128)(2,1)S(1)} %slice.43), channel_id=1, source_target_pairs={{0,96},{32,0},{64,32},{96,64},{1,97},{33,1},{65,33},{97,65},{2,98}... | collective-permute-start | bytes 1179656 | tf_op jit(solution)/shard_map/ppermute | solution.py:29
  61.7 2.8 %shard_map.105.refs_4_.refs_1_ = bf16[768,512]{1,0:T(8,128)(2,1)} custom-call(s32[2]{0:T(128)S(1)} %pad_add_fusion.1.refs_0_, bf16[4,208,512]{2,1,0:T(8,128)(2,1)} %all-to-all-done.refs_1_.refs_4_, f32[64,512]{1,0:T(8,128)S(1)} %shard_map.103.refs_2_), custom_call_target="tpu_custom_call" | custom-call | flops 1048576 | bytes 1024 | tf_op jit(solution)/shard_map/pallas_call | solution.py:61
  64.6 2.3 %collective-permute-start.10 = (bf16[768,512]{1,0:T(8,128)(2,1)}, bf16[768,512]{1,0:T(8,128)(2,1)}, u32[]{:S(2)}, u32[]{:S(2)}) collective-permute-start(bf16[768,512]{1,0:T(8,128)(2,1)} %shard_map.105.refs_4_.refs_1_), channel_id=1, source_target_pairs={{0,1},{1,0},{2,3},{3,2},{4,5},{5,4},{6,7},{7,6},{8,9},{9,8},{10,11... | collective-permute-start | bytes 2359304 | tf_op jit(solution)/shard_map/ppermute | solution.py:17
  70.9 3.1 %shard_map.106.refs_6_ = bf16[2,768,512]{2,1,0:T(8,128)(2,1)} custom-call(s32[1]{0:T(128)} %bitcast.13.refs_0_, bf16[4,2,192,1024]{3,2,1,0:T(8,128)(2,1)S(1)} %bitcast.109, bf16[2,512,1024]{2,1,0:T(8,128)(2,1)S(1)} %copy-done.3, bf16[768,512]{1,0:T(8,128)(2,1)} %shard_map.104.refs_3_.refs_2_, bf16[768,512]{1,0:T(8,128)(2,1)} %shard_map.105.refs_4_.refs_1_), custom_call_target="tpu_custom_call" | custom-call | flops 1048576 | bytes 1024 | tf_op jit(solution)/shard_map/pallas_call | solution.py:61
  74.5 5.4 %shard_map.107.refs_6_ = bf16[2,512,1024]{2,1,0:T(8,128)(2,1)S(1)} custom-call(s32[2]{0:T(128)S(1)} %pad_add_fusion.refs_0_, bf16[768,512]{1,0:T(8,128)(2,1)} %shard_map.105.refs_4_.refs_1_, bf16[768,512]{1,0:T(8,128)(2,1)} %shard_map.104.refs_3_.refs_2_, bf16[768,512]{1,0:T(8,128)(2,1)} %collective-permute-done.10.refs_3_, ...), custom_call_target="tpu_custom_call" | custom-call | flops 1048576 | bytes 1024 | tf_op jit(solution)/shard_map/pallas_call | solution.py:61
  84.5 5.3 %shard_map.108 = bf16[4,2,192,1024]{3,2,1,0:T(8,128)(2,1)S(1)} custom-call(s32[2]{0:T(128)S(1)} %pad_add_fusion.refs_0_, bf16[768,512]{1,0:T(8,128)(2,1)} %shard_map.105.refs_4_.refs_1_, bf16[768,512]{1,0:T(8,128)(2,1)} %shard_map.104.refs_3_.refs_2_, bf16[768,512]{1,0:T(8,128)(2,1)} %collective-permute-done.10.refs_3_, ...), custom_call_target="tpu_custom_call" | custom-call | flops 1048576 | bytes 1024 | tf_op jit(solution)/shard_map/pallas_call | solution.py:61
  90.0 2.7 %collective-permute-start.14 = (bf16[384,512]{1,0:T(8,128)(2,1)S(1)}, bf16[384,512]{1,0:T(8,128)(2,1)S(1)}, u32[]{:S(2)}, u32[]{:S(2)}) collective-permute-start(bf16[384,512]{1,0:T(8,128)(2,1)S(1)} %get-tuple-element.20), channel_id=1, source_target_pairs={{0,96},{32,0},{64,32},{96,64},{1,97},{33,1},{65,33},{97,65},{2,98}... | collective-permute-start | bytes 1179656 | tf_op jit(solution)/shard_map/ppermute | solution.py:29
  92.7 6.2 %shard_map.109 = (bf16[768,512]{1,0:T(8,128)(2,1)S(1)}, f32[768,512]{1,0:T(8,128)S(1)}, f32[2,64,512]{2,1,0:T(8,128)S(1)}) custom-call(s32[2]{0:T(128)S(1)} %pad_add_fusion.refs_0_, bf16[4,2,192,1024]{3,2,1,0:T(8,128)(2,1)S(1)} %bitcast.111, bf16[2,512,1024]{2,1,0:T(8,128)(2,1)S(1)} %copy-done.4, bf16[2,768,512]{2,1,0:T(8,128)(2,1)} %collective-permute-done.9.refs_3_, ...), custom_call_target="tpu_custom_call" | custom-call | flops 1048576 | bytes 1024 | tf_op jit(solution)/shard_map/pallas_call | solution.py:61
  105.0 4.8 %collective-permute-done.18 = bf16[2,32,512]{2,1,0:T(8,128)(2,1)S(1)} collective-permute-done((bf16[2,32,512]{2,1,0:T(8,128)(2,1)S(1)}, bf16[2,32,512]{2,1,0:T(8,128)(2,1)S(1)}, u32[]{:S(2)}, u32[]{:S(2)}) %collective-permute-start.18) | collective-permute-done | bytes 65568 | tf_op jit(solution)/shard_map/ppermute | solution.py:280
  111.2 4.9 %collective-permute-done.19 = bf16[2,32,512]{2,1,0:T(8,128)(2,1)S(1)} collective-permute-done((bf16[2,32,512]{2,1,0:T(8,128)(2,1)S(1)}, bf16[2,32,512]{2,1,0:T(8,128)(2,1)S(1)}, u32[]{:S(2)}, u32[]{:S(2)}) %collective-permute-start.19) | collective-permute-done | bytes 65568 | tf_op jit(solution)/shard_map/ppermute | solution.py:280
  116.1 5.3 %collective-permute-start.22 = (bf16[2,32,512]{2,1,0:T(8,128)(2,1)S(1)}, bf16[2,32,512]{2,1,0:T(8,128)(2,1)S(1)}, u32[]{:S(2)}, u32[]{:S(2)}) collective-permute-start(bf16[2,32,512]{2,1,0:T(8,128)(2,1)S(1)} %add_convert_fusion.refs_5_), channel_id=1, source_target_pairs={{0,16},{4,20},{8,24},{12,28},{16,0},{20,4},{24,8},{28,12},{1,17},{... | collective-permute-start | bytes 196616 | tf_op jit(solution)/shard_map/ppermute | solution.py:280
  123.4 3.6 %all-to-all-start.1 = ((bf16[4,192,512]{2,1,0:T(8,128)(2,1)}), bf16[4,192,512]{2,1,0:T(8,128)(2,1)S(1)}, u32[]{:S(2)}, u32[]{:S(2)}) async-start(bf16[4,192,512]{2,1,0:T(8,128)(2,1)} %bitcast.26), calls=%async_computation.1 | async-start | bytes 1572864 | tf_op jit(solution)/shard_map/all_to_all | solution.py:21
  127.9 8.1 %all-to-all-done.1.refs_3_ = bf16[4,192,512]{2,1,0:T(8,128)(2,1)S(1)} async-done(((bf16[4,192,512]{2,1,0:T(8,128)(2,1)}), bf16[4,192,512]{2,1,0:T(8,128)(2,1)S(1)}, u32[]{:S(2)}, u32[]{:S(2)}) %all-to-all-start.1) | async-done | bytes 786464 | tf_op jit(solution)/shard_map/all_to_all | solution.py:21
  136.8 4.2 %collective-permute-start.20 = (bf16[2,192,512]{2,1,0:T(8,128)(2,1)}, bf16[2,192,512]{2,1,0:T(8,128)(2,1)S(1)}, u32[]{:S(2)}, u32[]{:S(2)}) collective-permute-start(bf16[2,192,512]{2,1,0:T(8,128)(2,1)} %dynamic-slice_bitcast_fusion.1), channel_id=1, source_target_pairs={{0,1},{1,0},{2,3},{3,2},{4,5},{5,4},{6,7},{7,6},{8,9},{9,8},{10,11... | collective-permute-start | bytes 1179656 | tf_op jit(solution)/shard_map/ppermute | solution.py:17
  141.0 2.3 %collective-permute-start.24 = (f32[32,512]{1,0:T(8,128)S(1)}, f32[32,512]{1,0:T(8,128)S(1)}, u32[]{:S(2)}, u32[]{:S(2)}) collective-permute-start(f32[32,512]{1,0:T(8,128)S(1)} %fusion.14.refs_1_), channel_id=1, source_target_pairs={{0,128},{128,0},{1,129},{129,1},{2,130},{130,2},{3,131},{131,3},{4... | collective-permute-start | bytes 196616 | tf_op jit(solution)/shard_map/ppermute | solution.py:17
  143.3 2.3 %fusion.1 = bf16[384,1024]{1,0:T(8,128)(2,1)} fusion(bf16[384,1024]{1,0:T(8,128)(2,1)S(1)} %collective-permute-done.17.refs_4_, bf16[384,1024]{1,0:T(8,128)(2,1)S(1)} %collective-permute-done.16.refs_3_, bf16[4,384,1024]{2,1,0:T(8,128)(2,1)} %bitcast.115, s32[]{:T(128)S(6)} %select_n.127), kind=kLoop, calls=%fused_computation.2 | loop fusion | flops 2359296 | bytes 3145732 | tf_op jit(solution)/shard_map/convert_element_type | solution.py:303
  147.6 3.4 %all-to-all-start.2 = ((f32[4,32,512]{2,1,0:T(8,128)}), f32[4,32,512]{2,1,0:T(8,128)S(1)}, u32[]{:S(2)}, u32[]{:S(2)}) async-start(f32[4,32,512]{2,1,0:T(8,128)} %broadcast_in_dim.34), calls=%async_computation.3 | async-start | bytes 524288 | tf_op jit(solution)/shard_map/all_to_all | solution.py:21
  152.2 2.3 %collective-permute-start.21 = (bf16[64,1024]{1,0:T(8,128)(2,1)S(1)}, bf16[64,1024]{1,0:T(8,128)(2,1)S(1)}, u32[]{:S(2)}, u32[]{:S(2)}) collective-permute-start(bf16[64,1024]{1,0:T(8,128)(2,1)S(1)} %dynamic-slice_bitcast_fusion.3), channel_id=1, source_target_pairs={{0,128},{128,0},{1,129},{129,1},{2,130},{130,2},{3,131},{131,3},{4... | collective-permute-start | bytes 393224 | tf_op jit(solution)/shard_map/ppermute | solution.py:17
  154.4 3.0 %fusion.2 = bf16[384,1024]{1,0:T(8,128)(2,1)} fusion(bf16[384,1024]{1,0:T(8,128)(2,1)} %bitcast.131, f32[64,1024]{1,0:T(8,128)S(1)} %fusion.19, bf16[384,512]{1,0:T(8,128)(2,1)S(1)} %bitcast.129, bf16[384,512]{1,0:T(8,128)(2,1)S(1)} %bitcast.128, s32[384]{0:T(512)S(1)} %bitcast.130), kind=kOutput, calls=%fused_computation.4 | convolution fusion | flops 305553408 | bytes 2622976 | tf_op jit(solution)/shard_map/dot_general | solution.py:197
  (123 shorter events, 46.0 us)
Async XLA Ops:
  7.2 62.1 %all-gather.2.cloned.1.call-start = ((), (), s32[]{:S(2)}) async-start(), calls=%async_computation.4 | async-start | bytes 2359296 | tf_op jit(solution)/shard_map/all_gather | solution.py:230
  8.3 10.1 %collective-permute-start.5 = (bf16[192,1024]{1,0:T(8,128)(2,1)S(1)}, bf16[192,1024]{1,0:T(8,128)(2,1)S(1)}, u32[]{:S(2)}, u32[]{:S(2)}) collective-permute-start(bf16[192,1024]{1,0:T(8,128)(2,1)S(1)} %dynamic-slice_bitcast_fusion.2), channel_id=1, source_target_pairs={{0,1},{1,0},{2,3},{3,2},{4,5},{5,4},{6,7},{7,6},{8,9},{9,8},{10,11... | collective-permute-start | bytes 1179656 | tf_op jit(solution)/shard_map/ppermute | solution.py:17
  11.7 6.8 %collective-permute-start.4 = (bf16[64,1024]{1,0:T(8,128)(2,1)}, bf16[64,1024]{1,0:T(8,128)(2,1)S(1)}, u32[]{:S(2)}, u32[]{:S(2)}) collective-permute-start(bf16[64,1024]{1,0:T(8,128)(2,1)} %refs_1_.1), channel_id=1, source_target_pairs={{0,128},{128,0},{1,129},{129,1},{2,130},{130,2},{3,131},{131,3},{4... | collective-permute-start | bytes 393224 | tf_op jit(solution)/shard_map/ppermute | solution.py:17
  21.4 16.5 %all-to-all-start = ((bf16[4,208,512]{2,1,0:T(8,128)(2,1)}), bf16[4,208,512]{2,1,0:T(8,128)(2,1)}, u32[]{:S(2)}, u32[]{:S(2)}) async-start(bf16[4,208,512]{2,1,0:T(8,128)(2,1)} %pad_maximum_fusion), calls=%async_computation | async-start | bytes 1703936 | tf_op jit(solution)/shard_map/all_to_all | solution.py:21
  25.7 125.6 %reduce-scatter.2.cloned.1.call-start = ((), (), s32[]{:S(2)}) async-start(), calls=%async_computation.5 | async-start | bytes 2359296 | tf_op jit(solution)/shard_map/reduce_scatter | solution.py:268
  25.7 28.7 %collective-permute-start = (bf16[384,1024]{1,0:T(8,128)(2,1)}, bf16[384,1024]{1,0:T(8,128)(2,1)}, u32[]{:S(2)}, u32[]{:S(2)}) collective-permute-start(bf16[384,1024]{1,0:T(8,128)(2,1)} %bitcast.4), channel_id=1, source_target_pairs={{0,32},{32,64},{64,96},{96,0},{1,33},{33,65},{65,97},{97,1},{2,34}... | collective-permute-start | bytes 2359304 | tf_op jit(solution)/shard_map/ppermute | solution.py:29
  27.1 28.5 %collective-permute-start.1 = (bf16[384,1024]{1,0:T(8,128)(2,1)}, bf16[384,1024]{1,0:T(8,128)(2,1)}, u32[]{:S(2)}, u32[]{:S(2)}) collective-permute-start(bf16[384,1024]{1,0:T(8,128)(2,1)} %bitcast.4), channel_id=1, source_target_pairs={{0,96},{32,0},{64,32},{96,64},{1,97},{33,1},{65,33},{97,65},{2,98}... | collective-permute-start | bytes 2359304 | tf_op jit(solution)/shard_map/ppermute | solution.py:29
  28.5 11.2 %collective-permute-start.7 = (bf16[64,1024]{1,0:T(8,128)(2,1)S(1)}, bf16[64,1024]{1,0:T(8,128)(2,1)S(1)}, u32[]{:S(2)}, u32[]{:S(2)}) collective-permute-start(bf16[64,1024]{1,0:T(8,128)(2,1)S(1)} %copy-done.7), channel_id=1, source_target_pairs={{0,1},{1,0},{2,3},{3,2},{4,5},{5,4},{6,7},{7,6},{8,9},{9,8},{10,11... | collective-permute-start | bytes 393224 | tf_op jit(solution)/shard_map/ppermute | solution.py:17
  37.9 29.0 %collective-permute-start.6 = (bf16[4,208,512]{2,1,0:T(8,128)(2,1)}, bf16[4,208,512]{2,1,0:T(8,128)(2,1)S(1)}, u32[]{:S(2)}, u32[]{:S(2)}) collective-permute-start(bf16[4,208,512]{2,1,0:T(8,128)(2,1)} %all-to-all-done.refs_1_.refs_4_), channel_id=1, source_target_pairs={{0,2},{2,0},{1,3},{3,1},{4,6},{6,4},{5,7},{7,5},{8,10},{10,8},{9,1... | collective-permute-start | bytes 2555912 | tf_op jit(solution)/shard_map/ppermute | solution.py:17
  40.5 26.4 %collective-permute-start.8 = (f32[64,512]{1,0:T(8,128)S(1)}, f32[64,512]{1,0:T(8,128)S(1)}, u32[]{:S(2)}, u32[]{:S(2)}) collective-permute-start(f32[64,512]{1,0:T(8,128)S(1)} %shard_map.103.refs_2_), channel_id=1, source_target_pairs={{0,2},{2,0},{1,3},{3,1},{4,6},{6,4},{5,7},{7,5},{8,10},{10,8},{9,1... | collective-permute-start | bytes 393224 | tf_op jit(solution)/shard_map/ppermute | solution.py:17
  55.5 13.7 %collective-permute-start.2 = (bf16[384,512]{1,0:T(8,128)(2,1)S(1)}, bf16[384,512]{1,0:T(8,128)(2,1)S(1)}, u32[]{:S(2)}, u32[]{:S(2)}) collective-permute-start(bf16[384,512]{1,0:T(8,128)(2,1)S(1)} %slice.42), channel_id=1, source_target_pairs={{0,32},{32,64},{64,96},{96,0},{1,33},{33,65},{65,97},{97,1},{2,34}... | collective-permute-start | bytes 1179656 | tf_op jit(solution)/shard_map/ppermute | solution.py:29
  56.6 12.6 %collective-permute-start.3 = (bf16[384,512]{1,0:T(8,128)(2,1)S(1)}, bf16[384,512]{1,0:T(8,128)(2,1)S(1)}, u32[]{:S(2)}, u32[]{:S(2)}) collective-permute-start(bf16[384,512]{1,0:T(8,128)(2,1)S(1)} %slice.43), channel_id=1, source_target_pairs={{0,96},{32,0},{64,32},{96,64},{1,97},{33,1},{65,33},{97,65},{2,98}... | collective-permute-start | bytes 1179656 | tf_op jit(solution)/shard_map/ppermute | solution.py:29
  64.6 10.0 %collective-permute-start.10 = (bf16[768,512]{1,0:T(8,128)(2,1)}, bf16[768,512]{1,0:T(8,128)(2,1)}, u32[]{:S(2)}, u32[]{:S(2)}) collective-permute-start(bf16[768,512]{1,0:T(8,128)(2,1)} %shard_map.105.refs_4_.refs_1_), channel_id=1, source_target_pairs={{0,1},{1,0},{2,3},{3,2},{4,5},{5,4},{6,7},{7,6},{8,9},{9,8},{10,11... | collective-permute-start | bytes 2359304 | tf_op jit(solution)/shard_map/ppermute | solution.py:17
  74.0 18.7 %collective-permute-start.9 = (bf16[2,768,512]{2,1,0:T(8,128)(2,1)}, bf16[2,768,512]{2,1,0:T(8,128)(2,1)}, u32[]{:S(2)}, u32[]{:S(2)}) collective-permute-start(bf16[2,768,512]{2,1,0:T(8,128)(2,1)} %shard_map.106.refs_6_), channel_id=1, source_target_pairs={{0,1},{1,0},{2,3},{3,2},{4,5},{5,4},{6,7},{7,6},{8,9},{9,8},{10,11... | collective-permute-start | bytes 4718600 | tf_op jit(solution)/shard_map/ppermute | solution.py:17
  90.0 12.0 %collective-permute-start.13 = (bf16[384,512]{1,0:T(8,128)(2,1)S(1)}, bf16[384,512]{1,0:T(8,128)(2,1)S(1)}, u32[]{:S(2)}, u32[]{:S(2)}) collective-permute-start(bf16[384,512]{1,0:T(8,128)(2,1)S(1)} %get-tuple-element.21), channel_id=1, source_target_pairs={{0,32},{32,64},{64,96},{96,0},{1,33},{33,65},{65,97},{97,1},{2,34}... | collective-permute-start | bytes 1179656 | tf_op jit(solution)/shard_map/ppermute | solution.py:29
  90.0 11.9 %collective-permute-start.14 = (bf16[384,512]{1,0:T(8,128)(2,1)S(1)}, bf16[384,512]{1,0:T(8,128)(2,1)S(1)}, u32[]{:S(2)}, u32[]{:S(2)}) collective-permute-start(bf16[384,512]{1,0:T(8,128)(2,1)S(1)} %get-tuple-element.20), channel_id=1, source_target_pairs={{0,96},{32,0},{64,32},{96,64},{1,97},{33,1},{65,33},{97,65},{2,98}... | collective-permute-start | bytes 1179656 | tf_op jit(solution)/shard_map/ppermute | solution.py:29
  99.6 21.8 %collective-permute-start.12 = (bf16[768,512]{1,0:T(8,128)(2,1)S(1)}, bf16[768,512]{1,0:T(8,128)(2,1)S(1)}, u32[]{:S(2)}, u32[]{:S(2)}) collective-permute-start(bf16[768,512]{1,0:T(8,128)(2,1)S(1)} %get-tuple-element.10), channel_id=1, source_target_pairs={{0,2},{2,0},{1,3},{3,1},{4,6},{6,4},{5,7},{7,5},{8,10},{10,8},{9,1... | collective-permute-start | bytes 2359304 | tf_op jit(solution)/shard_map/ppermute | solution.py:17
  102.2 19.7 %collective-permute-start.16 = (bf16[384,1024]{1,0:T(8,128)(2,1)S(1)}, bf16[384,1024]{1,0:T(8,128)(2,1)S(1)}, u32[]{:S(2)}, u32[]{:S(2)}) collective-permute-start(bf16[384,1024]{1,0:T(8,128)(2,1)S(1)} %get-tuple-element.12), channel_id=1, source_target_pairs={{0,32},{32,64},{64,96},{96,0},{1,33},{33,65},{65,97},{97,1},{2,34}... | collective-permute-start | bytes 2359304 | tf_op jit(solution)/shard_map/ppermute | solution.py:29
  102.9 18.9 %collective-permute-start.17 = (bf16[384,1024]{1,0:T(8,128)(2,1)S(1)}, bf16[384,1024]{1,0:T(8,128)(2,1)S(1)}, u32[]{:S(2)}, u32[]{:S(2)}) collective-permute-start(bf16[384,1024]{1,0:T(8,128)(2,1)S(1)} %get-tuple-element.13), channel_id=1, source_target_pairs={{0,96},{32,0},{64,32},{96,64},{1,97},{33,1},{65,33},{97,65},{2,98}... | collective-permute-start | bytes 2359304 | tf_op jit(solution)/shard_map/ppermute | solution.py:29
  116.1 11.2 %collective-permute-start.22 = (bf16[2,32,512]{2,1,0:T(8,128)(2,1)S(1)}, bf16[2,32,512]{2,1,0:T(8,128)(2,1)S(1)}, u32[]{:S(2)}, u32[]{:S(2)}) collective-permute-start(bf16[2,32,512]{2,1,0:T(8,128)(2,1)S(1)} %add_convert_fusion.refs_5_), channel_id=1, source_target_pairs={{0,16},{4,20},{8,24},{12,28},{16,0},{20,4},{24,8},{28,12},{1,17},{... | collective-permute-start | bytes 196616 | tf_op jit(solution)/shard_map/ppermute | solution.py:280
  123.4 12.6 %all-to-all-start.1 = ((bf16[4,192,512]{2,1,0:T(8,128)(2,1)}), bf16[4,192,512]{2,1,0:T(8,128)(2,1)S(1)}, u32[]{:S(2)}, u32[]{:S(2)}) async-start(bf16[4,192,512]{2,1,0:T(8,128)(2,1)} %bitcast.26), calls=%async_computation.1 | async-start | bytes 1572864 | tf_op jit(solution)/shard_map/all_to_all | solution.py:21
  127.3 13.7 %collective-permute-start.23 = (f32[32,512]{1,0:T(8,128)S(1)}, f32[32,512]{1,0:T(8,128)S(1)}, u32[]{:S(2)}, u32[]{:S(2)}) collective-permute-start(f32[32,512]{1,0:T(8,128)S(1)} %slice_bitcast_fusion), channel_id=1, source_target_pairs={{0,2},{2,0},{1,3},{3,1},{4,6},{6,4},{5,7},{7,5},{8,10},{10,8},{9,1... | collective-permute-start | bytes 196616 | tf_op jit(solution)/shard_map/ppermute | solution.py:17
  136.8 14.2 %collective-permute-start.20 = (bf16[2,192,512]{2,1,0:T(8,128)(2,1)}, bf16[2,192,512]{2,1,0:T(8,128)(2,1)S(1)}, u32[]{:S(2)}, u32[]{:S(2)}) collective-permute-start(bf16[2,192,512]{2,1,0:T(8,128)(2,1)} %dynamic-slice_bitcast_fusion.1), channel_id=1, source_target_pairs={{0,1},{1,0},{2,3},{3,2},{4,5},{5,4},{6,7},{7,6},{8,9},{9,8},{10,11... | collective-permute-start | bytes 1179656 | tf_op jit(solution)/shard_map/ppermute | solution.py:17
  147.6 9.8 %all-to-all-start.2 = ((f32[4,32,512]{2,1,0:T(8,128)}), f32[4,32,512]{2,1,0:T(8,128)S(1)}, u32[]{:S(2)}, u32[]{:S(2)}) async-start(f32[4,32,512]{2,1,0:T(8,128)} %broadcast_in_dim.34), calls=%async_computation.3 | async-start | bytes 524288 | tf_op jit(solution)/shard_map/all_to_all | solution.py:21
  (20 other events, 107.6 us)
Sparse Core Ops, SparseCore 0:
  20.2 39.0 all-gather.1
  81.4 40.4 reduce-scatter.1

commit v8 on v7

--- a/solution.py
+++ b/solution.py
@@ -82,7 +82,7 @@
 
 
 def add_body(at, a, b, out):
-    out[...] = a[...].astype(F32) + b[...].astype(F32)
+    out[...] = (a[...].astype(F32) + b[...].astype(F32)).astype(out.dtype)
 
 
 def pair_body(at, own, other, out):
@@ -272,26 +272,26 @@
     table_part = table_part.reshape(XL, NC, strategies // NC, wide)
     sent = (pick(table_part, c, 1) + swap(pick(table_part, 1 - c, 1), "c")).astype(BF)
     head_near = near_blocks(head_grad, head_far, y, (sent,))
-    for bit in (1, 2, 4):
-        if bit == 4:
-            home = jax.ShapeDtypeStruct(away.shape, BF)
-            home = call(home_body, at, (stay, swap(away, "xl")), home, head_near + (sent,))
-            home = exchange(home.reshape(NY, half, wide), "y")
-        table_sum = sent.astype(F32) + lax.ppermute(sent, "z", [(i, i ^ bit) for i in range(NZ)]).astype(F32)
-        sent = table_sum.astype(BF)
+    beside = lambda a, bit: lax.ppermute(a, "z", [(i, i ^ bit) for i in range(NZ)])
+    sent = (sent.astype(F32) + beside(sent, 1).astype(F32)).astype(BF)
+    sent = (sent.astype(F32) + beside(sent, 2).astype(F32)).astype(BF)
+    home = jax.ShapeDtypeStruct(away.shape, BF)
+    home = call(home_body, at, (stay, swap(away, "xl")), home, head_near + (sent,))
+    table_sum = call(add_body, at, (sent, beside(sent, 4)), jax.ShapeDtypeStruct(sent.shape, F32), (home,))
+    home = exchange(home.reshape(NY, half, wide), "y")
     table_sum = table_sum[0] + swap(table_sum[1], "xl")
     table_sum = call(
-        add_body, at, (table_sum, swap(table_sum, "xh")), jax.ShapeDtypeStruct(table_sum.shape, F32), (home,)
+        add_body, at, (table_sum, swap(table_sum, "xh")), jax.ShapeDtypeStruct(table_sum.shape, F32), (home, wg_other)
     )
     table_all = spread(table_sum, "y", NY).reshape(NC, 2, strategies // NC, wide)
-    rest = jax.ShapeDtypeStruct(table_all.shape[1:], F32)
-    rest = swap(call(take_body, (1 - c).reshape(1).astype(jnp.int32), (table_all,), rest, (wg_other,)), "c")
-    table_sum = in_order(c, pick(table_all, c, 0), rest, 1)
-    table_sum = table_sum.reshape(2, strategies, wide).transpose(1, 0, 2).reshape(strategies, cols)
-    table_grad = jnp.dot(mixing.T, table_sum, precision=HIGHEST) * grad_scale
+    rest = swap(pick(table_all, 1 - c, 0), "c")
+    table_full = in_order(c, pick(table_all, c, 0), rest, 1)
+    table_full = table_full.reshape(2, strategies, wide).transpose(1, 0, 2).reshape(strategies, cols)
+    table_grad = jnp.dot(mixing.T, table_full, precision=HIGHEST) * grad_scale
 
     parts = home.reshape(NC, 2, half, wide)
-    back = swap(pick(parts, 1 - c, 0), "c")
+    back = jax.ShapeDtypeStruct(parts.shape[1:], BF)
+    back = swap(call(take_body, (1 - c).reshape(1).astype(jnp.int32), (parts,), back, (table_sum,)), "c")
     proj = in_order(c, pick(parts, c, 0), back, 1).reshape(2, rows, wide)
     gating = 1.0 + rows_of(members(ids, strategies), table)
     proj = jnp.concatenate([proj[0], proj[1]], axis=1).astype(F32)

time: 170 us -> 170 us (level)
  waiting for transfers between devices: 48.3 us -> 43.2 us
  starting transfers between devices: 51 us -> 56 us
    all_to_all x3, waiting for transfers between devices: 16 us -> 11.3 us  [exchange(): return lax.all_to_all(a, axis, 0, 0, tiled=True)]
    ppermute x15, starting transfers between devices: 22 us -> 25.4 us  [swap(): return lax.ppermute(a, axis, [(0, 1), (1, 0)])]
    unnamed x26, local copies, waits for them, and re-layouts: 7.05 us -> 9.21 us
    pallas_call x12 -> x13, Pallas kernels: 28.8 us -> 28.4 us  [call(): pl.pallas_call(lambda *refs: body(*refs[:count], *refs[count + len(after)...]
  transfers between devices with their start and end apart: 31 -> 31, of which waited for: 12 -> 12; matrix products, arithmetic and copies ran while one was open for 10% -> 8% of each run, Pallas kernels for 17% -> 13%
where the time goes in v8:
time: 170 us; the launch traced here: 169 us
  starting transfers between devices  56 us (33%)
  waiting for transfers between devices  43.2 us (25%)
  Pallas kernels  28.4 us (17%)
  local copies, waits for them, and re-layouts  18.3 us (11%)
  between operations  14.5 us (9%)
  other arithmetic  4.97 us (3%)
  matrix products  3.25 us (2%)
    pallas_call x13, Pallas kernels, call(): pl.pallas_call(lambda *refs: body(*refs[:count], *refs[count + len(after)...  28.4 us
    ppermute x15, starting transfers between devices, swap(): return lax.ppermute(a, axis, [(0, 1), (1, 0)])  25.4 us
    ppermute x8, waiting for transfers between devices, turn(): return lax.ppermute(a, 'y', [(i, (i + k) % NY) for i in range(NY)])  14.1 us
    all_to_all x3, starting transfers between devices, exchange(): return lax.all_to_all(a, axis, 0, 0, tiled=True)  11.9 us
    all_to_all x3, waiting for transfers between devices, exchange(): return lax.all_to_all(a, axis, 0, 0, tiled=True)  11.3 us
    ppermute x8, starting transfers between devices, turn(): return lax.ppermute(a, 'y', [(i, (i + k) % NY) for i in range(NY)])  11.1 us
    unnamed x26, local copies, waits for them, and re-layouts  9.21 us
    ppermute x3, waiting for transfers between devices, on_device(): lax.ppermute(a, 'z', [(i, i ^ bit) for i in range(NZ)])  9.18 us
  transfers between devices with their start and end apart: 31, of which 12 were waited for; matrix products, arithmetic and copies ran while one was open for 8% of the time, Pallas kernels for 13%

profile of v8, /device:TPU:1, one launch (start us, length us, event | category | flops | bytes accessed | tf_op | source)
XLA Modules:
  0.0 168.7 jit_solution(6538071563349166033)
XLA Ops:
  8.3 3.3 %collective-permute-start.5 = (bf16[192,1024]{1,0:T(8,128)(2,1)S(1)}, bf16[192,1024]{1,0:T(8,128)(2,1)S(1)}, u32[]{:S(2)}, u32[]{:S(2)}) collective-permute-start(bf16[192,1024]{1,0:T(8,128)(2,1)S(1)} %dynamic-slice_bitcast_fusion.1), channel_id=1, source_target_pairs={{0,1},{1,0},{2,3},{3,2},{4,5},{5,4},{6,7},{7,6},{8,9},{9,8},{10,11... | collective-permute-start | bytes 1179656 | tf_op jit(solution)/shard_map/ppermute | solution.py:17
  12.7 5.7 %collective-permute-done.4.refs_2_ = bf16[64,1024]{1,0:T(8,128)(2,1)S(1)} collective-permute-done((bf16[64,1024]{1,0:T(8,128)(2,1)}, bf16[64,1024]{1,0:T(8,128)(2,1)S(1)}, u32[]{:S(2)}, u32[]{:S(2)}) %collective-permute-start.4) | collective-permute-done | bytes 131104 | tf_op jit(solution)/shard_map/ppermute | solution.py:17
  21.4 4.2 %all-to-all-start = ((bf16[4,208,512]{2,1,0:T(8,128)(2,1)}), bf16[4,208,512]{2,1,0:T(8,128)(2,1)}, u32[]{:S(2)}, u32[]{:S(2)}) async-start(bf16[4,208,512]{2,1,0:T(8,128)(2,1)} %pad_maximum_fusion), calls=%async_computation | async-start | bytes 1703936 | tf_op jit(solution)/shard_map/all_to_all | solution.py:21
  29.9 8.0 %all-to-all-done.refs_1_.refs_4_ = bf16[4,208,512]{2,1,0:T(8,128)(2,1)} async-done(((bf16[4,208,512]{2,1,0:T(8,128)(2,1)}), bf16[4,208,512]{2,1,0:T(8,128)(2,1)}, u32[]{:S(2)}, u32[]{:S(2)}) %all-to-all-start) | async-done | bytes 852000 | tf_op jit(solution)/shard_map/all_to_all | solution.py:21
  42.3 12.1 %collective-permute-done = bf16[384,1024]{1,0:T(8,128)(2,1)} collective-permute-done((bf16[384,1024]{1,0:T(8,128)(2,1)}, bf16[384,1024]{1,0:T(8,128)(2,1)}, u32[]{:S(2)}, u32[]{:S(2)}) %collective-permute-start) | collective-permute-done | bytes 786464 | tf_op jit(solution)/shard_map/ppermute | solution.py:29
  56.6 2.7 %collective-permute-start.3 = (bf16[384,512]{1,0:T(8,128)(2,1)S(1)}, bf16[384,512]{1,0:T(8,128)(2,1)S(1)}, u32[]{:S(2)}, u32[]{:S(2)}) collective-permute-start(bf16[384,512]{1,0:T(8,128)(2,1)S(1)} %slice.43), channel_id=1, source_target_pairs={{0,96},{32,0},{64,32},{96,64},{1,97},{33,1},{65,33},{97,65},{2,98}... | collective-permute-start | bytes 1179656 | tf_op jit(solution)/shard_map/ppermute | solution.py:29
  59.3 2.8 %shard_map.105.refs_4_.refs_1_ = bf16[768,512]{1,0:T(8,128)(2,1)} custom-call(s32[2]{0:T(128)S(1)} %pad_add_fusion.1.refs_0_, bf16[4,208,512]{2,1,0:T(8,128)(2,1)} %all-to-all-done.refs_1_.refs_4_, f32[64,512]{1,0:T(8,128)S(1)} %shard_map.103.refs_2_), custom_call_target="tpu_custom_call" | custom-call | flops 1048576 | bytes 1024 | tf_op jit(solution)/shard_map/pallas_call | solution.py:61
  62.2 2.3 %collective-permute-start.10 = (bf16[768,512]{1,0:T(8,128)(2,1)}, bf16[768,512]{1,0:T(8,128)(2,1)}, u32[]{:S(2)}, u32[]{:S(2)}) collective-permute-start(bf16[768,512]{1,0:T(8,128)(2,1)} %shard_map.105.refs_4_.refs_1_), channel_id=1, source_target_pairs={{0,1},{1,0},{2,3},{3,2},{4,5},{5,4},{6,7},{7,6},{8,9},{9,8},{10,11... | collective-permute-start | bytes 2359304 | tf_op jit(solution)/shard_map/ppermute | solution.py:17
  64.5 2.9 %shard_map.104.refs_3_.refs_2_ = bf16[768,512]{1,0:T(8,128)(2,1)} custom-call(s32[2]{0:T(128)S(1)} %pad_add_fusion.1.refs_0_, bf16[4,208,512]{2,1,0:T(8,128)(2,1)} %collective-permute-done.6.refs_1_.refs_5_, f32[64,512]{1,0:T(8,128)S(1)} %collective-permute-done.8.refs_2_), custom_call_target="tpu_custom_call" | custom-call | flops 1048576 | bytes 1024 | tf_op jit(solution)/shard_map/pallas_call | solution.py:61
  73.3 5.3 %shard_map.107.refs_6_ = bf16[2,512,1024]{2,1,0:T(8,128)(2,1)S(1)} custom-call(s32[2]{0:T(128)S(1)} %pad_add_fusion.refs_0_, bf16[768,512]{1,0:T(8,128)(2,1)} %shard_map.105.refs_4_.refs_1_, bf16[768,512]{1,0:T(8,128)(2,1)} %shard_map.104.refs_3_.refs_2_, bf16[768,512]{1,0:T(8,128)(2,1)} %collective-permute-done.10.refs_3_, ...), custom_call_target="tpu_custom_call" | custom-call | flops 1048576 | bytes 1024 | tf_op jit(solution)/shard_map/pallas_call | solution.py:61
  85.0 5.3 %shard_map.108 = bf16[4,2,192,1024]{3,2,1,0:T(8,128)(2,1)S(1)} custom-call(s32[2]{0:T(128)S(1)} %pad_add_fusion.refs_0_, bf16[768,512]{1,0:T(8,128)(2,1)} %shard_map.105.refs_4_.refs_1_, bf16[768,512]{1,0:T(8,128)(2,1)} %shard_map.104.refs_3_.refs_2_, bf16[768,512]{1,0:T(8,128)(2,1)} %collective-permute-done.10.refs_3_, ...), custom_call_target="tpu_custom_call" | custom-call | flops 1048576 | bytes 1024 | tf_op jit(solution)/shard_map/pallas_call | solution.py:61
  90.5 2.7 %collective-permute-start.14 = (bf16[384,512]{1,0:T(8,128)(2,1)S(1)}, bf16[384,512]{1,0:T(8,128)(2,1)S(1)}, u32[]{:S(2)}, u32[]{:S(2)}) collective-permute-start(bf16[384,512]{1,0:T(8,128)(2,1)S(1)} %get-tuple-element.20), channel_id=1, source_target_pairs={{0,96},{32,0},{64,32},{96,64},{1,97},{33,1},{65,33},{97,65},{2,98}... | collective-permute-start | bytes 1179656 | tf_op jit(solution)/shard_map/ppermute | solution.py:29
  93.2 5.9 %shard_map.109 = (bf16[768,512]{1,0:T(8,128)(2,1)S(1)}, f32[768,512]{1,0:T(8,128)S(1)}, f32[2,64,512]{2,1,0:T(8,128)S(1)}) custom-call(s32[2]{0:T(128)S(1)} %pad_add_fusion.refs_0_, bf16[4,2,192,1024]{3,2,1,0:T(8,128)(2,1)S(1)} %bitcast.111, bf16[2,512,1024]{2,1,0:T(8,128)(2,1)S(1)} %copy-done.4, bf16[2,768,512]{2,1,0:T(8,128)(2,1)S(1)} %collective-permute-done.9.refs_3_, ...), custom_call_target="tpu_custom_call" | custom-call | flops 1048576 | bytes 1024 | tf_op jit(solution)/shard_map/pallas_call | solution.py:61
  102.8 2.7 %collective-permute-start.17 = (bf16[384,1024]{1,0:T(8,128)(2,1)S(1)}, bf16[384,1024]{1,0:T(8,128)(2,1)S(1)}, u32[]{:S(2)}, u32[]{:S(2)}) collective-permute-start(bf16[384,1024]{1,0:T(8,128)(2,1)S(1)} %get-tuple-element.13), channel_id=1, source_target_pairs={{0,96},{32,0},{64,32},{96,64},{1,97},{33,1},{65,33},{97,65},{2,98}... | collective-permute-start | bytes 2359304 | tf_op jit(solution)/shard_map/ppermute | solution.py:29
  105.5 4.5 %collective-permute-done.18 = bf16[2,32,512]{2,1,0:T(8,128)(2,1)S(1)} collective-permute-done((bf16[2,32,512]{2,1,0:T(8,128)(2,1)S(1)}, bf16[2,32,512]{2,1,0:T(8,128)(2,1)S(1)}, u32[]{:S(2)}, u32[]{:S(2)}) %collective-permute-start.18) | collective-permute-done | bytes 65568 | tf_op jit(solution)/shard_map/ppermute | solution.py:275
  111.7 4.7 %collective-permute-done.19 = bf16[2,32,512]{2,1,0:T(8,128)(2,1)S(1)} collective-permute-done((bf16[2,32,512]{2,1,0:T(8,128)(2,1)S(1)}, bf16[2,32,512]{2,1,0:T(8,128)(2,1)S(1)}, u32[]{:S(2)}, u32[]{:S(2)}) %collective-permute-start.19) | collective-permute-done | bytes 65568 | tf_op jit(solution)/shard_map/ppermute | solution.py:275
  116.4 5.9 %collective-permute-start.20 = (bf16[2,32,512]{2,1,0:T(8,128)(2,1)S(1)}, bf16[2,32,512]{2,1,0:T(8,128)(2,1)S(1)}, u32[]{:S(2)}, u32[]{:S(2)}) collective-permute-start(bf16[2,32,512]{2,1,0:T(8,128)(2,1)S(1)} %add_convert_fusion.refs_5_.refs_1_), channel_id=1, source_target_pairs={{0,16},{4,20},{8,24},{12,28},{16,0},{20,4},{24,8},{28,12},{1,17},{... | collective-permute-start | bytes 196616 | tf_op jit(solution)/shard_map/ppermute | solution.py:275
  125.6 3.5 %all-to-all-start.1 = ((bf16[4,192,512]{2,1,0:T(8,128)(2,1)}), bf16[4,192,512]{2,1,0:T(8,128)(2,1)S(1)}, u32[]{:S(2)}, u32[]{:S(2)}) async-start(bf16[4,192,512]{2,1,0:T(8,128)(2,1)} %bitcast.26), calls=%async_computation.1 | async-start | bytes 1572864 | tf_op jit(solution)/shard_map/all_to_all | solution.py:21
  129.1 2.8 %collective-permute-start.22 = (f32[32,512]{1,0:T(8,128)S(1)}, f32[32,512]{1,0:T(8,128)S(1)}, u32[]{:S(2)}, u32[]{:S(2)}) collective-permute-start(f32[32,512]{1,0:T(8,128)S(1)} %fusion.14.refs_1_), channel_id=1, source_target_pairs={{0,128},{128,0},{1,129},{129,1},{2,130},{130,2},{3,131},{131,3},{4... | collective-permute-start | bytes 196616 | tf_op jit(solution)/shard_map/ppermute | solution.py:17
  134.2 3.2 %all-to-all-done.1.refs_3_ = bf16[4,192,512]{2,1,0:T(8,128)(2,1)S(1)} async-done(((bf16[4,192,512]{2,1,0:T(8,128)(2,1)}), bf16[4,192,512]{2,1,0:T(8,128)(2,1)S(1)}, u32[]{:S(2)}, u32[]{:S(2)}) %all-to-all-start.1) | async-done | bytes 786464 | tf_op jit(solution)/shard_map/all_to_all | solution.py:21
  139.5 4.2 %all-to-all-start.2 = ((f32[4,32,512]{2,1,0:T(8,128)}), f32[4,32,512]{2,1,0:T(8,128)S(1)}, u32[]{:S(2)}, u32[]{:S(2)}) async-start(f32[4,32,512]{2,1,0:T(8,128)} %broadcast_in_dim.34), calls=%async_computation.3 | async-start | bytes 524288 | tf_op jit(solution)/shard_map/all_to_all | solution.py:21
  143.7 2.5 %fusion.1 = bf16[384,1024]{1,0:T(8,128)(2,1)} fusion(bf16[384,1024]{1,0:T(8,128)(2,1)S(1)} %collective-permute-done.17.refs_4_, bf16[384,1024]{1,0:T(8,128)(2,1)S(1)} %collective-permute-done.16.refs_3_, bf16[4,384,1024]{2,1,0:T(8,128)(2,1)} %bitcast.115, s32[]{:T(128)S(6)} %select_n.128), kind=kLoop, calls=%fused_computation.2 | loop fusion | flops 2359296 | bytes 3145732 | tf_op jit(solution)/shard_map/convert_element_type | solution.py:303
  146.2 6.2 %collective-permute-start.24 = (bf16[2,192,512]{2,1,0:T(8,128)(2,1)S(1)}, bf16[2,192,512]{2,1,0:T(8,128)(2,1)S(1)}, u32[]{:S(2)}, u32[]{:S(2)}) collective-permute-start(bf16[2,192,512]{2,1,0:T(8,128)(2,1)S(1)} %shard_map.114), channel_id=1, source_target_pairs={{0,1},{1,0},{2,3},{3,2},{4,5},{5,4},{6,7},{7,6},{8,9},{9,8},{10,11... | collective-permute-start | bytes 1179656 | tf_op jit(solution)/shard_map/ppermute | solution.py:17
  152.5 4.2 %collective-permute-start.25 = (f32[2,32,512]{2,1,0:T(8,128)S(1)}, f32[2,32,512]{2,1,0:T(8,128)S(1)}, u32[]{:S(2)}, u32[]{:S(2)}) collective-permute-start(f32[2,32,512]{2,1,0:T(8,128)S(1)} %dynamic-slice_bitcast_fusion.2), channel_id=1, source_target_pairs={{0,1},{1,0},{2,3},{3,2},{4,5},{5,4},{6,7},{7,6},{8,9},{9,8},{10,11... | collective-permute-start | bytes 393224 | tf_op jit(solution)/shard_map/ppermute | solution.py:17
  (122 shorter events, 46.5 us)
Async XLA Ops:
  7.2 62.7 %all-gather.2.cloned.1.call-start = ((), (), s32[]{:S(2)}) async-start(), calls=%async_computation.4 | async-start | bytes 2359296 | tf_op jit(solution)/shard_map/all_gather | solution.py:230
  8.3 10.1 %collective-permute-start.5 = (bf16[192,1024]{1,0:T(8,128)(2,1)S(1)}, bf16[192,1024]{1,0:T(8,128)(2,1)S(1)}, u32[]{:S(2)}, u32[]{:S(2)}) collective-permute-start(bf16[192,1024]{1,0:T(8,128)(2,1)S(1)} %dynamic-slice_bitcast_fusion.1), channel_id=1, source_target_pairs={{0,1},{1,0},{2,3},{3,2},{4,5},{5,4},{6,7},{7,6},{8,9},{9,8},{10,11... | collective-permute-start | bytes 1179656 | tf_op jit(solution)/shard_map/ppermute | solution.py:17
  11.7 6.8 %collective-permute-start.4 = (bf16[64,1024]{1,0:T(8,128)(2,1)}, bf16[64,1024]{1,0:T(8,128)(2,1)S(1)}, u32[]{:S(2)}, u32[]{:S(2)}) collective-permute-start(bf16[64,1024]{1,0:T(8,128)(2,1)} %refs_1_.1), channel_id=1, source_target_pairs={{0,128},{128,0},{1,129},{129,1},{2,130},{130,2},{3,131},{131,3},{4... | collective-permute-start | bytes 393224 | tf_op jit(solution)/shard_map/ppermute | solution.py:17
  21.4 16.5 %all-to-all-start = ((bf16[4,208,512]{2,1,0:T(8,128)(2,1)}), bf16[4,208,512]{2,1,0:T(8,128)(2,1)}, u32[]{:S(2)}, u32[]{:S(2)}) async-start(bf16[4,208,512]{2,1,0:T(8,128)(2,1)} %pad_maximum_fusion), calls=%async_computation | async-start | bytes 1703936 | tf_op jit(solution)/shard_map/all_to_all | solution.py:21
  25.6 106.3 %reduce-scatter.2.cloned.1.call-start = ((), (), s32[]{:S(2)}) async-start(), calls=%async_computation.5 | async-start | bytes 2359296 | tf_op jit(solution)/shard_map/reduce_scatter | solution.py:268
  25.7 28.7 %collective-permute-start = (bf16[384,1024]{1,0:T(8,128)(2,1)}, bf16[384,1024]{1,0:T(8,128)(2,1)}, u32[]{:S(2)}, u32[]{:S(2)}) collective-permute-start(bf16[384,1024]{1,0:T(8,128)(2,1)} %bitcast.4), channel_id=1, source_target_pairs={{0,32},{32,64},{64,96},{96,0},{1,33},{33,65},{65,97},{97,1},{2,34}... | collective-permute-start | bytes 2359304 | tf_op jit(solution)/shard_map/ppermute | solution.py:29
  27.1 28.5 %collective-permute-start.1 = (bf16[384,1024]{1,0:T(8,128)(2,1)}, bf16[384,1024]{1,0:T(8,128)(2,1)}, u32[]{:S(2)}, u32[]{:S(2)}) collective-permute-start(bf16[384,1024]{1,0:T(8,128)(2,1)} %bitcast.4), channel_id=1, source_target_pairs={{0,96},{32,0},{64,32},{96,64},{1,97},{33,1},{65,33},{97,65},{2,98}... | collective-permute-start | bytes 2359304 | tf_op jit(solution)/shard_map/ppermute | solution.py:29
  28.4 9.9 %collective-permute-start.7 = (bf16[64,1024]{1,0:T(8,128)(2,1)S(1)}, bf16[64,1024]{1,0:T(8,128)(2,1)S(1)}, u32[]{:S(2)}, u32[]{:S(2)}) collective-permute-start(bf16[64,1024]{1,0:T(8,128)(2,1)S(1)} %copy-done.6), channel_id=1, source_target_pairs={{0,1},{1,0},{2,3},{3,2},{4,5},{5,4},{6,7},{7,6},{8,9},{9,8},{10,11... | collective-permute-start | bytes 393224 | tf_op jit(solution)/shard_map/ppermute | solution.py:17
  37.9 26.6 %collective-permute-start.6 = (bf16[4,208,512]{2,1,0:T(8,128)(2,1)}, bf16[4,208,512]{2,1,0:T(8,128)(2,1)}, u32[]{:S(2)}, u32[]{:S(2)}) collective-permute-start(bf16[4,208,512]{2,1,0:T(8,128)(2,1)} %all-to-all-done.refs_1_.refs_4_), channel_id=1, source_target_pairs={{0,2},{2,0},{1,3},{3,1},{4,6},{6,4},{5,7},{7,5},{8,10},{10,8},{9,1... | collective-permute-start | bytes 2555912 | tf_op jit(solution)/shard_map/ppermute | solution.py:17
  39.1 25.4 %collective-permute-start.8 = (f32[64,512]{1,0:T(8,128)S(1)}, f32[64,512]{1,0:T(8,128)S(1)}, u32[]{:S(2)}, u32[]{:S(2)}) collective-permute-start(f32[64,512]{1,0:T(8,128)S(1)} %shard_map.103.refs_2_), channel_id=1, source_target_pairs={{0,2},{2,0},{1,3},{3,1},{4,6},{6,4},{5,7},{7,5},{8,10},{10,8},{9,1... | collective-permute-start | bytes 393224 | tf_op jit(solution)/shard_map/ppermute | solution.py:17
  55.5 14.3 %collective-permute-start.2 = (bf16[384,512]{1,0:T(8,128)(2,1)S(1)}, bf16[384,512]{1,0:T(8,128)(2,1)S(1)}, u32[]{:S(2)}, u32[]{:S(2)}) collective-permute-start(bf16[384,512]{1,0:T(8,128)(2,1)S(1)} %slice.42), channel_id=1, source_target_pairs={{0,32},{32,64},{64,96},{96,0},{1,33},{33,65},{65,97},{97,1},{2,34}... | collective-permute-start | bytes 1179656 | tf_op jit(solution)/shard_map/ppermute | solution.py:29
  56.6 13.2 %collective-permute-start.3 = (bf16[384,512]{1,0:T(8,128)(2,1)S(1)}, bf16[384,512]{1,0:T(8,128)(2,1)S(1)}, u32[]{:S(2)}, u32[]{:S(2)}) collective-permute-start(bf16[384,512]{1,0:T(8,128)(2,1)S(1)} %slice.43), channel_id=1, source_target_pairs={{0,96},{32,0},{64,32},{96,64},{1,97},{33,1},{65,33},{97,65},{2,98}... | collective-permute-start | bytes 1179656 | tf_op jit(solution)/shard_map/ppermute | solution.py:29
  62.2 11.2 %collective-permute-start.10 = (bf16[768,512]{1,0:T(8,128)(2,1)}, bf16[768,512]{1,0:T(8,128)(2,1)}, u32[]{:S(2)}, u32[]{:S(2)}) collective-permute-start(bf16[768,512]{1,0:T(8,128)(2,1)} %shard_map.105.refs_4_.refs_1_), channel_id=1, source_target_pairs={{0,1},{1,0},{2,3},{3,2},{4,5},{5,4},{6,7},{7,6},{8,9},{9,8},{10,11... | collective-permute-start | bytes 2359304 | tf_op jit(solution)/shard_map/ppermute | solution.py:17
  81.2 11.9 %collective-permute-start.9 = (bf16[2,768,512]{2,1,0:T(8,128)(2,1)}, bf16[2,768,512]{2,1,0:T(8,128)(2,1)S(1)}, u32[]{:S(2)}, u32[]{:S(2)}) collective-permute-start(bf16[2,768,512]{2,1,0:T(8,128)(2,1)} %copy-done.5), channel_id=1, source_target_pairs={{0,1},{1,0},{2,3},{3,2},{4,5},{5,4},{6,7},{7,6},{8,9},{9,8},{10,11... | collective-permute-start | bytes 4718600 | tf_op jit(solution)/shard_map/ppermute | solution.py:17
  90.4 12.1 %collective-permute-start.13 = (bf16[384,512]{1,0:T(8,128)(2,1)S(1)}, bf16[384,512]{1,0:T(8,128)(2,1)S(1)}, u32[]{:S(2)}, u32[]{:S(2)}) collective-permute-start(bf16[384,512]{1,0:T(8,128)(2,1)S(1)} %get-tuple-element.21), channel_id=1, source_target_pairs={{0,32},{32,64},{64,96},{96,0},{1,33},{33,65},{65,97},{97,1},{2,34}... | collective-permute-start | bytes 1179656 | tf_op jit(solution)/shard_map/ppermute | solution.py:29
  90.5 12.0 %collective-permute-start.14 = (bf16[384,512]{1,0:T(8,128)(2,1)S(1)}, bf16[384,512]{1,0:T(8,128)(2,1)S(1)}, u32[]{:S(2)}, u32[]{:S(2)}) collective-permute-start(bf16[384,512]{1,0:T(8,128)(2,1)S(1)} %get-tuple-element.20), channel_id=1, source_target_pairs={{0,96},{32,0},{64,32},{96,64},{1,97},{33,1},{65,33},{97,65},{2,98}... | collective-permute-start | bytes 1179656 | tf_op jit(solution)/shard_map/ppermute | solution.py:29
  99.8 22.5 %collective-permute-start.12 = (bf16[768,512]{1,0:T(8,128)(2,1)S(1)}, bf16[768,512]{1,0:T(8,128)(2,1)S(1)}, u32[]{:S(2)}, u32[]{:S(2)}) collective-permute-start(bf16[768,512]{1,0:T(8,128)(2,1)S(1)} %get-tuple-element.10), channel_id=1, source_target_pairs={{0,2},{2,0},{1,3},{3,1},{4,6},{6,4},{5,7},{7,5},{8,10},{10,8},{9,1... | collective-permute-start | bytes 2359304 | tf_op jit(solution)/shard_map/ppermute | solution.py:17
  102.7 19.8 %collective-permute-start.16 = (bf16[384,1024]{1,0:T(8,128)(2,1)S(1)}, bf16[384,1024]{1,0:T(8,128)(2,1)S(1)}, u32[]{:S(2)}, u32[]{:S(2)}) collective-permute-start(bf16[384,1024]{1,0:T(8,128)(2,1)S(1)} %get-tuple-element.12), channel_id=1, source_target_pairs={{0,32},{32,64},{64,96},{96,0},{1,33},{33,65},{65,97},{97,1},{2,34}... | collective-permute-start | bytes 2359304 | tf_op jit(solution)/shard_map/ppermute | solution.py:29
  102.8 19.7 %collective-permute-start.17 = (bf16[384,1024]{1,0:T(8,128)(2,1)S(1)}, bf16[384,1024]{1,0:T(8,128)(2,1)S(1)}, u32[]{:S(2)}, u32[]{:S(2)}) collective-permute-start(bf16[384,1024]{1,0:T(8,128)(2,1)S(1)} %get-tuple-element.13), channel_id=1, source_target_pairs={{0,96},{32,0},{64,32},{96,64},{1,97},{33,1},{65,33},{97,65},{2,98}... | collective-permute-start | bytes 2359304 | tf_op jit(solution)/shard_map/ppermute | solution.py:29
  110.1 6.3 %collective-permute-start.19 = (bf16[2,32,512]{2,1,0:T(8,128)(2,1)S(1)}, bf16[2,32,512]{2,1,0:T(8,128)(2,1)S(1)}, u32[]{:S(2)}, u32[]{:S(2)}) collective-permute-start(bf16[2,32,512]{2,1,0:T(8,128)(2,1)S(1)} %add_convert_fusion.1), channel_id=1, source_target_pairs={{0,8},{4,12},{8,0},{12,4},{16,24},{20,28},{24,16},{28,20},{1,9},{5... | collective-permute-start | bytes 196616 | tf_op jit(solution)/shard_map/ppermute | solution.py:275
  116.4 7.7 %collective-permute-start.20 = (bf16[2,32,512]{2,1,0:T(8,128)(2,1)S(1)}, bf16[2,32,512]{2,1,0:T(8,128)(2,1)S(1)}, u32[]{:S(2)}, u32[]{:S(2)}) collective-permute-start(bf16[2,32,512]{2,1,0:T(8,128)(2,1)S(1)} %add_convert_fusion.refs_5_.refs_1_), channel_id=1, source_target_pairs={{0,16},{4,20},{8,24},{12,28},{16,0},{20,4},{24,8},{28,12},{1,17},{... | collective-permute-start | bytes 196616 | tf_op jit(solution)/shard_map/ppermute | solution.py:275
  125.6 11.8 %all-to-all-start.1 = ((bf16[4,192,512]{2,1,0:T(8,128)(2,1)}), bf16[4,192,512]{2,1,0:T(8,128)(2,1)S(1)}, u32[]{:S(2)}, u32[]{:S(2)}) async-start(bf16[4,192,512]{2,1,0:T(8,128)(2,1)} %bitcast.26), calls=%async_computation.1 | async-start | bytes 1572864 | tf_op jit(solution)/shard_map/all_to_all | solution.py:21
  139.5 12.9 %all-to-all-start.2 = ((f32[4,32,512]{2,1,0:T(8,128)}), f32[4,32,512]{2,1,0:T(8,128)S(1)}, u32[]{:S(2)}, u32[]{:S(2)}) async-start(f32[4,32,512]{2,1,0:T(8,128)} %broadcast_in_dim.34), calls=%async_computation.3 | async-start | bytes 524288 | tf_op jit(solution)/shard_map/all_to_all | solution.py:21
  146.2 12.6 %collective-permute-start.24 = (bf16[2,192,512]{2,1,0:T(8,128)(2,1)S(1)}, bf16[2,192,512]{2,1,0:T(8,128)(2,1)S(1)}, u32[]{:S(2)}, u32[]{:S(2)}) collective-permute-start(bf16[2,192,512]{2,1,0:T(8,128)(2,1)S(1)} %shard_map.114), channel_id=1, source_target_pairs={{0,1},{1,0},{2,3},{3,2},{4,5},{5,4},{6,7},{7,6},{8,9},{9,8},{10,11... | collective-permute-start | bytes 1179656 | tf_op jit(solution)/shard_map/ppermute | solution.py:17
  (20 other events, 118.2 us)
Sparse Core Ops, SparseCore 0:
  20.2 38.9 all-gather.1
  81.3 39.2 reduce-scatter.1

commit v9 on v8

--- a/solution.py
+++ b/solution.py
@@ -54,6 +54,9 @@
 VMEM = pl.BlockSpec(memory_space=pltpu.VMEM)
 SMEM = pl.BlockSpec(memory_space=pltpu.SMEM)
 STEP = 256
+
+
+TOKEN = jax.ShapeDtypeStruct((8, 128), F32)
 
 
 def call(body, at, operands, out_shape, after=()):
@@ -66,6 +69,14 @@
         compiler_params=pltpu.CompilerParams(vmem_limit_bytes=16 * 2**20),
         cost_estimate=pl.CostEstimate(flops=2**20, bytes_accessed=2**10, transcendentals=0),
     )(at, *operands, *after)
+
+
+def call_token(body, at, operands, out_shape, after=()):
+    def both(*refs):
+        body(*refs[:-1])
+        refs[-1][...] = jnp.zeros(refs[-1].shape, F32)
+
+    return call(both, at, operands, (out_shape, TOKEN), after)
 
 
 def pass_body(at, a, from_below, from_above, up, down):
@@ -241,7 +252,7 @@
     pieces = (near, far, swap(near, "c"), swap(far, "c"))
     at = jnp.stack([xl, c]).astype(jnp.int32)
 
-    give = call(
+    give, given = call_token(
         project_body,
         (1 - c).reshape(1).astype(jnp.int32),
         (ho_y, weight),
@@ -249,8 +260,10 @@
         (far, near),
     )
     theirs = swap(give, "c")
-    wg = call(weight_body, at, pieces + (ho_y,), jax.ShapeDtypeStruct((XH, NZ * wr, cols), BF), (give,))
-    head_grad = call(head_body, at, pieces + (weight,), jax.ShapeDtypeStruct((NY, NC, half, cols), BF), (wg,))
+    wg, weighed = call_token(weight_body, at, pieces + (ho_y,), jax.ShapeDtypeStruct((XH, NZ * wr, cols), BF), (given,))
+    head_grad, headed = call_token(
+        head_body, at, pieces + (weight,), jax.ShapeDtypeStruct((NY, NC, half, cols), BF), (weighed,)
+    )
     head_grad = head_grad.reshape(NY, rows, cols)
     head_far = far_blocks(head_grad, y)
     away, stay, table_part = call(
@@ -262,7 +275,7 @@
             jax.ShapeDtypeStruct((NY * half, wide), F32),
             jax.ShapeDtypeStruct((XL, strategies, wide), F32),
         ),
-        (head_grad,),
+        (headed,),
     )
 
     wg_part = lax.psum_scatter(wg, "z", scatter_dimension=1, tiled=True)

time: 170 us -> 168 us (0.988)
  starting transfers between devices: 56 us -> 58.3 us
  waiting for transfers between devices: 43.2 us -> 41.1 us
    ppermute x3, waiting for transfers between devices: 9.18 us -> 7.47 us  [on_device(): lax.ppermute(a, 'z', [(i, i ^ bit) for i in range(NZ)])]
where the time goes in v9:
time: 168 us
  starting transfers between devices  58.3 us (35%)
  waiting for transfers between devices  41.1 us (24%)
  Pallas kernels  28.6 us (17%)
  local copies, waits for them, and re-layouts  16.7 us (10%)
  between operations  14.5 us (9%)
  other arithmetic  4.97 us (3%)
  matrix products  3.25 us (2%)
    pallas_call x13, Pallas kernels, call(): pl.pallas_call(lambda *refs: body(*refs[:count], *refs[count + len(after)...  28.6 us
    ppermute x15, starting transfers between devices, swap(): return lax.ppermute(a, axis, [(0, 1), (1, 0)])  26.4 us
    ppermute x8, waiting for transfers between devices, turn(): return lax.ppermute(a, 'y', [(i, (i + k) % NY) for i in range(NY)])  14.1 us
    all_to_all x3, starting transfers between devices, exchange(): return lax.all_to_all(a, axis, 0, 0, tiled=True)  11.9 us
    all_to_all x3, waiting for transfers between devices, exchange(): return lax.all_to_all(a, axis, 0, 0, tiled=True)  11.6 us
    ppermute x8, starting transfers between devices, turn(): return lax.ppermute(a, 'y', [(i, (i + k) % NY) for i in range(NY)])  11.1 us
    ppermute x3, starting transfers between devices, on_device(): lax.ppermute(a, 'z', [(i, i ^ bit) for i in range(NZ)])  8.88 us
    ppermute x15, waiting for transfers between devices, swap(): return lax.ppermute(a, axis, [(0, 1), (1, 0)])  7.9 us
  transfers between devices with their start and end apart: 31, of which 12 were waited for; matrix products, arithmetic and copies ran while one was open for 8% of the time, Pallas kernels for 13%

profile of v9, /device:TPU:1, one launch (start us, length us, event | category | flops | bytes accessed | tf_op | source)
XLA Modules:
  0.0 167.5 jit_solution(2859973055794316240)
XLA Ops:
  8.3 3.3 %collective-permute-start.5 = (bf16[192,1024]{1,0:T(8,128)(2,1)S(1)}, bf16[192,1024]{1,0:T(8,128)(2,1)S(1)}, u32[]{:S(2)}, u32[]{:S(2)}) collective-permute-start(bf16[192,1024]{1,0:T(8,128)(2,1)S(1)} %dynamic-slice_bitcast_fusion.1), channel_id=1, source_target_pairs={{0,1},{1,0},{2,3},{3,2},{4,5},{5,4},{6,7},{7,6},{8,9},{9,8},{10,11... | collective-permute-start | bytes 1179656 | tf_op jit(solution)/shard_map/ppermute | solution.py:17
  12.7 5.7 %collective-permute-done.4.refs_2_ = bf16[64,1024]{1,0:T(8,128)(2,1)S(1)} collective-permute-done((bf16[64,1024]{1,0:T(8,128)(2,1)}, bf16[64,1024]{1,0:T(8,128)(2,1)S(1)}, u32[]{:S(2)}, u32[]{:S(2)}) %collective-permute-start.4) | collective-permute-done | bytes 131104 | tf_op jit(solution)/shard_map/ppermute | solution.py:17
  21.4 4.2 %all-to-all-start = ((bf16[4,208,512]{2,1,0:T(8,128)(2,1)}), bf16[4,208,512]{2,1,0:T(8,128)(2,1)}, u32[]{:S(2)}, u32[]{:S(2)}) async-start(bf16[4,208,512]{2,1,0:T(8,128)(2,1)} %pad_maximum_fusion), calls=%async_computation | async-start | bytes 1703936 | tf_op jit(solution)/shard_map/all_to_all | solution.py:21
  29.9 8.0 %all-to-all-done.refs_1_.refs_4_ = bf16[4,208,512]{2,1,0:T(8,128)(2,1)} async-done(((bf16[4,208,512]{2,1,0:T(8,128)(2,1)}), bf16[4,208,512]{2,1,0:T(8,128)(2,1)}, u32[]{:S(2)}, u32[]{:S(2)}) %all-to-all-start) | async-done | bytes 852000 | tf_op jit(solution)/shard_map/all_to_all | solution.py:21
  42.3 12.1 %collective-permute-done = bf16[384,1024]{1,0:T(8,128)(2,1)} collective-permute-done((bf16[384,1024]{1,0:T(8,128)(2,1)}, bf16[384,1024]{1,0:T(8,128)(2,1)}, u32[]{:S(2)}, u32[]{:S(2)}) %collective-permute-start) | collective-permute-done | bytes 786464 | tf_op jit(solution)/shard_map/ppermute | solution.py:29
  56.6 2.7 %collective-permute-start.3 = (bf16[384,512]{1,0:T(8,128)(2,1)S(1)}, bf16[384,512]{1,0:T(8,128)(2,1)S(1)}, u32[]{:S(2)}, u32[]{:S(2)}) collective-permute-start(bf16[384,512]{1,0:T(8,128)(2,1)S(1)} %slice.43), channel_id=1, source_target_pairs={{0,96},{32,0},{64,32},{96,64},{1,97},{33,1},{65,33},{97,65},{2,98}... | collective-permute-start | bytes 1179656 | tf_op jit(solution)/shard_map/ppermute | solution.py:29
  59.4 2.8 %shard_map.105.refs_4_.refs_1_ = bf16[768,512]{1,0:T(8,128)(2,1)} custom-call(s32[2]{0:T(128)S(1)} %pad_add_fusion.1.refs_0_, bf16[4,208,512]{2,1,0:T(8,128)(2,1)} %all-to-all-done.refs_1_.refs_4_, f32[64,512]{1,0:T(8,128)S(1)} %shard_map.103.refs_2_), custom_call_target="tpu_custom_call" | custom-call | flops 1048576 | bytes 1024 | tf_op jit(solution)/shard_map/pallas_call | solution.py:64
  62.2 2.3 %collective-permute-start.10 = (bf16[768,512]{1,0:T(8,128)(2,1)}, bf16[768,512]{1,0:T(8,128)(2,1)}, u32[]{:S(2)}, u32[]{:S(2)}) collective-permute-start(bf16[768,512]{1,0:T(8,128)(2,1)} %shard_map.105.refs_4_.refs_1_), channel_id=1, source_target_pairs={{0,1},{1,0},{2,3},{3,2},{4,5},{5,4},{6,7},{7,6},{8,9},{9,8},{10,11... | collective-permute-start | bytes 2359304 | tf_op jit(solution)/shard_map/ppermute | solution.py:17
  64.5 2.8 %shard_map.104.refs_3_.refs_2_ = bf16[768,512]{1,0:T(8,128)(2,1)} custom-call(s32[2]{0:T(128)S(1)} %pad_add_fusion.1.refs_0_, bf16[4,208,512]{2,1,0:T(8,128)(2,1)} %collective-permute-done.6.refs_1_.refs_5_, f32[64,512]{1,0:T(8,128)S(1)} %collective-permute-done.8.refs_2_), custom_call_target="tpu_custom_call" | custom-call | flops 1048576 | bytes 1024 | tf_op jit(solution)/shard_map/pallas_call | solution.py:64
  74.5 5.3 %shard_map.107 = (bf16[2,512,1024]{2,1,0:T(8,128)(2,1)S(1)}, f32[8,128]{1,0:T(8,128)S(1)}) custom-call(s32[2]{0:T(128)S(1)} %pad_add_fusion.refs_0_, bf16[768,512]{1,0:T(8,128)(2,1)} %shard_map.105.refs_4_.refs_1_, bf16[768,512]{1,0:T(8,128)(2,1)} %shard_map.104.refs_3_.refs_2_, bf16[768,512]{1,0:T(8,128)(2,1)} %collective-permute-done.10.refs_3_, ...), custom_call_target="tpu_custom_call" | custom-call | flops 1048576 | bytes 1024 | tf_op jit(solution)/shard_map/pallas_call | solution.py:64
  83.4 5.3 %shard_map.108 = (bf16[4,2,192,1024]{3,2,1,0:T(8,128)(2,1)S(1)}, f32[8,128]{1,0:T(8,128)S(1)}) custom-call(s32[2]{0:T(128)S(1)} %pad_add_fusion.refs_0_, bf16[768,512]{1,0:T(8,128)(2,1)} %shard_map.105.refs_4_.refs_1_, bf16[768,512]{1,0:T(8,128)(2,1)} %shard_map.104.refs_3_.refs_2_, bf16[768,512]{1,0:T(8,128)(2,1)} %collective-permute-done.10.refs_3_, ...), custom_call_target="tpu_custom_call" | custom-call | flops 1048576 | bytes 1024 | tf_op jit(solution)/shard_map/pallas_call | solution.py:64
  88.9 2.7 %collective-permute-start.14 = (bf16[384,512]{1,0:T(8,128)(2,1)S(1)}, bf16[384,512]{1,0:T(8,128)(2,1)S(1)}, u32[]{:S(2)}, u32[]{:S(2)}) collective-permute-start(bf16[384,512]{1,0:T(8,128)(2,1)S(1)} %get-tuple-element.32), channel_id=1, source_target_pairs={{0,96},{32,0},{64,32},{96,64},{1,97},{33,1},{65,33},{97,65},{2,98}... | collective-permute-start | bytes 1179656 | tf_op jit(solution)/shard_map/ppermute | solution.py:29
  91.6 6.1 %shard_map.109 = (bf16[768,512]{1,0:T(8,128)(2,1)S(1)}, f32[768,512]{1,0:T(8,128)S(1)}, f32[2,64,512]{2,1,0:T(8,128)S(1)}) custom-call(s32[2]{0:T(128)S(1)} %pad_add_fusion.refs_0_, bf16[4,2,192,1024]{3,2,1,0:T(8,128)(2,1)S(1)} %bitcast.111, bf16[2,512,1024]{2,1,0:T(8,128)(2,1)S(1)} %copy-done.2, bf16[2,768,512]{2,1,0:T(8,128)(2,1)S(1)} %collective-permute-done.9.refs_3_, ...), custom_call_target="tpu_custom_call" | custom-call | flops 1048576 | bytes 1024 | tf_op jit(solution)/shard_map/pallas_call | solution.py:64
  101.2 2.6 %collective-permute-start.17 = (bf16[384,1024]{1,0:T(8,128)(2,1)S(1)}, bf16[384,1024]{1,0:T(8,128)(2,1)S(1)}, u32[]{:S(2)}, u32[]{:S(2)}) collective-permute-start(bf16[384,1024]{1,0:T(8,128)(2,1)S(1)} %get-tuple-element.24), channel_id=1, source_target_pairs={{0,96},{32,0},{64,32},{96,64},{1,97},{33,1},{65,33},{97,65},{2,98}... | collective-permute-start | bytes 2359304 | tf_op jit(solution)/shard_map/ppermute | solution.py:29
  103.9 4.1 %collective-permute-done.18 = bf16[2,32,512]{2,1,0:T(8,128)(2,1)S(1)} collective-permute-done((bf16[2,32,512]{2,1,0:T(8,128)(2,1)S(1)}, bf16[2,32,512]{2,1,0:T(8,128)(2,1)S(1)}, u32[]{:S(2)}, u32[]{:S(2)}) %collective-permute-start.18) | collective-permute-done | bytes 65568 | tf_op jit(solution)/shard_map/ppermute | solution.py:288
  109.4 3.3 %collective-permute-done.19 = bf16[2,32,512]{2,1,0:T(8,128)(2,1)S(1)} collective-permute-done((bf16[2,32,512]{2,1,0:T(8,128)(2,1)S(1)}, bf16[2,32,512]{2,1,0:T(8,128)(2,1)S(1)}, u32[]{:S(2)}, u32[]{:S(2)}) %collective-permute-start.19) | collective-permute-done | bytes 65568 | tf_op jit(solution)/shard_map/ppermute | solution.py:288
  112.7 7.5 %collective-permute-start.20 = (bf16[2,32,512]{2,1,0:T(8,128)(2,1)S(1)}, bf16[2,32,512]{2,1,0:T(8,128)(2,1)S(1)}, u32[]{:S(2)}, u32[]{:S(2)}) collective-permute-start(bf16[2,32,512]{2,1,0:T(8,128)(2,1)S(1)} %add_convert_fusion.refs_5_.refs_1_), channel_id=1, source_target_pairs={{0,16},{4,20},{8,24},{12,28},{16,0},{20,4},{24,8},{28,12},{1,17},{... | collective-permute-start | bytes 196616 | tf_op jit(solution)/shard_map/ppermute | solution.py:288
  124.2 3.5 %all-to-all-start.1 = ((bf16[4,192,512]{2,1,0:T(8,128)(2,1)}), bf16[4,192,512]{2,1,0:T(8,128)(2,1)S(1)}, u32[]{:S(2)}, u32[]{:S(2)}) async-start(bf16[4,192,512]{2,1,0:T(8,128)(2,1)} %bitcast.26), calls=%async_computation.1 | async-start | bytes 1572864 | tf_op jit(solution)/shard_map/all_to_all | solution.py:21
  127.7 2.5 %collective-permute-start.22 = (f32[32,512]{1,0:T(8,128)S(1)}, f32[32,512]{1,0:T(8,128)S(1)}, u32[]{:S(2)}, u32[]{:S(2)}) collective-permute-start(f32[32,512]{1,0:T(8,128)S(1)} %fusion.14.refs_1_), channel_id=1, source_target_pairs={{0,128},{128,0},{1,129},{129,1},{2,130},{130,2},{3,131},{131,3},{4... | collective-permute-start | bytes 196616 | tf_op jit(solution)/shard_map/ppermute | solution.py:17
  132.4 3.6 %all-to-all-done.1.refs_3_ = bf16[4,192,512]{2,1,0:T(8,128)(2,1)S(1)} async-done(((bf16[4,192,512]{2,1,0:T(8,128)(2,1)}), bf16[4,192,512]{2,1,0:T(8,128)(2,1)S(1)}, u32[]{:S(2)}, u32[]{:S(2)}) %all-to-all-start.1) | async-done | bytes 786464 | tf_op jit(solution)/shard_map/all_to_all | solution.py:21
  137.8 4.2 %all-to-all-start.2 = ((f32[4,32,512]{2,1,0:T(8,128)}), f32[4,32,512]{2,1,0:T(8,128)S(1)}, u32[]{:S(2)}, u32[]{:S(2)}) async-start(f32[4,32,512]{2,1,0:T(8,128)} %broadcast_in_dim.34), calls=%async_computation.3 | async-start | bytes 524288 | tf_op jit(solution)/shard_map/all_to_all | solution.py:21
  142.0 2.5 %fusion.1 = bf16[384,1024]{1,0:T(8,128)(2,1)} fusion(bf16[384,1024]{1,0:T(8,128)(2,1)S(1)} %collective-permute-done.17.refs_4_, bf16[384,1024]{1,0:T(8,128)(2,1)S(1)} %collective-permute-done.16.refs_3_, bf16[4,384,1024]{2,1,0:T(8,128)(2,1)} %bitcast.116, s32[]{:T(128)S(6)} %select_n.128), kind=kLoop, calls=%fused_computation.2 | loop fusion | flops 2359296 | bytes 3145732 | tf_op jit(solution)/shard_map/convert_element_type | solution.py:316
  144.5 6.8 %collective-permute-start.24 = (bf16[2,192,512]{2,1,0:T(8,128)(2,1)S(1)}, bf16[2,192,512]{2,1,0:T(8,128)(2,1)S(1)}, u32[]{:S(2)}, u32[]{:S(2)}) collective-permute-start(bf16[2,192,512]{2,1,0:T(8,128)(2,1)S(1)} %shard_map.114), channel_id=1, source_target_pairs={{0,1},{1,0},{2,3},{3,2},{4,5},{5,4},{6,7},{7,6},{8,9},{9,8},{10,11... | collective-permute-start | bytes 1179656 | tf_op jit(solution)/shard_map/ppermute | solution.py:17
  151.3 4.2 %collective-permute-start.25 = (f32[2,32,512]{2,1,0:T(8,128)S(1)}, f32[2,32,512]{2,1,0:T(8,128)S(1)}, u32[]{:S(2)}, u32[]{:S(2)}) collective-permute-start(f32[2,32,512]{2,1,0:T(8,128)S(1)} %dynamic-slice_bitcast_fusion.2), channel_id=1, source_target_pairs={{0,1},{1,0},{2,3},{3,2},{4,5},{5,4},{6,7},{7,6},{8,9},{9,8},{10,11... | collective-permute-start | bytes 393224 | tf_op jit(solution)/shard_map/ppermute | solution.py:17
  (122 shorter events, 44.6 us)
Async XLA Ops:
  7.2 62.7 %all-gather.2.cloned.1.call-start = ((), (), s32[]{:S(2)}) async-start(), calls=%async_computation.4 | async-start | bytes 2359296 | tf_op jit(solution)/shard_map/all_gather | solution.py:241
  8.3 10.1 %collective-permute-start.5 = (bf16[192,1024]{1,0:T(8,128)(2,1)S(1)}, bf16[192,1024]{1,0:T(8,128)(2,1)S(1)}, u32[]{:S(2)}, u32[]{:S(2)}) collective-permute-start(bf16[192,1024]{1,0:T(8,128)(2,1)S(1)} %dynamic-slice_bitcast_fusion.1), channel_id=1, source_target_pairs={{0,1},{1,0},{2,3},{3,2},{4,5},{5,4},{6,7},{7,6},{8,9},{9,8},{10,11... | collective-permute-start | bytes 1179656 | tf_op jit(solution)/shard_map/ppermute | solution.py:17
  11.7 6.8 %collective-permute-start.4 = (bf16[64,1024]{1,0:T(8,128)(2,1)}, bf16[64,1024]{1,0:T(8,128)(2,1)S(1)}, u32[]{:S(2)}, u32[]{:S(2)}) collective-permute-start(bf16[64,1024]{1,0:T(8,128)(2,1)} %refs_1_.1), channel_id=1, source_target_pairs={{0,128},{128,0},{1,129},{129,1},{2,130},{130,2},{3,131},{131,3},{4... | collective-permute-start | bytes 393224 | tf_op jit(solution)/shard_map/ppermute | solution.py:17
  21.4 16.5 %all-to-all-start = ((bf16[4,208,512]{2,1,0:T(8,128)(2,1)}), bf16[4,208,512]{2,1,0:T(8,128)(2,1)}, u32[]{:S(2)}, u32[]{:S(2)}) async-start(bf16[4,208,512]{2,1,0:T(8,128)(2,1)} %pad_maximum_fusion), calls=%async_computation | async-start | bytes 1703936 | tf_op jit(solution)/shard_map/all_to_all | solution.py:21
  25.7 104.5 %reduce-scatter.2.cloned.1.call-start = ((), (), s32[]{:S(2)}) async-start(), calls=%async_computation.5 | async-start | bytes 2359296 | tf_op jit(solution)/shard_map/reduce_scatter | solution.py:281
  25.7 28.7 %collective-permute-start = (bf16[384,1024]{1,0:T(8,128)(2,1)}, bf16[384,1024]{1,0:T(8,128)(2,1)}, u32[]{:S(2)}, u32[]{:S(2)}) collective-permute-start(bf16[384,1024]{1,0:T(8,128)(2,1)} %bitcast.4), channel_id=1, source_target_pairs={{0,32},{32,64},{64,96},{96,0},{1,33},{33,65},{65,97},{97,1},{2,34}... | collective-permute-start | bytes 2359304 | tf_op jit(solution)/shard_map/ppermute | solution.py:29
  27.1 28.5 %collective-permute-start.1 = (bf16[384,1024]{1,0:T(8,128)(2,1)}, bf16[384,1024]{1,0:T(8,128)(2,1)}, u32[]{:S(2)}, u32[]{:S(2)}) collective-permute-start(bf16[384,1024]{1,0:T(8,128)(2,1)} %bitcast.4), channel_id=1, source_target_pairs={{0,96},{32,0},{64,32},{96,64},{1,97},{33,1},{65,33},{97,65},{2,98}... | collective-permute-start | bytes 2359304 | tf_op jit(solution)/shard_map/ppermute | solution.py:29
  28.5 9.9 %collective-permute-start.7 = (bf16[64,1024]{1,0:T(8,128)(2,1)S(1)}, bf16[64,1024]{1,0:T(8,128)(2,1)S(1)}, u32[]{:S(2)}, u32[]{:S(2)}) collective-permute-start(bf16[64,1024]{1,0:T(8,128)(2,1)S(1)} %copy-done.5), channel_id=1, source_target_pairs={{0,1},{1,0},{2,3},{3,2},{4,5},{5,4},{6,7},{7,6},{8,9},{9,8},{10,11... | collective-permute-start | bytes 393224 | tf_op jit(solution)/shard_map/ppermute | solution.py:17
  37.9 26.6 %collective-permute-start.6 = (bf16[4,208,512]{2,1,0:T(8,128)(2,1)}, bf16[4,208,512]{2,1,0:T(8,128)(2,1)}, u32[]{:S(2)}, u32[]{:S(2)}) collective-permute-start(bf16[4,208,512]{2,1,0:T(8,128)(2,1)} %all-to-all-done.refs_1_.refs_4_), channel_id=1, source_target_pairs={{0,2},{2,0},{1,3},{3,1},{4,6},{6,4},{5,7},{7,5},{8,10},{10,8},{9,1... | collective-permute-start | bytes 2555912 | tf_op jit(solution)/shard_map/ppermute | solution.py:17
  39.2 25.4 %collective-permute-start.8 = (f32[64,512]{1,0:T(8,128)S(1)}, f32[64,512]{1,0:T(8,128)S(1)}, u32[]{:S(2)}, u32[]{:S(2)}) collective-permute-start(f32[64,512]{1,0:T(8,128)S(1)} %shard_map.103.refs_2_), channel_id=1, source_target_pairs={{0,2},{2,0},{1,3},{3,1},{4,6},{6,4},{5,7},{7,5},{8,10},{10,8},{9,1... | collective-permute-start | bytes 393224 | tf_op jit(solution)/shard_map/ppermute | solution.py:17
  55.5 14.3 %collective-permute-start.2 = (bf16[384,512]{1,0:T(8,128)(2,1)S(1)}, bf16[384,512]{1,0:T(8,128)(2,1)S(1)}, u32[]{:S(2)}, u32[]{:S(2)}) collective-permute-start(bf16[384,512]{1,0:T(8,128)(2,1)S(1)} %slice.42), channel_id=1, source_target_pairs={{0,32},{32,64},{64,96},{96,0},{1,33},{33,65},{65,97},{97,1},{2,34}... | collective-permute-start | bytes 1179656 | tf_op jit(solution)/shard_map/ppermute | solution.py:29
  56.6 13.2 %collective-permute-start.3 = (bf16[384,512]{1,0:T(8,128)(2,1)S(1)}, bf16[384,512]{1,0:T(8,128)(2,1)S(1)}, u32[]{:S(2)}, u32[]{:S(2)}) collective-permute-start(bf16[384,512]{1,0:T(8,128)(2,1)S(1)} %slice.43), channel_id=1, source_target_pairs={{0,96},{32,0},{64,32},{96,64},{1,97},{33,1},{65,33},{97,65},{2,98}... | collective-permute-start | bytes 1179656 | tf_op jit(solution)/shard_map/ppermute | solution.py:29
  62.2 12.3 %collective-permute-start.10 = (bf16[768,512]{1,0:T(8,128)(2,1)}, bf16[768,512]{1,0:T(8,128)(2,1)}, u32[]{:S(2)}, u32[]{:S(2)}) collective-permute-start(bf16[768,512]{1,0:T(8,128)(2,1)} %shard_map.105.refs_4_.refs_1_), channel_id=1, source_target_pairs={{0,1},{1,0},{2,3},{3,2},{4,5},{5,4},{6,7},{7,6},{8,9},{9,8},{10,11... | collective-permute-start | bytes 2359304 | tf_op jit(solution)/shard_map/ppermute | solution.py:17
  67.4 7.1 %collective-permute-start.11 = (bf16[768,512]{1,0:T(8,128)(2,1)}, bf16[768,512]{1,0:T(8,128)(2,1)}, u32[]{:S(2)}, u32[]{:S(2)}) collective-permute-start(bf16[768,512]{1,0:T(8,128)(2,1)} %shard_map.104.refs_3_.refs_2_), channel_id=1, source_target_pairs={{0,1},{1,0},{2,3},{3,2},{4,5},{5,4},{6,7},{7,6},{8,9},{9,8},{10,11... | collective-permute-start | bytes 2359304 | tf_op jit(solution)/shard_map/ppermute | solution.py:17
  81.2 10.4 %collective-permute-start.9 = (bf16[2,768,512]{2,1,0:T(8,128)(2,1)}, bf16[2,768,512]{2,1,0:T(8,128)(2,1)S(1)}, u32[]{:S(2)}, u32[]{:S(2)}) collective-permute-start(bf16[2,768,512]{2,1,0:T(8,128)(2,1)} %copy-done.7), channel_id=1, source_target_pairs={{0,1},{1,0},{2,3},{3,2},{4,5},{5,4},{6,7},{7,6},{8,9},{9,8},{10,11... | collective-permute-start | bytes 4718600 | tf_op jit(solution)/shard_map/ppermute | solution.py:17
  88.8 12.0 %collective-permute-start.13 = (bf16[384,512]{1,0:T(8,128)(2,1)S(1)}, bf16[384,512]{1,0:T(8,128)(2,1)S(1)}, u32[]{:S(2)}, u32[]{:S(2)}) collective-permute-start(bf16[384,512]{1,0:T(8,128)(2,1)S(1)} %get-tuple-element.33), channel_id=1, source_target_pairs={{0,32},{32,64},{64,96},{96,0},{1,33},{33,65},{65,97},{97,1},{2,34}... | collective-permute-start | bytes 1179656 | tf_op jit(solution)/shard_map/ppermute | solution.py:29
  88.9 11.9 %collective-permute-start.14 = (bf16[384,512]{1,0:T(8,128)(2,1)S(1)}, bf16[384,512]{1,0:T(8,128)(2,1)S(1)}, u32[]{:S(2)}, u32[]{:S(2)}) collective-permute-start(bf16[384,512]{1,0:T(8,128)(2,1)S(1)} %get-tuple-element.32), channel_id=1, source_target_pairs={{0,96},{32,0},{64,32},{96,64},{1,97},{33,1},{65,33},{97,65},{2,98}... | collective-permute-start | bytes 1179656 | tf_op jit(solution)/shard_map/ppermute | solution.py:29
  98.3 21.9 %collective-permute-start.12 = (bf16[768,512]{1,0:T(8,128)(2,1)S(1)}, bf16[768,512]{1,0:T(8,128)(2,1)S(1)}, u32[]{:S(2)}, u32[]{:S(2)}) collective-permute-start(bf16[768,512]{1,0:T(8,128)(2,1)S(1)} %get-tuple-element.20), channel_id=1, source_target_pairs={{0,2},{2,0},{1,3},{3,1},{4,6},{6,4},{5,7},{7,5},{8,10},{10,8},{9,1... | collective-permute-start | bytes 2359304 | tf_op jit(solution)/shard_map/ppermute | solution.py:17
  101.1 19.6 %collective-permute-start.16 = (bf16[384,1024]{1,0:T(8,128)(2,1)S(1)}, bf16[384,1024]{1,0:T(8,128)(2,1)S(1)}, u32[]{:S(2)}, u32[]{:S(2)}) collective-permute-start(bf16[384,1024]{1,0:T(8,128)(2,1)S(1)} %get-tuple-element.23), channel_id=1, source_target_pairs={{0,32},{32,64},{64,96},{96,0},{1,33},{33,65},{65,97},{97,1},{2,34}... | collective-permute-start | bytes 2359304 | tf_op jit(solution)/shard_map/ppermute | solution.py:29
  101.2 19.5 %collective-permute-start.17 = (bf16[384,1024]{1,0:T(8,128)(2,1)S(1)}, bf16[384,1024]{1,0:T(8,128)(2,1)S(1)}, u32[]{:S(2)}, u32[]{:S(2)}) collective-permute-start(bf16[384,1024]{1,0:T(8,128)(2,1)S(1)} %get-tuple-element.24), channel_id=1, source_target_pairs={{0,96},{32,0},{64,32},{96,64},{1,97},{33,1},{65,33},{97,65},{2,98}... | collective-permute-start | bytes 2359304 | tf_op jit(solution)/shard_map/ppermute | solution.py:29
  112.7 9.5 %collective-permute-start.20 = (bf16[2,32,512]{2,1,0:T(8,128)(2,1)S(1)}, bf16[2,32,512]{2,1,0:T(8,128)(2,1)S(1)}, u32[]{:S(2)}, u32[]{:S(2)}) collective-permute-start(bf16[2,32,512]{2,1,0:T(8,128)(2,1)S(1)} %add_convert_fusion.refs_5_.refs_1_), channel_id=1, source_target_pairs={{0,16},{4,20},{8,24},{12,28},{16,0},{20,4},{24,8},{28,12},{1,17},{... | collective-permute-start | bytes 196616 | tf_op jit(solution)/shard_map/ppermute | solution.py:288
  124.2 11.8 %all-to-all-start.1 = ((bf16[4,192,512]{2,1,0:T(8,128)(2,1)}), bf16[4,192,512]{2,1,0:T(8,128)(2,1)S(1)}, u32[]{:S(2)}, u32[]{:S(2)}) async-start(bf16[4,192,512]{2,1,0:T(8,128)(2,1)} %bitcast.26), calls=%async_computation.1 | async-start | bytes 1572864 | tf_op jit(solution)/shard_map/all_to_all | solution.py:21
  137.8 13.5 %all-to-all-start.2 = ((f32[4,32,512]{2,1,0:T(8,128)}), f32[4,32,512]{2,1,0:T(8,128)S(1)}, u32[]{:S(2)}, u32[]{:S(2)}) async-start(f32[4,32,512]{2,1,0:T(8,128)} %broadcast_in_dim.34), calls=%async_computation.3 | async-start | bytes 524288 | tf_op jit(solution)/shard_map/all_to_all | solution.py:21
  144.5 13.2 %collective-permute-start.24 = (bf16[2,192,512]{2,1,0:T(8,128)(2,1)S(1)}, bf16[2,192,512]{2,1,0:T(8,128)(2,1)S(1)}, u32[]{:S(2)}, u32[]{:S(2)}) collective-permute-start(bf16[2,192,512]{2,1,0:T(8,128)(2,1)S(1)} %shard_map.114), channel_id=1, source_target_pairs={{0,1},{1,0},{2,3},{3,2},{4,5},{5,4},{6,7},{7,6},{8,9},{9,8},{10,11... | collective-permute-start | bytes 1179656 | tf_op jit(solution)/shard_map/ppermute | solution.py:17
  (20 other events, 118.4 us)
Sparse Core Ops, SparseCore 0:
  20.2 38.9 all-gather.1
  81.4 39.5 reduce-scatter.1

commit v10 on v9

--- a/solution.py
+++ b/solution.py
@@ -86,6 +86,10 @@
     up[:, half:] = a[above, :, half:]
     down[:, :half] = a[below, :, :half]
     down[:, half:] = (a[below, :, half:].astype(F32) + from_above[...].astype(F32)).astype(BF)
+
+
+def copy_body(at, a, out):
+    out[...] = a[...]
 
 
 def take_body(at, a, out):
@@ -248,7 +252,9 @@
     gate = lambda block, table: call(gate_body, source, (block, table), jax.ShapeDtypeStruct((NY * half, wide), BF))
     got_far = swap(got, "xl")
 
-    near, far = gate(got, table_y), gate(got_far, swap(table_y, "xl"))
+    near = gate(got, table_y)
+    table_out = call(copy_body, source, (table_y,), jax.ShapeDtypeStruct(table_y.shape, F32), (near,))
+    far = gate(got_far, swap(table_out, "xl"))
     pieces = (near, far, swap(near, "c"), swap(far, "c"))
     at = jnp.stack([xl, c]).astype(jnp.int32)
 

time: 168 us -> 168 us (level)
  waiting for transfers between devices: 41.1 us -> 38.2 us
  starting transfers between devices: 58.3 us -> 60.6 us
    ppermute x8, waiting for transfers between devices: 14.1 us -> 11.6 us  [turn(): return lax.ppermute(a, 'y', [(i, (i + k) % NY) for i in range(NY)])]
    pallas_call x13 -> x14, Pallas kernels: 28.6 us -> 29 us  [call(): pl.pallas_call(lambda *refs: body(*refs[:count], *refs[count + len(after)...]
  transfers between devices with their start and end apart: 31 -> 31, of which waited for: 12 -> 13; matrix products, arithmetic and copies ran while one was open for 8% -> 8% of each run, Pallas kernels for 13% -> 13%
where the time goes in v10:
time: 168 us; the launch traced here: 167 us
  starting transfers between devices  60.6 us (36%)
  waiting for transfers between devices  38.2 us (23%)
  Pallas kernels  29 us (17%)
  local copies, waits for them, and re-layouts  16.7 us (10%)
  between operations  14.6 us (9%)
  other arithmetic  4.97 us (3%)
  matrix products  3.25 us (2%)
    pallas_call x14, Pallas kernels, call(): pl.pallas_call(lambda *refs: body(*refs[:count], *refs[count + len(after)...  29 us
    ppermute x15, starting transfers between devices, swap(): return lax.ppermute(a, axis, [(0, 1), (1, 0)])  27.2 us
    all_to_all x3, starting transfers between devices, exchange(): return lax.all_to_all(a, axis, 0, 0, tiled=True)  11.9 us
    ppermute x8, starting transfers between devices, turn(): return lax.ppermute(a, 'y', [(i, (i + k) % NY) for i in range(NY)])  11.9 us
    ppermute x8, waiting for transfers between devices, turn(): return lax.ppermute(a, 'y', [(i, (i + k) % NY) for i in range(NY)])  11.6 us
    all_to_all x3, waiting for transfers between devices, exchange(): return lax.all_to_all(a, axis, 0, 0, tiled=True)  11.6 us
    ppermute x3, starting transfers between devices, on_device(): lax.ppermute(a, 'z', [(i, i ^ bit) for i in range(NZ)])  9.49 us
    ppermute x15, waiting for transfers between devices, swap(): return lax.ppermute(a, axis, [(0, 1), (1, 0)])  7.92 us
  transfers between devices with their start and end apart: 31, of which 13 were waited for; matrix products, arithmetic and copies ran while one was open for 8% of the time, Pallas kernels for 13%

profile of v10, /device:TPU:1, one launch (start us, length us, event | category | flops | bytes accessed | tf_op | source)
XLA Modules:
  0.0 167.3 jit_solution(17742776841039463353)
XLA Ops:
  8.3 3.3 %collective-permute-start.5 = (bf16[192,1024]{1,0:T(8,128)(2,1)S(1)}, bf16[192,1024]{1,0:T(8,128)(2,1)S(1)}, u32[]{:S(2)}, u32[]{:S(2)}) collective-permute-start(bf16[192,1024]{1,0:T(8,128)(2,1)S(1)} %dynamic-slice_bitcast_fusion.1), channel_id=1, source_target_pairs={{0,1},{1,0},{2,3},{3,2},{4,5},{5,4},{6,7},{7,6},{8,9},{9,8},{10,11... | collective-permute-start | bytes 1179656 | tf_op jit(solution)/shard_map/ppermute | solution.py:17
  12.7 5.7 %collective-permute-done.4.refs_2_ = bf16[64,1024]{1,0:T(8,128)(2,1)S(1)} collective-permute-done((bf16[64,1024]{1,0:T(8,128)(2,1)}, bf16[64,1024]{1,0:T(8,128)(2,1)S(1)}, u32[]{:S(2)}, u32[]{:S(2)}) %collective-permute-start.4) | collective-permute-done | bytes 131104 | tf_op jit(solution)/shard_map/ppermute | solution.py:17
  21.4 4.2 %all-to-all-start = ((bf16[4,208,512]{2,1,0:T(8,128)(2,1)}), bf16[4,208,512]{2,1,0:T(8,128)(2,1)}, u32[]{:S(2)}, u32[]{:S(2)}) async-start(bf16[4,208,512]{2,1,0:T(8,128)(2,1)} %pad_maximum_fusion), calls=%async_computation | async-start | bytes 1703936 | tf_op jit(solution)/shard_map/all_to_all | solution.py:21
  29.9 8.0 %all-to-all-done.refs_1_.refs_4_ = bf16[4,208,512]{2,1,0:T(8,128)(2,1)} async-done(((bf16[4,208,512]{2,1,0:T(8,128)(2,1)}), bf16[4,208,512]{2,1,0:T(8,128)(2,1)}, u32[]{:S(2)}, u32[]{:S(2)}) %all-to-all-start) | async-done | bytes 852000 | tf_op jit(solution)/shard_map/all_to_all | solution.py:21
  39.2 2.9 %shard_map.104.refs_2_.refs_4_.refs_1_ = bf16[768,512]{1,0:T(8,128)(2,1)} custom-call(s32[2]{0:T(128)S(1)} %pad_add_fusion.1.refs_0_, bf16[4,208,512]{2,1,0:T(8,128)(2,1)} %all-to-all-done.refs_1_.refs_4_, f32[64,512]{1,0:T(8,128)S(1)} %shard_map.103.refs_2_.refs_1_), custom_call_target="tpu_custom_call" | custom-call | flops 1048576 | bytes 1024 | tf_op jit(solution)/shard_map/pallas_call | solution.py:64
  45.7 8.7 %collective-permute-done = bf16[384,1024]{1,0:T(8,128)(2,1)} collective-permute-done((bf16[384,1024]{1,0:T(8,128)(2,1)}, bf16[384,1024]{1,0:T(8,128)(2,1)}, u32[]{:S(2)}, u32[]{:S(2)}) %collective-permute-start) | collective-permute-done | bytes 786464 | tf_op jit(solution)/shard_map/ppermute | solution.py:29
  56.6 2.7 %collective-permute-start.3 = (bf16[384,512]{1,0:T(8,128)(2,1)S(1)}, bf16[384,512]{1,0:T(8,128)(2,1)S(1)}, u32[]{:S(2)}, u32[]{:S(2)}) collective-permute-start(bf16[384,512]{1,0:T(8,128)(2,1)S(1)} %slice.43), channel_id=1, source_target_pairs={{0,96},{32,0},{64,32},{96,64},{1,97},{33,1},{65,33},{97,65},{2,98}... | collective-permute-start | bytes 1179656 | tf_op jit(solution)/shard_map/ppermute | solution.py:29
  59.4 2.3 %collective-permute-start.10 = (bf16[768,512]{1,0:T(8,128)(2,1)}, bf16[768,512]{1,0:T(8,128)(2,1)}, u32[]{:S(2)}, u32[]{:S(2)}) collective-permute-start(bf16[768,512]{1,0:T(8,128)(2,1)} %shard_map.104.refs_2_.refs_4_.refs_1_), channel_id=1, source_target_pairs={{0,1},{1,0},{2,3},{3,2},{4,5},{5,4},{6,7},{7,6},{8,9},{9,8},{10,11... | collective-permute-start | bytes 2359304 | tf_op jit(solution)/shard_map/ppermute | solution.py:17
  61.7 2.9 %shard_map.106.refs_3_.refs_2_ = bf16[768,512]{1,0:T(8,128)(2,1)} custom-call(s32[2]{0:T(128)S(1)} %pad_add_fusion.1.refs_0_, bf16[4,208,512]{2,1,0:T(8,128)(2,1)} %collective-permute-done.6.refs_1_.refs_5_, f32[64,512]{1,0:T(8,128)S(1)} %collective-permute-done.8.refs_2_), custom_call_target="tpu_custom_call" | custom-call | flops 1048576 | bytes 1024 | tf_op jit(solution)/shard_map/pallas_call | solution.py:64
  72.3 5.3 %shard_map.108 = (bf16[2,512,1024]{2,1,0:T(8,128)(2,1)S(1)}, f32[8,128]{1,0:T(8,128)S(1)}) custom-call(s32[2]{0:T(128)S(1)} %pad_add_fusion.refs_0_, bf16[768,512]{1,0:T(8,128)(2,1)} %shard_map.104.refs_2_.refs_4_.refs_1_, bf16[768,512]{1,0:T(8,128)(2,1)} %shard_map.106.refs_3_.refs_2_, bf16[768,512]{1,0:T(8,128)(2,1)} %collective-permute-done.10.refs_3_, ...), custom_call_target="tpu_custom_call" | custom-call | flops 1048576 | bytes 1024 | tf_op jit(solution)/shard_map/pallas_call | solution.py:64
  81.8 5.3 %shard_map.109 = (bf16[4,2,192,1024]{3,2,1,0:T(8,128)(2,1)S(1)}, f32[8,128]{1,0:T(8,128)S(1)}) custom-call(s32[2]{0:T(128)S(1)} %pad_add_fusion.refs_0_, bf16[768,512]{1,0:T(8,128)(2,1)} %shard_map.104.refs_2_.refs_4_.refs_1_, bf16[768,512]{1,0:T(8,128)(2,1)} %shard_map.106.refs_3_.refs_2_, bf16[768,512]{1,0:T(8,128)(2,1)} %collective-permute-done.10.refs_3_, ...), custom_call_target="tpu_custom_call" | custom-call | flops 1048576 | bytes 1024 | tf_op jit(solution)/shard_map/pallas_call | solution.py:64
  87.3 3.5 %collective-permute-start.14 = (bf16[384,512]{1,0:T(8,128)(2,1)S(1)}, bf16[384,512]{1,0:T(8,128)(2,1)S(1)}, u32[]{:S(2)}, u32[]{:S(2)}) collective-permute-start(bf16[384,512]{1,0:T(8,128)(2,1)S(1)} %get-tuple-element.32), channel_id=1, source_target_pairs={{0,96},{32,0},{64,32},{96,64},{1,97},{33,1},{65,33},{97,65},{2,98}... | collective-permute-start | bytes 1179656 | tf_op jit(solution)/shard_map/ppermute | solution.py:29
  90.8 5.9 %shard_map.110 = (bf16[768,512]{1,0:T(8,128)(2,1)S(1)}, f32[768,512]{1,0:T(8,128)S(1)}, f32[2,64,512]{2,1,0:T(8,128)S(1)}) custom-call(s32[2]{0:T(128)S(1)} %pad_add_fusion.refs_0_, bf16[4,2,192,1024]{3,2,1,0:T(8,128)(2,1)S(1)} %bitcast.111, bf16[2,512,1024]{2,1,0:T(8,128)(2,1)S(1)} %copy-done.2, bf16[2,768,512]{2,1,0:T(8,128)(2,1)S(1)} %collective-permute-done.9.refs_3_, ...), custom_call_target="tpu_custom_call" | custom-call | flops 1048576 | bytes 1024 | tf_op jit(solution)/shard_map/pallas_call | solution.py:64
  98.2 2.0 %collective-permute-done.13.refs_2_ = bf16[384,512]{1,0:T(8,128)(2,1)S(1)} collective-permute-done((bf16[384,512]{1,0:T(8,128)(2,1)S(1)}, bf16[384,512]{1,0:T(8,128)(2,1)S(1)}, u32[]{:S(2)}, u32[]{:S(2)}) %collective-permute-start.13) | collective-permute-done | bytes 393248 | tf_op jit(solution)/shard_map/ppermute | solution.py:29
  103.1 4.0 %collective-permute-done.18 = bf16[2,32,512]{2,1,0:T(8,128)(2,1)S(1)} collective-permute-done((bf16[2,32,512]{2,1,0:T(8,128)(2,1)S(1)}, bf16[2,32,512]{2,1,0:T(8,128)(2,1)S(1)}, u32[]{:S(2)}, u32[]{:S(2)}) %collective-permute-start.18) | collective-permute-done | bytes 65568 | tf_op jit(solution)/shard_map/ppermute | solution.py:294
  109.0 2.7 %collective-permute-done.19 = bf16[2,32,512]{2,1,0:T(8,128)(2,1)S(1)} collective-permute-done((bf16[2,32,512]{2,1,0:T(8,128)(2,1)S(1)}, bf16[2,32,512]{2,1,0:T(8,128)(2,1)S(1)}, u32[]{:S(2)}, u32[]{:S(2)}) %collective-permute-start.19) | collective-permute-done | bytes 65568 | tf_op jit(solution)/shard_map/ppermute | solution.py:294
  111.7 7.6 %collective-permute-start.20 = (bf16[2,32,512]{2,1,0:T(8,128)(2,1)S(1)}, bf16[2,32,512]{2,1,0:T(8,128)(2,1)S(1)}, u32[]{:S(2)}, u32[]{:S(2)}) collective-permute-start(bf16[2,32,512]{2,1,0:T(8,128)(2,1)S(1)} %add_convert_fusion.refs_5_.refs_1_), channel_id=1, source_target_pairs={{0,16},{4,20},{8,24},{12,28},{16,0},{20,4},{24,8},{28,12},{1,17},{... | collective-permute-start | bytes 196616 | tf_op jit(solution)/shard_map/ppermute | solution.py:294
  123.9 3.5 %all-to-all-start.1 = ((bf16[4,192,512]{2,1,0:T(8,128)(2,1)}), bf16[4,192,512]{2,1,0:T(8,128)(2,1)S(1)}, u32[]{:S(2)}, u32[]{:S(2)}) async-start(bf16[4,192,512]{2,1,0:T(8,128)(2,1)} %bitcast.26), calls=%async_computation.1 | async-start | bytes 1572864 | tf_op jit(solution)/shard_map/all_to_all | solution.py:21
  127.5 2.4 %collective-permute-start.22 = (f32[32,512]{1,0:T(8,128)S(1)}, f32[32,512]{1,0:T(8,128)S(1)}, u32[]{:S(2)}, u32[]{:S(2)}) collective-permute-start(f32[32,512]{1,0:T(8,128)S(1)} %fusion.14.refs_1_), channel_id=1, source_target_pairs={{0,128},{128,0},{1,129},{129,1},{2,130},{130,2},{3,131},{131,3},{4... | collective-permute-start | bytes 196616 | tf_op jit(solution)/shard_map/ppermute | solution.py:17
  132.2 3.6 %all-to-all-done.1.refs_3_ = bf16[4,192,512]{2,1,0:T(8,128)(2,1)S(1)} async-done(((bf16[4,192,512]{2,1,0:T(8,128)(2,1)}), bf16[4,192,512]{2,1,0:T(8,128)(2,1)S(1)}, u32[]{:S(2)}, u32[]{:S(2)}) %all-to-all-start.1) | async-done | bytes 786464 | tf_op jit(solution)/shard_map/all_to_all | solution.py:21
  137.5 4.2 %all-to-all-start.2 = ((f32[4,32,512]{2,1,0:T(8,128)}), f32[4,32,512]{2,1,0:T(8,128)S(1)}, u32[]{:S(2)}, u32[]{:S(2)}) async-start(f32[4,32,512]{2,1,0:T(8,128)} %broadcast_in_dim.34), calls=%async_computation.3 | async-start | bytes 524288 | tf_op jit(solution)/shard_map/all_to_all | solution.py:21
  141.7 2.5 %fusion.1 = bf16[384,1024]{1,0:T(8,128)(2,1)} fusion(bf16[384,1024]{1,0:T(8,128)(2,1)S(1)} %collective-permute-done.17.refs_4_, bf16[384,1024]{1,0:T(8,128)(2,1)S(1)} %collective-permute-done.16.refs_3_, bf16[4,384,1024]{2,1,0:T(8,128)(2,1)} %bitcast.116, s32[]{:T(128)S(6)} %select_n.128), kind=kLoop, calls=%fused_computation.2 | loop fusion | flops 2359296 | bytes 3145732 | tf_op jit(solution)/shard_map/convert_element_type | solution.py:322
  144.2 6.8 %collective-permute-start.24 = (bf16[2,192,512]{2,1,0:T(8,128)(2,1)S(1)}, bf16[2,192,512]{2,1,0:T(8,128)(2,1)S(1)}, u32[]{:S(2)}, u32[]{:S(2)}) collective-permute-start(bf16[2,192,512]{2,1,0:T(8,128)(2,1)S(1)} %shard_map.115), channel_id=1, source_target_pairs={{0,1},{1,0},{2,3},{3,2},{4,5},{5,4},{6,7},{7,6},{8,9},{9,8},{10,11... | collective-permute-start | bytes 1179656 | tf_op jit(solution)/shard_map/ppermute | solution.py:17
  151.1 4.2 %collective-permute-start.25 = (f32[2,32,512]{2,1,0:T(8,128)S(1)}, f32[2,32,512]{2,1,0:T(8,128)S(1)}, u32[]{:S(2)}, u32[]{:S(2)}) collective-permute-start(f32[2,32,512]{2,1,0:T(8,128)S(1)} %dynamic-slice_bitcast_fusion.2), channel_id=1, source_target_pairs={{0,1},{1,0},{2,3},{3,2},{4,5},{5,4},{6,7},{7,6},{8,9},{9,8},{10,11... | collective-permute-start | bytes 393224 | tf_op jit(solution)/shard_map/ppermute | solution.py:17
  (123 shorter events, 48.4 us)
Async XLA Ops:
  7.2 60.5 %all-gather.2.cloned.1.call-start = ((), (), s32[]{:S(2)}) async-start(), calls=%async_computation.4 | async-start | bytes 2359296 | tf_op jit(solution)/shard_map/all_gather | solution.py:245
  8.3 10.1 %collective-permute-start.5 = (bf16[192,1024]{1,0:T(8,128)(2,1)S(1)}, bf16[192,1024]{1,0:T(8,128)(2,1)S(1)}, u32[]{:S(2)}, u32[]{:S(2)}) collective-permute-start(bf16[192,1024]{1,0:T(8,128)(2,1)S(1)} %dynamic-slice_bitcast_fusion.1), channel_id=1, source_target_pairs={{0,1},{1,0},{2,3},{3,2},{4,5},{5,4},{6,7},{7,6},{8,9},{9,8},{10,11... | collective-permute-start | bytes 1179656 | tf_op jit(solution)/shard_map/ppermute | solution.py:17
  11.7 6.8 %collective-permute-start.4 = (bf16[64,1024]{1,0:T(8,128)(2,1)}, bf16[64,1024]{1,0:T(8,128)(2,1)S(1)}, u32[]{:S(2)}, u32[]{:S(2)}) collective-permute-start(bf16[64,1024]{1,0:T(8,128)(2,1)} %refs_1_.1), channel_id=1, source_target_pairs={{0,128},{128,0},{1,129},{129,1},{2,130},{130,2},{3,131},{131,3},{4... | collective-permute-start | bytes 393224 | tf_op jit(solution)/shard_map/ppermute | solution.py:17
  21.4 16.5 %all-to-all-start = ((bf16[4,208,512]{2,1,0:T(8,128)(2,1)}), bf16[4,208,512]{2,1,0:T(8,128)(2,1)}, u32[]{:S(2)}, u32[]{:S(2)}) async-start(bf16[4,208,512]{2,1,0:T(8,128)(2,1)} %pad_maximum_fusion), calls=%async_computation | async-start | bytes 1703936 | tf_op jit(solution)/shard_map/all_to_all | solution.py:21
  25.7 104.3 %reduce-scatter.2.cloned.1.call-start = ((), (), s32[]{:S(2)}) async-start(), calls=%async_computation.5 | async-start | bytes 2359296 | tf_op jit(solution)/shard_map/reduce_scatter | solution.py:287
  25.7 28.7 %collective-permute-start = (bf16[384,1024]{1,0:T(8,128)(2,1)}, bf16[384,1024]{1,0:T(8,128)(2,1)}, u32[]{:S(2)}, u32[]{:S(2)}) collective-permute-start(bf16[384,1024]{1,0:T(8,128)(2,1)} %bitcast.4), channel_id=1, source_target_pairs={{0,32},{32,64},{64,96},{96,0},{1,33},{33,65},{65,97},{97,1},{2,34}... | collective-permute-start | bytes 2359304 | tf_op jit(solution)/shard_map/ppermute | solution.py:29
  27.1 28.5 %collective-permute-start.1 = (bf16[384,1024]{1,0:T(8,128)(2,1)}, bf16[384,1024]{1,0:T(8,128)(2,1)}, u32[]{:S(2)}, u32[]{:S(2)}) collective-permute-start(bf16[384,1024]{1,0:T(8,128)(2,1)} %bitcast.4), channel_id=1, source_target_pairs={{0,96},{32,0},{64,32},{96,64},{1,97},{33,1},{65,33},{97,65},{2,98}... | collective-permute-start | bytes 2359304 | tf_op jit(solution)/shard_map/ppermute | solution.py:29
  28.5 9.9 %collective-permute-start.7 = (bf16[64,1024]{1,0:T(8,128)(2,1)S(1)}, bf16[64,1024]{1,0:T(8,128)(2,1)S(1)}, u32[]{:S(2)}, u32[]{:S(2)}) collective-permute-start(bf16[64,1024]{1,0:T(8,128)(2,1)S(1)} %copy-done.5), channel_id=1, source_target_pairs={{0,1},{1,0},{2,3},{3,2},{4,5},{5,4},{6,7},{7,6},{8,9},{9,8},{10,11... | collective-permute-start | bytes 393224 | tf_op jit(solution)/shard_map/ppermute | solution.py:17
  37.9 23.7 %collective-permute-start.6 = (bf16[4,208,512]{2,1,0:T(8,128)(2,1)}, bf16[4,208,512]{2,1,0:T(8,128)(2,1)}, u32[]{:S(2)}, u32[]{:S(2)}) collective-permute-start(bf16[4,208,512]{2,1,0:T(8,128)(2,1)} %all-to-all-done.refs_1_.refs_4_), channel_id=1, source_target_pairs={{0,2},{2,0},{1,3},{3,1},{4,6},{6,4},{5,7},{7,5},{8,10},{10,8},{9,1... | collective-permute-start | bytes 2555912 | tf_op jit(solution)/shard_map/ppermute | solution.py:17
  42.6 19.1 %collective-permute-start.8 = (f32[64,512]{1,0:T(8,128)S(1)}, f32[64,512]{1,0:T(8,128)S(1)}, u32[]{:S(2)}, u32[]{:S(2)}) collective-permute-start(f32[64,512]{1,0:T(8,128)S(1)} %shard_map.105), channel_id=1, source_target_pairs={{0,2},{2,0},{1,3},{3,1},{4,6},{6,4},{5,7},{7,5},{8,10},{10,8},{9,1... | collective-permute-start | bytes 393224 | tf_op jit(solution)/shard_map/ppermute | solution.py:17
  55.5 12.1 %collective-permute-start.2 = (bf16[384,512]{1,0:T(8,128)(2,1)S(1)}, bf16[384,512]{1,0:T(8,128)(2,1)S(1)}, u32[]{:S(2)}, u32[]{:S(2)}) collective-permute-start(bf16[384,512]{1,0:T(8,128)(2,1)S(1)} %slice.42), channel_id=1, source_target_pairs={{0,32},{32,64},{64,96},{96,0},{1,33},{33,65},{65,97},{97,1},{2,34}... | collective-permute-start | bytes 1179656 | tf_op jit(solution)/shard_map/ppermute | solution.py:29
  56.6 11.0 %collective-permute-start.3 = (bf16[384,512]{1,0:T(8,128)(2,1)S(1)}, bf16[384,512]{1,0:T(8,128)(2,1)S(1)}, u32[]{:S(2)}, u32[]{:S(2)}) collective-permute-start(bf16[384,512]{1,0:T(8,128)(2,1)S(1)} %slice.43), channel_id=1, source_target_pairs={{0,96},{32,0},{64,32},{96,64},{1,97},{33,1},{65,33},{97,65},{2,98}... | collective-permute-start | bytes 1179656 | tf_op jit(solution)/shard_map/ppermute | solution.py:29
  59.4 12.9 %collective-permute-start.10 = (bf16[768,512]{1,0:T(8,128)(2,1)}, bf16[768,512]{1,0:T(8,128)(2,1)}, u32[]{:S(2)}, u32[]{:S(2)}) collective-permute-start(bf16[768,512]{1,0:T(8,128)(2,1)} %shard_map.104.refs_2_.refs_4_.refs_1_), channel_id=1, source_target_pairs={{0,1},{1,0},{2,3},{3,2},{4,5},{5,4},{6,7},{7,6},{8,9},{9,8},{10,11... | collective-permute-start | bytes 2359304 | tf_op jit(solution)/shard_map/ppermute | solution.py:17
  64.5 7.8 %collective-permute-start.11 = (bf16[768,512]{1,0:T(8,128)(2,1)}, bf16[768,512]{1,0:T(8,128)(2,1)}, u32[]{:S(2)}, u32[]{:S(2)}) collective-permute-start(bf16[768,512]{1,0:T(8,128)(2,1)} %shard_map.106.refs_3_.refs_2_), channel_id=1, source_target_pairs={{0,1},{1,0},{2,3},{3,2},{4,5},{5,4},{6,7},{7,6},{8,9},{9,8},{10,11... | collective-permute-start | bytes 2359304 | tf_op jit(solution)/shard_map/ppermute | solution.py:17
  79.0 11.7 %collective-permute-start.9 = (bf16[2,768,512]{2,1,0:T(8,128)(2,1)}, bf16[2,768,512]{2,1,0:T(8,128)(2,1)S(1)}, u32[]{:S(2)}, u32[]{:S(2)}) collective-permute-start(bf16[2,768,512]{2,1,0:T(8,128)(2,1)} %copy-done.7), channel_id=1, source_target_pairs={{0,1},{1,0},{2,3},{3,2},{4,5},{5,4},{6,7},{7,6},{8,9},{9,8},{10,11... | collective-permute-start | bytes 4718600 | tf_op jit(solution)/shard_map/ppermute | solution.py:17
  87.2 13.0 %collective-permute-start.13 = (bf16[384,512]{1,0:T(8,128)(2,1)S(1)}, bf16[384,512]{1,0:T(8,128)(2,1)S(1)}, u32[]{:S(2)}, u32[]{:S(2)}) collective-permute-start(bf16[384,512]{1,0:T(8,128)(2,1)S(1)} %get-tuple-element.33), channel_id=1, source_target_pairs={{0,32},{32,64},{64,96},{96,0},{1,33},{33,65},{65,97},{97,1},{2,34}... | collective-permute-start | bytes 1179656 | tf_op jit(solution)/shard_map/ppermute | solution.py:29
  87.3 12.9 %collective-permute-start.14 = (bf16[384,512]{1,0:T(8,128)(2,1)S(1)}, bf16[384,512]{1,0:T(8,128)(2,1)S(1)}, u32[]{:S(2)}, u32[]{:S(2)}) collective-permute-start(bf16[384,512]{1,0:T(8,128)(2,1)S(1)} %get-tuple-element.32), channel_id=1, source_target_pairs={{0,96},{32,0},{64,32},{96,64},{1,97},{33,1},{65,33},{97,65},{2,98}... | collective-permute-start | bytes 1179656 | tf_op jit(solution)/shard_map/ppermute | solution.py:29
  97.1 22.3 %collective-permute-start.12 = (bf16[768,512]{1,0:T(8,128)(2,1)S(1)}, bf16[768,512]{1,0:T(8,128)(2,1)S(1)}, u32[]{:S(2)}, u32[]{:S(2)}) collective-permute-start(bf16[768,512]{1,0:T(8,128)(2,1)S(1)} %get-tuple-element.20), channel_id=1, source_target_pairs={{0,2},{2,0},{1,3},{3,1},{4,6},{6,4},{5,7},{7,5},{8,10},{10,8},{9,1... | collective-permute-start | bytes 2359304 | tf_op jit(solution)/shard_map/ppermute | solution.py:17
  100.4 19.9 %collective-permute-start.16 = (bf16[384,1024]{1,0:T(8,128)(2,1)S(1)}, bf16[384,1024]{1,0:T(8,128)(2,1)S(1)}, u32[]{:S(2)}, u32[]{:S(2)}) collective-permute-start(bf16[384,1024]{1,0:T(8,128)(2,1)S(1)} %get-tuple-element.23), channel_id=1, source_target_pairs={{0,32},{32,64},{64,96},{96,0},{1,33},{33,65},{65,97},{97,1},{2,34}... | collective-permute-start | bytes 2359304 | tf_op jit(solution)/shard_map/ppermute | solution.py:29
  101.2 19.1 %collective-permute-start.17 = (bf16[384,1024]{1,0:T(8,128)(2,1)S(1)}, bf16[384,1024]{1,0:T(8,128)(2,1)S(1)}, u32[]{:S(2)}, u32[]{:S(2)}) collective-permute-start(bf16[384,1024]{1,0:T(8,128)(2,1)S(1)} %get-tuple-element.24), channel_id=1, source_target_pairs={{0,96},{32,0},{64,32},{96,64},{1,97},{33,1},{65,33},{97,65},{2,98}... | collective-permute-start | bytes 2359304 | tf_op jit(solution)/shard_map/ppermute | solution.py:29
  111.7 10.4 %collective-permute-start.20 = (bf16[2,32,512]{2,1,0:T(8,128)(2,1)S(1)}, bf16[2,32,512]{2,1,0:T(8,128)(2,1)S(1)}, u32[]{:S(2)}, u32[]{:S(2)}) collective-permute-start(bf16[2,32,512]{2,1,0:T(8,128)(2,1)S(1)} %add_convert_fusion.refs_5_.refs_1_), channel_id=1, source_target_pairs={{0,16},{4,20},{8,24},{12,28},{16,0},{20,4},{24,8},{28,12},{1,17},{... | collective-permute-start | bytes 196616 | tf_op jit(solution)/shard_map/ppermute | solution.py:294
  123.9 11.8 %all-to-all-start.1 = ((bf16[4,192,512]{2,1,0:T(8,128)(2,1)}), bf16[4,192,512]{2,1,0:T(8,128)(2,1)S(1)}, u32[]{:S(2)}, u32[]{:S(2)}) async-start(bf16[4,192,512]{2,1,0:T(8,128)(2,1)} %bitcast.26), calls=%async_computation.1 | async-start | bytes 1572864 | tf_op jit(solution)/shard_map/all_to_all | solution.py:21
  137.5 13.5 %all-to-all-start.2 = ((f32[4,32,512]{2,1,0:T(8,128)}), f32[4,32,512]{2,1,0:T(8,128)S(1)}, u32[]{:S(2)}, u32[]{:S(2)}) async-start(f32[4,32,512]{2,1,0:T(8,128)} %broadcast_in_dim.34), calls=%async_computation.3 | async-start | bytes 524288 | tf_op jit(solution)/shard_map/all_to_all | solution.py:21
  144.2 13.2 %collective-permute-start.24 = (bf16[2,192,512]{2,1,0:T(8,128)(2,1)S(1)}, bf16[2,192,512]{2,1,0:T(8,128)(2,1)S(1)}, u32[]{:S(2)}, u32[]{:S(2)}) collective-permute-start(bf16[2,192,512]{2,1,0:T(8,128)(2,1)S(1)} %shard_map.115), channel_id=1, source_target_pairs={{0,1},{1,0},{2,3},{3,2},{4,5},{5,4},{6,7},{7,6},{8,9},{9,8},{10,11... | collective-permute-start | bytes 1179656 | tf_op jit(solution)/shard_map/ppermute | solution.py:17
  (20 other events, 119.6 us)
Sparse Core Ops, SparseCore 0:
  20.2 38.9 all-gather.1
  79.2 40.7 reduce-scatter.1

commit v11 on v10

--- a/solution.py
+++ b/solution.py
@@ -302,10 +302,10 @@
     table_sum = call(
         add_body, at, (table_sum, swap(table_sum, "xh")), jax.ShapeDtypeStruct(table_sum.shape, F32), (home, wg_other)
     )
-    table_all = spread(table_sum, "y", NY).reshape(NC, 2, strategies // NC, wide)
+    table_all = spread(table_sum.astype(BF), "y", NY).reshape(NC, 2, strategies // NC, wide)
     rest = swap(pick(table_all, 1 - c, 0), "c")
     table_full = in_order(c, pick(table_all, c, 0), rest, 1)
-    table_full = table_full.reshape(2, strategies, wide).transpose(1, 0, 2).reshape(strategies, cols)
+    table_full = table_full.astype(F32).reshape(2, strategies, wide).transpose(1, 0, 2).reshape(strategies, cols)
     table_grad = jnp.dot(mixing.T, table_full, precision=HIGHEST) * grad_scale
 
     parts = home.reshape(NC, 2, half, wide)

time: 168 us -> 166 us (0.988)
  transfers between devices with their start and end apart: 31 -> 31, of which waited for: 13 -> 13; matrix products, arithmetic and copies ran while one was open for 8% -> 8% of each run, Pallas kernels for 13% -> 14%
where the time goes in v11:
time: 166 us; the launch traced here: 165 us
  starting transfers between devices  59.8 us (36%)
  waiting for transfers between devices  38.1 us (23%)
  Pallas kernels  29 us (17%)
  local copies, waits for them, and re-layouts  15.6 us (9%)
  between operations  14.6 us (9%)
  other arithmetic  4.96 us (3%)
  matrix products  3.16 us (2%)
    pallas_call x14, Pallas kernels, call(): pl.pallas_call(lambda *refs: body(*refs[:count], *refs[count + len(after)...  29 us
    ppermute x15, starting transfers between devices, swap(): return lax.ppermute(a, axis, [(0, 1), (1, 0)])  26.4 us
    all_to_all x3, starting transfers between devices, exchange(): return lax.all_to_all(a, axis, 0, 0, tiled=True)  11.9 us
    ppermute x8, starting transfers between devices, turn(): return lax.ppermute(a, 'y', [(i, (i + k) % NY) for i in range(NY)])  11.9 us
    ppermute x8, waiting for transfers between devices, turn(): return lax.ppermute(a, 'y', [(i, (i + k) % NY) for i in range(NY)])  11.6 us
    all_to_all x3, waiting for transfers between devices, exchange(): return lax.all_to_all(a, axis, 0, 0, tiled=True)  11.6 us
    ppermute x3, starting transfers between devices, on_device(): lax.ppermute(a, 'z', [(i, i ^ bit) for i in range(NZ)])  9.49 us
    ppermute x15, waiting for transfers between devices, swap(): return lax.ppermute(a, axis, [(0, 1), (1, 0)])  7.83 us
  transfers between devices with their start and end apart: 31, of which 13 were waited for; matrix products, arithmetic and copies ran while one was open for 8% of the time, Pallas kernels for 14%

profile of v11, /device:TPU:1, one launch (start us, length us, event | category | flops | bytes accessed | tf_op | source)
XLA Modules:
  0.0 165.3 jit_solution(403028126130670528)
XLA Ops:
  8.3 3.3 %collective-permute-start.5 = (bf16[192,1024]{1,0:T(8,128)(2,1)S(1)}, bf16[192,1024]{1,0:T(8,128)(2,1)S(1)}, u32[]{:S(2)}, u32[]{:S(2)}) collective-permute-start(bf16[192,1024]{1,0:T(8,128)(2,1)S(1)} %dynamic-slice_bitcast_fusion.1), channel_id=1, source_target_pairs={{0,1},{1,0},{2,3},{3,2},{4,5},{5,4},{6,7},{7,6},{8,9},{9,8},{10,11... | collective-permute-start | bytes 1179656 | tf_op jit(solution)/shard_map/ppermute | solution.py:17
  12.7 5.7 %collective-permute-done.4.refs_2_ = bf16[64,1024]{1,0:T(8,128)(2,1)S(1)} collective-permute-done((bf16[64,1024]{1,0:T(8,128)(2,1)}, bf16[64,1024]{1,0:T(8,128)(2,1)S(1)}, u32[]{:S(2)}, u32[]{:S(2)}) %collective-permute-start.4) | collective-permute-done | bytes 131104 | tf_op jit(solution)/shard_map/ppermute | solution.py:17
  21.4 4.2 %all-to-all-start = ((bf16[4,208,512]{2,1,0:T(8,128)(2,1)}), bf16[4,208,512]{2,1,0:T(8,128)(2,1)}, u32[]{:S(2)}, u32[]{:S(2)}) async-start(bf16[4,208,512]{2,1,0:T(8,128)(2,1)} %pad_maximum_fusion), calls=%async_computation | async-start | bytes 1703936 | tf_op jit(solution)/shard_map/all_to_all | solution.py:21
  29.9 8.0 %all-to-all-done.refs_1_.refs_4_ = bf16[4,208,512]{2,1,0:T(8,128)(2,1)} async-done(((bf16[4,208,512]{2,1,0:T(8,128)(2,1)}), bf16[4,208,512]{2,1,0:T(8,128)(2,1)}, u32[]{:S(2)}, u32[]{:S(2)}) %all-to-all-start) | async-done | bytes 852000 | tf_op jit(solution)/shard_map/all_to_all | solution.py:21
  39.2 2.9 %shard_map.104.refs_2_.refs_4_.refs_1_ = bf16[768,512]{1,0:T(8,128)(2,1)} custom-call(s32[2]{0:T(128)S(1)} %pad_add_fusion.1.refs_0_, bf16[4,208,512]{2,1,0:T(8,128)(2,1)} %all-to-all-done.refs_1_.refs_4_, f32[64,512]{1,0:T(8,128)S(1)} %shard_map.103.refs_2_.refs_1_), custom_call_target="tpu_custom_call" | custom-call | flops 1048576 | bytes 1024 | tf_op jit(solution)/shard_map/pallas_call | solution.py:64
  45.7 8.7 %collective-permute-done = bf16[384,1024]{1,0:T(8,128)(2,1)} collective-permute-done((bf16[384,1024]{1,0:T(8,128)(2,1)}, bf16[384,1024]{1,0:T(8,128)(2,1)}, u32[]{:S(2)}, u32[]{:S(2)}) %collective-permute-start) | collective-permute-done | bytes 786464 | tf_op jit(solution)/shard_map/ppermute | solution.py:29
  56.6 2.7 %collective-permute-start.3 = (bf16[384,512]{1,0:T(8,128)(2,1)S(1)}, bf16[384,512]{1,0:T(8,128)(2,1)S(1)}, u32[]{:S(2)}, u32[]{:S(2)}) collective-permute-start(bf16[384,512]{1,0:T(8,128)(2,1)S(1)} %slice.43), channel_id=1, source_target_pairs={{0,96},{32,0},{64,32},{96,64},{1,97},{33,1},{65,33},{97,65},{2,98}... | collective-permute-start | bytes 1179656 | tf_op jit(solution)/shard_map/ppermute | solution.py:29
  59.4 2.3 %collective-permute-start.10 = (bf16[768,512]{1,0:T(8,128)(2,1)}, bf16[768,512]{1,0:T(8,128)(2,1)}, u32[]{:S(2)}, u32[]{:S(2)}) collective-permute-start(bf16[768,512]{1,0:T(8,128)(2,1)} %shard_map.104.refs_2_.refs_4_.refs_1_), channel_id=1, source_target_pairs={{0,1},{1,0},{2,3},{3,2},{4,5},{5,4},{6,7},{7,6},{8,9},{9,8},{10,11... | collective-permute-start | bytes 2359304 | tf_op jit(solution)/shard_map/ppermute | solution.py:17
  61.7 2.9 %shard_map.106.refs_3_.refs_2_ = bf16[768,512]{1,0:T(8,128)(2,1)} custom-call(s32[2]{0:T(128)S(1)} %pad_add_fusion.1.refs_0_, bf16[4,208,512]{2,1,0:T(8,128)(2,1)} %collective-permute-done.6.refs_1_.refs_5_, f32[64,512]{1,0:T(8,128)S(1)} %collective-permute-done.8.refs_2_), custom_call_target="tpu_custom_call" | custom-call | flops 1048576 | bytes 1024 | tf_op jit(solution)/shard_map/pallas_call | solution.py:64
  72.3 5.3 %shard_map.108 = (bf16[2,512,1024]{2,1,0:T(8,128)(2,1)S(1)}, f32[8,128]{1,0:T(8,128)S(1)}) custom-call(s32[2]{0:T(128)S(1)} %pad_add_fusion.refs_0_, bf16[768,512]{1,0:T(8,128)(2,1)} %shard_map.104.refs_2_.refs_4_.refs_1_, bf16[768,512]{1,0:T(8,128)(2,1)} %shard_map.106.refs_3_.refs_2_, bf16[768,512]{1,0:T(8,128)(2,1)} %collective-permute-done.10.refs_3_, ...), custom_call_target="tpu_custom_call" | custom-call | flops 1048576 | bytes 1024 | tf_op jit(solution)/shard_map/pallas_call | solution.py:64
  81.8 5.3 %shard_map.109 = (bf16[4,2,192,1024]{3,2,1,0:T(8,128)(2,1)S(1)}, f32[8,128]{1,0:T(8,128)S(1)}) custom-call(s32[2]{0:T(128)S(1)} %pad_add_fusion.refs_0_, bf16[768,512]{1,0:T(8,128)(2,1)} %shard_map.104.refs_2_.refs_4_.refs_1_, bf16[768,512]{1,0:T(8,128)(2,1)} %shard_map.106.refs_3_.refs_2_, bf16[768,512]{1,0:T(8,128)(2,1)} %collective-permute-done.10.refs_3_, ...), custom_call_target="tpu_custom_call" | custom-call | flops 1048576 | bytes 1024 | tf_op jit(solution)/shard_map/pallas_call | solution.py:64
  87.3 3.5 %collective-permute-start.14 = (bf16[384,512]{1,0:T(8,128)(2,1)S(1)}, bf16[384,512]{1,0:T(8,128)(2,1)S(1)}, u32[]{:S(2)}, u32[]{:S(2)}) collective-permute-start(bf16[384,512]{1,0:T(8,128)(2,1)S(1)} %get-tuple-element.32), channel_id=1, source_target_pairs={{0,96},{32,0},{64,32},{96,64},{1,97},{33,1},{65,33},{97,65},{2,98}... | collective-permute-start | bytes 1179656 | tf_op jit(solution)/shard_map/ppermute | solution.py:29
  90.8 5.9 %shard_map.110 = (bf16[768,512]{1,0:T(8,128)(2,1)S(1)}, f32[768,512]{1,0:T(8,128)S(1)}, f32[2,64,512]{2,1,0:T(8,128)S(1)}) custom-call(s32[2]{0:T(128)S(1)} %pad_add_fusion.refs_0_, bf16[4,2,192,1024]{3,2,1,0:T(8,128)(2,1)S(1)} %bitcast.111, bf16[2,512,1024]{2,1,0:T(8,128)(2,1)S(1)} %copy-done.2, bf16[2,768,512]{2,1,0:T(8,128)(2,1)S(1)} %collective-permute-done.9.refs_3_, ...), custom_call_target="tpu_custom_call" | custom-call | flops 1048576 | bytes 1024 | tf_op jit(solution)/shard_map/pallas_call | solution.py:64
  98.2 2.0 %collective-permute-done.13.refs_2_ = bf16[384,512]{1,0:T(8,128)(2,1)S(1)} collective-permute-done((bf16[384,512]{1,0:T(8,128)(2,1)S(1)}, bf16[384,512]{1,0:T(8,128)(2,1)S(1)}, u32[]{:S(2)}, u32[]{:S(2)}) %collective-permute-start.13) | collective-permute-done | bytes 393248 | tf_op jit(solution)/shard_map/ppermute | solution.py:29
  103.1 4.0 %collective-permute-done.18 = bf16[2,32,512]{2,1,0:T(8,128)(2,1)S(1)} collective-permute-done((bf16[2,32,512]{2,1,0:T(8,128)(2,1)S(1)}, bf16[2,32,512]{2,1,0:T(8,128)(2,1)S(1)}, u32[]{:S(2)}, u32[]{:S(2)}) %collective-permute-start.18) | collective-permute-done | bytes 65568 | tf_op jit(solution)/shard_map/ppermute | solution.py:294
  109.0 2.7 %collective-permute-done.19 = bf16[2,32,512]{2,1,0:T(8,128)(2,1)S(1)} collective-permute-done((bf16[2,32,512]{2,1,0:T(8,128)(2,1)S(1)}, bf16[2,32,512]{2,1,0:T(8,128)(2,1)S(1)}, u32[]{:S(2)}, u32[]{:S(2)}) %collective-permute-start.19) | collective-permute-done | bytes 65568 | tf_op jit(solution)/shard_map/ppermute | solution.py:294
  111.7 7.6 %collective-permute-start.20 = (bf16[2,32,512]{2,1,0:T(8,128)(2,1)S(1)}, bf16[2,32,512]{2,1,0:T(8,128)(2,1)S(1)}, u32[]{:S(2)}, u32[]{:S(2)}) collective-permute-start(bf16[2,32,512]{2,1,0:T(8,128)(2,1)S(1)} %add_convert_fusion.refs_5_.refs_1_), channel_id=1, source_target_pairs={{0,16},{4,20},{8,24},{12,28},{16,0},{20,4},{24,8},{28,12},{1,17},{... | collective-permute-start | bytes 196616 | tf_op jit(solution)/shard_map/ppermute | solution.py:294
  123.9 3.5 %all-to-all-start.1 = ((bf16[4,192,512]{2,1,0:T(8,128)(2,1)}), bf16[4,192,512]{2,1,0:T(8,128)(2,1)S(1)}, u32[]{:S(2)}, u32[]{:S(2)}) async-start(bf16[4,192,512]{2,1,0:T(8,128)(2,1)} %bitcast.26), calls=%async_computation.1 | async-start | bytes 1572864 | tf_op jit(solution)/shard_map/all_to_all | solution.py:21
  127.5 2.4 %collective-permute-start.22 = (f32[32,512]{1,0:T(8,128)S(1)}, f32[32,512]{1,0:T(8,128)S(1)}, u32[]{:S(2)}, u32[]{:S(2)}) collective-permute-start(f32[32,512]{1,0:T(8,128)S(1)} %fusion.12.refs_1_), channel_id=1, source_target_pairs={{0,128},{128,0},{1,129},{129,1},{2,130},{130,2},{3,131},{131,3},{4... | collective-permute-start | bytes 196616 | tf_op jit(solution)/shard_map/ppermute | solution.py:17
  132.2 3.6 %all-to-all-done.1.refs_3_ = bf16[4,192,512]{2,1,0:T(8,128)(2,1)S(1)} async-done(((bf16[4,192,512]{2,1,0:T(8,128)(2,1)}), bf16[4,192,512]{2,1,0:T(8,128)(2,1)S(1)}, u32[]{:S(2)}, u32[]{:S(2)}) %all-to-all-start.1) | async-done | bytes 786464 | tf_op jit(solution)/shard_map/all_to_all | solution.py:21
  137.5 4.2 %all-to-all-start.2 = ((bf16[4,32,512]{2,1,0:T(8,128)(2,1)}), bf16[4,32,512]{2,1,0:T(8,128)(2,1)S(1)}, u32[]{:S(2)}, u32[]{:S(2)}) async-start(bf16[4,32,512]{2,1,0:T(8,128)(2,1)} %broadcast_in_dim.34), calls=%async_computation.3 | async-start | bytes 262144 | tf_op jit(solution)/shard_map/all_to_all | solution.py:21
  141.7 2.5 %fusion.1 = bf16[384,1024]{1,0:T(8,128)(2,1)} fusion(bf16[384,1024]{1,0:T(8,128)(2,1)S(1)} %collective-permute-done.17.refs_4_, bf16[384,1024]{1,0:T(8,128)(2,1)S(1)} %collective-permute-done.16.refs_3_, bf16[4,384,1024]{2,1,0:T(8,128)(2,1)} %bitcast.116, s32[]{:T(128)S(6)} %select_n.128), kind=kLoop, calls=%fused_computation.2 | loop fusion | flops 2359296 | bytes 3145732 | tf_op jit(solution)/shard_map/convert_element_type | solution.py:322
  144.2 6.8 %collective-permute-start.24 = (bf16[2,192,512]{2,1,0:T(8,128)(2,1)S(1)}, bf16[2,192,512]{2,1,0:T(8,128)(2,1)S(1)}, u32[]{:S(2)}, u32[]{:S(2)}) collective-permute-start(bf16[2,192,512]{2,1,0:T(8,128)(2,1)S(1)} %shard_map.115), channel_id=1, source_target_pairs={{0,1},{1,0},{2,3},{3,2},{4,5},{5,4},{6,7},{7,6},{8,9},{9,8},{10,11... | collective-permute-start | bytes 1179656 | tf_op jit(solution)/shard_map/ppermute | solution.py:17
  151.0 3.4 %collective-permute-start.25 = (bf16[2,32,512]{2,1,0:T(8,128)(2,1)S(1)}, bf16[2,32,512]{2,1,0:T(8,128)(2,1)S(1)}, u32[]{:S(2)}, u32[]{:S(2)}) collective-permute-start(bf16[2,32,512]{2,1,0:T(8,128)(2,1)S(1)} %dynamic-slice_bitcast_fusion.4), channel_id=1, source_target_pairs={{0,1},{1,0},{2,3},{3,2},{4,5},{5,4},{6,7},{7,6},{8,9},{9,8},{10,11... | collective-permute-start | bytes 196616 | tf_op jit(solution)/shard_map/ppermute | solution.py:17
  (124 shorter events, 47.2 us)
Async XLA Ops:
  7.2 60.5 %all-gather.2.cloned.1.call-start = ((), (), s32[]{:S(2)}) async-start(), calls=%async_computation.4 | async-start | bytes 2359296 | tf_op jit(solution)/shard_map/all_gather | solution.py:245
  8.3 10.1 %collective-permute-start.5 = (bf16[192,1024]{1,0:T(8,128)(2,1)S(1)}, bf16[192,1024]{1,0:T(8,128)(2,1)S(1)}, u32[]{:S(2)}, u32[]{:S(2)}) collective-permute-start(bf16[192,1024]{1,0:T(8,128)(2,1)S(1)} %dynamic-slice_bitcast_fusion.1), channel_id=1, source_target_pairs={{0,1},{1,0},{2,3},{3,2},{4,5},{5,4},{6,7},{7,6},{8,9},{9,8},{10,11... | collective-permute-start | bytes 1179656 | tf_op jit(solution)/shard_map/ppermute | solution.py:17
  11.7 6.8 %collective-permute-start.4 = (bf16[64,1024]{1,0:T(8,128)(2,1)}, bf16[64,1024]{1,0:T(8,128)(2,1)S(1)}, u32[]{:S(2)}, u32[]{:S(2)}) collective-permute-start(bf16[64,1024]{1,0:T(8,128)(2,1)} %refs_1_.1), channel_id=1, source_target_pairs={{0,128},{128,0},{1,129},{129,1},{2,130},{130,2},{3,131},{131,3},{4... | collective-permute-start | bytes 393224 | tf_op jit(solution)/shard_map/ppermute | solution.py:17
  21.4 16.5 %all-to-all-start = ((bf16[4,208,512]{2,1,0:T(8,128)(2,1)}), bf16[4,208,512]{2,1,0:T(8,128)(2,1)}, u32[]{:S(2)}, u32[]{:S(2)}) async-start(bf16[4,208,512]{2,1,0:T(8,128)(2,1)} %pad_maximum_fusion), calls=%async_computation | async-start | bytes 1703936 | tf_op jit(solution)/shard_map/all_to_all | solution.py:21
  25.7 104.3 %reduce-scatter.2.cloned.1.call-start = ((), (), s32[]{:S(2)}) async-start(), calls=%async_computation.5 | async-start | bytes 2359296 | tf_op jit(solution)/shard_map/reduce_scatter | solution.py:287
  25.7 28.7 %collective-permute-start = (bf16[384,1024]{1,0:T(8,128)(2,1)}, bf16[384,1024]{1,0:T(8,128)(2,1)}, u32[]{:S(2)}, u32[]{:S(2)}) collective-permute-start(bf16[384,1024]{1,0:T(8,128)(2,1)} %bitcast.4), channel_id=1, source_target_pairs={{0,32},{32,64},{64,96},{96,0},{1,33},{33,65},{65,97},{97,1},{2,34}... | collective-permute-start | bytes 2359304 | tf_op jit(solution)/shard_map/ppermute | solution.py:29
  27.1 28.5 %collective-permute-start.1 = (bf16[384,1024]{1,0:T(8,128)(2,1)}, bf16[384,1024]{1,0:T(8,128)(2,1)}, u32[]{:S(2)}, u32[]{:S(2)}) collective-permute-start(bf16[384,1024]{1,0:T(8,128)(2,1)} %bitcast.4), channel_id=1, source_target_pairs={{0,96},{32,0},{64,32},{96,64},{1,97},{33,1},{65,33},{97,65},{2,98}... | collective-permute-start | bytes 2359304 | tf_op jit(solution)/shard_map/ppermute | solution.py:29
  28.5 9.9 %collective-permute-start.7 = (bf16[64,1024]{1,0:T(8,128)(2,1)S(1)}, bf16[64,1024]{1,0:T(8,128)(2,1)S(1)}, u32[]{:S(2)}, u32[]{:S(2)}) collective-permute-start(bf16[64,1024]{1,0:T(8,128)(2,1)S(1)} %copy-done.5), channel_id=1, source_target_pairs={{0,1},{1,0},{2,3},{3,2},{4,5},{5,4},{6,7},{7,6},{8,9},{9,8},{10,11... | collective-permute-start | bytes 393224 | tf_op jit(solution)/shard_map/ppermute | solution.py:17
  37.9 23.7 %collective-permute-start.6 = (bf16[4,208,512]{2,1,0:T(8,128)(2,1)}, bf16[4,208,512]{2,1,0:T(8,128)(2,1)}, u32[]{:S(2)}, u32[]{:S(2)}) collective-permute-start(bf16[4,208,512]{2,1,0:T(8,128)(2,1)} %all-to-all-done.refs_1_.refs_4_), channel_id=1, source_target_pairs={{0,2},{2,0},{1,3},{3,1},{4,6},{6,4},{5,7},{7,5},{8,10},{10,8},{9,1... | collective-permute-start | bytes 2555912 | tf_op jit(solution)/shard_map/ppermute | solution.py:17
  42.6 19.1 %collective-permute-start.8 = (f32[64,512]{1,0:T(8,128)S(1)}, f32[64,512]{1,0:T(8,128)S(1)}, u32[]{:S(2)}, u32[]{:S(2)}) collective-permute-start(f32[64,512]{1,0:T(8,128)S(1)} %shard_map.105), channel_id=1, source_target_pairs={{0,2},{2,0},{1,3},{3,1},{4,6},{6,4},{5,7},{7,5},{8,10},{10,8},{9,1... | collective-permute-start | bytes 393224 | tf_op jit(solution)/shard_map/ppermute | solution.py:17
  55.5 12.1 %collective-permute-start.2 = (bf16[384,512]{1,0:T(8,128)(2,1)S(1)}, bf16[384,512]{1,0:T(8,128)(2,1)S(1)}, u32[]{:S(2)}, u32[]{:S(2)}) collective-permute-start(bf16[384,512]{1,0:T(8,128)(2,1)S(1)} %slice.42), channel_id=1, source_target_pairs={{0,32},{32,64},{64,96},{96,0},{1,33},{33,65},{65,97},{97,1},{2,34}... | collective-permute-start | bytes 1179656 | tf_op jit(solution)/shard_map/ppermute | solution.py:29
  56.6 11.0 %collective-permute-start.3 = (bf16[384,512]{1,0:T(8,128)(2,1)S(1)}, bf16[384,512]{1,0:T(8,128)(2,1)S(1)}, u32[]{:S(2)}, u32[]{:S(2)}) collective-permute-start(bf16[384,512]{1,0:T(8,128)(2,1)S(1)} %slice.43), channel_id=1, source_target_pairs={{0,96},{32,0},{64,32},{96,64},{1,97},{33,1},{65,33},{97,65},{2,98}... | collective-permute-start | bytes 1179656 | tf_op jit(solution)/shard_map/ppermute | solution.py:29
  59.4 12.9 %collective-permute-start.10 = (bf16[768,512]{1,0:T(8,128)(2,1)}, bf16[768,512]{1,0:T(8,128)(2,1)}, u32[]{:S(2)}, u32[]{:S(2)}) collective-permute-start(bf16[768,512]{1,0:T(8,128)(2,1)} %shard_map.104.refs_2_.refs_4_.refs_1_), channel_id=1, source_target_pairs={{0,1},{1,0},{2,3},{3,2},{4,5},{5,4},{6,7},{7,6},{8,9},{9,8},{10,11... | collective-permute-start | bytes 2359304 | tf_op jit(solution)/shard_map/ppermute | solution.py:17
  64.5 7.8 %collective-permute-start.11 = (bf16[768,512]{1,0:T(8,128)(2,1)}, bf16[768,512]{1,0:T(8,128)(2,1)}, u32[]{:S(2)}, u32[]{:S(2)}) collective-permute-start(bf16[768,512]{1,0:T(8,128)(2,1)} %shard_map.106.refs_3_.refs_2_), channel_id=1, source_target_pairs={{0,1},{1,0},{2,3},{3,2},{4,5},{5,4},{6,7},{7,6},{8,9},{9,8},{10,11... | collective-permute-start | bytes 2359304 | tf_op jit(solution)/shard_map/ppermute | solution.py:17
  79.0 11.7 %collective-permute-start.9 = (bf16[2,768,512]{2,1,0:T(8,128)(2,1)}, bf16[2,768,512]{2,1,0:T(8,128)(2,1)S(1)}, u32[]{:S(2)}, u32[]{:S(2)}) collective-permute-start(bf16[2,768,512]{2,1,0:T(8,128)(2,1)} %copy-done.7), channel_id=1, source_target_pairs={{0,1},{1,0},{2,3},{3,2},{4,5},{5,4},{6,7},{7,6},{8,9},{9,8},{10,11... | collective-permute-start | bytes 4718600 | tf_op jit(solution)/shard_map/ppermute | solution.py:17
  87.2 13.0 %collective-permute-start.13 = (bf16[384,512]{1,0:T(8,128)(2,1)S(1)}, bf16[384,512]{1,0:T(8,128)(2,1)S(1)}, u32[]{:S(2)}, u32[]{:S(2)}) collective-permute-start(bf16[384,512]{1,0:T(8,128)(2,1)S(1)} %get-tuple-element.33), channel_id=1, source_target_pairs={{0,32},{32,64},{64,96},{96,0},{1,33},{33,65},{65,97},{97,1},{2,34}... | collective-permute-start | bytes 1179656 | tf_op jit(solution)/shard_map/ppermute | solution.py:29
  87.3 12.9 %collective-permute-start.14 = (bf16[384,512]{1,0:T(8,128)(2,1)S(1)}, bf16[384,512]{1,0:T(8,128)(2,1)S(1)}, u32[]{:S(2)}, u32[]{:S(2)}) collective-permute-start(bf16[384,512]{1,0:T(8,128)(2,1)S(1)} %get-tuple-element.32), channel_id=1, source_target_pairs={{0,96},{32,0},{64,32},{96,64},{1,97},{33,1},{65,33},{97,65},{2,98}... | collective-permute-start | bytes 1179656 | tf_op jit(solution)/shard_map/ppermute | solution.py:29
  97.1 22.3 %collective-permute-start.12 = (bf16[768,512]{1,0:T(8,128)(2,1)S(1)}, bf16[768,512]{1,0:T(8,128)(2,1)S(1)}, u32[]{:S(2)}, u32[]{:S(2)}) collective-permute-start(bf16[768,512]{1,0:T(8,128)(2,1)S(1)} %get-tuple-element.20), channel_id=1, source_target_pairs={{0,2},{2,0},{1,3},{3,1},{4,6},{6,4},{5,7},{7,5},{8,10},{10,8},{9,1... | collective-permute-start | bytes 2359304 | tf_op jit(solution)/shard_map/ppermute | solution.py:17
  100.4 19.9 %collective-permute-start.16 = (bf16[384,1024]{1,0:T(8,128)(2,1)S(1)}, bf16[384,1024]{1,0:T(8,128)(2,1)S(1)}, u32[]{:S(2)}, u32[]{:S(2)}) collective-permute-start(bf16[384,1024]{1,0:T(8,128)(2,1)S(1)} %get-tuple-element.23), channel_id=1, source_target_pairs={{0,32},{32,64},{64,96},{96,0},{1,33},{33,65},{65,97},{97,1},{2,34}... | collective-permute-start | bytes 2359304 | tf_op jit(solution)/shard_map/ppermute | solution.py:29
  101.2 19.1 %collective-permute-start.17 = (bf16[384,1024]{1,0:T(8,128)(2,1)S(1)}, bf16[384,1024]{1,0:T(8,128)(2,1)S(1)}, u32[]{:S(2)}, u32[]{:S(2)}) collective-permute-start(bf16[384,1024]{1,0:T(8,128)(2,1)S(1)} %get-tuple-element.24), channel_id=1, source_target_pairs={{0,96},{32,0},{64,32},{96,64},{1,97},{33,1},{65,33},{97,65},{2,98}... | collective-permute-start | bytes 2359304 | tf_op jit(solution)/shard_map/ppermute | solution.py:29
  111.7 10.4 %collective-permute-start.20 = (bf16[2,32,512]{2,1,0:T(8,128)(2,1)S(1)}, bf16[2,32,512]{2,1,0:T(8,128)(2,1)S(1)}, u32[]{:S(2)}, u32[]{:S(2)}) collective-permute-start(bf16[2,32,512]{2,1,0:T(8,128)(2,1)S(1)} %add_convert_fusion.refs_5_.refs_1_), channel_id=1, source_target_pairs={{0,16},{4,20},{8,24},{12,28},{16,0},{20,4},{24,8},{28,12},{1,17},{... | collective-permute-start | bytes 196616 | tf_op jit(solution)/shard_map/ppermute | solution.py:294
  123.9 11.8 %all-to-all-start.1 = ((bf16[4,192,512]{2,1,0:T(8,128)(2,1)}), bf16[4,192,512]{2,1,0:T(8,128)(2,1)S(1)}, u32[]{:S(2)}, u32[]{:S(2)}) async-start(bf16[4,192,512]{2,1,0:T(8,128)(2,1)} %bitcast.26), calls=%async_computation.1 | async-start | bytes 1572864 | tf_op jit(solution)/shard_map/all_to_all | solution.py:21
  137.5 13.5 %all-to-all-start.2 = ((bf16[4,32,512]{2,1,0:T(8,128)(2,1)}), bf16[4,32,512]{2,1,0:T(8,128)(2,1)S(1)}, u32[]{:S(2)}, u32[]{:S(2)}) async-start(bf16[4,32,512]{2,1,0:T(8,128)(2,1)} %broadcast_in_dim.34), calls=%async_computation.3 | async-start | bytes 262144 | tf_op jit(solution)/shard_map/all_to_all | solution.py:21
  144.2 12.2 %collective-permute-start.24 = (bf16[2,192,512]{2,1,0:T(8,128)(2,1)S(1)}, bf16[2,192,512]{2,1,0:T(8,128)(2,1)S(1)}, u32[]{:S(2)}, u32[]{:S(2)}) collective-permute-start(bf16[2,192,512]{2,1,0:T(8,128)(2,1)S(1)} %shard_map.115), channel_id=1, source_target_pairs={{0,1},{1,0},{2,3},{3,2},{4,5},{5,4},{6,7},{7,6},{8,9},{9,8},{10,11... | collective-permute-start | bytes 1179656 | tf_op jit(solution)/shard_map/ppermute | solution.py:17
  (20 other events, 118.0 us)
Sparse Core Ops, SparseCore 0:
  20.2 38.9 all-gather.1
  79.2 40.7 reduce-scatter.1
